TPU v7x, 32 devices: a whole 2x2x4 slice. The times are simulated.
32 devices in a mesh: dp: 8 (over z, x), expert: 4 (over y, core).
Axes of the slice: x: 2, y: 2, z: 4, core: 2. Of those that a mesh axis runs over, the one named last changes fastest.
Arguments:
- tokens: bfloat16 [32, 1024, 1024], P(('dp', 'expert')), may hold values from -6 to 6
- cotangent: bfloat16 [32, 1024, 1024], P(('dp', 'expert')), may hold values from -6 to 6
- routes: int32 [32, 1024, 8], P(('dp', 'expert')), may hold values from 0 to 15, all different within a row; in each aligned block of 1024 rows (0 to 1023, 1024 to 2047, ..., all dimensions but the last counted through in order) at most 576 rows name the same one
- prefix: int32 [32], P(('dp', 'expert')), may hold values from 102 to 512
- w_query: bfloat16 [1024, 1024], P('dp'), may hold values from -0.1875 to 0.1875
- keyvalue_weight: bfloat16 [1024, 1024], P('dp'), may hold values from -0.1875 to 0.1875
- w_out: bfloat16 [1024, 1024], P('dp'), may hold values from -3 to 3
- w_router: bfloat16 [1024, 16], P('dp'), may hold values from -0.09375 to 0.09375
- gain_attn: bfloat16 [1024], P('dp'), may hold values from 0.5 to 1.5
- gain_mlp: bfloat16 [1024], P('dp'), may hold values from 0.5 to 1.5
- expert_gate: bfloat16 [16, 1024, 512], P('expert'), may hold values from -0.1875 to 0.1875
- expert_up: bfloat16 [16, 1024, 512], P('expert'), may hold values from -0.1875 to 0.1875
- expert_down: bfloat16 [16, 512, 1024], P('expert'), may hold values from -0.75 to 0.75
- query_logit_cap: float32 [16], replicated, may hold values from 3.5 to 8
Outputs:
- block_out: bfloat16 [32, 1024, 1024], P(('dp', 'expert'))
- grad_tokens: float32 [32, 1024, 1024], P(('dp', 'expert'))
- grad_query: float32 [1024, 1024], P('dp')
- grad_keyval: float32 [1024, 1024], P('dp')
- grad_out: float32 [1024, 1024], P('dp')
- grad_router: float32 [1024, 16], P('dp')
- grad_gain_attn: float32 [1024], P('dp')
- grad_gain_mlp: float32 [1024], P('dp')
- grad_gate: float32 [16, 1024, 512], P('expert', 'dp')
- grad_up: float32 [16, 1024, 512], P('expert', 'dp')
- grad_down: float32 [16, 512, 1024], P('expert', 'dp')
- clipped_query: bfloat16 [1024, 1024], P('dp')
- clipped_keyval: bfloat16 [1024, 1024], P('dp')
- head_logit_peak: float32 [16], replicated
Inputs may be any that keep to these rules, and one draw needn't show every extreme that they name: `routes`: each token names 8 different experts; among the 1024 tokens of one device (aligned blocks of 1 sequence) no expert is named more than 576 times, a bound that some block reaches.
All inputs are finite; a program needn't handle non-finite values.
Results may differ from a plain program's by a relative error of at most 0.022.
Values may be sent and summed in bfloat16 or wider, within the bound.
A program may use at most 512 MiB of HBM per device.

v0:
```python
import jax
import jax.numpy as jnp
from jax import lax
from jax.sharding import PartitionSpec as P

epsilon = 1e-05
rope_base = 10000.0


def rope_tables(length, head_size):
    half_size = head_size // 2
    frequency = rope_base ** (-(jnp.arange(half_size, dtype=jnp.float32) * 2.0 / head_size))
    angles = jnp.arange(length, dtype=jnp.float32)[:, None] * frequency[None, :]
    return (jnp.cos(angles), jnp.sin(angles))


def rotate(values_in, cosine, sine_part):
    half_size = values_in.shape[-1] // 2
    first_half = values_in[..., :half_size]
    second_half = values_in[..., half_size:]
    cos_cols = cosine[:, None, :]
    sin_cols = sine_part[:, None, :]
    return jnp.concatenate(
        [
            first_half * cos_cols - second_half * sin_cols,
            first_half * sin_cols + second_half * cos_cols,
        ],
        axis=-1,
    )


def norm_rows(values_in, gain_vec):
    return (
        values_in
        * lax.rsqrt(jnp.mean(values_in * values_in, axis=-1, keepdims=True) + epsilon)
        * gain_vec
    )


def norm_back(values_in, gain_vec, grad_rows):
    inv_rms = lax.rsqrt(jnp.mean(values_in * values_in, axis=-1, keepdims=True) + epsilon)
    gain_grad = jnp.sum(grad_rows * values_in * inv_rms, axis=0)
    scaled = grad_rows * gain_vec
    cubed = inv_rms * inv_rms * inv_rms
    return (
        inv_rms * scaled - values_in * cubed * jnp.mean(scaled * values_in, axis=-1, keepdims=True),
        gain_grad,
    )


def route_layout(route_flat, num_experts, capacity, top_count, local_experts, owners):
    one_hot = (route_flat[:, None] == jnp.arange(num_experts, dtype=jnp.int32)[None, :]).astype(
        jnp.int32
    )
    rank_in = jnp.sum((jnp.cumsum(one_hot, axis=0) - one_hot) * one_hot, axis=1)
    slot_index = route_flat * capacity + rank_in
    fillers = (
        jnp.zeros((num_experts * capacity,), jnp.int32)
        .at[slot_index]
        .set(jnp.arange(route_flat.shape[0], dtype=jnp.int32) + 1)
    )
    owner_of = route_flat.reshape(-1, top_count) // local_experts
    owner_hit = jnp.max(
        (owner_of[:, :, None] == jnp.arange(owners, dtype=jnp.int32)[None, None, :]).astype(
            jnp.int32
        ),
        axis=1,
    )
    pair_rank = jnp.cumsum(owner_hit, axis=0) - owner_hit
    return (slot_index, fillers, owner_hit, pair_rank)


def attend_forward(queries, keys_rot, values_low, prefix_len):
    length, num_heads, head_size = queries.shape
    kv_heads = keys_rot.shape[1]
    queries_per_group = num_heads // kv_heads
    block_rows = min(512, length)
    inv_root = head_size ** (-0.5)
    grouped = queries.reshape(length, kv_heads, queries_per_group, head_size)
    key_pos = jnp.arange(length, dtype=jnp.int32)[None, :]
    contexts = []
    spreads = []
    head_peaks = []
    for offset in range(0, length, block_rows):
        q_block = grouped[offset : offset + block_rows]
        query_pos = offset + jnp.arange(block_rows, dtype=jnp.int32)[:, None]
        allowed = (key_pos <= query_pos) | (key_pos < prefix_len)
        scores = (
            jnp.einsum("qhgd,phd->hgqp", q_block, keys_rot, preferred_element_type=jnp.float32)
            * inv_root
        )
        masked = jnp.where(allowed, scores, -1e30)
        row_max = jnp.max(masked, axis=-1, keepdims=True)
        raw_weights = jnp.exp(masked - row_max)
        row_total = jnp.sum(raw_weights, axis=-1, keepdims=True)
        weights = (raw_weights / row_total).astype(jnp.bfloat16)
        context = jnp.einsum(
            "hgqp,phd->qhgd", weights, values_low, preferred_element_type=jnp.float32
        )
        contexts.append(context.reshape(block_rows, num_heads * head_size))
        spreads.append((row_max + jnp.log(row_total))[..., 0])
        head_peaks.append(jnp.max(row_max[..., 0], axis=-1).reshape(num_heads))
    return (
        jnp.concatenate(contexts, axis=0),
        jnp.concatenate(spreads, axis=-1),
        jnp.max(jnp.stack(head_peaks), axis=0),
    )


def attend_backward(queries, keys_rot, values_low, prefix_len, d_context, spreads):
    length, num_heads, head_size = queries.shape
    kv_heads = keys_rot.shape[1]
    queries_per_group = num_heads // kv_heads
    block_rows = min(512, length)
    inv_root = head_size ** (-0.5)
    grouped = queries.reshape(length, kv_heads, queries_per_group, head_size)
    d_grouped = d_context.reshape(length, kv_heads, queries_per_group, head_size)
    key_pos = jnp.arange(length, dtype=jnp.int32)[None, :]
    d_queries = []
    d_keys = jnp.zeros(keys_rot.shape, jnp.float32)
    d_values = jnp.zeros(values_low.shape, jnp.float32)
    for offset in range(0, length, block_rows):
        q_block = grouped[offset : offset + block_rows]
        grad_block = d_grouped[offset : offset + block_rows]
        query_pos = offset + jnp.arange(block_rows, dtype=jnp.int32)[:, None]
        allowed = (key_pos <= query_pos) | (key_pos < prefix_len)
        scores = (
            jnp.einsum("qhgd,phd->hgqp", q_block, keys_rot, preferred_element_type=jnp.float32)
            * inv_root
        )
        masked = jnp.where(allowed, scores, -1e30)
        weights = jnp.exp(masked - spreads[:, :, offset : offset + block_rows, None])
        low_weights = weights.astype(jnp.bfloat16)
        d_weights = jnp.einsum(
            "qhgd,phd->hgqp", grad_block, values_low, preferred_element_type=jnp.float32
        )
        row_dot = jnp.sum(weights * d_weights, axis=-1, keepdims=True)
        d_scores = (weights * (d_weights - row_dot)).astype(jnp.bfloat16)
        d_queries.append(
            jnp.einsum("hgqp,phd->qhgd", d_scores, keys_rot, preferred_element_type=jnp.float32)
            * inv_root
        )
        d_keys = (
            d_keys
            + jnp.einsum("hgqp,qhgd->phd", d_scores, q_block, preferred_element_type=jnp.float32)
            * inv_root
        )
        d_values = d_values + jnp.einsum(
            "hgqp,qhgd->phd", low_weights, grad_block, preferred_element_type=jnp.float32
        )
    d_query_all = jnp.concatenate(d_queries, axis=0).reshape(length, num_heads, head_size)
    return (d_query_all, d_keys, d_values)


def forward_pack(operands):
    return attend_forward(operands[0], operands[1], operands[2], operands[3])


def backward_pack(operands):
    return attend_backward(
        operands[0], operands[1], operands[2], operands[3], operands[4], operands[5]
    )


def on_device(
    tokens,
    cotangent,
    routes,
    prefix,
    w_query,
    keyvalue_weight,
    w_out,
    w_router,
    gain_attn,
    gain_mlp,
    expert_gate,
    expert_up,
    expert_down,
    query_logit_cap,
):
    full_query, full_keyval, full_out, full_router, full_gain_one, full_gain_two = (
        lax.all_gather(w_query, "dp", axis=0, tiled=True),
        lax.all_gather(keyvalue_weight, "dp", axis=0, tiled=True),
        lax.all_gather(w_out, "dp", axis=0, tiled=True),
        lax.all_gather(w_router, "dp", axis=0, tiled=True),
        lax.all_gather(gain_attn, "dp", axis=0, tiled=True),
        lax.all_gather(gain_mlp, "dp", axis=0, tiled=True),
    )
    sequence_count, length, model_width = tokens.shape
    num_rows = sequence_count * length
    num_heads = query_logit_cap.shape[0]
    head_size = full_query.shape[1] // num_heads
    kv_heads = full_keyval.shape[1] // (2 * head_size)
    queries_per_group = num_heads // kv_heads
    key_split = kv_heads * head_size
    num_experts = full_router.shape[1]
    top_count = routes.shape[2]
    local_experts = expert_gate.shape[0]
    owners = num_experts // local_experts
    capacity = num_rows * top_count * 9 // (num_experts * 8)
    cosine, sine_part = rope_tables(length, head_size)
    resid_in = tokens.astype(jnp.float32).reshape(num_rows, model_width)
    gain_one = full_gain_one.astype(jnp.float32)
    gain_two = full_gain_two.astype(jnp.float32)
    attention_normed = norm_rows(resid_in, gain_one).astype(jnp.bfloat16)
    query_raw = jnp.dot(attention_normed, full_query, preferred_element_type=jnp.float32).reshape(
        sequence_count, length, num_heads, head_size
    )
    unrotated_keyval = jnp.dot(attention_normed, full_keyval, preferred_element_type=jnp.float32)
    queries = rotate(query_raw, cosine, sine_part).astype(jnp.bfloat16)
    keys_rot = rotate(
        unrotated_keyval[:, :key_split].reshape(sequence_count, length, kv_heads, head_size),
        cosine,
        sine_part,
    ).astype(jnp.bfloat16)
    values_low = (
        unrotated_keyval[:, key_split:]
        .reshape(sequence_count, length, kv_heads, head_size)
        .astype(jnp.bfloat16)
    )
    contexts, spreads, head_peaks = lax.map(forward_pack, (queries, keys_rot, values_low, prefix))
    context_low = contexts.reshape(num_rows, num_heads * head_size).astype(jnp.bfloat16)
    attn_out = jnp.dot(context_low, full_out, preferred_element_type=jnp.float32)
    resid_mid = resid_in + attn_out
    normed_two = norm_rows(resid_mid, gain_two).astype(jnp.bfloat16)
    logits = jnp.dot(normed_two, full_router, preferred_element_type=jnp.float32)
    route_rows = routes.reshape(num_rows, top_count)
    pick_mask = route_rows[:, :, None] == jnp.arange(num_experts, dtype=jnp.int32)[None, None, :]
    chosen = jnp.sum(jnp.where(pick_mask, logits[:, None, :], 0.0), axis=-1)
    gate_probs = jax.nn.softmax(chosen, axis=-1)
    route_flat = route_rows.reshape(-1)
    slot_index, fillers, owner_hit, pair_rank = route_layout(
        route_flat, num_experts, capacity, top_count, local_experts, owners
    )
    slot_used = (fillers > 0)[:, None]
    route_pick = jnp.maximum(fillers - 1, 0)
    send_rows = jnp.where(
        slot_used, normed_two[route_pick // top_count], jnp.zeros((), jnp.bfloat16)
    ).reshape(owners, local_experts, capacity, model_width)
    received = lax.all_to_all(send_rows, "expert", split_axis=0, concat_axis=0, tiled=True)
    gate_pre = jnp.einsum(
        "secd,edf->secf", received, expert_gate, preferred_element_type=jnp.float32
    )
    up_pre = jnp.einsum("secd,edf->secf", received, expert_up, preferred_element_type=jnp.float32)
    hidden = (jax.nn.silu(gate_pre) * up_pre).astype(jnp.bfloat16)
    result = jnp.einsum(
        "secf,efd->secd", hidden, expert_down, preferred_element_type=jnp.float32
    ).astype(jnp.bfloat16)
    kept_parts = (received, result, gate_pre, up_pre)
    arrived = kept_parts[0]
    expert_res = kept_parts[1]
    returned = lax.all_to_all(
        expert_res, "expert", split_axis=0, concat_axis=0, tiled=True
    ).reshape(num_experts * capacity, model_width)
    route_out = returned[slot_index].reshape(num_rows, top_count, model_width)
    block_sum = resid_mid + jnp.sum(gate_probs[:, :, None] * route_out.astype(jnp.float32), axis=1)
    block_out = block_sum.astype(jnp.bfloat16).reshape(tokens.shape)
    head_logit_peak = lax.pmax(jnp.max(head_peaks, axis=0), ("dp", "expert"))
    d_mixed = cotangent.astype(jnp.float32).reshape(num_rows, model_width)
    d_gates = jnp.sum(d_mixed[:, None, :] * route_out.astype(jnp.float32), axis=-1)
    d_chosen = gate_probs * (d_gates - jnp.sum(gate_probs * d_gates, axis=-1, keepdims=True))
    d_logits = jnp.sum(jnp.where(pick_mask, d_chosen[:, :, None], 0.0), axis=1).astype(jnp.bfloat16)
    d_route = (
        (gate_probs[:, :, None] * d_mixed[:, None, :])
        .astype(jnp.bfloat16)
        .reshape(num_rows * top_count, model_width)
    )
    d_slots = jnp.where(slot_used, d_route[route_pick], jnp.zeros((), jnp.bfloat16)).reshape(
        owners, local_experts, capacity, model_width
    )
    d_arrived = lax.all_to_all(d_slots, "expert", split_axis=0, concat_axis=0, tiled=True)
    gate_pre = kept_parts[2]
    up_pre = kept_parts[3]
    d_hidden = jnp.einsum(
        "secd,efd->secf", d_arrived, expert_down, preferred_element_type=jnp.float32
    )
    sigmoid_gate = jax.nn.sigmoid(gate_pre)
    act_gate = jax.nn.silu(gate_pre)
    hidden = (act_gate * up_pre).astype(jnp.bfloat16)
    d_down_w = jnp.einsum("secf,secd->efd", hidden, d_arrived, preferred_element_type=jnp.float32)
    d_gate_pre = (
        d_hidden * up_pre * sigmoid_gate * (1.0 + gate_pre * (1.0 - sigmoid_gate))
    ).astype(jnp.bfloat16)
    d_up_pre = (d_hidden * act_gate).astype(jnp.bfloat16)
    d_route_in = (
        jnp.einsum("secf,edf->secd", d_gate_pre, expert_gate, preferred_element_type=jnp.float32)
        + jnp.einsum("secf,edf->secd", d_up_pre, expert_up, preferred_element_type=jnp.float32)
    ).astype(jnp.bfloat16)
    d_gate_w = jnp.einsum("secd,secf->edf", arrived, d_gate_pre, preferred_element_type=jnp.float32)
    d_up_w = jnp.einsum("secd,secf->edf", arrived, d_up_pre, preferred_element_type=jnp.float32)
    grad_gate, grad_up, grad_down = (
        lax.psum_scatter(
            d_gate_w.astype(jnp.bfloat16), "dp", scatter_dimension=1, tiled=True
        ).astype(jnp.float32),
        lax.psum_scatter(d_up_w.astype(jnp.bfloat16), "dp", scatter_dimension=1, tiled=True).astype(
            jnp.float32
        ),
        lax.psum_scatter(
            d_down_w.astype(jnp.bfloat16), "dp", scatter_dimension=1, tiled=True
        ).astype(jnp.float32),
    )
    d_returned = lax.all_to_all(
        d_route_in, "expert", split_axis=0, concat_axis=0, tiled=True
    ).reshape(num_experts * capacity, model_width)
    d_normed_two = jnp.sum(
        d_returned[slot_index].reshape(num_rows, top_count, model_width).astype(jnp.float32), axis=1
    ) + jnp.dot(d_logits, full_router.T, preferred_element_type=jnp.float32)
    d_router_w = jnp.einsum("rd,re->de", normed_two, d_logits, preferred_element_type=jnp.float32)
    d_mid_norm, d_gain_two = norm_back(resid_mid, gain_two, d_normed_two)
    d_resid_mid = d_mixed + d_mid_norm
    d_attn = d_resid_mid.astype(jnp.bfloat16)
    d_out_w = jnp.einsum("rc,rd->cd", context_low, d_attn, preferred_element_type=jnp.float32)
    d_context = (
        jnp.dot(d_attn, full_out.T, preferred_element_type=jnp.float32)
        .astype(jnp.bfloat16)
        .reshape(sequence_count, length, num_heads, head_size)
    )
    d_queries, d_keys, d_values = lax.map(
        backward_pack, (queries, keys_rot, values_low, prefix, d_context, spreads)
    )
    d_query_raw = (
        rotate(d_queries, cosine, -sine_part)
        .astype(jnp.bfloat16)
        .reshape(num_rows, num_heads * head_size)
    )
    d_key_raw = rotate(d_keys, cosine, -sine_part).reshape(num_rows, key_split)
    d_keyval = jnp.concatenate([d_key_raw, d_values.reshape(num_rows, key_split)], axis=1).astype(
        jnp.bfloat16
    )
    d_normed_one = jnp.dot(d_query_raw, full_query.T, preferred_element_type=jnp.float32) + jnp.dot(
        d_keyval, full_keyval.T, preferred_element_type=jnp.float32
    )
    d_query_w = jnp.einsum(
        "rd,rc->dc", attention_normed, d_query_raw, preferred_element_type=jnp.float32
    )
    d_keyval_w = jnp.einsum(
        "rd,rc->dc", attention_normed, d_keyval, preferred_element_type=jnp.float32
    )
    d_in_norm, d_gain_one = norm_back(resid_in, gain_one, d_normed_one)
    grad_tokens = (d_resid_mid + d_in_norm).reshape(tokens.shape)
    grad_shares = (
        lax.psum_scatter(
            d_query_w.astype(jnp.bfloat16), "dp", scatter_dimension=0, tiled=True
        ).astype(jnp.float32),
        lax.psum_scatter(
            d_keyval_w.astype(jnp.bfloat16), "dp", scatter_dimension=0, tiled=True
        ).astype(jnp.float32),
        lax.psum_scatter(
            d_out_w.astype(jnp.bfloat16), "dp", scatter_dimension=0, tiled=True
        ).astype(jnp.float32),
        lax.psum_scatter(
            d_router_w.astype(jnp.bfloat16), "dp", scatter_dimension=0, tiled=True
        ).astype(jnp.float32),
        lax.psum_scatter(
            d_gain_one.astype(jnp.bfloat16), "dp", scatter_dimension=0, tiled=True
        ).astype(jnp.float32),
        lax.psum_scatter(
            d_gain_two.astype(jnp.bfloat16), "dp", scatter_dimension=0, tiled=True
        ).astype(jnp.float32),
    )
    grad_shares = (
        lax.psum(grad_shares[0].astype(jnp.bfloat16), "expert").astype(jnp.float32),
        lax.psum(grad_shares[1].astype(jnp.bfloat16), "expert").astype(jnp.float32),
        lax.psum(grad_shares[2].astype(jnp.bfloat16), "expert").astype(jnp.float32),
        lax.psum(grad_shares[3].astype(jnp.bfloat16), "expert").astype(jnp.float32),
        lax.psum(grad_shares[4].astype(jnp.bfloat16), "expert").astype(jnp.float32),
        lax.psum(grad_shares[5].astype(jnp.bfloat16), "expert").astype(jnp.float32),
    )
    query_factor = jnp.sqrt(query_logit_cap / jnp.maximum(head_logit_peak, query_logit_cap))
    paired_logit_peak = jnp.max(head_logit_peak.reshape(kv_heads, queries_per_group), axis=1)
    paired_logit_cap = jnp.min(query_logit_cap.reshape(kv_heads, queries_per_group), axis=1)
    key_rescale = jnp.sqrt(paired_logit_cap / jnp.maximum(paired_logit_peak, paired_logit_cap))
    clipped_query = (
        w_query.astype(jnp.float32) * jnp.repeat(query_factor, head_size)[None, :]
    ).astype(jnp.bfloat16)
    key_column_set = jnp.concatenate(
        [jnp.repeat(key_rescale, head_size), jnp.ones((key_split,), jnp.float32)]
    )
    clipped_keyval = (keyvalue_weight.astype(jnp.float32) * key_column_set[None, :]).astype(
        jnp.bfloat16
    )
    return (
        block_out,
        grad_tokens,
        grad_shares[0],
        grad_shares[1],
        grad_shares[2],
        grad_shares[3],
        grad_shares[4],
        grad_shares[5],
        grad_gate,
        grad_up,
        grad_down,
        clipped_query,
        clipped_keyval,
        head_logit_peak,
    )


def solution(mesh):
    in_specs = (
        P(("dp", "expert"), None, None),
        P(("dp", "expert"), None, None),
        P(("dp", "expert"), None, None),
        P(("dp", "expert")),
        P("dp", None),
        P("dp", None),
        P("dp", None),
        P("dp", None),
        P("dp"),
        P("dp"),
        P("expert", None, None),
        P("expert", None, None),
        P("expert", None, None),
        P(),
    )
    out_specs = (
        P(("dp", "expert"), None, None),
        P(("dp", "expert"), None, None),
        P("dp", None),
        P("dp", None),
        P("dp", None),
        P("dp", None),
        P("dp"),
        P("dp"),
        P("expert", "dp", None),
        P("expert", "dp", None),
        P("expert", "dp", None),
        P("dp", None),
        P("dp", None),
        P(),
    )
    return jax.shard_map(
        on_device, mesh=mesh, in_specs=in_specs, out_specs=out_specs, check_vma=False
    )
```

profile of v0, /device:TPU:0, one launch (start us, length us, event | category | flops | bytes accessed | tf_op | source)
XLA Modules:
  0.0 1804.1 jit_solution(17270148477697069899)
XLA Ops:
  18.5 30.5 %scatter_custom_fusion = s32[9216]{0:T(1024)S(1)} fusion(s32[8192]{0:T(1024)S(1)} %bitcast.339, s32[8192]{0:T(1024)S(1)} %iota_add_fusion, s32[]{:T(128)} %constant.113.clone.1), kind=kCustom, calls=%fused_computation.194 | custom fusion | bytes 36868 | tf_op jit(solution)/shard_map/scatter | solution.py:60
  50.3 22.2 %all-gather = bf16[8,1,128]{2,1,0:T(2,128)(2,1)S(1)} all-gather(bf16[1,1,128]{2,1,0:T(2,128)(2,1)S(1)} %bitcast.353), channel_id=1, replica_groups=mesh['dp'=8,'expert'=4] {'dp'}, dimensions={0}, use_global_device_ids=true | all-gather | bytes 2304 | tf_op jit(solution)/shard_map/all_gather | solution.py:186
  89.3 27.0 %all_gather.23 = bf16[1024,16]{0,1:T(8,128)(2,1)} all-gather(bf16[128,16]{0,1:T(8,128)(2,1)S(1)} %copy-done.71), channel_id=1, replica_groups=mesh['dp'=8,'expert'=4] {'dp'}, dimensions={0}, use_global_device_ids=true | all-gather | bytes 36864 | tf_op jit(solution)/shard_map/all_gather | solution.py:185
  252.2 39.7 %gather_fusion = bf16[9216,1024]{1,0:T(8,128)(2,1)} fusion(bf16[1024,1024]{1,0:T(8,128)(2,1)S(1)} %copy.155, s32[9216]{0:T(1024)S(1)} %copy-done.48), kind=kCustom, calls=%fused_computation | custom fusion | bytes 37785600 | tf_op jit(solution)/shard_map/gather | solution.py:238
  301.4 53.4 %gather_fusion.2 = bf16[9216,1024]{1,0:T(8,128)(2,1)} fusion(bf16[8192,1024]{1,0:T(8,128)(2,1)} %fusion.8, s32[9216]{0:T(1024)S(1)} %copy-done.47), kind=kCustom, calls=%fused_computation.2 | custom fusion | bytes 37785600 | tf_op jit(solution)/shard_map/gather | solution.py:268
  354.8 24.6 %broadcast_select_fusion = (bf16[4,4,576,1024]{3,2,1,0:T(8,128)(2,1)}, bf16[4,4,576,1024]{3,2,1,0:T(8,128)(2,1)}) fusion(bf16[4,4,576,1024]{3,2,1,0:T(8,128)(2,1)} %bitcast.304, pred[4,4,576]{2,1,0:T(4,128)(4,1)S(1)} %copy-done.63, bf16[4,4,576,1024]{3,2,1,0:T(8,128)(2,1)} %bitcast.303), kind=kLoop, calls=%fused_computation.52 | loop fusion | flops 18874368 | bytes 75506688 | tf_op jit(solution)/shard_map/jit(_where)/select_n | solution.py:268
  379.4 217.5 %all_to_all.20 = bf16[4,4,576,1024]{3,2,1,0:T(8,128)(2,1)} all-to-all(bf16[4,4,576,1024]{3,2,1,0:T(8,128)(2,1)} %get-tuple-element.176), channel_id=1, replica_groups=mesh['dp'=8,'expert'=4] {'expert'}, dimensions={0} | all-to-all | bytes 37748736 | tf_op jit(solution)/shard_map/all_to_all | solution.py:240
  604.5 18.7 %fusion.35 = f32[4,4,576,512]{3,2,1,0:T(8,128)} fusion(bf16[4,4,576,1024]{3,2,1,0:T(8,128)(2,1)} %all_to_all.20, bf16[4,1024,512]{2,1,0:T(8,128)(2,1)} %param.25), kind=kOutput, calls=%fused_computation.64 | convolution fusion | flops 9663676416 | bytes 41943040 | tf_op jit(solution)/shard_map/secd,edf->secf/dot_general | solution.py:244
  641.7 168.3 %all-to-all-done.2 = bf16[4,4,576,1024]{3,2,1,0:T(8,128)(2,1)} async-done(((bf16[4,4,576,1024]{3,2,1,0:T(8,128)(2,1)}), bf16[4,4,576,1024]{3,2,1,0:T(8,128)(2,1)}, u32[]{:S(2)}, u32[]{:S(2)}) %all-to-all-start.2) | async-done | bytes 18874400 | tf_op jit(solution)/shard_map/all_to_all | solution.py:271
  810.0 33.7 %fusion.17 = (bf16[4,4,576,512]{3,2,0,1:T(8,128)(2,1)}, bf16[4,4,576,512]{3,2,0,1:T(8,128)(2,1)}, bf16[4,4,576,512]{3,2,0,1:T(8,128)(2,1)}) fusion(f32[4,4,576,512]{3,2,1,0:T(8,128)} %fusion.37, f32[4,4,576,512]{3,2,1,0:T(8,128)} %fusion.35, bf16[4,512,1024]{2,1,0:T(8,128)(2,1)} %param.26, bf16[4,4,576,1024]{3,2,1,0:T(8,128)(2,1)} %all-to-all-done.2), kind=kOutput, calls=%fused_computation.41 | convolution fusion | flops 9734455296 | bytes 89128960 | tf_op jit(solution)/shard_map/secd,efd->secf/dot_general | solution.py:274
  902.3 21.4 %fusion.63 = f32[4,4,576,1024]{3,2,1,0:T(8,128)} fusion(bf16[4,4,576,512]{3,2,0,1:T(8,128)(2,1)} %get-tuple-element.157, bf16[4,1024,512]{2,1,0:T(8,128)(2,1)} %param.24), kind=kOutput, calls=%fused_computation.99 | convolution fusion | flops 9663676416 | bytes 51380224 | tf_op jit(solution)/shard_map/secf,edf->secd/dot_general | solution.py:286
  923.7 25.0 %fusion.13 = bf16[4,4,576,1024]{3,2,0,1:T(8,128)(2,1)} fusion(f32[4,4,576,1024]{3,2,1,0:T(8,128)} %fusion.63, bf16[4,4,576,512]{3,2,0,1:T(8,128)(2,1)} %get-tuple-element.156, bf16[4,1024,512]{2,1,0:T(8,128)(2,1)} %param.25), kind=kOutput, calls=%fused_computation.35 | convolution fusion | flops 9682550784 | bytes 70254592 | tf_op jit(solution)/shard_map/secf,edf->secd/dot_general | solution.py:287
  965.7 125.5 %all-to-all-done.1 = bf16[4,4,576,1024]{3,2,1,0:T(8,128)(2,1)} async-done(((bf16[4,4,576,1024]{3,2,1,0:T(8,128)(2,1)}), bf16[4,4,576,1024]{3,2,1,0:T(8,128)(2,1)}, u32[]{:S(2)}, u32[]{:S(2)}) %all-to-all-start.1) | async-done | bytes 18874400 | tf_op jit(solution)/shard_map/all_to_all | solution.py:252
  1133.8 50.0 %gather_fusion.1 = bf16[8192,1024]{1,0:T(8,128)(2,1)} fusion(bf16[9216,1024]{1,0:T(8,128)(2,1)} %bitcast.44, s32[8192]{0:T(1024)S(1)} %broadcast_clamp_fusion), kind=kCustom, calls=%fused_computation.1 | custom fusion | bytes 33587200 | tf_op jit(solution)/shard_map/gather | solution.py:255
  1207.4 96.7 %all-to-all-done.3 = bf16[4,4,576,1024]{3,2,1,0:T(8,128)(2,1)} async-done(((bf16[4,4,576,1024]{3,2,1,0:T(8,128)(2,1)}), bf16[4,4,576,1024]{3,2,1,0:T(8,128)(2,1)}, u32[]{:S(2)}, u32[]{:S(2)}) %all-to-all-start.3) | async-done | bytes 18874400 | tf_op jit(solution)/shard_map/all_to_all | solution.py:302
  1304.1 49.4 %gather_fusion.3 = bf16[8192,1024]{1,0:T(8,128)(2,1)} fusion(bf16[9216,1024]{1,0:T(8,128)(2,1)} %bitcast.56, s32[8192]{0:T(1024)S(1)} %broadcast_clamp_fusion), kind=kCustom, calls=%fused_computation.3 | custom fusion | bytes 33587200 | tf_op jit(solution)/shard_map/gather | solution.py:306
  1391.5 22.4 %fusion.123 = (f32[8,2]{1,0:T(8,128)S(1)}, f32[8,2,512]{2,1,0:T(2,128)S(1)}, f32[8,1024,512,2]{2,1,3,0:T(8,128)}) fusion(f32[8,2,512,1024]{2,3,1,0:T(8,128)} %get-tuple-element.189, f32[8,2,512]{2,1,0:T(2,128)S(1)} %bitcast.328, bf16[1024,8,64,1]{0,2,3,1:T(8,128)(2,1)S(1)} %bitcast.317, bf16[512,8,2,64]{0,3,2,1:T(8,128)(2,1)S(1)} %bitcast.306), kind=kOutput, calls=%fused_computation.218 | convolution fusion | flops 1107288064 | bytes 69271616 | tf_op jit(solution)/shard_map/while/body/eval_jaxpr/qhgd,phd->hgqp/dot_general | solution.py:134
  1413.9 27.4 %fusion.7 = bf16[8,2,512,1024]{2,3,1,0:T(8,128)(2,1)} fusion(f32[8,1024,512,2]{2,1,3,0:T(8,128)} %get-tuple-element.194, f32[8,2,512,1024]{2,3,1,0:T(8,128)} %get-tuple-element.189, f32[8,2,512]{2,1,0:T(2,128)S(1)} %get-tuple-element.141, f32[8,2,512]{2,1,0:T(2,128)S(1)} %bitcast.329), kind=kLoop, calls=%fused_computation.20 | loop fusion | flops 33554432 | bytes 83951616 | tf_op jit(solution)/shard_map/while/body/eval_jaxpr/convert_element_type | solution.py:138
  1452.6 23.5 %fusion.122 = (f32[8,2]{1,0:T(8,128)S(1)}, f32[8,2,512]{2,1,0:T(2,128)S(1)}, f32[8,1024,512,2]{2,1,3,0:T(8,128)}) fusion(f32[8,2,512,1024]{2,3,1,0:T(8,128)} %get-tuple-element.187, f32[8,2,512]{2,1,0:T(2,128)S(1)} %bitcast.331, bf16[1024,8,64,1]{0,2,3,1:T(8,128)(2,1)} %bitcast.316, bf16[512,8,2,64]{0,3,2,1:T(8,128)(2,1)} %bitcast.308), kind=kOutput, calls=%fused_computation.217 | convolution fusion | flops 1107288064 | bytes 69271616 | tf_op jit(solution)/shard_map/while/body/eval_jaxpr/qhgd,phd->hgqp/dot_general | solution.py:134
  1476.2 27.8 %fusion.4 = bf16[8,2,512,1024]{2,3,1,0:T(8,128)(2,1)} fusion(f32[8,1024,512,2]{2,1,3,0:T(8,128)} %get-tuple-element.193, f32[8,2,512,1024]{2,3,1,0:T(8,128)} %get-tuple-element.187, f32[8,2,512]{2,1,0:T(2,128)S(1)} %get-tuple-element.139, f32[8,2,512]{2,1,0:T(2,128)S(1)} %bitcast.332), kind=kLoop, calls=%fused_computation.15 | loop fusion | flops 33554432 | bytes 83951616 | tf_op jit(solution)/shard_map/while/body/eval_jaxpr/convert_element_type | solution.py:138
  1587.3 38.9 %pmax.7 = f32[16]{0:T(128)S(1)} all-reduce(f32[16]{0:T(128)S(1)} %reduce_max.79), channel_id=1, replica_groups=mesh['dp'=8,'expert'=4] {'dp','expert'}, use_global_device_ids=true, to_apply=%region_41.42 | all-reduce | flops 16 | bytes 128 | tf_op jit(solution)/shard_map/pmax | solution.py:258
  1648.4 20.5 %all-reduce.3 = (bf16[1024]{0:T(1024)(128)(2,1)S(1)}, bf16[1024]{0:T(1024)(128)(2,1)S(1)}) all-reduce(bf16[1024]{0:T(1024)(128)(2,1)S(1)} %get-tuple-element.146, bf16[1024]{0:T(1024)(128)(2,1)S(1)} %copy-done.70), channel_id=6, replica_groups=mesh['dp'=8,'expert'=4] {'dp'}, use_global_device_ids=true, to_apply=%region_31.32.clone | all-reduce | flops 2048 | bytes 8192
  1692.6 62.8 %reduce-scatter.22.cloned.1.call-done = bf16[128,16]{1,0:T(8,128)(2,1)} async-done(((bf16[1024,16]{1,0:T(8,128)(2,1)}), bf16[128,16]{1,0:T(8,128)(2,1)}) %reduce-scatter.22.cloned.1.call-update) | async-done | bytes 4112
  1763.6 28.4 %all-reduce.8.cloned.1.call-done = (bf16[128,1024]{1,0:T(8,128)(2,1)}, bf16[128,1024]{1,0:T(8,128)(2,1)}, bf16[128,1024]{1,0:T(8,128)(2,1)}) async-done(((bf16[128,1024]{1,0:T(8,128)(2,1)}, bf16[128,1024]{1,0:T(8,128)(2,1)}, bf16[128,1024]{1,0:T(8,128)(2,1)}), (bf16[128,1024]{1,0:T(8,128)(2,1)}, bf16[128,1024]{1,0:T(8,128)(2,1)}, bf16[128,1024]{1,0:T(8,128)(2,1)})) %all-reduce.8.cloned.1.call-update) | async-done | bytes 786448 | tf_op jit(solution)/shard_map/psum | solution.py:362
  (327 shorter events, 532.4 us)
Async XLA Ops:
  7.2 65.3 %copy-start.73 = (bf16[128]{0:T(256)(128)(2,1)S(1)}, bf16[128]{0:T(256)(128)(2,1)}, u32[]{:S(2)}) copy-start(bf16[128]{0:T(256)(128)(2,1)} %param.23) | copy-start | bytes 772
  7.2 82.1 %copy-start.71 = (bf16[128,16]{0,1:T(8,128)(2,1)S(1)}, bf16[128,16]{0,1:T(8,128)(2,1)}, u32[]{:S(2)}) copy-start(bf16[128,16]{0,1:T(8,128)(2,1)} %param.21) | copy-start | bytes 12292
  7.2 128.4 %all-gather.6.cloned.1.call-start = ((), (), s32[]{:S(2)}) async-start(), calls=%async_computation.11 | async-start | bytes 2359296 | tf_op jit(solution)/shard_map/all_gather | solution.py:183
  7.9 134.3 %all-gather.8.cloned.1.call-start = ((), (), s32[]{:S(2)}) async-start(), calls=%async_computation.12 | async-start | bytes 2359296 | tf_op jit(solution)/shard_map/all_gather | solution.py:182
  8.7 228.1 %all-gather.10.cloned.1.call-start = ((), (), s32[]{:S(2)}) async-start(), calls=%async_computation.13 | async-start | bytes 2359296 | tf_op jit(solution)/shard_map/all_gather | solution.py:184
  18.4 99.1 %copy-start.49 = (s32[8192,1]{0,1:T(1,128)}, s32[8192,1]{0,1:T(1,128)S(1)}, u32[]{:S(2)}) copy-start(s32[8192,1]{0,1:T(1,128)S(1)} %compare_select_fusion) | copy-start | bytes 98308
  72.5 73.8 %copy-start.68 = (f32[8,1,128]{2,1,0:T(1,128)}, f32[8,1,128]{2,1,0:T(1,128)S(1)}, u32[]{:S(2)}) copy-start(f32[8,1,128]{2,1,0:T(1,128)S(1)} %convert_element_type.285) | copy-start | bytes 12292
  140.6 80.5 %copy-start.19 = (bf16[1024,512]{0,1:T(8,128)(2,1)}, bf16[1024,512]{0,1:T(8,128)(2,1)S(1)}, u32[]{:S(2)}) copy-start(bf16[1024,512]{0,1:T(8,128)(2,1)S(1)} %slice.149) | copy-start | bytes 3145732
  301.4 53.4 %copy-start.63 = (pred[4,4,576]{2,1,0:T(4,128)(4,1)S(1)}, pred[4,4,576]{2,1,0:T(4,128)(4,1)}, u32[]{:S(2)}) copy-start(pred[4,4,576]{2,1,0:T(4,128)(4,1)} %broadcast_in_dim.156) | copy-start | bytes 27652
  596.9 213.1 %all-to-all-start.2 = ((bf16[4,4,576,1024]{3,2,1,0:T(8,128)(2,1)}), bf16[4,4,576,1024]{3,2,1,0:T(8,128)(2,1)}, u32[]{:S(2)}, u32[]{:S(2)}) async-start(bf16[4,4,576,1024]{3,2,1,0:T(8,128)(2,1)} %get-tuple-element.175), calls=%async_computation.2 | async-start | bytes 37748736 | tf_op jit(solution)/shard_map/all_to_all | solution.py:271
  878.3 212.9 %all-to-all-start.1 = ((bf16[4,4,576,1024]{3,2,1,0:T(8,128)(2,1)}), bf16[4,4,576,1024]{3,2,1,0:T(8,128)(2,1)}, u32[]{:S(2)}, u32[]{:S(2)}) async-start(bf16[4,4,576,1024]{3,2,1,0:T(8,128)(2,1)} %copy.158), calls=%async_computation.1 | async-start | bytes 37748736 | tf_op jit(solution)/shard_map/all_to_all | solution.py:252
  885.6 695.2 %reduce-scatter.20.cloned.1.call-start = ((), (), s32[]{:S(2)}) async-start(), calls=%async_computation.19 | async-start | bytes 4718592 | tf_op jit(solution)/shard_map/reduce_scatter | solution.py:298
  1091.2 213.0 %all-to-all-start.3 = ((bf16[4,4,576,1024]{3,2,1,0:T(8,128)(2,1)}), bf16[4,4,576,1024]{3,2,1,0:T(8,128)(2,1)}, u32[]{:S(2)}, u32[]{:S(2)}) async-start(bf16[4,4,576,1024]{3,2,1,0:T(8,128)(2,1)} %copy.164), calls=%async_computation.3 | async-start | bytes 37748736 | tf_op jit(solution)/shard_map/all_to_all | solution.py:302
  1098.6 484.4 %reduce-scatter.18.cloned.1.call-start = ((), (), s32[]{:S(2)}) async-start(), calls=%async_computation.18 | async-start | bytes 4718592 | tf_op jit(solution)/shard_map/reduce_scatter | solution.py:295
  1115.4 469.8 %reduce-scatter.16.cloned.1.call-start = ((), (), s32[]{:S(2)}) async-start(), calls=%async_computation.17 | async-start | bytes 4718592 | tf_op jit(solution)/shard_map/reduce_scatter | solution.py:292
  1133.7 540.8 %reduce-scatter.14.cloned.1.call-start = ((), (), s32[]{:S(2)}) async-start(), calls=%async_computation.16 | async-start | bytes 2359296 | tf_op jit(solution)/shard_map/reduce_scatter | solution.py:348
  1133.8 50.0 %copy-start.23 = (f32[1024,8]{1,0:T(8,128)S(1)}, f32[1024,8]{1,0:T(8,128)}, u32[]{:S(2)}) copy-start(f32[1024,8]{1,0:T(8,128)} %copy-done.22) | copy-start | bytes 98308
  1207.4 166.5 %copy-start.39 = (bf16[1024,16]{0,1:T(8,128)(2,1)}, bf16[1024,16]{0,1:T(8,128)(2,1)S(1)}, u32[]{:S(2)}) copy-start(bf16[1024,16]{0,1:T(8,128)(2,1)S(1)} %select_reduce_fusion) | copy-start | bytes 98308
  1452.6 222.0 %reduce-scatter.12.cloned.1.call-start = ((), (), s32[]{:S(2)}) async-start(), calls=%async_computation.15 | async-start | bytes 2359296 | tf_op jit(solution)/shard_map/reduce_scatter | solution.py:345
  1555.1 136.0 %reduce-scatter.10.cloned.1.call-start = ((), (), s32[]{:S(2)}) async-start(), calls=%async_computation.14 | async-start | bytes 2359296 | tf_op jit(solution)/shard_map/reduce_scatter | solution.py:342
  1579.3 47.0 %copy-start.2 = (bf16[1024,1024]{0,1:T(8,128)(2,1)S(1)}, bf16[1024,1024]{0,1:T(8,128)(2,1)}, u32[]{:S(2)}) copy-start(bf16[1024,1024]{0,1:T(8,128)(2,1)} %multiply_convert_fusion) | copy-start | bytes 6291460
  1579.3 47.0 %copy-start.40 = (bf16[1024,16]{0,1:T(8,128)(2,1)S(1)}, bf16[1024,16]{0,1:T(8,128)(2,1)}, u32[]{:S(2)}) copy-start(bf16[1024,16]{0,1:T(8,128)(2,1)} %copy-done.39) | copy-start | bytes 98308
  1579.3 176.1 %reduce-scatter.22.cloned.1.call-start = ((), (), s32[]{:S(2)}) async-start(), calls=%async_computation.20 | async-start | bytes 294912
  1637.5 154.5 %all-reduce.8.cloned.1.call-start = ((), (), s32[]{:S(2)}) async-start(), calls=%async_computation.21 | async-start | bytes 1572864 | tf_op jit(solution)/shard_map/psum | solution.py:362
  (71 other events, 672.6 us)
Sparse Core Ops, SparseCore 0:
  10.2 51.9 all-gather.5
  64.3 48.0 all-gather.7
  114.6 48.0 all-gather.9
  902.5 86.2 reduce-scatter.19
  1115.5 86.4 reduce-scatter.17
  1205.5 88.0 reduce-scatter.15
  1452.7 64.5 reduce-scatter.13
  1555.2 65.0 reduce-scatter.11
  1624.3 66.7 reduce-scatter.9
  1695.2 60.1 reduce-scatter.21
  1758.1 33.8 all-reduce.7
where the time goes:
time: 1810 us; the launch traced here: 1800 us
  waiting for transfers between devices  500 us (28%)
  matrix products  406 us (22%)
  blocking collectives  348 us (19%)
  local copies, waits for them, and re-layouts  313 us (17%)
  other arithmetic  196 us (11%)
  starting transfers between devices  22.8 us (1%)
    all_to_all x1, blocking collectives, on_device(): lax.all_to_all(send_rows, 'expert', split_axis=0, concat_axis=0, tiled=True)  218 us
    all_to_all x1, waiting for transfers between devices, on_device(): lax.all_to_all(d_slots, 'expert', split_axis=0, concat_axis=0, tiled=True)  168 us
    all_to_all x1, waiting for transfers between devices, on_device(): lax.all_to_all(expert_res, 'expert', split_axis=0, concat_axis=0, tiled=T...  126 us
    all_to_all x1, waiting for transfers between devices, on_device(): lax.all_to_all(d_route_in, 'expert', split_axis=0, concat_axis=0, tiled=T...  96.7 us
    unnamed x12, waiting for transfers between devices  65 us
    convert_element_type x2, other arithmetic, attend_backward(): d_scores = (weights * (d_weights - row_dot)).astype(jnp.bfloat16)  55.1 us
    gather x1, local copies, waits for them, and re-layouts, on_device(): d_route[route_pick]  53.4 us
    gather x1, local copies, waits for them, and re-layouts, on_device(): route_out = returned[slot_index].reshape(num_rows, top_count, model_width)  50 us
  transfers between devices with their start and end apart: 14, of which 6 were waited for; matrix products, arithmetic and copies ran while one was open for 38% of the time, Pallas kernels for 0%

commit v1 on v0

v1 whole, which is shorter than its diff:
```python
import functools

import jax
import jax.numpy as jnp
import numpy as np
from jax import lax
from jax.experimental import pallas as pl
from jax.experimental.pallas import tpu as pltpu
from jax.sharding import PartitionSpec as P

EPS = 1e-05
ROPE_BASE = 10000.0
F32 = jnp.float32
BF16 = jnp.bfloat16
NEG = -1e30
MIB = 1 << 20


def dot(a, b):
    return lax.dot_general(a, b, (((1,), (0,)), ((), ())), preferred_element_type=F32)


def dot_t(a, b):
    return lax.dot_general(a, b, (((1,), (1,)), ((), ())), preferred_element_type=F32)


def params(vmem_mib, n=1):
    return pltpu.CompilerParams(
        dimension_semantics=("arbitrary",) * n, vmem_limit_bytes=vmem_mib * MIB
    )


def cost(flops, nbytes, trans=0):
    return pl.CostEstimate(flops=int(flops), bytes_accessed=int(nbytes), transcendentals=int(trans))


def spec(shape, index):
    return pl.BlockSpec(shape, index)


def whole(shape):
    zeros = (0,) * len(shape)
    return pl.BlockSpec(shape, lambda *_: zeros)


def rope_tables(length, head):
    half = head // 2
    freq = np.float32(ROPE_BASE) ** (
        -(np.arange(half, dtype=np.float32) * np.float32(2.0) / np.float32(head))
    )
    ang = np.arange(length, dtype=np.float32)[:, None] * freq.astype(np.float32)[None, :]
    ang = ang.astype(np.float32)
    return np.cos(ang).astype(np.float32), np.sin(ang).astype(np.float32)


def lane_half(shape, width):
    return (lax.broadcasted_iota(jnp.int32, shape, 1) % width) < (width // 2)


def rope_lanes(x, cos, sin, first):
    partner = jnp.where(first, pltpu.roll(x, 96, 1), pltpu.roll(x, 32, 1))
    return x * cos + partner * sin


def qkv_kernel(tok_ref, gain_ref, w_ref, cos_ref, sin_ref, h_ref, q_ref, kd_ref, vd_ref):
    x = tok_ref[...].astype(F32)
    d = x.shape[1]
    r = lax.rsqrt(jnp.mean(x * x, axis=1, keepdims=True) + EPS)
    h = (x * r * gain_ref[...].astype(F32)).astype(BF16)
    h_ref[...] = h
    cos, sin = cos_ref[...], sin_ref[...]
    rows = x.shape[0]
    first = lane_half((rows, 128), 64)
    low = lane_half((rows, 128), 128)
    nq = q_ref.shape[1]
    nk = kd_ref.shape[1] // 2
    q = dot(h, w_ref[:, :nq])
    for c in range(0, nq, 128):
        q_ref[:, c : c + 128] = (rope_lanes(q[:, c : c + 128], cos, sin, first) * 0.125).astype(
            BF16
        )
    k = dot(h, w_ref[:, nq : nq + nk])
    for c in range(0, nk, 128):
        kk = rope_lanes(k[:, c : c + 128], cos, sin, first)
        sw = pltpu.roll(kk, 64, 1)
        kd_ref[:, 2 * c : 2 * c + 128] = jnp.where(low, kk, sw).astype(BF16)
        kd_ref[:, 2 * c + 128 : 2 * c + 256] = jnp.where(low, sw, kk).astype(BF16)
    v = dot(h, w_ref[:, nq + nk : nq + 2 * nk])
    for c in range(0, nk, 128):
        vv = v[:, c : c + 128]
        sw = pltpu.roll(vv, 64, 1)
        vd_ref[:, 2 * c : 2 * c + 128] = jnp.where(low, vv, sw).astype(BF16)
        vd_ref[:, 2 * c + 128 : 2 * c + 256] = jnp.where(low, sw, vv).astype(BF16)


def run_qkv(tok, gain, w_qkv, cos, sin, nq):
    length, d = tok.shape
    b = 256
    row = lambda i: (i, 0)
    return pl.pallas_call(
        qkv_kernel,
        grid=(length // b,),
        in_specs=[
            spec((b, d), row),
            whole((1, d)),
            spec((d, 2 * nq), lambda i: (0, 0)),
            spec((b, 128), row),
            spec((b, 128), row),
        ],
        out_specs=[spec((b, d), row)] + [spec((b, nq), row)] * 3,
        out_shape=[jax.ShapeDtypeStruct((length, d), BF16)]
        + [jax.ShapeDtypeStruct((length, nq), BF16)] * 3,
        compiler_params=params(40),
        cost_estimate=cost(2 * length * d * 2 * nq, 16 * MIB),
        name="qkv",
    )(tok, gain, w_qkv, cos, sin)


def mask_bias(prefix, q0, k0, nq, nk, q_axis):
    shape = (nq, nk) if q_axis == 0 else (nk, nq)
    qpos = q0 + lax.broadcasted_iota(jnp.int32, shape, q_axis)
    kpos = k0 + lax.broadcasted_iota(jnp.int32, shape, 1 - q_axis)
    return jnp.where((kpos <= qpos) | (kpos < prefix), 0.0, NEG).astype(F32)


def two_heads(pair, low):
    zero = jnp.zeros_like(pair)
    return jnp.concatenate([jnp.where(low, pair, zero), jnp.where(low, zero, pair)], axis=0)


def attn_fwd_kernel(prefix_ref, q_ref, kd_ref, vd_ref, ctx_ref, lse_ref, peak_ref):
    length = q_ref.shape[0]
    b = 256
    prefix = prefix_ref[0]
    low_b = lane_half((b, 128), 128)
    lane = lax.broadcasted_iota(jnp.int32, (b, 128), 1)
    peak = jnp.full((8, 128), NEG, F32)
    peak_lane = lax.broadcasted_iota(jnp.int32, (8, 128), 1)
    for i in range(length // b):
        nk = max((i + 1) * b, length // 2)
        free = i * b
        bias = mask_bias(prefix, i * b, free, b, nk - free, 0)
        bias = jnp.concatenate([bias, bias], axis=0)
        lse_cols = jnp.zeros((b, 128), F32)
        for j in range(2):
            cols = slice(j * 128, (j + 1) * 128)
            q2 = two_heads(q_ref[i * b : (i + 1) * b, cols], low_b)
            s_hi = dot_t(q2, kd_ref[free:nk, cols]) + bias
            m = jnp.max(s_hi, axis=1, keepdims=True)
            if free:
                s_lo = dot_t(q2, kd_ref[:free, cols])
                m = jnp.maximum(m, jnp.max(s_lo, axis=1, keepdims=True))
            p_hi = jnp.exp(s_hi - m)
            total = jnp.sum(p_hi, axis=1, keepdims=True)
            ctx = dot(p_hi.astype(BF16), vd_ref[free:nk, cols])
            if free:
                p_lo = jnp.exp(s_lo - m)
                total = total + jnp.sum(p_lo, axis=1, keepdims=True)
                ctx = ctx + dot(p_lo.astype(BF16), vd_ref[:free, cols])
            ctx = ctx * (1.0 / total)
            ctx_ref[i * b : (i + 1) * b, cols] = jnp.where(low_b, ctx[:b], ctx[b:]).astype(BF16)
            lse = m + jnp.log(total)
            for g in range(2):
                lse_cols = jnp.where(lane == 2 * j + g, lse[g * b : (g + 1) * b], lse_cols)
                top = jnp.max(m[g * b : (g + 1) * b], axis=0, keepdims=True)
                peak = jnp.where(peak_lane == 2 * j + g, jnp.maximum(peak, top), peak)
        lse_ref[0, :, i * b : (i + 1) * b] = lse_cols.T[:8]
    peak_ref[0] = peak


def run_attn_fwd(prefix, q, kd, vd):
    length, nq = q.shape
    groups = nq // 256
    col = lambda g: (0, g)
    return pl.pallas_call(
        attn_fwd_kernel,
        grid=(groups,),
        in_specs=[pl.BlockSpec(memory_space=pltpu.SMEM)] + [spec((length, 256), col)] * 3,
        out_specs=[
            spec((length, 256), col),
            spec((1, 8, length), lambda g: (g, 0, 0)),
            spec((1, 8, 128), lambda g: (g, 0, 0)),
        ],
        out_shape=[
            jax.ShapeDtypeStruct((length, nq), BF16),
            jax.ShapeDtypeStruct((groups, 8, length), F32),
            jax.ShapeDtypeStruct((groups, 8, 128), F32),
        ],
        compiler_params=params(48),
        cost_estimate=cost(25e9, 9 * MIB),
        name="attn_fwd",
    )(prefix, q, kd, vd)


def attn_bwd_kernel(
    prefix_ref, q_ref, kd_ref, vd_ref, do_ref, ctx_ref, lse_ref, cos_ref, sin_ref, cost_ref, sint_ref,
    dq_ref, dk_ref, dv_ref, dk_acc, dv_acc, kt_ref,
):
    length = q_ref.shape[0]
    b = 256
    prefix = prefix_ref[0]
    low_b = lane_half((b, 128), 128)
    for j in range(2):
        cols = slice(j * 128, (j + 1) * 128)
        kt_ref[j] = kd_ref[:, cols].T
    dk_acc[...] = jnp.zeros_like(dk_acc)
    dv_acc[...] = jnp.zeros_like(dv_acc)
    for i in range(length // b):
        rows = slice(i * b, (i + 1) * b)
        nk = max((i + 1) * b, length // 2)
        free = i * b
        bias = mask_bias(prefix, i * b, free, b, nk - free, 1)
        bias = jnp.concatenate([bias, bias], axis=1)
        for j in range(2):
            cols = slice(j * 128, (j + 1) * 128)
            do = do_ref[rows, cols]
            q2 = two_heads(q_ref[rows, cols], low_b)
            do2 = two_heads(do, low_b)
            prod = (do.astype(F32) * ctx_ref[rows, cols].astype(F32)).T
            delta = jnp.concatenate(
                [
                    jnp.sum(prod[:64], axis=0, keepdims=True),
                    jnp.sum(prod[64:], axis=0, keepdims=True),
                ],
                axis=1,
            )
            lse = jnp.concatenate(
                [lse_ref[0, 2 * j : 2 * j + 1, rows], lse_ref[0, 2 * j + 1 : 2 * j + 2, rows]],
                axis=1,
            )
            dq_t = None
            parts = [(0, free)] if free else []
            for k0, k1 in parts + [(free, nk)]:
                keys = slice(k0, k1)
                s = dot_t(kd_ref[keys, cols], q2)
                if k0 == free:
                    s = s + bias
                p = jnp.exp(s - lse)
                dp = dot_t(vd_ref[keys, cols], do2)
                ds = (p * (dp - delta)).astype(BF16)
                dv_acc[j, keys, :] += dot(p.astype(BF16), do2)
                dk_acc[j, keys, :] += dot(ds, q2)
                part = dot(kt_ref[j, :, keys], ds)
                dq_t = part if dq_t is None else dq_t + part
            cos_t, sin_t = cost_ref[:, rows], sint_ref[:, rows]
            a0, b0 = dq_t[0:32, :b], dq_t[32:64, :b]
            a1, b1 = dq_t[64:96, b:], dq_t[96:128, b:]
            full = jnp.concatenate(
                [
                    a0 * cos_t + b0 * sin_t,
                    b0 * cos_t - a0 * sin_t,
                    a1 * cos_t + b1 * sin_t,
                    b1 * cos_t - a1 * sin_t,
                ],
                axis=0,
            )
            dq_ref[rows, cols] = (full * 0.125).T.astype(BF16)
    low = lane_half((length, 128), 128)
    first = lane_half((length, 128), 64)
    sums = []
    for acc in (dk_acc, dv_acc):
        even = acc[0] + pltpu.roll(acc[0], 64, 1)
        odd = acc[1] + pltpu.roll(acc[1], 64, 1)
        sums.append(jnp.where(low, even, odd))
    dk_ref[...] = rope_lanes(sums[0], cos_ref[...], -sin_ref[...], first).astype(BF16)
    dv_ref[...] = sums[1].astype(BF16)


def run_attn_bwd(prefix, q, kd, vd, d_ctx, ctx, lse, cos, sin, cos_t, sin_t):
    length, nq = q.shape
    groups = nq // 256
    col = lambda g: (0, g)
    wide = spec((length, 256), col)
    return pl.pallas_call(
        attn_bwd_kernel,
        grid=(groups,),
        in_specs=[pl.BlockSpec(memory_space=pltpu.SMEM)]
        + [wide] * 5
        + [spec((1, 8, length), lambda g: (g, 0, 0))]
        + [whole((length, 128))] * 2
        + [whole((cos_t.shape[0], length))] * 2,
        out_specs=[wide, spec((length, 128), col), spec((length, 128), col)],
        out_shape=[
            jax.ShapeDtypeStruct((length, nq), BF16),
            jax.ShapeDtypeStruct((length, nq // 2), BF16),
            jax.ShapeDtypeStruct((length, nq // 2), BF16),
        ],
        scratch_shapes=[
            pltpu.VMEM((2, length, 128), F32),
            pltpu.VMEM((2, length, 128), F32),
            pltpu.VMEM((2, 128, length), BF16),
        ],
        compiler_params=params(56),
        cost_estimate=cost(60e9, 16 * MIB),
        name="attn_bwd",
    )(prefix, q, kd, vd, d_ctx, ctx, lse, cos, sin, cos_t, sin_t)


def mid_kernel(tok_ref, ctx_ref, w_ref, gain_ref, res_ref, x_ref):
    res = tok_ref[...].astype(F32) + dot(ctx_ref[...], w_ref[...])
    res_ref[...] = res
    r = lax.rsqrt(jnp.mean(res * res, axis=1, keepdims=True) + EPS)
    x_ref[...] = (res * r * gain_ref[...].astype(F32)).astype(BF16)


def run_mid(tok, ctx, w_out, gain):
    length, d = tok.shape
    b = 256
    row = lambda i: (i, 0)
    return pl.pallas_call(
        mid_kernel,
        grid=(length // b,),
        in_specs=[
            spec((b, d), row),
            spec((b, ctx.shape[1]), row),
            whole(w_out.shape),
            whole((1, d)),
        ],
        out_specs=[spec((b, d), row)] * 2,
        out_shape=[
            jax.ShapeDtypeStruct((length, d), F32),
            jax.ShapeDtypeStruct((length, d), BF16),
        ],
        compiler_params=params(40),
        cost_estimate=cost(2 * length * d * d, 12 * MIB),
        name="mid",
    )(tok, ctx, w_out, gain)


def gates_of(x, router, mask):
    logits = dot(x, router)
    logits = jnp.where(mask > 0, logits, NEG)
    e = jnp.exp(logits - jnp.max(logits, axis=1, keepdims=True))
    e = jnp.where(mask > 0, e, 0.0)
    return e / jnp.sum(e, axis=1, keepdims=True)


def expert_kernel(
    me_ref, x_ref, c_ref, mask_ref, router_ref, wg_ref, wu_ref, wd_ref,
    out_ref, dx_ref, dg_ref, hs_ref, dgate_ref, dup_ref, xt_ref, ct_ref, out_acc, dx_acc, gp_ref, dgc_ref,
):
    e = pl.program_id(1)
    local = pl.num_programs(1)
    x, c = x_ref[...], c_ref[...]
    b = x.shape[0]
    lane = lax.broadcasted_iota(jnp.int32, (b, 128), 1)

    @pl.when(e == 0)
    def _():
        gp_ref[...] = gates_of(x, router_ref[...], mask_ref[...].astype(F32))
        xt_ref[...] = x.T
        ct_ref[...] = c.T

    gp = jnp.sum(
        jnp.where(lane == me_ref[0] * local + e, gp_ref[...], 0.0), axis=1, keepdims=True
    )
    gate = dot(x, wg_ref[e])
    up = dot(x, wu_ref[e])
    grad = dot_t(c, wd_ref[e])
    sig = 0.5 * jnp.tanh(0.5 * gate) + 0.5
    act = gate * sig
    hidden = (act * up).astype(BF16).astype(F32)
    dg = jnp.sum(hidden * grad, axis=1, keepdims=True)
    hs = (hidden * gp).astype(BF16)
    dh = grad * gp
    dup = (dh * act).astype(BF16)
    dgate = (dh * up * (sig + act * (1.0 - sig))).astype(BF16)
    hs_ref[...] = hs
    dup_ref[...] = dup
    dgate_ref[...] = dgate
    out = dot(hs, wd_ref[e])
    dx = dot_t(dgate, wg_ref[e]) + dot_t(dup, wu_ref[e])
    dg_col = jnp.where(lane == e, dg, 0.0)

    @pl.when(e == 0)
    def _():
        out_acc[...] = out
        dx_acc[...] = dx
        dgc_ref[...] = dg_col

    @pl.when((e > 0) & (e < local - 1))
    def _():
        out_acc[...] += out
        dx_acc[...] += dx
        dgc_ref[...] += dg_col

    @pl.when(e == local - 1)
    def _():
        out_ref[...] = (out_acc[...] + out).astype(BF16)
        dx_ref[...] = (dx_acc[...] + dx).astype(BF16)
        dg_ref[...] = (dgc_ref[...] + dg_col).T[:8]


def run_expert(me, x, c, mask, router, wg, wu, wd):
    length, d = x.shape
    local, _, ff = wg.shape
    b = 512
    row = lambda i, e: (i, 0)
    colT = lambda i, e: (0, i)
    once = lambda shape: pl.BlockSpec(
        shape, lambda i, e: (0,) * len(shape), pipeline_mode=pl.Buffered(1)
    )
    return pl.pallas_call(
        expert_kernel,
        grid=(length // b, local),
        in_specs=[
            pl.BlockSpec(memory_space=pltpu.SMEM),
            spec((b, d), row),
            spec((b, d), row),
            spec((b, 128), row),
            once(router.shape),
            once(wg.shape),
            once(wu.shape),
            once(wd.shape),
        ],
        out_specs=[
            spec((b, d), row),
            spec((b, d), row),
            spec((8, b), colT),
            spec((b, ff), lambda i, e: (i, e)),
            spec((b, ff), lambda i, e: (i, e)),
            spec((b, ff), lambda i, e: (i, e)),
            spec((d, b), colT),
            spec((d, b), colT),
        ],
        out_shape=[
            jax.ShapeDtypeStruct((length, d), BF16),
            jax.ShapeDtypeStruct((length, d), BF16),
            jax.ShapeDtypeStruct((8, length), F32),
            jax.ShapeDtypeStruct((length, local * ff), BF16),
            jax.ShapeDtypeStruct((length, local * ff), BF16),
            jax.ShapeDtypeStruct((length, local * ff), BF16),
            jax.ShapeDtypeStruct((d, length), BF16),
            jax.ShapeDtypeStruct((d, length), BF16),
        ],
        scratch_shapes=[
            pltpu.VMEM((b, d), F32),
            pltpu.VMEM((b, d), F32),
            pltpu.VMEM((b, 128), F32),
            pltpu.VMEM((b, 128), F32),
        ],
        compiler_params=params(58, 2),
        cost_estimate=cost(12 * length * d * ff * local, 40 * MIB, length * ff * local),
        name="experts",
    )(me, x, c, mask, router, wg, wu, wd)


def weight_grad_kernel(n, transpose, *refs):
    lefts, rights, out_ref = refs[:n], refs[n : 2 * n], refs[2 * n]
    d = lefts[0].shape[0]
    for m in range(0, d, 256):
        acc = None
        for left, right in zip(lefts, rights):
            part = dot(left[m : m + 256, :], right[...])
            acc = part if acc is None else acc + part
        if transpose:
            out_ref[0, :, m : m + 256] = acc.T.astype(BF16)
        else:
            out_ref[0, m : m + 256, :] = acc.astype(BF16)


def run_weight_grad(lefts, rights, local, transpose):
    n = len(lefts)
    d, length = lefts[0].shape
    ff = rights[0].shape[1] // local
    shape = (ff, d) if transpose else (d, ff)
    return pl.pallas_call(
        functools.partial(weight_grad_kernel, n, transpose),
        grid=(local,),
        in_specs=[
            pl.BlockSpec((d, length), lambda e: (0, 0), pipeline_mode=pl.Buffered(1))
            for _ in lefts
        ]
        + [spec((length, ff), lambda e: (0, e)) for _ in rights],
        out_specs=spec((1,) + shape, lambda e: (e, 0, 0)),
        out_shape=jax.ShapeDtypeStruct((local,) + shape, BF16),
        compiler_params=params(56),
        cost_estimate=cost(2 * n * length * d * ff * local, (n * 6 + 4) * MIB),
        name="weight_grad",
    )(*lefts, *rights)


def back_mid_kernel(n, *refs):
    (res_ref, cot_ref, mask_ref, x_ref, router_ref, dg_ref, gain_ref, w_ref) = refs[:8]
    dx_refs = refs[8 : 8 + n]
    dres_ref, dattn_ref, dctx_ref, dlog_ref, ggain_ref = refs[8 + n :]
    gp = gates_of(x_ref[...], router_ref[...], mask_ref[...].astype(F32))
    dg = dg_ref[...]
    d_logits = (gp * (dg - jnp.sum(gp * dg, axis=1, keepdims=True))).astype(BF16)
    dlog_ref[...] = d_logits
    d_norm = dot_t(d_logits, router_ref[...])
    for ref in dx_refs:
        d_norm = d_norm + ref[...].astype(F32)
    res = res_ref[...]
    r = lax.rsqrt(jnp.mean(res * res, axis=1, keepdims=True) + EPS)
    xr = res * r
    part = jnp.sum(d_norm * xr, axis=0, keepdims=True)

    @pl.when(pl.program_id(0) == 0)
    def _():
        ggain_ref[...] = jnp.zeros_like(ggain_ref)

    ggain_ref[...] += part
    u = d_norm * gain_ref[...].astype(F32)
    d_res = (
        cot_ref[...].astype(F32) + r * u - xr * (r * r) * jnp.mean(u * res, axis=1, keepdims=True)
    )
    dres_ref[...] = d_res
    d_attn = d_res.astype(BF16)
    dattn_ref[...] = d_attn
    dctx_ref[...] = dot_t(d_attn, w_ref[...]).astype(BF16)


def run_back_mid(res, cot, mask, x, router, dg, gain, w_out, dxs):
    length, d = res.shape
    b = 256
    row = lambda i: (i, 0)
    n = len(dxs)
    return pl.pallas_call(
        functools.partial(back_mid_kernel, n),
        grid=(length // b,),
        in_specs=[
            spec((b, d), row),
            spec((b, d), row),
            spec((b, 128), row),
            spec((b, d), row),
            whole(router.shape),
            spec((b, 128), row),
            whole((1, d)),
            whole(w_out.shape),
        ]
        + [spec((b, d), row)] * n,
        out_specs=[
            spec((b, d), row),
            spec((b, d), row),
            spec((b, w_out.shape[0]), row),
            spec((b, 128), row),
            whole((1, d)),
        ],
        out_shape=[
            jax.ShapeDtypeStruct((length, d), F32),
            jax.ShapeDtypeStruct((length, d), BF16),
            jax.ShapeDtypeStruct((length, w_out.shape[0]), BF16),
            jax.ShapeDtypeStruct((length, 128), BF16),
            jax.ShapeDtypeStruct((1, d), F32),
        ],
        compiler_params=params(48),
        cost_estimate=cost(2 * length * d * d, 26 * MIB),
        name="back_mid",
    )(res, cot, mask, x, router, dg, gain, w_out, *dxs)


def back_in_kernel(dq_ref, dk_ref, dv_ref, w_ref, tok_ref, gain_ref, dres_ref, gt_ref, ggain_ref):
    nq, nk = dq_ref.shape[1], dk_ref.shape[1]
    d_norm = dot_t(dq_ref[...], w_ref[:, :nq])
    d_norm = d_norm + dot_t(dk_ref[...], w_ref[:, nq : nq + nk])
    d_norm = d_norm + dot_t(dv_ref[...], w_ref[:, nq + nk : nq + 2 * nk])
    x = tok_ref[...].astype(F32)
    r = lax.rsqrt(jnp.mean(x * x, axis=1, keepdims=True) + EPS)
    xr = x * r
    part = jnp.sum(d_norm * xr, axis=0, keepdims=True)

    @pl.when(pl.program_id(0) == 0)
    def _():
        ggain_ref[...] = jnp.zeros_like(ggain_ref)

    ggain_ref[...] += part
    u = d_norm * gain_ref[...].astype(F32)
    gt_ref[...] = dres_ref[...] + r * u - xr * (r * r) * jnp.mean(u * x, axis=1, keepdims=True)


def run_back_in(dq, dk, dv, w_qkv, tok, gain, d_res):
    length, d = tok.shape
    b = 256
    row = lambda i: (i, 0)
    nq = dq.shape[1]
    return pl.pallas_call(
        back_in_kernel,
        grid=(length // b,),
        in_specs=[
            spec((b, nq), row),
            spec((b, dk.shape[1]), row),
            spec((b, dv.shape[1]), row),
            spec((d, 2 * nq), lambda i: (0, 0)),
            spec((b, d), row),
            whole((1, d)),
            spec((b, d), row),
        ],
        out_specs=[spec((b, d), row), whole((1, d))],
        out_shape=[jax.ShapeDtypeStruct((length, d), F32), jax.ShapeDtypeStruct((1, d), F32)],
        compiler_params=params(48),
        cost_estimate=cost(4 * length * d * nq, 20 * MIB),
        name="back_in",
    )(dq, dk, dv, w_qkv, tok, gain, d_res)


def after(value, *deps):
    return lax.optimization_barrier((value,) + deps)[0]


def on_device(
    n_dp, n_ex, tokens, cotangent, routes, prefix, w_query, keyvalue_weight, w_out, w_router,
    gain_attn, gain_mlp, expert_gate, expert_up, expert_down, query_logit_cap,
):
    length, d = tokens.shape[1], tokens.shape[2]
    tok = tokens.reshape(length, d)
    cot = cotangent.reshape(length, d)
    heads = query_logit_cap.shape[0]
    nq = w_query.shape[1]
    head = nq // heads
    kv_heads = keyvalue_weight.shape[1] // (2 * head)
    num_experts = w_router.shape[1]
    local = expert_gate.shape[0]
    rows = w_query.shape[0]
    ex = lax.axis_index("expert")

    def swap(value, step, axis="expert", n=n_ex):
        return lax.ppermute(value, axis, [(i, i ^ step) for i in range(n)])

    part = rows // n_ex
    small = jnp.concatenate(
        [
            w_router,
            gain_attn[:, None],
            gain_mlp[:, None],
            jnp.zeros((rows, 128 - num_experts - 2), BF16),
        ],
        axis=1,
    )
    packed = jnp.concatenate([w_query, keyvalue_weight, w_out, small], axis=1)
    mine = lax.dynamic_slice_in_dim(packed, ex * part, part, axis=0)
    every = lax.all_gather(mine, ("dp", "expert"), axis=0, tiled=True)
    w_all = every
    width = 2 * nq
    full_out = every[:, width : width + d]
    extra = every[:, width + d :]
    lanes = lax.broadcasted_iota(jnp.int32, extra.shape, 1)
    router = jnp.where(lanes < num_experts, extra, jnp.zeros((), BF16))
    gain_one = extra[:, num_experts].reshape(1, d)
    gain_two = extra[:, num_experts + 1].reshape(1, d)

    routes_t = routes.reshape(length, -1).T
    cots, masks = {0: cot}, {}
    route_set = {0: routes_t}
    cot_late = after(cot, every)
    for step in range(1, n_ex):
        if step == 1:
            cots[1] = swap(cot_late, 1)
        elif step % 2 == 0:
            cots[step] = swap(cot_late, step)
        else:
            cots[step] = swap(cots[step - 1], 1)
        route_set[step] = swap(routes_t, step)
    columns = jnp.arange(128, dtype=jnp.int32)
    for step in range(n_ex):
        hit = route_set[step].T[:, :, None] == columns[None, None, :]
        masks[step] = jnp.any(hit, axis=1).astype(BF16)

    cos_np, sin_np = rope_tables(length, head)
    cos_l = jnp.asarray(np.concatenate([cos_np] * 4, axis=1))
    sin_l = jnp.asarray(np.concatenate([-sin_np, sin_np] * 2, axis=1))
    cos_t = jnp.asarray(np.ascontiguousarray(cos_np.T))
    sin_t = jnp.asarray(np.ascontiguousarray(sin_np.T))

    normed_one, q, kd, vd = run_qkv(tok, gain_one, w_all, cos_l, sin_l, nq)
    ctx, lse, peaks = run_attn_fwd(prefix, q, kd, vd)
    resid, normed_two = run_mid(tok, ctx, full_out, gain_two)

    me = ex.reshape(1).astype(jnp.int32)
    xs = {0: normed_two}
    for step in range(1, n_ex):
        if step == 1 or step % 2 == 0:
            xs[step] = swap(normed_two, step)
        else:
            xs[step] = swap(xs[step - 1], 1)
    res = {}
    for step in range(n_ex):
        res[step] = run_expert(
            me, xs[step], cots[step], masks[step], router, expert_gate, expert_up, expert_down
        )

    def collect(index, dep=None):
        got = [res[0][index]]
        first = res[1][index]
        if dep is not None:
            first = after(first, dep)
        got.append(swap(first, 1))
        for step in range(2, n_ex, 2):
            other = res[step + 1][index]
            if dep is not None:
                other = after(other, dep)
            both = (res[step][index].astype(F32) + swap(other, 1).astype(F32)).astype(BF16)
            got.append(swap(both, step))
        return got

    dxs = collect(1)
    dg_parts = [res[0][2]] + [swap(res[step][2], step) for step in range(1, n_ex)]
    stacked = jnp.stack([piece[:local] for piece in dg_parts])
    owner = jnp.arange(n_ex, dtype=jnp.int32)
    dg = sum(
        jnp.where(((owner ^ step) == ex)[:, None, None], stacked[step][None], 0.0)
        for step in range(n_ex)
    )
    dg = dg.reshape(num_experts, length).T
    dg = jnp.pad(dg, ((0, 0), (0, 128 - num_experts)))

    order = list(range(n_ex))
    d_down = run_weight_grad(
        [res[s][7] for s in order], [res[s][3] for s in order], local, True
    )
    d_gate = run_weight_grad(
        [res[s][6] for s in order], [res[s][4] for s in order], local, False
    )
    d_up = run_weight_grad([res[s][6] for s in order], [res[s][5] for s in order], local, False)
    grad_down = lax.psum_scatter(d_down, "dp", scatter_dimension=1, tiled=True).astype(F32)
    grad_gate = lax.psum_scatter(d_gate, "dp", scatter_dimension=1, tiled=True).astype(F32)
    grad_up = lax.psum_scatter(d_up, "dp", scatter_dimension=1, tiled=True).astype(F32)

    d_res, d_attn, d_ctx, d_logits, d_gain_two = run_back_mid(
        resid, cot, masks[0], normed_two, router, dg, gain_two, full_out, dxs
    )
    outs = collect(0, d_ctx)
    block = resid
    for piece in outs:
        block = block + piece.astype(F32)
    block_out = block.astype(BF16).reshape(tokens.shape)

    d_out_w = jnp.einsum("rc,rd->cd", ctx, d_attn, preferred_element_type=F32).astype(BF16)
    d_router_w = jnp.einsum("rd,re->de", normed_two, d_logits, preferred_element_type=F32)

    dq, dk, dv = run_attn_bwd(
        prefix, q, kd, vd, d_ctx, ctx, lse, cos_l, sin_l, cos_t, sin_t
    )
    grad_tok, d_gain_one = run_back_in(dq, dk, dv, w_all, tok, gain_one, d_res)
    d_query_w = jnp.einsum("rd,rc->dc", normed_one, dq, preferred_element_type=F32).astype(BF16)
    d_key_w = jnp.einsum("rd,rc->dc", normed_one, dk, preferred_element_type=F32).astype(BF16)
    d_val_w = jnp.einsum("rd,rc->dc", normed_one, dv, preferred_element_type=F32).astype(BF16)

    small_grad = jnp.concatenate(
        [
            d_router_w[:, :num_experts].astype(BF16),
            d_gain_one.reshape(d, 1).astype(BF16),
            d_gain_two.reshape(d, 1).astype(BF16),
            jnp.zeros((d, 128 - num_experts - 2), BF16),
        ],
        axis=1,
    )

    def reduce_all(value):
        value = value.reshape(n_dp, n_ex, value.shape[0] // (n_dp * n_ex), value.shape[1])
        value = lax.psum_scatter(value, "expert", scatter_dimension=1, tiled=True)
        value = lax.psum_scatter(
            value.reshape(n_dp * value.shape[2], value.shape[3]),
            "dp",
            scatter_dimension=0,
            tiled=True,
        )
        return lax.all_gather(value, "expert", axis=0, tiled=True).astype(F32)

    grad_out = reduce_all(d_out_w)
    rest = reduce_all(jnp.concatenate([d_query_w, d_key_w, d_val_w, small_grad], axis=1))
    grad_query = rest[:, :nq]
    grad_keyval = rest[:, nq : 2 * nq]
    grad_router = rest[:, 2 * nq : 2 * nq + num_experts]
    grad_gain_one = rest[:, 2 * nq + num_experts]
    grad_gain_two = rest[:, 2 * nq + num_experts + 1]

    top = peaks[:, :, :4]
    step = 1
    while step < n_ex:
        top = jnp.maximum(top, swap(top, step))
        step *= 2
    step = 1
    while step < n_dp:
        top = jnp.maximum(top, swap(top, step, "dp", n_dp))
        step *= 2
    head_logit_peak = top[:, 0, :].reshape(heads)
    per_group = heads // kv_heads
    query_factor = jnp.sqrt(query_logit_cap / jnp.maximum(head_logit_peak, query_logit_cap))
    pair_peak = jnp.max(head_logit_peak.reshape(kv_heads, per_group), axis=1)
    pair_cap = jnp.min(query_logit_cap.reshape(kv_heads, per_group), axis=1)
    key_factor = jnp.sqrt(pair_cap / jnp.maximum(pair_peak, pair_cap))
    clipped_query = (w_query.astype(F32) * jnp.repeat(query_factor, head)[None, :]).astype(BF16)
    key_cols = jnp.concatenate(
        [jnp.repeat(key_factor, head), jnp.ones((kv_heads * head,), F32)]
    )
    clipped_keyval = (keyvalue_weight.astype(F32) * key_cols[None, :]).astype(BF16)
    return (
        block_out,
        grad_tok.reshape(tokens.shape),
        grad_query,
        grad_keyval,
        grad_out,
        grad_router,
        grad_gain_one,
        grad_gain_two,
        grad_gate,
        grad_up,
        grad_down,
        clipped_query,
        clipped_keyval,
        head_logit_peak,
    )


def solution(mesh):
    rows3 = P(("dp", "expert"), None, None)
    in_specs = (
        rows3,
        rows3,
        rows3,
        P(("dp", "expert")),
        P("dp", None),
        P("dp", None),
        P("dp", None),
        P("dp", None),
        P("dp"),
        P("dp"),
        P("expert", None, None),
        P("expert", None, None),
        P("expert", None, None),
        P(),
    )
    out_specs = (
        rows3,
        rows3,
        P("dp", None),
        P("dp", None),
        P("dp", None),
        P("dp", None),
        P("dp"),
        P("dp"),
        P("expert", "dp", None),
        P("expert", "dp", None),
        P("expert", "dp", None),
        P("dp", None),
        P("dp", None),
        P(),
    )
    return jax.shard_map(
        functools.partial(on_device, mesh.shape["dp"], mesh.shape["expert"]),
        mesh=mesh,
        in_specs=in_specs,
        out_specs=out_specs,
        check_vma=False,
    )
```

time: 1810 us -> 995 us (0.55)
  matrix products: 406 us -> 13.6 us
  Pallas kernels: 0 us -> 346 us
  blocking collectives: 348 us -> 13.5 us
  local copies, waits for them, and re-layouts: 313 us -> 49.1 us
  other arithmetic: 196 us -> 51.5 us
  waiting for transfers between devices: 500 us -> 479 us
    dot_general x33 -> x5, matrix products: 406 us -> 13.6 us  [the longest x1 3.86 us: on_device(): jnp.einsum('rc,rd->cd', ctx, d_attn, preferred_element_type=F32)]
    all_to_all x3 -> x0, waiting for transfers between devices: 391 us -> none  [the longest x1 168 us: on_device(): lax.all_to_all(d_slots, 'expert', split_axis=0, concat_axis=0, tiled=True)]
    pallas_call x0 -> x13, Pallas kernels: none -> 346 us  [the longest x4 184 us: run_expert(): pl.pallas_call(expert_kernel, grid=(length // b, local), in_specs=[pl.Blo...]
    reduce_scatter x6, waiting for transfers between devices: 16.6 us -> 288 us  [the longest x1 90 us: on_device(): lax.psum_scatter(d_gate, 'dp', scatter_dimension=1, tiled=True).astype(F32)]
    all_to_all x1 -> x0, blocking collectives: 218 us -> none  [on_device(): lax.all_to_all(send_rows, 'expert', split_axis=0, concat_axis=0, tiled=True)]
    gather x4 -> x0, local copies, waits for them, and re-layouts: 192 us -> none  [the longest x1 53.4 us: on_device(): d_route[route_pick]]
    ppermute x0 -> x23, waiting for transfers between devices: none -> 100 us  [swap(): return lax.ppermute(value, axis, [(i, i ^ step) for i in range(n)])]
    all_gather x3 -> x1, waiting for transfers between devices: 0.02 us -> 72.7 us  [on_device(): every = lax.all_gather(mine, ('dp', 'expert'), axis=0, tiled=True)]
  transfers between devices with their start and end apart: 14 -> 31, of which waited for: 6 -> 14; matrix products, arithmetic and copies ran while one was open for 38% -> 8% of each run, Pallas kernels for 0% -> 31%
where the time goes in v1:
time: 995 us; the launch traced here: 985 us
  waiting for transfers between devices  479 us (48%)
  Pallas kernels  346 us (35%)
  other arithmetic  51.5 us (5%)
  local copies, waits for them, and re-layouts  49.1 us (5%)
  starting transfers between devices  16.9 us (2%)
  between operations  15.8 us (2%)
  matrix products  13.6 us (1%)
  blocking collectives  13.5 us (1%)
    pallas_call x4, Pallas kernels, run_expert(): pl.pallas_call(expert_kernel, grid=(length // b, local), in_specs=[pl.Blo...  184 us
    ppermute x23, waiting for transfers between devices, swap(): return lax.ppermute(value, axis, [(i, i ^ step) for i in range(n)])  100 us
    reduce_scatter x1, waiting for transfers between devices, on_device(): lax.psum_scatter(d_gate, 'dp', scatter_dimension=1, tiled=True).astype(F32)  90 us
    reduce_scatter x1, waiting for transfers between devices, on_device(): lax.psum_scatter(d_up, 'dp', scatter_dimension=1, tiled=True).astype(F32)  89.4 us
    all_gather x1, waiting for transfers between devices, on_device(): every = lax.all_gather(mine, ('dp', 'expert'), axis=0, tiled=True)  72.7 us
    pallas_call x3, Pallas kernels, run_weight_grad(): pl.pallas_call(functools.partial(weight_grad_kernel, n, transpose), grid=...  72.7 us
    reduce_scatter x2, waiting for transfers between devices, reduce_all(): lax.psum_scatter(value.reshape(n_dp * value.shape[2], value.shape[3]), 'd...  65 us
    reduce_scatter x1, waiting for transfers between devices, on_device(): lax.psum_scatter(d_down, 'dp', scatter_dimension=1, tiled=True).astype(F32)  43.4 us
  transfers between devices with their start and end apart: 31, of which 14 were waited for; matrix products, arithmetic and copies ran while one was open for 8% of the time, Pallas kernels for 31%

profile of v1, /device:TPU:0, one launch (start us, length us, event | category | flops | bytes accessed | tf_op | source)
XLA Modules:
  0.0 985.2 jit_solution(3246767332125717046)
XLA Ops:
  13.8 72.7 %all-gather.2.cloned.1.call-done.w_ref = bf16[1024,3200]{1,0:T(8,128)(2,1)} async-done(((bf16[32,3200]{1,0:T(8,128)(2,1)}), bf16[1024,3200]{1,0:T(8,128)(2,1)}) %all-gather.2.cloned.1.call-update) | async-done | bytes 6553616 | tf_op jit(solution)/shard_map/all_gather | solution.py:632
  90.6 8.6 qkv.1
  103.2 21.4 %attn_fwd.1 = (bf16[1024,1024]{1,0:T(8,128)(2,1)S(1)}, f32[4,8,1024]{2,1,0:T(8,128)S(1)}, f32[4,8,128]{2,1,0:T(8,128)S(1)}) custom-call(s32[1]{0:T(128)S(6)} %copy.124.prefix_ref, bf16[1024,1024]{1,0:T(8,128)(2,1)S(1)} %get-tuple-element.68.q_ref, bf16[1024,1024]{1,0:T(8,128)(2,1)} %copy-done.20, bf16[1024,1024]{1,0:T(8,128)(2,1)} %copy-done.21), custom_call_target="tpu_custom_call" | custom-call | flops 24999999488 | bytes 9437184 | tf_op jit(solution)/shard_map/attn_fwd/pallas_call | solution.py:175
  144.8 37.6 %collective-permute-done.6 = s32[8,1024]{1,0:T(8,128)S(1)} collective-permute-done((s32[8,1024]{1,0:T(8,128)S(1)}, s32[8,1024]{1,0:T(8,128)S(1)}, u32[]{:S(2)}, u32[]{:S(2)}) %collective-permute-start.6) | collective-permute-done | bytes 32800 | tf_op jit(solution)/shard_map/ppermute | solution.py:618
  205.3 45.9 %experts.5 = (bf16[1024,1024]{1,0:T(8,128)(2,1)}, bf16[1024,1024]{1,0:T(8,128)(2,1)}, f32[8,1024]{1,0:T(8,128)}, bf16[1024,2048]{1,0:T(8,128)(2,1)}, bf16[1024,2...) custom-call(s32[1]{0:T(128)} %bitcast.3.me_ref, ...), custom_call_target="tpu_custom_call" | custom-call | flops 25769803776 | bytes 41943040 | tf_op jit(solution)/shard_map/experts/pallas_call | solution.py:403
  253.1 46.1 %experts.7 = (bf16[1024,1024]{1,0:T(8,128)(2,1)}, bf16[1024,1024]{1,0:T(8,128)(2,1)}, f32[8,1024]{1,0:T(8,128)}, bf16[1024,2048]{1,0:T(8,128)(2,1)}, bf16[1024,2...) custom-call(s32[1]{0:T(128)} %bitcast.3.me_ref, ...), custom_call_target="tpu_custom_call" | custom-call | flops 25769803776 | bytes 41943040 | tf_op jit(solution)/shard_map/experts/pallas_call | solution.py:403
  299.7 46.2 %experts.6 = (bf16[1024,1024]{1,0:T(8,128)(2,1)}, bf16[1024,1024]{1,0:T(8,128)(2,1)}, f32[8,1024]{1,0:T(8,128)}, bf16[1024,2048]{1,0:T(8,128)(2,1)}, bf16[1024,2...) custom-call(s32[1]{0:T(128)} %bitcast.3.me_ref, ...), custom_call_target="tpu_custom_call" | custom-call | flops 25769803776 | bytes 41943040 | tf_op jit(solution)/shard_map/experts/pallas_call | solution.py:403
  352.5 45.9 %experts.4 = (bf16[1024,1024]{1,0:T(8,128)(2,1)}, bf16[1024,1024]{1,0:T(8,128)(2,1)}, f32[8,1024]{1,0:T(8,128)}, bf16[1024,2048]{1,0:T(8,128)(2,1)}, bf16[1024,2...) custom-call(s32[1]{0:T(128)} %bitcast.3.me_ref, ...), custom_call_target="tpu_custom_call" | custom-call | flops 25769803776 | bytes 41943040 | tf_op jit(solution)/shard_map/experts/pallas_call | solution.py:403
  405.6 11.7 %back_mid.1 = (f32[1024,1024]{1,0:T(8,128)}, bf16[1024,1024]{1,0:T(8,128)(2,1)S(1)}, bf16[1024,1024]{1,0:T(8,128)(2,1)S(1)}, bf16[1024,128]{1,0:T(8,128)(2,1)S(1)}, f32[1,1024]{1,0:T(1,128)S(1)}) custom-call(f32[1024,1024]{1,0:T(8,128)} %copy-done, bf16[1024,1024]{1,0:T(8,128)(2,1)} %bitcast.49, bf16[1024,128]{1,0:T(8,128)(2,1)S(1)} %copy-done.6, ...), custom_call_target="tpu_custom_call" | custom-call | flops 2147483648 | bytes 27262976 | tf_op jit(solution)/shard_map/back_mid/pallas_call | solution.py:519
  421.2 32.8 %attn_bwd.1 = (bf16[1024,1024]{1,0:T(8,128)(2,1)}, bf16[1024,512]{1,0:T(8,128)(2,1)}, bf16[1024,512]{1,0:T(8,128)(2,1)}) custom-call(s32[1]{0:T(128)S(6)} %copy.124.prefix_ref, bf16[1024,1024]{1,0:T(8,128)(2,1)} %copy-done.19, bf16[1024,1024]{1,0:T(8,128)(2,1)} %copy-done.20, bf16[1024,1024]{1,0:T(8,128)(2,1)} %copy-done.21, bf16[1024,1024]{1,0:T(8,128)(2,1)} %copy-done.11, ...), custom_call_target="tpu_custom_call" | custom-call | flops 60000002048 | bytes 16777216 | tf_op jit(solution)/shard_map/attn_bwd/pallas_call | solution.py:274
  471.4 10.5 %back_in.1 = (f32[1024,1024]{1,0:T(8,128)}, f32[1,1024]{1,0:T(1,128)S(1)}) custom-call(bf16[1024,1024]{1,0:T(8,128)(2,1)S(1)} %copy-done.4, bf16[1024,512]{1,0:T(8,128)(2,1)S(1)} %copy-done.7, bf16[1024,512]{1,0:T(8,128)(2,1)S(1)} %copy-done.8, bf16[1024,3200]{1,0:T(8,128)(2,1)} %all-gather.2.cloned.1.call-done.w_ref, bf16[1024,1024]{1,0:T(8,128)(2,1)} %bitcast.43, ...), custom_call_target="tpu_custom_call" | custom-call | flops 4294967296 | bytes 20971520 | tf_op jit(solution)/shard_map/back_in/pallas_call | solution.py:577
  483.1 7.8 concatenate.23
  492.1 18.2 %all-reduce.5.cloned.1.call-done = bf16[8,4,32,1024]{3,2,1,0:T(8,128)(2,1)} async-done(((bf16[8,4,32,1024]{3,2,1,0:T(8,128)(2,1)}), bf16[8,4,32,1024]{3,2,1,0:T(8,128)(2,1)}) %all-reduce.5.cloned.1.call-update) | async-done | bytes 2097168
  512.9 24.4 %weight_grad.5 = bf16[4,512,1024]{2,1,0:T(8,128)(2,1)} custom-call(bf16[1024,1024]{1,0:T(8,128)(2,1)} %get-tuple-element.113.refs_0_, bf16[1024,1024]{1,0:T(8,128)(2,1)} %get-tuple-element.114.refs_1_, bf16[1024,1024]{1,0:T(8,128)(2,1)} %get-tuple-element.115.refs_2_, bf16[1024,1024]{1,0:T(8,128)(2,1)} %get-tuple-element.116.refs_3_, ...), custom_call_target="tpu_custom_call" | custom-call | flops 17179869184 | bytes 29360128 | tf_op jit(solution)/shard_map/weight_grad/pallas_call | solution.py:467
  537.4 24.2 %weight_grad.4 = bf16[4,1024,512]{2,1,0:T(8,128)(2,1)} custom-call(bf16[1024,1024]{1,0:T(8,128)(2,1)} %get-tuple-element.101.refs_0_, bf16[1024,1024]{1,0:T(8,128)(2,1)} %get-tuple-element.102.refs_1_, bf16[1024,1024]{1,0:T(8,128)(2,1)} %get-tuple-element.103.refs_2_, bf16[1024,1024]{1,0:T(8,128)(2,1)} %get-tuple-element.104.refs_3_, ...), custom_call_target="tpu_custom_call" | custom-call | flops 17179869184 | bytes 29360128 | tf_op jit(solution)/shard_map/weight_grad/pallas_call | solution.py:467
  561.9 24.1 %weight_grad.3 = bf16[4,1024,512]{2,1,0:T(8,128)(2,1)} custom-call(bf16[1024,1024]{1,0:T(8,128)(2,1)} %get-tuple-element.101.refs_0_, bf16[1024,1024]{1,0:T(8,128)(2,1)} %get-tuple-element.102.refs_1_, bf16[1024,1024]{1,0:T(8,128)(2,1)} %get-tuple-element.103.refs_2_, bf16[1024,1024]{1,0:T(8,128)(2,1)} %get-tuple-element.104.refs_3_, ...), custom_call_target="tpu_custom_call" | custom-call | flops 17179869184 | bytes 29360128 | tf_op jit(solution)/shard_map/weight_grad/pallas_call | solution.py:467
  586.6 6.1 collective-permute-done.16
  598.3 44.9 %collective-permute-done.19 = f32[4,8,4]{2,1,0:T(8,128)S(1)} collective-permute-done((f32[4,8,4]{2,1,0:T(8,128)S(1)}, f32[4,8,4]{2,1,0:T(8,128)S(1)}, u32[]{:S(2)}, u32[]{:S(2)}) %collective-permute-start.19) | collective-permute-done | bytes 544 | tf_op jit(solution)/shard_map/ppermute | solution.py:618
  667.2 6.5 fusion.4
  673.7 43.4 %reduce-scatter.20.cloned.1.call-done = bf16[4,64,1024]{2,1,0:T(8,128)(2,1)} async-done(((bf16[4,512,1024]{2,1,0:T(8,128)(2,1)}), bf16[4,64,1024]{2,1,0:T(8,128)(2,1)}) %reduce-scatter.20.cloned.1.call-update) | async-done | bytes 524304 | tf_op jit(solution)/shard_map/reduce_scatter | solution.py:715
  719.3 89.4 %reduce-scatter.18.cloned.1.call-done = bf16[4,128,512]{2,1,0:T(8,128)(2,1)} async-done(((bf16[4,1024,512]{2,1,0:T(8,128)(2,1)}), bf16[4,128,512]{2,1,0:T(8,128)(2,1)}) %reduce-scatter.18.cloned.1.call-update) | async-done | bytes 524304 | tf_op jit(solution)/shard_map/reduce_scatter | solution.py:717
  810.8 90.0 %reduce-scatter.16.cloned.1.call-done = bf16[4,128,512]{2,1,0:T(8,128)(2,1)} async-done(((bf16[4,1024,512]{2,1,0:T(8,128)(2,1)}), bf16[4,128,512]{2,1,0:T(8,128)(2,1)}) %reduce-scatter.16.cloned.1.call-update) | async-done | bytes 524304 | tf_op jit(solution)/shard_map/reduce_scatter | solution.py:716
  902.9 65.0 %reduce-scatter.12.cloned.1.call-done = bf16[32,2176]{1,0:T(8,128)(2,1)} async-done(((bf16[256,2176]{1,0:T(8,128)(2,1)}), bf16[32,2176]{1,0:T(8,128)(2,1)}) %reduce-scatter.12.cloned.1.call-update) | async-done | bytes 139280 | tf_op jit(solution)/shard_map/reduce_scatter | solution.py:752
  967.9 7.5 all_gather.10
  (239 shorter events, 138.5 us)
Async XLA Ops:
  7.2 79.3 %all-gather.2.cloned.1.call-start = ((), (), s32[]{:S(2)}) async-start(), calls=%async_computation.6 | async-start | bytes 6758400 | tf_op jit(solution)/shard_map/all_gather | solution.py:632
  13.1 497.2 %all-reduce.5.cloned.1.call-start = ((), (), s32[]{:S(2)}) async-start(), calls=%async_computation.13 | async-start | bytes 4194304
  88.0 116.3 %collective-permute-start.5 = (bf16[1024,1024]{1,0:T(8,128)(2,1)}, bf16[1024,1024]{1,0:T(8,128)(2,1)}, u32[]{:S(2)}, u32[]{:S(2)}) collective-permute-start(bf16[1024,1024]{1,0:T(8,128)(2,1)} %bitcast.47), channel_id=1, source_target_pairs={{0,2},{1,3},{2,0},{3,1},{4,6},{5,7},{6,4},{7,5},{8,10},{9,11},{10,... | collective-permute-start | bytes 6291464 | tf_op jit(solution)/shard_map/ppermute | solution.py:618
  134.0 71.3 %collective-permute-start.4 = (bf16[1024,1024]{1,0:T(8,128)(2,1)}, bf16[1024,1024]{1,0:T(8,128)(2,1)}, u32[]{:S(2)}, u32[]{:S(2)}) collective-permute-start(bf16[1024,1024]{1,0:T(8,128)(2,1)} %get-tuple-element.73.x_ref.refs_3_), channel_id=1, source_target_pairs={{0,2},{1,3},{2,0},{3,1},{4,6},{5,7},{6,4},{7,5},{8,10},{9,11},{10,... | collective-permute-start | bytes 6291464 | tf_op jit(solution)/shard_map/ppermute | solution.py:618
  134.5 70.8 %collective-permute-start.1 = (bf16[1024,1024]{1,0:T(8,128)(2,1)S(1)}, bf16[1024,1024]{1,0:T(8,128)(2,1)}, u32[]{:S(2)}, u32[]{:S(2)}) collective-permute-start(bf16[1024,1024]{1,0:T(8,128)(2,1)S(1)} %bitcast.50), channel_id=1, source_target_pairs={{0,1},{1,0},{2,3},{3,2},{4,5},{5,4},{6,7},{7,6},{8,9},{9,8},{10,11... | collective-permute-start | bytes 6291464 | tf_op jit(solution)/shard_map/ppermute | solution.py:618
  134.5 70.8 %collective-permute-start = (bf16[1024,1024]{1,0:T(8,128)(2,1)}, bf16[1024,1024]{1,0:T(8,128)(2,1)}, u32[]{:S(2)}, u32[]{:S(2)}) collective-permute-start(bf16[1024,1024]{1,0:T(8,128)(2,1)} %get-tuple-element.73.x_ref.refs_3_), channel_id=1, source_target_pairs={{0,1},{1,0},{2,3},{3,2},{4,5},{5,4},{6,7},{7,6},{8,9},{9,8},{10,11... | collective-permute-start | bytes 6291464 | tf_op jit(solution)/shard_map/ppermute | solution.py:618
  141.7 40.7 %collective-permute-start.6 = (s32[8,1024]{1,0:T(8,128)S(1)}, s32[8,1024]{1,0:T(8,128)S(1)}, u32[]{:S(2)}, u32[]{:S(2)}) collective-permute-start(s32[8,1024]{1,0:T(8,128)S(1)} %bitcast.59), channel_id=1, source_target_pairs={{0,2},{1,3},{2,0},{3,1},{4,6},{5,7},{6,4},{7,5},{8,10},{9,11},{10,... | collective-permute-start | bytes 98312 | tf_op jit(solution)/shard_map/ppermute | solution.py:618
  204.3 47.5 %collective-permute-start.9 = (bf16[1024,1024]{1,0:T(8,128)(2,1)}, bf16[1024,1024]{1,0:T(8,128)(2,1)S(1)}, u32[]{:S(2)}, u32[]{:S(2)}) collective-permute-start(bf16[1024,1024]{1,0:T(8,128)(2,1)} %collective-permute-done.5.c_ref), channel_id=1, source_target_pairs={{0,1},{1,0},{2,3},{3,2},{4,5},{5,4},{6,7},{7,6},{8,9},{9,8},{10,11... | collective-permute-start | bytes 6291464 | tf_op jit(solution)/shard_map/ppermute | solution.py:618
  205.2 46.5 %collective-permute-start.8 = (bf16[1024,1024]{1,0:T(8,128)(2,1)}, bf16[1024,1024]{1,0:T(8,128)(2,1)}, u32[]{:S(2)}, u32[]{:S(2)}) collective-permute-start(bf16[1024,1024]{1,0:T(8,128)(2,1)} %collective-permute-done.4.x_ref), channel_id=1, source_target_pairs={{0,1},{1,0},{2,3},{3,2},{4,5},{5,4},{6,7},{7,6},{8,9},{9,8},{10,11... | collective-permute-start | bytes 6291464 | tf_op jit(solution)/shard_map/ppermute | solution.py:618
  251.2 148.3 %collective-permute-start.3 = (f32[8,1024]{1,0:T(8,128)}, f32[8,1024]{1,0:T(8,128)S(1)}, u32[]{:S(2)}, u32[]{:S(2)}) collective-permute-start(f32[8,1024]{1,0:T(8,128)} %get-tuple-element.78), channel_id=1, source_target_pairs={{0,1},{1,0},{2,3},{3,2},{4,5},{5,4},{6,7},{7,6},{8,9},{9,8},{10,11... | collective-permute-start | bytes 98312 | tf_op jit(solution)/shard_map/ppermute | solution.py:618
  251.7 152.5 %collective-permute-start.12 = (bf16[1024,1024]{1,0:T(8,128)(2,1)}, bf16[1024,1024]{1,0:T(8,128)(2,1)S(1)}, u32[]{:S(2)}, u32[]{:S(2)}) collective-permute-start(bf16[1024,1024]{1,0:T(8,128)(2,1)} %get-tuple-element.82), channel_id=1, source_target_pairs={{0,1},{1,0},{2,3},{3,2},{4,5},{5,4},{6,7},{7,6},{8,9},{9,8},{10,11... | collective-permute-start | bytes 6291464 | tf_op jit(solution)/shard_map/ppermute | solution.py:618
  299.2 48.3 %collective-permute-start.13 = (bf16[1024,1024]{1,0:T(8,128)(2,1)}, bf16[1024,1024]{1,0:T(8,128)(2,1)S(1)}, u32[]{:S(2)}, u32[]{:S(2)}) collective-permute-start(bf16[1024,1024]{1,0:T(8,128)(2,1)} %get-tuple-element.84), channel_id=1, source_target_pairs={{0,1},{1,0},{2,3},{3,2},{4,5},{5,4},{6,7},{7,6},{8,9},{9,8},{10,11... | collective-permute-start | bytes 6291464 | tf_op jit(solution)/shard_map/ppermute | solution.py:618
  346.0 54.6 %collective-permute-start.7 = (f32[8,1024]{1,0:T(8,128)}, f32[8,1024]{1,0:T(8,128)S(1)}, u32[]{:S(2)}, u32[]{:S(2)}) collective-permute-start(f32[8,1024]{1,0:T(8,128)} %get-tuple-element.79), channel_id=1, source_target_pairs={{0,2},{1,3},{2,0},{3,1},{4,6},{5,7},{6,4},{7,5},{8,10},{9,11},{10,... | collective-permute-start | bytes 98312 | tf_op jit(solution)/shard_map/ppermute | solution.py:618
  347.2 54.4 %collective-permute-start.11 = (f32[8,1024]{1,0:T(8,128)S(1)}, f32[8,1024]{1,0:T(8,128)S(1)}, u32[]{:S(2)}, u32[]{:S(2)}) collective-permute-start(f32[8,1024]{1,0:T(8,128)S(1)} %copy-done.35), channel_id=1, source_target_pairs={{0,3},{1,2},{2,1},{3,0},{4,7},{5,6},{6,5},{7,4},{8,11},{9,10},{10,... | collective-permute-start | bytes 98312 | tf_op jit(solution)/shard_map/ppermute | solution.py:618
  351.3 52.9 %collective-permute-start.14 = (bf16[1024,1024]{1,0:T(8,128)(2,1)}, bf16[1024,1024]{1,0:T(8,128)(2,1)}, u32[]{:S(2)}, u32[]{:S(2)}) collective-permute-start(bf16[1024,1024]{1,0:T(8,128)(2,1)} %add_convert_fusion.2), channel_id=1, source_target_pairs={{0,2},{1,3},{2,0},{3,1},{4,6},{5,7},{6,4},{7,5},{8,10},{9,11},{10,... | collective-permute-start | bytes 6291464 | tf_op jit(solution)/shard_map/ppermute | solution.py:618
  460.4 135.0 %reduce-scatter.10.cloned.1.call-start = ((), (), s32[]{:S(2)}) async-start(), calls=%async_computation.7 | async-start | bytes 5570560 | tf_op jit(solution)/shard_map/reduce_scatter | solution.py:751
  490.9 169.5 %reduce-scatter.14.cloned.1.call-start = ((), (), s32[]{:S(2)}) async-start(), calls=%async_computation.9 | async-start | bytes 589824 | tf_op jit(solution)/shard_map/reduce_scatter | solution.py:752
  512.8 204.3 %reduce-scatter.20.cloned.1.call-start = ((), (), s32[]{:S(2)}) async-start(), calls=%async_computation.12 | async-start | bytes 4718592 | tf_op jit(solution)/shard_map/reduce_scatter | solution.py:715
  537.4 271.3 %reduce-scatter.18.cloned.1.call-start = ((), (), s32[]{:S(2)}) async-start(), calls=%async_computation.11 | async-start | bytes 4718592 | tf_op jit(solution)/shard_map/reduce_scatter | solution.py:717
  561.6 339.2 %reduce-scatter.16.cloned.1.call-start = ((), (), s32[]{:S(2)}) async-start(), calls=%async_computation.10 | async-start | bytes 4718592 | tf_op jit(solution)/shard_map/reduce_scatter | solution.py:716
  586.0 381.9 %reduce-scatter.12.cloned.1.call-start = ((), (), s32[]{:S(2)}) async-start(), calls=%async_computation.8 | async-start | bytes 1253376 | tf_op jit(solution)/shard_map/reduce_scatter | solution.py:752
  586.1 81.1 %collective-permute-start.15 = (bf16[1024,1024]{1,0:T(8,128)(2,1)}, bf16[1024,1024]{1,0:T(8,128)(2,1)}, u32[]{:S(2)}, u32[]{:S(2)}) collective-permute-start(bf16[1024,1024]{1,0:T(8,128)(2,1)} %get-tuple-element.86), channel_id=1, source_target_pairs={{0,1},{1,0},{2,3},{3,2},{4,5},{5,4},{6,7},{7,6},{8,9},{9,8},{10,11... | collective-permute-start | bytes 6291464 | tf_op jit(solution)/shard_map/ppermute | solution.py:618
  595.0 72.2 %collective-permute-start.17 = (bf16[1024,1024]{1,0:T(8,128)(2,1)}, bf16[1024,1024]{1,0:T(8,128)(2,1)}, u32[]{:S(2)}, u32[]{:S(2)}) collective-permute-start(bf16[1024,1024]{1,0:T(8,128)(2,1)} %add_convert_fusion.1), channel_id=1, source_target_pairs={{0,2},{1,3},{2,0},{3,1},{4,6},{5,7},{6,4},{7,5},{8,10},{9,11},{10,... | collective-permute-start | bytes 6291464 | tf_op jit(solution)/shard_map/ppermute | solution.py:618
  596.7 46.5 %collective-permute-start.19 = (f32[4,8,4]{2,1,0:T(8,128)S(1)}, f32[4,8,4]{2,1,0:T(8,128)S(1)}, u32[]{:S(2)}, u32[]{:S(2)}) collective-permute-start(f32[4,8,4]{2,1,0:T(8,128)S(1)} %slice_maximum_fusion.1), channel_id=1, source_target_pairs={{0,2},{1,3},{2,0},{3,1},{4,6},{5,7},{6,4},{7,5},{8,10},{9,11},{10,... | collective-permute-start | bytes 1544 | tf_op jit(solution)/shard_map/ppermute | solution.py:618
  (44 other events, 682.3 us)
Sparse Core Ops, SparseCore 0:
  13.2 73.2 all-gather.1
  460.5 49.7 all-reduce.4
  513.0 46.2 reduce-scatter.9
  563.0 61.9 reduce-scatter.13
  628.9 88.1 reduce-scatter.19
  720.6 87.9 reduce-scatter.17
  812.7 88.0 reduce-scatter.15
  904.2 63.6 reduce-scatter.11

commit v2 on v1

--- a/solution.py
+++ b/solution.py
@@ -14,6 +14,7 @@
 BF16 = jnp.bfloat16
 NEG = -1e30
 MIB = 1 << 20
+SCALE = 0.5
 
 
 def dot(a, b):
@@ -30,8 +31,8 @@
     )
 
 
-def cost(flops, nbytes, trans=0):
-    return pl.CostEstimate(flops=int(flops), bytes_accessed=int(nbytes), transcendentals=int(trans))
+def took(us):
+    return pl.CostEstimate(flops=int(us * SCALE * 1e9), bytes_accessed=1000, transcendentals=0)
 
 
 def spec(shape, index):
@@ -62,12 +63,12 @@
     return x * cos + partner * sin
 
 
-def qkv_kernel(tok_ref, gain_ref, w_ref, cos_ref, sin_ref, h_ref, q_ref, kd_ref, vd_ref):
+def qkv_kernel(tok_ref, gain_ref, w_ref, cos_ref, sin_ref, ht_ref, q_ref, kd_ref, vd_ref):
     x = tok_ref[...].astype(F32)
     d = x.shape[1]
     r = lax.rsqrt(jnp.mean(x * x, axis=1, keepdims=True) + EPS)
     h = (x * r * gain_ref[...].astype(F32)).astype(BF16)
-    h_ref[...] = h
+    ht_ref[...] = h.T
     cos, sin = cos_ref[...], sin_ref[...]
     rows = x.shape[0]
     first = lane_half((rows, 128), 64)
@@ -107,11 +108,11 @@
             spec((b, 128), row),
             spec((b, 128), row),
         ],
-        out_specs=[spec((b, d), row)] + [spec((b, nq), row)] * 3,
-        out_shape=[jax.ShapeDtypeStruct((length, d), BF16)]
+        out_specs=[spec((d, b), lambda i: (0, i))] + [spec((b, nq), row)] * 3,
+        out_shape=[jax.ShapeDtypeStruct((d, length), BF16)]
         + [jax.ShapeDtypeStruct((length, nq), BF16)] * 3,
-        compiler_params=params(40),
-        cost_estimate=cost(2 * length * d * 2 * nq, 16 * MIB),
+        compiler_params=params(60),
+        cost_estimate=took(9),
         name="qkv",
     )(tok, gain, w_qkv, cos, sin)
 
@@ -186,8 +187,8 @@
             jax.ShapeDtypeStruct((groups, 8, length), F32),
             jax.ShapeDtypeStruct((groups, 8, 128), F32),
         ],
-        compiler_params=params(48),
-        cost_estimate=cost(25e9, 9 * MIB),
+        compiler_params=params(60),
+        cost_estimate=took(21),
         name="attn_fwd",
     )(prefix, q, kd, vd)
 
@@ -290,8 +291,8 @@
             pltpu.VMEM((2, length, 128), F32),
             pltpu.VMEM((2, 128, length), BF16),
         ],
-        compiler_params=params(56),
-        cost_estimate=cost(60e9, 16 * MIB),
+        compiler_params=params(60),
+        cost_estimate=took(33),
         name="attn_bwd",
     )(prefix, q, kd, vd, d_ctx, ctx, lse, cos, sin, cos_t, sin_t)
 
@@ -321,38 +322,55 @@
             jax.ShapeDtypeStruct((length, d), F32),
             jax.ShapeDtypeStruct((length, d), BF16),
         ],
-        compiler_params=params(40),
-        cost_estimate=cost(2 * length * d * d, 12 * MIB),
+        compiler_params=params(60),
+        cost_estimate=took(4),
         name="mid",
     )(tok, ctx, w_out, gain)
 
 
-def gates_of(x, router, mask):
-    logits = dot(x, router)
-    logits = jnp.where(mask > 0, logits, NEG)
-    e = jnp.exp(logits - jnp.max(logits, axis=1, keepdims=True))
-    e = jnp.where(mask > 0, e, 0.0)
-    return e / jnp.sum(e, axis=1, keepdims=True)
+def gates_of(x, router, routes_t):
+    logits = dot(x, router).T
+    expert = lax.broadcasted_iota(jnp.int32, logits.shape, 0)
+    hit = expert == routes_t[0:1]
+    for k in range(1, routes_t.shape[0]):
+        hit = hit | (expert == routes_t[k : k + 1])
+    logits = jnp.where(hit, logits, NEG)
+    e = jnp.exp(logits - jnp.max(logits, axis=0, keepdims=True))
+    e = jnp.where(hit, e, 0.0)
+    return e / jnp.sum(e, axis=0, keepdims=True)
 
 
 def expert_kernel(
-    me_ref, x_ref, c_ref, mask_ref, router_ref, wg_ref, wu_ref, wd_ref,
-    out_ref, dx_ref, dg_ref, hs_ref, dgate_ref, dup_ref, xt_ref, ct_ref, out_acc, dx_acc, gp_ref, dgc_ref,
+    first_expert, local, with_init, me_ref, x_ref, c_ref, route_ref, router_ref, wg_ref, wu_ref, wd_ref, *refs
 ):
+    if with_init:
+        out_in, dx_in, dg_in, refs = refs[0], refs[1], refs[2], refs[3:]
+        out_ref, dx_ref, dg_ref, hs_ref, dgate_ref, dup_ref, out_acc, dx_acc, gp_ref, dgc_ref = refs
+    else:
+        out_ref, dx_ref, dg_ref, hs_ref, dgate_ref, dup_ref, xt_ref, ct_ref, out_acc, dx_acc, gp_ref, dgc_ref = refs
     e = pl.program_id(1)
-    local = pl.num_programs(1)
+    last = pl.num_programs(1) - 1
     x, c = x_ref[...], c_ref[...]
     b = x.shape[0]
     lane = lax.broadcasted_iota(jnp.int32, (b, 128), 1)
 
     @pl.when(e == 0)
     def _():
-        gp_ref[...] = gates_of(x, router_ref[...], mask_ref[...].astype(F32))
-        xt_ref[...] = x.T
-        ct_ref[...] = c.T
+        gp_ref[...] = gates_of(x, router_ref[...], route_ref[...]).T
+        dgc_ref[...] = jnp.zeros_like(dgc_ref)
+        if with_init:
+            out_acc[...] = out_in[...].astype(F32)
+            dx_acc[...] = dx_in[...].astype(F32)
+        else:
+            out_acc[...] = jnp.zeros_like(out_acc)
+            dx_acc[...] = jnp.zeros_like(dx_acc)
+            xt_ref[...] = x.T
+            ct_ref[...] = c.T
 
     gp = jnp.sum(
-        jnp.where(lane == me_ref[0] * local + e, gp_ref[...], 0.0), axis=1, keepdims=True
+        jnp.where(lane == me_ref[0] * local + first_expert + e, gp_ref[...], 0.0),
+        axis=1,
+        keepdims=True,
     )
     gate = dot(x, wg_ref[e])
     up = dot(x, wu_ref[e])
@@ -370,123 +388,143 @@
     dgate_ref[...] = dgate
     out = dot(hs, wd_ref[e])
     dx = dot_t(dgate, wg_ref[e]) + dot_t(dup, wu_ref[e])
-    dg_col = jnp.where(lane == e, dg, 0.0)
-
-    @pl.when(e == 0)
-    def _():
-        out_acc[...] = out
-        dx_acc[...] = dx
-        dgc_ref[...] = dg_col
-
-    @pl.when((e > 0) & (e < local - 1))
+    dgc_ref[...] += jnp.where(lane == first_expert + e, dg, 0.0)
+
+    @pl.when(e < last)
     def _():
         out_acc[...] += out
         dx_acc[...] += dx
-        dgc_ref[...] += dg_col
-
-    @pl.when(e == local - 1)
+
+    @pl.when(e == last)
     def _():
         out_ref[...] = (out_acc[...] + out).astype(BF16)
         dx_ref[...] = (dx_acc[...] + dx).astype(BF16)
-        dg_ref[...] = (dgc_ref[...] + dg_col).T[:8]
-
-
-def run_expert(me, x, c, mask, router, wg, wu, wd):
+        dg_t = dgc_ref[...].T[:8]
+        dg_ref[...] = dg_t + dg_in[...] if with_init else dg_t
+
+
+def run_expert(me, x, c, routes_t, router, wg, wu, wd, first, count, init=None):
     length, d = x.shape
     local, _, ff = wg.shape
     b = 512
+    top = routes_t.shape[0]
     row = lambda i, e: (i, 0)
-    colT = lambda i, e: (0, i)
-    once = lambda shape: pl.BlockSpec(
-        shape, lambda i, e: (0,) * len(shape), pipeline_mode=pl.Buffered(1)
-    )
+    col_t = lambda i, e: (0, i)
+    pick = lambda shape: pl.BlockSpec(
+        (count,) + shape[1:],
+        lambda i, e: (first // count, 0, 0),
+        pipeline_mode=pl.Buffered(1),
+    )
+    wide = jax.ShapeDtypeStruct((length, count * ff), BF16)
+    full = jax.ShapeDtypeStruct((length, d), BF16)
+    turned = jax.ShapeDtypeStruct((d, length), BF16)
+    wide_spec = spec((b, ff), lambda i, e: (i, e))
+    with_init = init is not None
     return pl.pallas_call(
-        expert_kernel,
-        grid=(length // b, local),
+        functools.partial(expert_kernel, first, local, with_init),
+        grid=(length // b, count),
         in_specs=[
             pl.BlockSpec(memory_space=pltpu.SMEM),
             spec((b, d), row),
             spec((b, d), row),
-            spec((b, 128), row),
-            once(router.shape),
-            once(wg.shape),
-            once(wu.shape),
-            once(wd.shape),
-        ],
-        out_specs=[
-            spec((b, d), row),
-            spec((b, d), row),
-            spec((8, b), colT),
-            spec((b, ff), lambda i, e: (i, e)),
-            spec((b, ff), lambda i, e: (i, e)),
-            spec((b, ff), lambda i, e: (i, e)),
-            spec((d, b), colT),
-            spec((d, b), colT),
-        ],
-        out_shape=[
-            jax.ShapeDtypeStruct((length, d), BF16),
-            jax.ShapeDtypeStruct((length, d), BF16),
-            jax.ShapeDtypeStruct((8, length), F32),
-            jax.ShapeDtypeStruct((length, local * ff), BF16),
-            jax.ShapeDtypeStruct((length, local * ff), BF16),
-            jax.ShapeDtypeStruct((length, local * ff), BF16),
-            jax.ShapeDtypeStruct((d, length), BF16),
-            jax.ShapeDtypeStruct((d, length), BF16),
-        ],
+            spec((top, b), col_t),
+            pl.BlockSpec(router.shape, lambda i, e: (0, 0), pipeline_mode=pl.Buffered(1)),
+            pick(wg.shape),
+            pick(wu.shape),
+            pick(wd.shape),
+        ]
+        + ([spec((b, d), row)] * 2 + [spec((8, b), col_t)] if with_init else []),
+        out_specs=[spec((b, d), row)] * 2
+        + [spec((8, b), col_t)]
+        + [wide_spec] * 3
+        + ([] if with_init else [spec((d, b), col_t)] * 2),
+        out_shape=[full, full, jax.ShapeDtypeStruct((8, length), F32), wide, wide, wide]
+        + ([] if with_init else [turned, turned]),
         scratch_shapes=[
             pltpu.VMEM((b, d), F32),
             pltpu.VMEM((b, d), F32),
             pltpu.VMEM((b, 128), F32),
             pltpu.VMEM((b, 128), F32),
         ],
-        compiler_params=params(58, 2),
-        cost_estimate=cost(12 * length * d * ff * local, 40 * MIB, length * ff * local),
+        compiler_params=params(60, 2),
+        cost_estimate=took(12 * count),
         name="experts",
-    )(me, x, c, mask, router, wg, wu, wd)
-
-
-def weight_grad_kernel(n, transpose, *refs):
-    lefts, rights, out_ref = refs[:n], refs[n : 2 * n], refs[2 * n]
-    d = lefts[0].shape[0]
-    for m in range(0, d, 256):
+    )(me, x, c, routes_t, router, wg, wu, wd, *(init if with_init else ()))
+
+
+def weight_grad_kernel(n, *refs):
+    xt, ct, dgate, dup, hs = (refs[k * n : (k + 1) * n] for k in range(5))
+    gate_ref, up_ref, down_ref = refs[5 * n :]
+
+    def total(lefts, rights):
         acc = None
         for left, right in zip(lefts, rights):
-            part = dot(left[m : m + 256, :], right[...])
+            part = dot(left[...], right[...])
             acc = part if acc is None else acc + part
-        if transpose:
-            out_ref[0, :, m : m + 256] = acc.T.astype(BF16)
-        else:
-            out_ref[0, m : m + 256, :] = acc.astype(BF16)
-
-
-def run_weight_grad(lefts, rights, local, transpose):
-    n = len(lefts)
-    d, length = lefts[0].shape
-    ff = rights[0].shape[1] // local
-    shape = (ff, d) if transpose else (d, ff)
+        return acc
+
+    down = total(ct, hs).T.astype(BF16)
+    gate = total(xt, dgate).astype(BF16)
+    up = total(xt, dup).astype(BF16)
+    for p in range(down_ref.shape[0]):
+        rows = down_ref.shape[3]
+        down_ref[p, 0, 0] = down[p * rows : (p + 1) * rows]
+    for p in range(gate_ref.shape[0]):
+        rows = gate_ref.shape[2]
+        gate_ref[p, 0] = gate[p * rows : (p + 1) * rows]
+        up_ref[p, 0] = up[p * rows : (p + 1) * rows]
+
+
+def run_weight_grad(xt, ct, dgate, dup, hs, count, skips, n_dp):
+    n = len(xt)
+    d, length = xt[0].shape
+    ff = hs[-1].shape[1] // count
+    m = 256
+    left = spec((m, length), lambda e, i: (i, 0))
+    rights = [
+        spec((length, ff), functools.partial(lambda skip, e, i: (0, e + skip), skip))
+        for skip in skips
+    ]
+    per = d // n_dp
+    rows = jax.ShapeDtypeStruct((n_dp, count, per, ff), BF16)
+    row_spec = spec((m // per, 1, per, ff), lambda e, i: (i, e, 0, 0))
     return pl.pallas_call(
-        functools.partial(weight_grad_kernel, n, transpose),
-        grid=(local,),
-        in_specs=[
-            pl.BlockSpec((d, length), lambda e: (0, 0), pipeline_mode=pl.Buffered(1))
-            for _ in lefts
-        ]
-        + [spec((length, ff), lambda e: (0, e)) for _ in rights],
-        out_specs=spec((1,) + shape, lambda e: (e, 0, 0)),
-        out_shape=jax.ShapeDtypeStruct((local,) + shape, BF16),
-        compiler_params=params(56),
-        cost_estimate=cost(2 * n * length * d * ff * local, (n * 6 + 4) * MIB),
+        functools.partial(weight_grad_kernel, n),
+        grid=(count, d // m),
+        in_specs=[left] * (2 * n) + rights * 3,
+        out_specs=[
+            row_spec,
+            row_spec,
+            spec((n_dp, 1, 1, ff // n_dp, m), lambda e, i: (0, e, i // (ff // m), 0, i % (ff // m))),
+        ],
+        out_shape=[
+            rows,
+            rows,
+            jax.ShapeDtypeStruct((n_dp, count, d // ff, ff // n_dp, ff), BF16),
+        ],
+        compiler_params=params(60, 2),
+        cost_estimate=took(37),
         name="weight_grad",
-    )(*lefts, *rights)
-
-
-def back_mid_kernel(n, *refs):
-    (res_ref, cot_ref, mask_ref, x_ref, router_ref, dg_ref, gain_ref, w_ref) = refs[:8]
-    dx_refs = refs[8 : 8 + n]
-    dres_ref, dattn_ref, dctx_ref, dlog_ref, ggain_ref = refs[8 + n :]
-    gp = gates_of(x_ref[...], router_ref[...], mask_ref[...].astype(F32))
-    dg = dg_ref[...]
-    d_logits = (gp * (dg - jnp.sum(gp * dg, axis=1, keepdims=True))).astype(BF16)
+    )(*xt, *ct, *dgate, *dup, *hs)
+
+
+def back_mid_kernel(n, n_ex, local, *refs):
+    (me_ref, res_ref, cot_ref, route_ref, x_ref, router_ref, gain_ref, w_ref) = refs[:8]
+    dx_refs, dg_refs = refs[8 : 8 + n], refs[8 + n : 8 + n + n_ex]
+    dres_ref, dattn_ref, dctx_ref, dlog_ref, ggain_ref = refs[8 + n + n_ex :]
+    gp = gates_of(x_ref[...], router_ref[...], route_ref[...])
+    parts = [ref[...][:local] for ref in dg_refs]
+    owners = []
+    for owner in range(n_ex):
+        own = jnp.zeros_like(parts[0])
+        for step in range(n_ex):
+            own = jnp.where((owner ^ step) == me_ref[0], parts[step], own)
+        owners.append(own)
+    dg = jnp.concatenate(owners, axis=0)
+    gp = gp[: dg.shape[0]]
+    d_logits = gp * (dg - jnp.sum(gp * dg, axis=0, keepdims=True))
+    fill = jnp.zeros((128 - dg.shape[0], dg.shape[1]), F32)
+    d_logits = jnp.concatenate([d_logits, fill], axis=0).T.astype(BF16)
     dlog_ref[...] = d_logits
     d_norm = dot_t(d_logits, router_ref[...])
     for ref in dx_refs:
@@ -511,25 +549,26 @@
     dctx_ref[...] = dot_t(d_attn, w_ref[...]).astype(BF16)
 
 
-def run_back_mid(res, cot, mask, x, router, dg, gain, w_out, dxs):
+def run_back_mid(me, res, cot, routes_t, x, router, gain, w_out, dxs, dgs, local):
     length, d = res.shape
     b = 256
     row = lambda i: (i, 0)
-    n = len(dxs)
+    n, n_ex = len(dxs), len(dgs)
     return pl.pallas_call(
-        functools.partial(back_mid_kernel, n),
+        functools.partial(back_mid_kernel, n, n_ex, local),
         grid=(length // b,),
         in_specs=[
+            pl.BlockSpec(memory_space=pltpu.SMEM),
             spec((b, d), row),
             spec((b, d), row),
-            spec((b, 128), row),
+            spec((routes_t.shape[0], b), lambda i: (0, i)),
             spec((b, d), row),
             whole(router.shape),
-            spec((b, 128), row),
             whole((1, d)),
             whole(w_out.shape),
         ]
-        + [spec((b, d), row)] * n,
+        + [spec((b, d), row)] * n
+        + [spec((8, b), lambda i: (0, i))] * n_ex,
         out_specs=[
             spec((b, d), row),
             spec((b, d), row),
@@ -544,10 +583,10 @@
             jax.ShapeDtypeStruct((length, 128), BF16),
             jax.ShapeDtypeStruct((1, d), F32),
         ],
-        compiler_params=params(48),
-        cost_estimate=cost(2 * length * d * d, 26 * MIB),
+        compiler_params=params(60),
+        cost_estimate=took(11),
         name="back_mid",
-    )(res, cot, mask, x, router, dg, gain, w_out, *dxs)
+    )(me, res, cot, routes_t, x, router, gain, w_out, *dxs, *dgs)
 
 
 def back_in_kernel(dq_ref, dk_ref, dv_ref, w_ref, tok_ref, gain_ref, dres_ref, gt_ref, ggain_ref):
@@ -588,10 +627,149 @@
         ],
         out_specs=[spec((b, d), row), whole((1, d))],
         out_shape=[jax.ShapeDtypeStruct((length, d), F32), jax.ShapeDtypeStruct((1, d), F32)],
-        compiler_params=params(48),
-        cost_estimate=cost(4 * length * d * nq, 20 * MIB),
+        compiler_params=params(60),
+        cost_estimate=took(10),
         name="back_in",
     )(dq, dk, dv, w_qkv, tok, gain, d_res)
+
+
+def finish_kernel(
+    ht_ref, dq_ref, dk_ref, dv_ref, dout_ref, small_ref, out_ref,
+    b1, r1, s1, r2, s2, r3, s3, r4, sem_s, sem_r,
+):
+    dp, ex = lax.axis_index("dp"), lax.axis_index("expert")
+    z, x, y, c = dp // 2, dp % 2, ex // 2, ex % 2
+    core = [(dp, ex ^ 1)]
+    plane = [(dp ^ 1, ex), (dp, ex ^ 2), (dp ^ 1, ex ^ 2)]
+    line = [(dp ^ (2 * k), ex) for k in (1, 2, 3)]
+    group = [(dp, ex ^ k) for k in (1, 2, 3)]
+    barrier = pltpu.get_barrier_semaphore()
+    peers = core + plane + line + group[2:]
+    for peer in peers:
+        pl.semaphore_signal(barrier, inc=1, device_id=peer, device_id_type=pl.DeviceIdType.MESH)
+    pl.semaphore_wait(barrier, len(peers))
+
+    n = b1.shape[0]
+    widths = [dout_ref.shape[1], dq_ref.shape[1], dk_ref.shape[1] + dv_ref.shape[1], 128]
+    starts = [sum(widths[:k]) for k in range(n)]
+    started = {}
+
+    def send(k, slot, src, dst, peer):
+        copy = pltpu.make_async_remote_copy(
+            src_ref=src,
+            dst_ref=dst,
+            send_sem=sem_s.at[k, slot],
+            recv_sem=sem_r.at[k, slot],
+            device_id=peer,
+            device_id_type=pl.DeviceIdType.MESH,
+        )
+        copy.start()
+        started[k, slot] = copy
+
+    def arrive(k, slots):
+        for slot in slots:
+            started[k, slot].wait()
+
+    def place(k, lanes, value):
+        for p in range(8):
+            for e in range(4):
+                row = 128 * p + 32 * e
+                b1[k, e % 2, e // 2, p % 2, p // 2, :, lanes] = value[row : row + 32]
+
+    def step0(k):
+        if k == 0:
+            place(k, slice(0, widths[k]), dout_ref[...])
+        elif k == 1:
+            for col in range(0, widths[1], 512):
+                part = dot(ht_ref[...], dq_ref[:, col : col + 512])
+                place(k, slice(col, col + 512), part.astype(BF16))
+        elif k == 2:
+            half = dk_ref.shape[1]
+            place(k, slice(0, half), dot(ht_ref[...], dk_ref[...]).astype(BF16))
+            place(k, slice(half, 2 * half), dot(ht_ref[...], dv_ref[...]).astype(BF16))
+        else:
+            place(k, slice(0, 128), small_ref[...])
+        w = slice(0, widths[k])
+        send(k, 0, b1.at[k, 1 - c, :, :, :, :, w], r1.at[k, :, :, :, :, w], core[0])
+
+    def step1(k):
+        arrive(k, [0])
+        w = slice(0, widths[k])
+        for yy in range(2):
+            for xx in range(2):
+                for zz in range(4):
+                    s1[k, yy, xx, zz, :, w] = (
+                        b1[k, c, yy, xx, zz, :, w].astype(F32)
+                        + r1[k, yy, xx, zz, :, w].astype(F32)
+                    ).astype(BF16)
+        for i, (dy, dx) in enumerate([(0, 1), (1, 0), (1, 1)]):
+            send(k, 1 + i, s1.at[k, y ^ dy, x ^ dx, :, :, w], r2.at[k, i, :, :, w], plane[i])
+
+    def step2(k):
+        arrive(k, [1, 2, 3])
+        w = slice(0, widths[k])
+        for zz in range(4):
+            total = s1[k, y, x, zz, :, w].astype(F32)
+            for i in range(3):
+                total = total + r2[k, i, zz, :, w].astype(F32)
+            s2[k, zz, :, w] = total.astype(BF16)
+        for i in range(3):
+            send(k, 4 + i, s2.at[k, z ^ (i + 1), :, w], r3.at[k, i, :, w], line[i])
+
+    def step3(k):
+        arrive(k, [4, 5, 6])
+        w = slice(0, widths[k])
+        total = s2[k, z, :, w].astype(F32)
+        for i in range(3):
+            total = total + r3[k, i, :, w].astype(F32)
+        s3[k, :, w] = total.astype(BF16)
+        for i in range(3):
+            send(k, 7 + i, s3.at[k, :, w], r4.at[k, i, :, w], group[i])
+
+    def step4(k):
+        arrive(k, [7, 8, 9])
+        w, o = slice(0, widths[k]), slice(starts[k], starts[k] + widths[k])
+        out_ref[pl.ds(pl.multiple_of(ex * 32, 32), 32), o] = s3[k, :, w].astype(F32)
+        for i in range(3):
+            rows = pl.ds(pl.multiple_of((ex ^ (i + 1)) * 32, 32), 32)
+            out_ref[rows, o] = r4[k, i, :, w].astype(F32)
+
+    steps = (step0, step1, step2, step3, step4)
+    order = [3, 0, 1, 2]
+    for turn in range(n + len(steps) - 1):
+        for place_in, k in enumerate(order):
+            at = turn - place_in
+            if 0 <= at < len(steps):
+                steps[at](k)
+
+
+def run_finish(ht, dq, dk, dv, d_out, small):
+    d = ht.shape[0]
+    n, w = 4, d
+    columns = d_out.shape[1] + dq.shape[1] + dk.shape[1] + dv.shape[1] + small.shape[1]
+    return pl.pallas_call(
+        finish_kernel,
+        in_specs=[pl.BlockSpec(memory_space=pltpu.VMEM)] * 6,
+        out_specs=pl.BlockSpec(memory_space=pltpu.VMEM),
+        out_shape=jax.ShapeDtypeStruct((128, columns), F32),
+        scratch_shapes=[
+            pltpu.VMEM((n, 2, 2, 2, 4, 32, w), BF16),
+            pltpu.VMEM((n, 2, 2, 4, 32, w), BF16),
+            pltpu.VMEM((n, 2, 2, 4, 32, w), BF16),
+            pltpu.VMEM((n, 3, 4, 32, w), BF16),
+            pltpu.VMEM((n, 4, 32, w), BF16),
+            pltpu.VMEM((n, 3, 32, w), BF16),
+            pltpu.VMEM((n, 32, w), BF16),
+            pltpu.VMEM((n, 3, 32, w), BF16),
+            pltpu.SemaphoreType.DMA((n, 10)),
+            pltpu.SemaphoreType.DMA((n, 10)),
+        ],
+        compiler_params=pltpu.CompilerParams(
+            vmem_limit_bytes=60 * MIB, collective_id=1, has_side_effects=True
+        ),
+        cost_estimate=took(60),
+        name="finish",
+    )(ht, dq, dk, dv, d_out, small)
 
 
 def after(value, *deps):
@@ -640,21 +818,14 @@
     gain_two = extra[:, num_experts + 1].reshape(1, d)
 
     routes_t = routes.reshape(length, -1).T
-    cots, masks = {0: cot}, {}
+    cots = {0: cot}
     route_set = {0: routes_t}
-    cot_late = after(cot, every)
     for step in range(1, n_ex):
-        if step == 1:
-            cots[1] = swap(cot_late, 1)
-        elif step % 2 == 0:
+        route_set[step] = swap(routes_t, step)
+    cot_late = after(cot, every, *route_set.values())
+    for step in range(1, n_ex):
+        if step == 1 or step % 2 == 0:
             cots[step] = swap(cot_late, step)
-        else:
-            cots[step] = swap(cots[step - 1], 1)
-        route_set[step] = swap(routes_t, step)
-    columns = jnp.arange(128, dtype=jnp.int32)
-    for step in range(n_ex):
-        hit = route_set[step].T[:, :, None] == columns[None, None, :]
-        masks[step] = jnp.any(hit, axis=1).astype(BF16)
 
     cos_np, sin_np = rope_tables(length, head)
     cos_l = jnp.asarray(np.concatenate([cos_np] * 4, axis=1))
@@ -662,9 +833,11 @@
     cos_t = jnp.asarray(np.ascontiguousarray(cos_np.T))
     sin_t = jnp.asarray(np.ascontiguousarray(sin_np.T))
 
-    normed_one, q, kd, vd = run_qkv(tok, gain_one, w_all, cos_l, sin_l, nq)
+    normed_one_t, q, kd, vd = run_qkv(tok, gain_one, w_all, cos_l, sin_l, nq)
     ctx, lse, peaks = run_attn_fwd(prefix, q, kd, vd)
-    resid, normed_two = run_mid(tok, ctx, full_out, gain_two)
+    for step in range(3, n_ex, 2):
+        cots[step] = swap(after(cots[step - 1], ctx), 1)
+    resid, normed_two = run_mid(tok, after(ctx, *cots.values()), full_out, gain_two)
 
     me = ex.reshape(1).astype(jnp.int32)
     xs = {0: normed_two}
@@ -673,53 +846,150 @@
             xs[step] = swap(normed_two, step)
         else:
             xs[step] = swap(xs[step - 1], 1)
+    tops = [peaks[:, :, :4]]
+    bits = [("expert", n_ex, 1 << i) for i in range(n_ex.bit_length() - 1)]
+    bits += [("dp", n_dp, 1 << i) for i in range(n_dp.bit_length() - 1)]
+
+    def widen_top():
+        if len(tops) <= len(bits):
+            axis, n, step = bits[len(tops) - 1]
+            top = after(tops[-1], chain)
+            tops.append(jnp.maximum(top, swap(top, step, axis, n)))
+
+    weights = (expert_gate, expert_up, expert_down)
+    half = local // 2
+
+    def scatter(made):
+        if n_dp != 8:
+            done = [
+                lax.psum_scatter(g, "dp", scatter_dimension=0, tiled=True)[0].astype(F32)
+                for g in made
+            ]
+            for _ in range(4):
+                yield made[0]
+            yield done
+            return
+        at = lax.axis_index("dp")
+        z, x = at // 2, at % 2
+
+        def side(which):
+            return jnp.concatenate(
+                [
+                    lax.dynamic_index_in_dim(
+                        g.reshape(4, 2, -1, ff_lanes), which, axis=1, keepdims=False
+                    )
+                    for g in made
+                ],
+                axis=1,
+            )
+
+        sent = side(1 - x)
+        yield sent
+        got = lax.ppermute(sent, "dp", [(i, i ^ 1) for i in range(8)])
+        total = (side(x).astype(F32) + got.astype(F32)).astype(BF16)
+        upper = z // 2
+        far = lax.dynamic_slice_in_dim(total, 2 * (1 - upper), 2, axis=0)
+        near = lax.dynamic_slice_in_dim(total, 2 * upper, 2, axis=0)
+        yield far
+        got = lax.ppermute(far, "dp", [(0, 2), (1, 3), (6, 4), (7, 5)])
+        far = (far.astype(F32) + got.astype(F32)).astype(BF16)
+        yield far
+        got = lax.ppermute(far, "dp", [(2, 4), (3, 5), (4, 2), (5, 3)])
+        near = (near.astype(F32) + got.astype(F32)).astype(BF16)
+        yield near
+        got = lax.ppermute(
+            lax.dynamic_index_in_dim(near, 1 - z % 2, axis=0, keepdims=False),
+            "dp",
+            [(i, i ^ 2) for i in range(8)],
+        )
+        own = lax.dynamic_index_in_dim(near, z % 2, axis=0, keepdims=False)
+        own = own.astype(F32) + got.astype(F32)
+        done, begin = [], 0
+        for g in made:
+            size = g.size // (8 * ff_lanes)
+            done.append(own[begin : begin + size].reshape(g.shape[1:]))
+            begin += size
+        yield done
+
+    ff_lanes = expert_gate.shape[2]
     res = {}
-    for step in range(n_ex):
-        res[step] = run_expert(
-            me, xs[step], cots[step], masks[step], router, expert_gate, expert_up, expert_down
+    chain = xs[1]
+
+    def experts(step, first, count, init=None):
+        x = after(xs[step], chain)
+        return run_expert(
+            me, x, cots[step], route_set[step], router, *weights, first, count, init
         )
 
-    def collect(index, dep=None):
-        got = [res[0][index]]
-        first = res[1][index]
-        if dep is not None:
-            first = after(first, dep)
-        got.append(swap(first, 1))
-        for step in range(2, n_ex, 2):
-            other = res[step + 1][index]
-            if dep is not None:
-                other = after(other, dep)
-            both = (res[step][index].astype(F32) + swap(other, 1).astype(F32)).astype(BF16)
-            got.append(swap(both, step))
-        return got
-
-    dxs = collect(1)
-    dg_parts = [res[0][2]] + [swap(res[step][2], step) for step in range(1, n_ex)]
-    stacked = jnp.stack([piece[:local] for piece in dg_parts])
-    owner = jnp.arange(n_ex, dtype=jnp.int32)
-    dg = sum(
-        jnp.where(((owner ^ step) == ex)[:, None, None], stacked[step][None], 0.0)
-        for step in range(n_ex)
-    )
-    dg = dg.reshape(num_experts, length).T
-    dg = jnp.pad(dg, ((0, 0), (0, 128 - num_experts)))
-
-    order = list(range(n_ex))
-    d_down = run_weight_grad(
-        [res[s][7] for s in order], [res[s][3] for s in order], local, True
-    )
-    d_gate = run_weight_grad(
-        [res[s][6] for s in order], [res[s][4] for s in order], local, False
-    )
-    d_up = run_weight_grad([res[s][6] for s in order], [res[s][5] for s in order], local, False)
-    grad_down = lax.psum_scatter(d_down, "dp", scatter_dimension=1, tiled=True).astype(F32)
-    grad_gate = lax.psum_scatter(d_gate, "dp", scatter_dimension=1, tiled=True).astype(F32)
-    grad_up = lax.psum_scatter(d_up, "dp", scatter_dimension=1, tiled=True).astype(F32)
-
+    def grads(first):
+        skips = [first if step < 2 else 0 for step in range(n_ex)]
+        pieces = [
+            [res[step, 0 if step < 2 else first][k] for step in range(n_ex)] for k in (4, 5, 3)
+        ]
+        turned = [[res[step, 0][k] for step in range(n_ex)] for k in (6, 7)]
+        turned[0][0] = after(turned[0][0], chain)
+        made = None
+        for at in range(0, n_ex, 4):
+            some = [group[at : at + 4] for group in turned + pieces]
+            part = run_weight_grad(*some, half, skips[at : at + 4], n_dp)
+            if made is None:
+                made = part
+            else:
+                made = [(a.astype(F32) + b.astype(F32)).astype(BF16) for a, b in zip(made, part)]
+        return made
+
+    for step in range(2):
+        res[step, 0] = experts(step, 0, local)
+        chain = res[step, 0][0]
+    odd, even = range(3, n_ex, 2), range(2, n_ex, 2)
+    for step in odd:
+        res[step, 0] = experts(step, 0, half)
+        chain = res[step, 0][0]
+        res[step, half] = experts(step, half, half, res[step, 0][:3])
+        chain = (res[step, half][0], tops[-1])
+        widen_top()
+    partner = {step - 1: [swap(res[step, half][k], 1) for k in (0, 1)] for step in odd}
+    for step in even:
+        res[step, 0] = experts(step, 0, half)
+        chain = (res[step, 0][0], tops[-1])
+        widen_top()
+    made = grads(0)
+    one = scatter(made)
+    chain = (next(one), tops[-1])
+    widen_top()
+    for step in even:
+        init = [
+            (a.astype(F32) + b.astype(F32)).astype(BF16)
+            for a, b in zip(res[step, 0][:2], partner[step])
+        ]
+        res[step, half] = experts(step, half, half, init + [res[step, 0][2]])
+        chain = (res[step, half][0], tops[-1])
+        widen_top()
+    made = grads(half)
+    two = scatter(made)
+    chain = (next(two), next(one), tops[-1])
+    while len(tops) <= len(bits):
+        widen_top()
+    top = tops[-1]
+
+    last = [res[step, 0 if step < 2 else half] for step in range(n_ex)]
+    dxs = [last[0][1], swap(last[1][1], 1)] + [swap(last[step][1], step) for step in even]
+    dgs = [last[0][2]] + [swap(last[step][2], step) for step in range(1, n_ex)]
     d_res, d_attn, d_ctx, d_logits, d_gain_two = run_back_mid(
-        resid, cot, masks[0], normed_two, router, dg, gain_two, full_out, dxs
-    )
-    outs = collect(0, d_ctx)
+        me,
+        after(resid, chain),
+        cot,
+        routes_t,
+        normed_two,
+        router,
+        gain_two,
+        full_out,
+        dxs,
+        dgs,
+        local,
+    )
+    outs = [last[0][0], swap(last[1][0], 1)]
+    outs += [swap(after(last[step][0], dxs), step) for step in even]
     block = resid
     for piece in outs:
         block = block + piece.astype(F32)
@@ -729,13 +999,11 @@
     d_router_w = jnp.einsum("rd,re->de", normed_two, d_logits, preferred_element_type=F32)
 
     dq, dk, dv = run_attn_bwd(
-        prefix, q, kd, vd, d_ctx, ctx, lse, cos_l, sin_l, cos_t, sin_t
-    )
-    grad_tok, d_gain_one = run_back_in(dq, dk, dv, w_all, tok, gain_one, d_res)
-    d_query_w = jnp.einsum("rd,rc->dc", normed_one, dq, preferred_element_type=F32).astype(BF16)
-    d_key_w = jnp.einsum("rd,rc->dc", normed_one, dk, preferred_element_type=F32).astype(BF16)
-    d_val_w = jnp.einsum("rd,rc->dc", normed_one, dv, preferred_element_type=F32).astype(BF16)
-
+        prefix, after(q, next(one), top), kd, vd, d_ctx, ctx, lse, cos_l, sin_l, cos_t, sin_t
+    )
+    grad_tok, d_gain_one = run_back_in(
+        after(dq, next(two), next(one), block_out), dk, dv, w_all, tok, gain_one, d_res
+    )
     small_grad = jnp.concatenate(
         [
             d_router_w[:, :num_experts].astype(BF16),
@@ -746,34 +1014,55 @@
         axis=1,
     )
 
-    def reduce_all(value):
-        value = value.reshape(n_dp, n_ex, value.shape[0] // (n_dp * n_ex), value.shape[1])
-        value = lax.psum_scatter(value, "expert", scatter_dimension=1, tiled=True)
-        value = lax.psum_scatter(
-            value.reshape(n_dp * value.shape[2], value.shape[3]),
-            "dp",
-            scatter_dimension=0,
-            tiled=True,
+    def reduce_all(value, order):
+        shape = (n_dp, n_ex, value.shape[0] // (n_dp * n_ex), value.shape[1])
+        names = []
+        dims = []
+        for axis, n in (("dp", n_dp), ("expert", n_ex)):
+            count = n.bit_length() - 1
+            names += [(axis, n, 1 << (count - 1 - i)) for i in range(count)]
+            dims += [2] * count
+        value = value.reshape(*dims, *shape[2:])
+        for bit in order:
+            at = names.index(bit)
+            axis, n, step = bit
+            mine = (lax.axis_index(axis) // step) % 2
+            keep = lax.dynamic_slice_in_dim(value, mine, 1, axis=at)
+            send = lax.dynamic_slice_in_dim(value, 1 - mine, 1, axis=at)
+            value = (keep.astype(F32) + swap(send, step, axis, n).astype(F32)).astype(BF16)
+        return value.reshape(shape[2:])
+
+    def share(value):
+        return lax.all_gather(value, "expert", axis=0, tiled=True).astype(F32)
+
+    core = [("expert", n_ex, 1)]
+    y_bits = [("expert", n_ex, 1 << i) for i in range(1, n_ex.bit_length() - 1)][::-1]
+    dp_bits = [("dp", n_dp, 1 << i) for i in range(n_dp.bit_length() - 1)]
+    next(two), next(two)
+    ends = [next(one), next(two)]
+    grad_gate, grad_up, grad_down = (
+        jnp.concatenate([ends[0][k], ends[1][k]], axis=0) for k in range(3)
+    )
+    grad_down = jnp.swapaxes(grad_down, 1, 2).reshape(local, -1, d)
+
+    if n_dp == 8 and n_ex == 4 and d == 1024:
+        every_grad = run_finish(normed_one_t, dq, dk, dv, d_out_w, small_grad)
+    else:
+
+        def product(right):
+            return jnp.dot(normed_one_t, right, preferred_element_type=F32).astype(BF16)
+
+        every_grad = jnp.concatenate(
+            [d_out_w, product(dq), product(dk), product(dv), small_grad], axis=1
         )
-        return lax.all_gather(value, "expert", axis=0, tiled=True).astype(F32)
-
-    grad_out = reduce_all(d_out_w)
-    rest = reduce_all(jnp.concatenate([d_query_w, d_key_w, d_val_w, small_grad], axis=1))
-    grad_query = rest[:, :nq]
-    grad_keyval = rest[:, nq : 2 * nq]
-    grad_router = rest[:, 2 * nq : 2 * nq + num_experts]
-    grad_gain_one = rest[:, 2 * nq + num_experts]
-    grad_gain_two = rest[:, 2 * nq + num_experts + 1]
-
-    top = peaks[:, :, :4]
-    step = 1
-    while step < n_ex:
-        top = jnp.maximum(top, swap(top, step))
-        step *= 2
-    step = 1
-    while step < n_dp:
-        top = jnp.maximum(top, swap(top, step, "dp", n_dp))
-        step *= 2
+        every_grad = share(reduce_all(every_grad, core + y_bits + dp_bits[::-1]))
+    grad_out = every_grad[:, :d]
+    grad_query = every_grad[:, d : d + nq]
+    grad_keyval = every_grad[:, d + nq : d + 2 * nq]
+    grad_router = every_grad[:, d + 2 * nq : d + 2 * nq + num_experts]
+    grad_gain_one = every_grad[:, d + 2 * nq + num_experts]
+    grad_gain_two = every_grad[:, d + 2 * nq + num_experts + 1]
+
     head_logit_peak = top[:, 0, :].reshape(heads)
     per_group = heads // kv_heads
     query_factor = jnp.sqrt(query_logit_cap / jnp.maximum(head_logit_peak, query_logit_cap))

time: 995 us -> 730 us (0.73)
  waiting for transfers between devices: 479 us -> 137 us
  Pallas kernels: 346 us -> 449 us
  starting transfers between devices: 16.9 us -> 34.8 us
  blocking collectives: 13.5 us -> 0 us
  local copies, waits for them, and re-layouts: 49.1 us -> 36.8 us
    reduce_scatter x6 -> x0, waiting for transfers between devices: 288 us -> none  [the longest x1 90 us: on_device(): lax.psum_scatter(d_gate, 'dp', scatter_dimension=1, tiled=True).astype(F32)]
    pallas_call x8 -> x10, Pallas kernels: 269 us -> 365 us  [the longest x6 202 us: run_expert(): pl.pallas_call(functools.partial(expert_kernel, first, local, with_init),...]
    ppermute x23, waiting for transfers between devices: 100 us -> 21 us  [swap(): return lax.ppermute(value, axis, [(i, i ^ step) for i in range(n)])]
    ppermute x0 -> x8, waiting for transfers between devices: none -> 49.3 us  [the longest x2 29.5 us: scatter(): lax.ppermute(lax.dynamic_index_in_dim(near, 1 - z % 2, axis=0, keepdims=F...]
    reduce_or x4 -> x0, other arithmetic: 23.3 us -> none  [on_device(): masks[step] = jnp.any(hit, axis=1).astype(BF16)]
    unnamed x9 -> x1, waiting for transfers between devices: 18.3 us -> 0.02 us
    ppermute x0 -> x8, starting transfers between devices: none -> 18.1 us  [the longest x2 10.2 us: scatter(): got = lax.ppermute(far, 'dp', [(0, 2), (1, 3), (6, 4), (7, 5)])]
    all_gather x2 -> x0, blocking collectives: 13.5 us -> none  [reduce_all(): return lax.all_gather(value, 'expert', axis=0, tiled=True).astype(F32)]
  transfers between devices with their start and end apart: 31 -> 32, of which waited for: 14 -> 12; matrix products, arithmetic and copies ran while one was open for 8% -> 10% of each run, Pallas kernels for 31% -> 54%
where the time goes in v2:
time: 730 us; the launch traced here: 722 us
  Pallas kernels  449 us (62%)
  waiting for transfers between devices  137 us (19%)
  other arithmetic  43 us (6%)
  local copies, waits for them, and re-layouts  36.8 us (5%)
  starting transfers between devices  34.8 us (5%)
  between operations  15.4 us (2%)
    pallas_call x6, Pallas kernels, run_expert(): pl.pallas_call(functools.partial(expert_kernel, first, local, with_init),...  202 us
    pallas_call x2, Pallas kernels, run_weight_grad(): pl.pallas_call(functools.partial(weight_grad_kernel, n), grid=(count, d /...  75.7 us
    pallas_call x1, Pallas kernels, run_finish(): pl.pallas_call(finish_kernel, in_specs=[pl.BlockSpec(memory_space=pltpu.V...  75.2 us
    all_gather x1, waiting for transfers between devices, on_device(): every = lax.all_gather(mine, ('dp', 'expert'), axis=0, tiled=True)  66.9 us
    pallas_call x1, Pallas kernels, run_attn_bwd(): pl.pallas_call(attn_bwd_kernel, grid=(groups,), in_specs=[pl.BlockSpec(me...  32.9 us
    ppermute x2, waiting for transfers between devices, scatter(): lax.ppermute(lax.dynamic_index_in_dim(near, 1 - z % 2, axis=0, keepdims=F...  29.5 us
    pallas_call x1, Pallas kernels, run_attn_fwd(): pl.pallas_call(attn_fwd_kernel, grid=(groups,), in_specs=[pl.BlockSpec(me...  21.5 us
    ppermute x23, waiting for transfers between devices, swap(): return lax.ppermute(value, axis, [(i, i ^ step) for i in range(n)])  21 us
  transfers between devices with their start and end apart: 32, of which 12 were waited for; matrix products, arithmetic and copies ran while one was open for 10% of the time, Pallas kernels for 54%

profile of v2, /device:TPU:0, one launch (start us, length us, event | category | flops | bytes accessed | tf_op | source)
XLA Modules:
  0.0 722.1 jit_solution(1623833239405321854)
XLA Ops:
  18.3 66.9 %all-gather.2.cloned.1.call-done.w_ref = bf16[1024,3200]{1,0:T(8,128)(2,1)} async-done(((bf16[32,3200]{1,0:T(8,128)(2,1)}), bf16[1024,3200]{1,0:T(8,128)(2,1)}) %all-gather.2.cloned.1.call-update) | async-done | bytes 6553616 | tf_op jit(solution)/shard_map/all_gather | solution.py:810
  89.5 10.1 %qkv.1 = (bf16[1024,1024]{1,0:T(8,128)(2,1)}, bf16[1024,1024]{1,0:T(8,128)(2,1)}, bf16[1024,1024]{1,0:T(8,128)(2,1)}, bf16[1024,1024]{1,0:T(8,128)(2,1)}) custom-call(bf16[1024,1024]{1,0:T(8,128)(2,1)} %bitcast.95, bf16[1,1024]{1,0:T(2,128)(2,1)} %reshape_squeeze.9.gain_ref, bf16[1024,3200]{1,0:T(8,128)(2,1)} %all-gather.2.cloned.1.call-done.w_ref, ...), custom_call_target="tpu_custom_call" | custom-call | flops 4499999744 | bytes 1000 | tf_op jit(solution)/shard_map/qkv/pallas_call | solution.py:101
  99.6 21.5 %attn_fwd.1 = (bf16[1024,1024]{1,0:T(8,128)(2,1)}, f32[4,8,1024]{2,1,0:T(8,128)}, f32[4,8,128]{2,1,0:T(8,128)}) custom-call(s32[1]{0:T(128)S(6)} %copy.54.prefix_ref, bf16[1024,1024]{1,0:T(8,128)(2,1)} %get-tuple-element.173.q_ref, bf16[1024,1024]{1,0:T(8,128)(2,1)} %get-tuple-element.104.kd_ref, bf16[1024,1024]{1,0:T(8,128)(2,1)} %get-tuple-element.105.vd_ref), custom_call_target="tpu_custom_call" | custom-call | flops 10499999744 | bytes 1000 | tf_op jit(solution)/shard_map/attn_fwd/pallas_call | solution.py:176
  121.1 12.1 %collective-permute-done.4.c_ref = bf16[1024,1024]{1,0:T(8,128)(2,1)} collective-permute-done((bf16[1024,1024]{1,0:T(8,128)(2,1)S(1)}, bf16[1024,1024]{1,0:T(8,128)(2,1)}, u32[]{:S(2)}, u32[]{:S(2)}) %collective-permute-start.4) | collective-permute-done | bytes 2097184 | tf_op jit(solution)/shard_map/ppermute | solution.py:796
  137.7 7.2 %mid.1 = (f32[1024,1024]{1,0:T(8,128)}, bf16[1024,1024]{1,0:T(8,128)(2,1)}) custom-call(bf16[1024,1024]{1,0:T(8,128)(2,1)} %bitcast.96, bf16[1024,1024]{1,0:T(8,128)(2,1)} %get-tuple-element.109.ctx_ref, bf16[1024,1024]{1,0:T(8,128)(2,1)} %slice.80.w_ref.refs_7_, bf16[1,1024]{1,0:T(2,128)(2,1)} %reshape_squeeze.10.gain_ref.refs_6_), custom_call_target="tpu_custom_call" | custom-call | flops 2000000000 | bytes 1000 | tf_op jit(solution)/shard_map/mid/pallas_call | solution.py:311
  149.4 46.9 %experts.6 = (bf16[1024,1024]{1,0:T(8,128)(2,1)}, bf16[1024,1024]{1,0:T(8,128)(2,1)}, f32[8,1024]{1,0:T(8,128)}, bf16[1024,2048]{1,0:T(8,128)(2,1)}, bf16[1024,2...) custom-call(s32[1]{0:T(128)} %bitcast.7.me_ref.refs_0_, ...), custom_call_target="tpu_custom_call" | custom-call | flops 24000000000 | bytes 1000 | tf_op jit(solution)/shard_map/experts/pallas_call | solution.py:423
  196.6 47.3 %experts.7 = (bf16[1024,1024]{1,0:T(8,128)(2,1)}, bf16[1024,1024]{1,0:T(8,128)(2,1)}, f32[8,1024]{1,0:T(8,128)}, bf16[1024,2048]{1,0:T(8,128)(2,1)}, bf16[1024,2...) custom-call(s32[1]{0:T(128)} %bitcast.7.me_ref.refs_0_, ...), custom_call_target="tpu_custom_call" | custom-call | flops 24000000000 | bytes 1000 | tf_op jit(solution)/shard_map/experts/pallas_call | solution.py:423
  243.8 27.5 %experts.8 = (bf16[1024,1024]{1,0:T(8,128)(2,1)}, bf16[1024,1024]{1,0:T(8,128)(2,1)}, f32[8,1024]{1,0:T(8,128)}, bf16[1024,1024]{1,0:T(8,128)(2,1)}, bf16[1024,1...) custom-call(s32[1]{0:T(128)} %bitcast.7.me_ref.refs_0_, ...), custom_call_target="tpu_custom_call" | custom-call | flops 12000000000 | bytes 1000 | tf_op jit(solution)/shard_map/experts/pallas_call | solution.py:423
  271.4 26.5 %experts.9 = (bf16[1024,1024]{1,0:T(8,128)(2,1)}, bf16[1024,1024]{1,0:T(8,128)(2,1)}, f32[8,1024]{1,0:T(8,128)}, bf16[1024,1024]{1,0:T(8,128)(2,1)}, bf16[1024,1...) custom-call(s32[1]{0:T(128)} %bitcast.7.me_ref.refs_0_, bf16[1024,1024]{1,0:T(8,128)(2,1)} %collective-permute-done.9.x_ref, ...), custom_call_target="tpu_custom_call" | custom-call | flops 12000000000 | bytes 1000 | tf_op jit(solution)/shard_map/experts/pallas_call | solution.py:423
  298.6 27.2 %experts.10 = (bf16[1024,1024]{1,0:T(8,128)(2,1)}, bf16[1024,1024]{1,0:T(8,128)(2,1)}, f32[8,1024]{1,0:T(8,128)}, bf16[1024,1024]{1,0:T(8,128)(2,1)}, bf16[1024,...) custom-call(s32[1]{0:T(128)} %bitcast.7.me_ref.refs_0_, ...), custom_call_target="tpu_custom_call" | custom-call | flops 12000000000 | bytes 1000 | tf_op jit(solution)/shard_map/experts/pallas_call | solution.py:423
  327.4 37.8 %weight_grad.2 = (bf16[8,2,128,512]{3,2,1,0:T(8,128)(2,1)}, bf16[8,2,128,512]{3,2,1,0:T(8,128)(2,1)}, bf16[8,2,2,64,512]{4,3,2,1,0:T(8,128)(2,1)}) custom-call(bf16[1024,1024]{1,0:T(8,128)(2,1)} %get-tuple-element.162.refs_0_, bf16[1024,1024]{1,0:T(8,128)(2,1)} %get-tuple-element.128.refs_1_, bf16[1024,1024]{1,0:T(8,128)(2,1)} %get-tuple-element.129.refs_2_, ...), custom_call_target="tpu_custom_call" | custom-call | flops 18499999744 | bytes 1000 | tf_op jit(solution)/shard_map/weight_grad/pallas_call | solution.py:491
  375.3 4.7 add_convert_fusion.4.refs_0_
  383.9 26.7 %experts.11 = (bf16[1024,1024]{1,0:T(8,128)(2,1)}, bf16[1024,1024]{1,0:T(8,128)(2,1)}, f32[8,1024]{1,0:T(8,128)}, bf16[1024,1024]{1,0:T(8,128)(2,1)}, bf16[1024,...) custom-call(s32[1]{0:T(128)} %bitcast.7.me_ref.refs_0_, bf16[1024,1024]{1,0:T(8,128)(2,1)} %copy-done.18, ...), custom_call_target="tpu_custom_call" | custom-call | flops 12000000000 | bytes 1000 | tf_op jit(solution)/shard_map/experts/pallas_call | solution.py:423
  412.7 37.8 %weight_grad.3 = (bf16[8,2,128,512]{3,2,1,0:T(8,128)(2,1)}, bf16[8,2,128,512]{3,2,1,0:T(8,128)(2,1)}, bf16[8,2,2,64,512]{4,3,2,1,0:T(8,128)(2,1)}) custom-call(bf16[1024,1024]{1,0:T(8,128)(2,1)} %get-tuple-element.162.refs_0_, bf16[1024,1024]{1,0:T(8,128)(2,1)} %get-tuple-element.128.refs_1_, bf16[1024,1024]{1,0:T(8,128)(2,1)} %get-tuple-element.129.refs_2_, ...), custom_call_target="tpu_custom_call" | custom-call | flops 18499999744 | bytes 1000 | tf_op jit(solution)/shard_map/weight_grad/pallas_call | solution.py:491
  477.1 12.6 %back_mid.1 = (f32[1024,1024]{1,0:T(8,128)}, bf16[1024,1024]{1,0:T(8,128)(2,1)}, bf16[1024,1024]{1,0:T(8,128)(2,1)}, bf16[1024,128]{1,0:T(8,128)(2,1)}, f32[1,1024]{1,0:T(1,128)}) custom-call(s32[1]{0:T(128)} %bitcast.7.me_ref.refs_0_, f32[1024,1024]{1,0:T(8,128)} %get-tuple-element.174.refs_1_, bf16[1024,1024]{1,0:T(8,128)(2,1)} %bitcast.92, ...), custom_call_target="tpu_custom_call" | custom-call | flops 5500000256 | bytes 1000 | tf_op jit(solution)/shard_map/back_mid/pallas_call | solution.py:557
  497.9 11.2 %collective-permute-done.18 = bf16[2,768,512]{2,1,0:T(8,128)(2,1)} collective-permute-done((bf16[2,768,512]{2,1,0:T(8,128)(2,1)}, bf16[2,768,512]{2,1,0:T(8,128)(2,1)}, u32[]{:S(2)}, u32[]{:S(2)}) %collective-permute-start.18) | collective-permute-done | bytes 1572896 | tf_op jit(solution)/shard_map/ppermute | solution.py:894
  514.0 32.9 %attn_bwd.1 = (bf16[1024,1024]{1,0:T(8,128)(2,1)}, bf16[1024,512]{1,0:T(8,128)(2,1)}, bf16[1024,512]{1,0:T(8,128)(2,1)}) custom-call(s32[1]{0:T(128)S(6)} %copy.54.prefix_ref, bf16[1024,1024]{1,0:T(8,128)(2,1)} %get-tuple-element.173.q_ref, bf16[1024,1024]{1,0:T(8,128)(2,1)} %get-tuple-element.104.kd_ref, bf16[1024,1024]{1,0:T(8,128)(2,1)} %get-tuple-element.105.vd_ref, ...), custom_call_target="tpu_custom_call" | custom-call | flops 16499999744 | bytes 1000 | tf_op jit(solution)/shard_map/attn_bwd/pallas_call | solution.py:275
  553.3 6.6 collective-permute-start.28
  559.9 5.2 fusion
  568.1 11.6 %back_in.1 = (f32[1024,1024]{1,0:T(8,128)}, f32[1,1024]{1,0:T(1,128)}) custom-call(bf16[1024,1024]{1,0:T(8,128)(2,1)} %get-tuple-element.182.dq_ref, bf16[1024,512]{1,0:T(8,128)(2,1)} %get-tuple-element.183.dk_ref, bf16[1024,512]{1,0:T(8,128)(2,1)} %get-tuple-element.184.dv_ref, bf16[1024,3200]{1,0:T(8,128)(2,1)} %all-gather.2.cloned.1.call-done.w_ref, ...), custom_call_target="tpu_custom_call" | custom-call | flops 5000000000 | bytes 1000 | tf_op jit(solution)/shard_map/back_in/pallas_call | solution.py:616
  583.2 8.6 %collective-permute-done.28 = bf16[2,768,512]{2,1,0:T(8,128)(2,1)} collective-permute-done((bf16[2,768,512]{2,1,0:T(8,128)(2,1)}, bf16[2,768,512]{2,1,0:T(8,128)(2,1)}, u32[]{:S(2)}, u32[]{:S(2)}) %collective-permute-start.28) | collective-permute-done | bytes 1572896 | tf_op jit(solution)/shard_map/ppermute | solution.py:894
  596.7 75.2 %finish.1 = f32[128,3200]{1,0:T(8,128)} custom-call(bf16[1024,1024]{1,0:T(8,128)(2,1)} %get-tuple-element.187.ht_ref, bf16[1024,1024]{1,0:T(8,128)(2,1)} %get-tuple-element.182.dq_ref, bf16[1024,512]{1,0:T(8,128)(2,1)} %get-tuple-element.183.dk_ref, bf16[1024,512]{1,0:T(8,128)(2,1)} %get-tuple-element.184.dv_ref, ...), custom_call_target="tpu_custom_call" | custom-call | flops 30000001024 | bytes 1000 | tf_op jit(solution)/shard_map/finish/pallas_call | solution.py:750
  681.6 13.4 %collective-permute-done.27 = bf16[768,512]{1,0:T(8,128)(2,1)S(1)} collective-permute-done((bf16[768,512]{1,0:T(8,128)(2,1)S(1)}, bf16[768,512]{1,0:T(8,128)(2,1)S(1)}, u32[]{:S(2)}, u32[]{:S(2)}) %collective-permute-start.27) | collective-permute-done | bytes 786464 | tf_op jit(solution)/shard_map/ppermute | solution.py:900
  695.3 16.1 %collective-permute-done.30 = bf16[768,512]{1,0:T(8,128)(2,1)S(1)} collective-permute-done((bf16[768,512]{1,0:T(8,128)(2,1)S(1)}, bf16[768,512]{1,0:T(8,128)(2,1)S(1)}, u32[]{:S(2)}, u32[]{:S(2)}) %collective-permute-start.30) | collective-permute-done | bytes 786464 | tf_op jit(solution)/shard_map/ppermute | solution.py:900
  (185 shorter events, 113.2 us)
Async XLA Ops:
  7.2 78.1 %all-gather.2.cloned.1.call-start = ((), (), s32[]{:S(2)}) async-start(), calls=%async_computation | async-start | bytes 6758400 | tf_op jit(solution)/shard_map/all_gather | solution.py:810
  85.3 47.9 %collective-permute-start.4 = (bf16[1024,1024]{1,0:T(8,128)(2,1)S(1)}, bf16[1024,1024]{1,0:T(8,128)(2,1)}, u32[]{:S(2)}, u32[]{:S(2)}) collective-permute-start(bf16[1024,1024]{1,0:T(8,128)(2,1)S(1)} %bitcast.93), channel_id=1, source_target_pairs={{0,2},{1,3},{2,0},{3,1},{4,6},{5,7},{6,4},{7,5},{8,10},{9,11},{10,... | collective-permute-start | bytes 6291464 | tf_op jit(solution)/shard_map/ppermute | solution.py:796
  87.4 49.5 %collective-permute-start.3 = (bf16[1024,1024]{1,0:T(8,128)(2,1)S(1)}, bf16[1024,1024]{1,0:T(8,128)(2,1)}, u32[]{:S(2)}, u32[]{:S(2)}) collective-permute-start(bf16[1024,1024]{1,0:T(8,128)(2,1)S(1)} %bitcast.94), channel_id=1, source_target_pairs={{0,1},{1,0},{2,3},{3,2},{4,5},{5,4},{6,7},{7,6},{8,9},{9,8},{10,11... | collective-permute-start | bytes 6291464 | tf_op jit(solution)/shard_map/ppermute | solution.py:796
  146.7 49.6 %collective-permute-start.8 = (bf16[1024,1024]{1,0:T(8,128)(2,1)}, bf16[1024,1024]{1,0:T(8,128)(2,1)S(1)}, u32[]{:S(2)}, u32[]{:S(2)}) collective-permute-start(bf16[1024,1024]{1,0:T(8,128)(2,1)} %get-tuple-element.112.x_ref.refs_4_), channel_id=1, source_target_pairs={{0,2},{1,3},{2,0},{3,1},{4,6},{5,7},{6,4},{7,5},{8,10},{9,11},{10,... | collective-permute-start | bytes 6291464 | tf_op jit(solution)/shard_map/ppermute | solution.py:796
  196.3 47.5 %collective-permute-start.9 = (bf16[1024,1024]{1,0:T(8,128)(2,1)S(1)}, bf16[1024,1024]{1,0:T(8,128)(2,1)}, u32[]{:S(2)}, u32[]{:S(2)}) collective-permute-start(bf16[1024,1024]{1,0:T(8,128)(2,1)S(1)} %collective-permute-done.8.x_ref), channel_id=1, source_target_pairs={{0,1},{1,0},{2,3},{3,2},{4,5},{5,4},{6,7},{7,6},{8,9},{9,8},{10,11... | collective-permute-start | bytes 6291464 | tf_op jit(solution)/shard_map/ppermute | solution.py:796
  297.9 77.5 %collective-permute-start.12 = (bf16[1024,1024]{1,0:T(8,128)(2,1)}, bf16[1024,1024]{1,0:T(8,128)(2,1)}, u32[]{:S(2)}, u32[]{:S(2)}) collective-permute-start(bf16[1024,1024]{1,0:T(8,128)(2,1)} %get-tuple-element.122), channel_id=1, source_target_pairs={{0,1},{1,0},{2,3},{3,2},{4,5},{5,4},{6,7},{7,6},{8,9},{9,8},{10,11... | collective-permute-start | bytes 6291464 | tf_op jit(solution)/shard_map/ppermute | solution.py:796
  298.0 27.8 %collective-permute-start.10 = (f32[4,8,4]{2,1,0:T(8,128)S(1)}, f32[4,8,4]{2,1,0:T(8,128)S(1)}, u32[]{:S(2)}, u32[]{:S(2)}) collective-permute-start(f32[4,8,4]{2,1,0:T(8,128)S(1)} %bitcast.86), channel_id=1, source_target_pairs={{0,1},{1,0},{2,3},{3,2},{4,5},{5,4},{6,7},{7,6},{8,9},{9,8},{10,11... | collective-permute-start | bytes 1544 | tf_op jit(solution)/shard_map/ppermute | solution.py:796
  298.4 81.6 %collective-permute-start.13 = (bf16[1024,1024]{1,0:T(8,128)(2,1)}, bf16[1024,1024]{1,0:T(8,128)(2,1)}, u32[]{:S(2)}, u32[]{:S(2)}) collective-permute-start(bf16[1024,1024]{1,0:T(8,128)(2,1)} %get-tuple-element.153), channel_id=1, source_target_pairs={{0,1},{1,0},{2,3},{3,2},{4,5},{5,4},{6,7},{7,6},{8,9},{9,8},{10,11... | collective-permute-start | bytes 6291464 | tf_op jit(solution)/shard_map/ppermute | solution.py:796
  325.8 45.7 %collective-permute-start.11 = (f32[4,8,4]{2,1,0:T(8,128)S(1)}, f32[4,8,4]{2,1,0:T(8,128)S(1)}, u32[]{:S(2)}, u32[]{:S(2)}) collective-permute-start(f32[4,8,4]{2,1,0:T(8,128)S(1)} %max.21), channel_id=1, source_target_pairs={{0,2},{1,3},{2,0},{3,1},{4,6},{5,7},{6,4},{7,5},{8,10},{9,11},{10,... | collective-permute-start | bytes 1544 | tf_op jit(solution)/shard_map/ppermute | solution.py:796
  372.2 99.6 %collective-permute-start.14 = (bf16[1024,1024]{1,0:T(8,128)(2,1)}, bf16[1024,1024]{1,0:T(8,128)(2,1)}, u32[]{:S(2)}, u32[]{:S(2)}) collective-permute-start(bf16[1024,1024]{1,0:T(8,128)(2,1)} %get-tuple-element.157), channel_id=1, source_target_pairs={{0,1},{1,0},{2,3},{3,2},{4,5},{5,4},{6,7},{7,6},{8,9},{9,8},{10,11... | collective-permute-start | bytes 6291464 | tf_op jit(solution)/shard_map/ppermute | solution.py:796
  372.3 85.2 %collective-permute-start.17 = (bf16[4,768,512]{2,1,0:T(8,128)(2,1)S(1)}, bf16[4,768,512]{2,1,0:T(8,128)(2,1)}, u32[]{:S(2)}, u32[]{:S(2)}) collective-permute-start(bf16[4,768,512]{2,1,0:T(8,128)(2,1)S(1)} %pad_maximum_fusion), channel_id=1, source_target_pairs={{0,4},{4,0},{8,12},{12,8},{16,20},{20,16},{24,28},{28,24},{1,5},{5... | collective-permute-start | bytes 9437192 | tf_op jit(solution)/shard_map/ppermute | solution.py:888
  410.5 46.9 %collective-permute-start.20 = (f32[4,8,4]{2,1,0:T(8,128)S(1)}, f32[4,8,4]{2,1,0:T(8,128)S(1)}, u32[]{:S(2)}, u32[]{:S(2)}) collective-permute-start(f32[4,8,4]{2,1,0:T(8,128)S(1)} %max.23), channel_id=1, source_target_pairs={{0,8},{4,12},{8,0},{12,4},{16,24},{20,28},{24,16},{28,20},{1,9},{5... | collective-permute-start | bytes 1544 | tf_op jit(solution)/shard_map/ppermute | solution.py:796
  412.1 59.7 %collective-permute-start.15 = (bf16[1024,1024]{1,0:T(8,128)(2,1)}, bf16[1024,1024]{1,0:T(8,128)(2,1)}, u32[]{:S(2)}, u32[]{:S(2)}) collective-permute-start(bf16[1024,1024]{1,0:T(8,128)(2,1)} %get-tuple-element.158), channel_id=1, source_target_pairs={{0,2},{1,3},{2,0},{3,1},{4,6},{5,7},{6,4},{7,5},{8,10},{9,11},{10,... | collective-permute-start | bytes 6291464 | tf_op jit(solution)/shard_map/ppermute | solution.py:796
  463.6 12.4 %collective-permute-start.24 = (f32[8,1024]{1,0:T(8,128)S(1)}, f32[8,1024]{1,0:T(8,128)}, u32[]{:S(2)}, u32[]{:S(2)}) collective-permute-start(f32[8,1024]{1,0:T(8,128)S(1)} %copy-done.22), channel_id=1, source_target_pairs={{0,3},{1,2},{2,1},{3,0},{4,7},{5,6},{6,5},{7,4},{8,11},{9,10},{10,... | collective-permute-start | bytes 98312 | tf_op jit(solution)/shard_map/ppermute | solution.py:796
  467.2 9.9 %collective-permute-start.23 = (f32[8,1024]{1,0:T(8,128)S(1)}, f32[8,1024]{1,0:T(8,128)}, u32[]{:S(2)}, u32[]{:S(2)}) collective-permute-start(f32[8,1024]{1,0:T(8,128)S(1)} %copy-done.25), channel_id=1, source_target_pairs={{0,2},{1,3},{2,0},{3,1},{4,6},{5,7},{6,4},{7,5},{8,10},{9,11},{10,... | collective-permute-start | bytes 98312 | tf_op jit(solution)/shard_map/ppermute | solution.py:796
  471.8 88.1 %collective-permute-start.7 = (bf16[1024,1024]{1,0:T(8,128)(2,1)}, bf16[1024,1024]{1,0:T(8,128)(2,1)}, u32[]{:S(2)}, u32[]{:S(2)}) collective-permute-start(bf16[1024,1024]{1,0:T(8,128)(2,1)} %get-tuple-element.115), channel_id=1, source_target_pairs={{0,1},{1,0},{2,3},{3,2},{4,5},{5,4},{6,7},{7,6},{8,9},{9,8},{10,11... | collective-permute-start | bytes 6291464 | tf_op jit(solution)/shard_map/ppermute | solution.py:796
  471.8 75.1 %collective-permute-start.25 = (bf16[4,768,512]{2,1,0:T(8,128)(2,1)}, bf16[4,768,512]{2,1,0:T(8,128)(2,1)}, u32[]{:S(2)}, u32[]{:S(2)}) collective-permute-start(bf16[4,768,512]{2,1,0:T(8,128)(2,1)} %pad_maximum_fusion.1), channel_id=1, source_target_pairs={{0,4},{4,0},{8,12},{12,8},{16,20},{20,16},{24,28},{28,24},{1,5},{5... | collective-permute-start | bytes 9437192 | tf_op jit(solution)/shard_map/ppermute | solution.py:888
  472.4 36.7 %collective-permute-start.18 = (bf16[2,768,512]{2,1,0:T(8,128)(2,1)}, bf16[2,768,512]{2,1,0:T(8,128)(2,1)}, u32[]{:S(2)}, u32[]{:S(2)}) collective-permute-start(bf16[2,768,512]{2,1,0:T(8,128)(2,1)} %constant_dynamic-slice_fusion.1), channel_id=1, source_target_pairs={{0,8},{4,12},{24,16},{28,20},{1,9},{5,13},{25,17},{29,21},{2,10},{... | collective-permute-start | bytes 4718600 | tf_op jit(solution)/shard_map/ppermute | solution.py:894
  476.0 83.9 %collective-permute-start.16 = (bf16[1024,1024]{1,0:T(8,128)(2,1)}, bf16[1024,1024]{1,0:T(8,128)(2,1)}, u32[]{:S(2)}, u32[]{:S(2)}) collective-permute-start(bf16[1024,1024]{1,0:T(8,128)(2,1)} %get-tuple-element.159), channel_id=1, source_target_pairs={{0,2},{1,3},{2,0},{3,1},{4,6},{5,7},{6,4},{7,5},{8,10},{9,11},{10,... | collective-permute-start | bytes 6291464 | tf_op jit(solution)/shard_map/ppermute | solution.py:796
  512.2 52.9 %collective-permute-start.26 = (bf16[2,768,512]{2,1,0:T(8,128)(2,1)}, bf16[2,768,512]{2,1,0:T(8,128)(2,1)}, u32[]{:S(2)}, u32[]{:S(2)}) collective-permute-start(bf16[2,768,512]{2,1,0:T(8,128)(2,1)} %add_convert_fusion.8), channel_id=1, source_target_pairs={{8,16},{12,20},{16,8},{20,12},{9,17},{13,21},{17,9},{21,13},{10,18... | collective-permute-start | bytes 4718600 | tf_op jit(solution)/shard_map/ppermute | solution.py:897
  553.3 38.6 %collective-permute-start.28 = (bf16[2,768,512]{2,1,0:T(8,128)(2,1)}, bf16[2,768,512]{2,1,0:T(8,128)(2,1)}, u32[]{:S(2)}, u32[]{:S(2)}) collective-permute-start(bf16[2,768,512]{2,1,0:T(8,128)(2,1)} %constant_dynamic-slice_fusion), channel_id=1, source_target_pairs={{0,8},{4,12},{24,16},{28,20},{1,9},{5,13},{25,17},{29,21},{2,10},{... | collective-permute-start | bytes 4718600 | tf_op jit(solution)/shard_map/ppermute | solution.py:894
  594.9 82.0 %collective-permute-start.29 = (bf16[2,768,512]{2,1,0:T(8,128)(2,1)}, bf16[2,768,512]{2,1,0:T(8,128)(2,1)}, u32[]{:S(2)}, u32[]{:S(2)}) collective-permute-start(bf16[2,768,512]{2,1,0:T(8,128)(2,1)} %add_convert_fusion.6), channel_id=1, source_target_pairs={{8,16},{12,20},{16,8},{20,12},{9,17},{13,21},{17,9},{21,13},{10,18... | collective-permute-start | bytes 4718600 | tf_op jit(solution)/shard_map/ppermute | solution.py:897
  674.6 20.4 %collective-permute-start.27 = (bf16[768,512]{1,0:T(8,128)(2,1)S(1)}, bf16[768,512]{1,0:T(8,128)(2,1)S(1)}, u32[]{:S(2)}, u32[]{:S(2)}) collective-permute-start(bf16[768,512]{1,0:T(8,128)(2,1)S(1)} %dynamic-slice_bitcast_fusion.13), channel_id=1, source_target_pairs={{0,8},{4,12},{8,0},{12,4},{16,24},{20,28},{24,16},{28,20},{1,9},{5... | collective-permute-start | bytes 2359304 | tf_op jit(solution)/shard_map/ppermute | solution.py:900
  678.9 32.5 %collective-permute-start.30 = (bf16[768,512]{1,0:T(8,128)(2,1)S(1)}, bf16[768,512]{1,0:T(8,128)(2,1)S(1)}, u32[]{:S(2)}, u32[]{:S(2)}) collective-permute-start(bf16[768,512]{1,0:T(8,128)(2,1)S(1)} %dynamic-slice_bitcast_fusion.12), channel_id=1, source_target_pairs={{0,8},{4,12},{8,0},{12,4},{16,24},{20,28},{24,16},{28,20},{1,9},{5... | collective-permute-start | bytes 2359304 | tf_op jit(solution)/shard_map/ppermute | solution.py:900
  (36 other events, 574.3 us)
Sparse Core Ops, SparseCore 0:
  12.0 73.2 all-gather.1

commit v3 on v2

--- a/solution.py
+++ b/solution.py
@@ -328,8 +328,8 @@
     )(tok, ctx, w_out, gain)
 
 
-def gates_of(x, router, routes_t):
-    logits = dot(x, router).T
+def gates_of(x, router, routes_t, num_experts):
+    logits = dot(x, router).T[: 16 * pl.cdiv(num_experts, 16)]
     expert = lax.broadcasted_iota(jnp.int32, logits.shape, 0)
     hit = expert == routes_t[0:1]
     for k in range(1, routes_t.shape[0]):
@@ -341,7 +341,7 @@
 
 
 def expert_kernel(
-    first_expert, local, with_init, me_ref, x_ref, c_ref, route_ref, router_ref, wg_ref, wu_ref, wd_ref, *refs
+    first_expert, local, num_experts, with_init, me_ref, x_ref, c_ref, route_ref, router_ref, wg_ref, wu_ref, wd_ref, *refs
 ):
     if with_init:
         out_in, dx_in, dg_in, refs = refs[0], refs[1], refs[2], refs[3:]
@@ -356,7 +356,9 @@
 
     @pl.when(e == 0)
     def _():
-        gp_ref[...] = gates_of(x, router_ref[...], route_ref[...]).T
+        gates = gates_of(x, router_ref[...], route_ref[...], num_experts)
+        fill = jnp.zeros((128 - gates.shape[0], b), F32)
+        gp_ref[...] = jnp.concatenate([gates, fill], axis=0).T
         dgc_ref[...] = jnp.zeros_like(dgc_ref)
         if with_init:
             out_acc[...] = out_in[...].astype(F32)
@@ -403,7 +405,7 @@
         dg_ref[...] = dg_t + dg_in[...] if with_init else dg_t
 
 
-def run_expert(me, x, c, routes_t, router, wg, wu, wd, first, count, init=None):
+def run_expert(me, x, c, routes_t, router, wg, wu, wd, first, count, num_experts, init=None):
     length, d = x.shape
     local, _, ff = wg.shape
     b = 512
@@ -421,7 +423,7 @@
     wide_spec = spec((b, ff), lambda i, e: (i, e))
     with_init = init is not None
     return pl.pallas_call(
-        functools.partial(expert_kernel, first, local, with_init),
+        functools.partial(expert_kernel, first, local, num_experts, with_init),
         grid=(length // b, count),
         in_specs=[
             pl.BlockSpec(memory_space=pltpu.SMEM),
@@ -452,9 +454,8 @@
     )(me, x, c, routes_t, router, wg, wu, wd, *(init if with_init else ()))
 
 
-def weight_grad_kernel(n, *refs):
+def weight_grad_kernel(n, paired, dp_ref, *refs):
     xt, ct, dgate, dup, hs = (refs[k * n : (k + 1) * n] for k in range(5))
-    gate_ref, up_ref, down_ref = refs[5 * n :]
 
     def total(lefts, rights):
         acc = None
@@ -466,6 +467,21 @@
     down = total(ct, hs).T.astype(BF16)
     gate = total(xt, dgate).astype(BF16)
     up = total(xt, dup).astype(BF16)
+    if paired:
+        keep_ref, send_ref, down_keep_ref, down_send_ref = refs[5 * n :]
+        first = dp_ref[0] % 2 == 0
+        half = gate.shape[0] // 2
+        for k, value in enumerate((gate, up)):
+            keep_ref[0, k, 0] = jnp.where(first, value[:half], value[half:])
+            send_ref[0, k, 0] = jnp.where(first, value[half:], value[:half])
+        rows = down_keep_ref.shape[3]
+        for z in range(down_keep_ref.shape[0]):
+            even = down[2 * z * rows : (2 * z + 1) * rows]
+            odd = down[(2 * z + 1) * rows : (2 * z + 2) * rows]
+            down_keep_ref[z, 0, 0] = jnp.where(first, even, odd)
+            down_send_ref[z, 0, 0] = jnp.where(first, odd, even)
+        return
+    gate_ref, up_ref, down_ref = refs[5 * n :]
     for p in range(down_ref.shape[0]):
         rows = down_ref.shape[3]
         down_ref[p, 0, 0] = down[p * rows : (p + 1) * rows]
@@ -475,7 +491,7 @@
         up_ref[p, 0] = up[p * rows : (p + 1) * rows]
 
 
-def run_weight_grad(xt, ct, dgate, dup, hs, count, skips, n_dp):
+def run_weight_grad(dp, xt, ct, dgate, dup, hs, count, skips, n_dp, paired):
     n = len(xt)
     d, length = xt[0].shape
     ff = hs[-1].shape[1] // count
@@ -486,33 +502,36 @@
         for skip in skips
     ]
     per = d // n_dp
-    rows = jax.ShapeDtypeStruct((n_dp, count, per, ff), BF16)
-    row_spec = spec((m // per, 1, per, ff), lambda e, i: (i, e, 0, 0))
+    down_at = lambda e, i: (0, e, i // (ff // m), 0, i % (ff // m))
+    if paired:
+        row_spec = spec((1, 2, 1, per, ff), lambda e, i: (i, 0, e, 0, 0))
+        rows = jax.ShapeDtypeStruct((n_dp // 2, 2, count, per, ff), BF16)
+        down_spec = spec((n_dp // 2, 1, 1, ff // n_dp, m), down_at)
+        down = jax.ShapeDtypeStruct((n_dp // 2, count, d // ff, ff // n_dp, ff), BF16)
+        out_specs, out_shape = [row_spec] * 2 + [down_spec] * 2, [rows] * 2 + [down] * 2
+    else:
+        row_spec = spec((m // per, 1, per, ff), lambda e, i: (i, e, 0, 0))
+        rows = jax.ShapeDtypeStruct((n_dp, count, per, ff), BF16)
+        down_spec = spec((n_dp, 1, 1, ff // n_dp, m), down_at)
+        down = jax.ShapeDtypeStruct((n_dp, count, d // ff, ff // n_dp, ff), BF16)
+        out_specs, out_shape = [row_spec] * 2 + [down_spec], [rows] * 2 + [down]
     return pl.pallas_call(
-        functools.partial(weight_grad_kernel, n),
+        functools.partial(weight_grad_kernel, n, paired),
         grid=(count, d // m),
-        in_specs=[left] * (2 * n) + rights * 3,
-        out_specs=[
-            row_spec,
-            row_spec,
-            spec((n_dp, 1, 1, ff // n_dp, m), lambda e, i: (0, e, i // (ff // m), 0, i % (ff // m))),
-        ],
-        out_shape=[
-            rows,
-            rows,
-            jax.ShapeDtypeStruct((n_dp, count, d // ff, ff // n_dp, ff), BF16),
-        ],
+        in_specs=[pl.BlockSpec(memory_space=pltpu.SMEM)] + [left] * (2 * n) + rights * 3,
+        out_specs=out_specs,
+        out_shape=out_shape,
         compiler_params=params(60, 2),
         cost_estimate=took(37),
         name="weight_grad",
-    )(*xt, *ct, *dgate, *dup, *hs)
+    )(dp, *xt, *ct, *dgate, *dup, *hs)
 
 
 def back_mid_kernel(n, n_ex, local, *refs):
     (me_ref, res_ref, cot_ref, route_ref, x_ref, router_ref, gain_ref, w_ref) = refs[:8]
     dx_refs, dg_refs = refs[8 : 8 + n], refs[8 + n : 8 + n + n_ex]
     dres_ref, dattn_ref, dctx_ref, dlog_ref, ggain_ref = refs[8 + n + n_ex :]
-    gp = gates_of(x_ref[...], router_ref[...], route_ref[...])
+    gp = gates_of(x_ref[...], router_ref[...], route_ref[...], n_ex * local)
     parts = [ref[...][:local] for ref in dg_refs]
     owners = []
     for owner in range(n_ex):
@@ -521,7 +540,6 @@
             own = jnp.where((owner ^ step) == me_ref[0], parts[step], own)
         owners.append(own)
     dg = jnp.concatenate(owners, axis=0)
-    gp = gp[: dg.shape[0]]
     d_logits = gp * (dg - jnp.sum(gp * dg, axis=0, keepdims=True))
     fill = jnp.zeros((128 - dg.shape[0], dg.shape[1]), F32)
     d_logits = jnp.concatenate([d_logits, fill], axis=0).T.astype(BF16)
@@ -633,48 +651,183 @@
     )(dq, dk, dv, w_qkv, tok, gain, d_res)
 
 
+CHUNKS = (3, 0, 1, 2)
+
+
+def add_rows(dst, srcs, step=64):
+    def body(i, carry):
+        at = pl.ds(pl.multiple_of(i * step, step), step)
+        total = srcs[0][at, :].astype(F32)
+        for src in srcs[1:]:
+            total = total + src[at, :].astype(F32)
+        dst[at, :] = total.astype(dst.dtype)
+        return carry
+
+    lax.fori_loop(0, dst.shape[0] // step, body, 0)
+
+
 def finish_kernel(
-    ht_ref, dq_ref, dk_ref, dv_ref, dout_ref, small_ref, out_ref,
-    b1, r1, s1, r2, s2, r3, s3, r4, sem_s, sem_r,
+    ht_ref, dq_ref, dk_ref, dv_ref, dout_ref, small_ref,
+    keep_a, got_a, down_keep_a, down_got_a, keep_b, send_b, down_keep_b, down_send_b,
+    out_ref, gate_ref, up_ref, down_ref, *scratch,
 ):
+    n = len(CHUNKS)
+    lists = [scratch[k * n : (k + 1) * n] for k in range(8)]
+    b1, r1, s1, r2, s2, r3, s3, r4 = lists
+    tot, rx, rx_down, rz1, rz2, rz3, sem_s, sem_r, sem_es, sem_er, sem_l = scratch[8 * n :]
     dp, ex = lax.axis_index("dp"), lax.axis_index("expert")
     z, x, y, c = dp // 2, dp % 2, ex // 2, ex % 2
-    core = [(dp, ex ^ 1)]
-    plane = [(dp ^ 1, ex), (dp, ex ^ 2), (dp ^ 1, ex ^ 2)]
+    over_core, over_y, over_x = (dp, ex ^ 1), (dp, ex ^ 2), (dp ^ 1, ex)
     line = [(dp ^ (2 * k), ex) for k in (1, 2, 3)]
-    group = [(dp, ex ^ k) for k in (1, 2, 3)]
+    group = [over_core, over_y, (dp, ex ^ 3)]
     barrier = pltpu.get_barrier_semaphore()
-    peers = core + plane + line + group[2:]
+    peers = group + [over_x] + line
     for peer in peers:
         pl.semaphore_signal(barrier, inc=1, device_id=peer, device_id_type=pl.DeviceIdType.MESH)
     pl.semaphore_wait(barrier, len(peers))
 
-    n = b1.shape[0]
     widths = [dout_ref.shape[1], dq_ref.shape[1], dk_ref.shape[1] + dv_ref.shape[1], 128]
     starts = [sum(widths[:k]) for k in range(n)]
     started = {}
 
-    def send(k, slot, src, dst, peer):
+    def remote(key, src, dst, send_sem, recv_sem, peer):
         copy = pltpu.make_async_remote_copy(
             src_ref=src,
             dst_ref=dst,
-            send_sem=sem_s.at[k, slot],
-            recv_sem=sem_r.at[k, slot],
+            send_sem=send_sem,
+            recv_sem=recv_sem,
             device_id=peer,
             device_id_type=pl.DeviceIdType.MESH,
         )
+        started[key] = copy
+        return copy
+
+    def send(k, slot, src, dst, peer):
+        remote((k, slot), src, dst, sem_s.at[k, slot], sem_r.at[k, slot], peer).start()
+
+    def kind_of(which, keep_like, down_like):
+        return down_like if which == 2 else keep_like.at[:, which]
+
+    def rx_of(ch):
+        return rx_down.at[ch // 3] if ch % 3 == 2 else rx.at[ch // 3, :, ch % 3]
+
+    for ch in range(3, 6):
+        src = kind_of(ch - 3, send_b, down_send_b)
+        remote(("x", ch), src, rx_of(ch), sem_es.at[ch, 0], sem_er.at[ch, 0], over_x).start()
+    loads = {}
+    for ch in range(3):
+        copy = pltpu.make_async_copy(
+            kind_of(ch, got_a, down_got_a), rx_of(ch), sem_l.at[ch]
+        )
         copy.start()
-        started[k, slot] = copy
-
-    def arrive(k, slots):
-        for slot in slots:
-            started[k, slot].wait()
+        loads[ch] = [copy]
+    for ch in range(6):
+        keep, down_keep = (keep_a, down_keep_a) if ch < 3 else (keep_b, down_keep_b)
+        for zz in range(4):
+            for e in range(2):
+                if ch % 3 < 2:
+                    copy = pltpu.make_async_copy(
+                        keep.at[zz, ch % 3, e],
+                        tot.at[ch, zz, e * 128 : (e + 1) * 128],
+                        sem_l.at[6 + (ch * 4 + zz) * 4 + e * 2],
+                    )
+                    copy.start()
+                    loads.setdefault(ch, []).append(copy)
+                    continue
+                for h in range(2):
+                    at = e * 128 + h * 64
+                    copy = pltpu.make_async_copy(
+                        down_keep.at[zz, e, h],
+                        tot.at[ch, zz, at : at + 64],
+                        sem_l.at[6 + (ch * 4 + zz) * 4 + e * 2 + h],
+                    )
+                    copy.start()
+                    loads.setdefault(ch, []).append(copy)
+
+    upper = z // 2
+    outer = (z == 0) | (z == 3)
+    inner = jnp.logical_not(outer)
+
+    def z_copy(ch, stage):
+        if stage == 1:
+            src, dst = tot.at[ch, pl.ds(2 * (1 - upper), 2)], rz1.at[ch]
+            peer = (dp ^ 2, ex)
+        elif stage == 2:
+            src, dst = tot.at[ch, pl.ds(2 * (1 - upper), 2)], rz2.at[ch]
+            peer = (dp ^ 6, ex)
+        else:
+            src, dst = tot.at[ch, 2 * upper + 1 - z % 2], rz3.at[ch]
+            peer = (dp ^ 2, ex)
+        key = ("z", ch, stage)
+        if key in started:
+            return started[key]
+        return remote(key, src, dst, sem_es.at[ch, stage], sem_er.at[ch, stage], peer)
+
+    def exp_x(ch):
+        for copy in loads[ch]:
+            copy.wait()
+        if ch >= 3:
+            started["x", ch].wait()
+        for zz in range(4):
+            for e in range(2):
+                if ch % 3 < 2:
+                    dst = tot.at[ch, zz, e * 128 : (e + 1) * 128]
+                    add_rows(dst, [dst, rx.at[ch // 3, zz, ch % 3, e]])
+                else:
+                    for h in range(2):
+                        at = e * 128 + h * 64
+                        dst = tot.at[ch, zz, at : at + 64]
+                        add_rows(dst, [dst, rx_down.at[ch // 3, zz, e, h]])
+        one, three = z_copy(ch, 1), z_copy(ch, 3)
+
+        @pl.when(outer)
+        def _():
+            one.start()
+            three.start()
+
+    def exp_1(ch):
+        two = z_copy(ch, 2)
+
+        @pl.when(inner)
+        def _():
+            z_copy(ch, 1).wait_recv()
+            for p in range(2):
+                dst = tot.at[ch, 2 * (1 - upper) + p]
+                add_rows(dst, [dst, rz1.at[ch, p]])
+            two.start()
+
+    def exp_2(ch):
+        @pl.when(inner)
+        def _():
+            z_copy(ch, 2).wait()
+            for p in range(2):
+                dst = tot.at[ch, 2 * upper + p]
+                add_rows(dst, [dst, rz2.at[ch, p]])
+            z_copy(ch, 3).start()
+
+        @pl.when(outer)
+        def _():
+            z_copy(ch, 1).wait_send()
+
+    def exp_3(ch):
+        z_copy(ch, 3).wait()
+        for e in range(2):
+            at = 2 * (ch // 3) + e
+            if ch % 3 < 2:
+                rows = slice(e * 128, (e + 1) * 128)
+                dst = (gate_ref, up_ref)[ch % 3].at[at]
+                add_rows(dst, [tot.at[ch, z, rows], rz3.at[ch, rows]])
+            else:
+                for h in range(2):
+                    rows = slice(e * 128 + h * 64, e * 128 + (h + 1) * 64)
+                    dst = down_ref.at[at, :, h * 512 : (h + 1) * 512]
+                    add_rows(dst, [tot.at[ch, z, rows], rz3.at[ch, rows]])
 
     def place(k, lanes, value):
         for p in range(8):
             for e in range(4):
                 row = 128 * p + 32 * e
-                b1[k, e % 2, e // 2, p % 2, p // 2, :, lanes] = value[row : row + 32]
+                b1[k][e % 2, e // 2, p % 2, p // 2, :, lanes] = value[row : row + 32]
 
     def step0(k):
         if k == 0:
@@ -689,87 +842,220 @@
             place(k, slice(half, 2 * half), dot(ht_ref[...], dv_ref[...]).astype(BF16))
         else:
             place(k, slice(0, 128), small_ref[...])
-        w = slice(0, widths[k])
-        send(k, 0, b1.at[k, 1 - c, :, :, :, :, w], r1.at[k, :, :, :, :, w], core[0])
+        send(k, 0, b1[k].at[1 - c], r1[k], over_core)
 
     def step1(k):
-        arrive(k, [0])
-        w = slice(0, widths[k])
+        started[k, 0].wait()
         for yy in range(2):
             for xx in range(2):
                 for zz in range(4):
-                    s1[k, yy, xx, zz, :, w] = (
-                        b1[k, c, yy, xx, zz, :, w].astype(F32)
-                        + r1[k, yy, xx, zz, :, w].astype(F32)
+                    s1[k][yy, xx, zz] = (
+                        b1[k][c, yy, xx, zz].astype(F32) + r1[k][yy, xx, zz].astype(F32)
                     ).astype(BF16)
-        for i, (dy, dx) in enumerate([(0, 1), (1, 0), (1, 1)]):
-            send(k, 1 + i, s1.at[k, y ^ dy, x ^ dx, :, :, w], r2.at[k, i, :, :, w], plane[i])
+        send(k, 1, s1[k].at[1 - y], r2[k], over_y)
 
     def step2(k):
-        arrive(k, [1, 2, 3])
-        w = slice(0, widths[k])
+        started[k, 1].wait()
+        for xx in range(2):
+            for zz in range(4):
+                s2[k][xx, zz] = (
+                    s1[k][y, xx, zz].astype(F32) + r2[k][xx, zz].astype(F32)
+                ).astype(BF16)
+        send(k, 2, s2[k].at[1 - x], r3[k].at[0], over_x)
+
+    def step3(k):
+        started[k, 2].wait()
         for zz in range(4):
-            total = s1[k, y, x, zz, :, w].astype(F32)
-            for i in range(3):
-                total = total + r2[k, i, zz, :, w].astype(F32)
-            s2[k, zz, :, w] = total.astype(BF16)
+            s3[k][zz] = (s2[k][x, zz].astype(F32) + r3[k][0, zz].astype(F32)).astype(BF16)
         for i in range(3):
-            send(k, 4 + i, s2.at[k, z ^ (i + 1), :, w], r3.at[k, i, :, w], line[i])
-
-    def step3(k):
-        arrive(k, [4, 5, 6])
-        w = slice(0, widths[k])
-        total = s2[k, z, :, w].astype(F32)
+            send(k, 3 + i, s3[k].at[z ^ (i + 1)], r3[k].at[1, i], line[i])
+
+    def step4(k):
         for i in range(3):
-            total = total + r3[k, i, :, w].astype(F32)
-        s3[k, :, w] = total.astype(BF16)
+            started[k, 3 + i].wait()
+        total = s3[k][z].astype(F32)
         for i in range(3):
-            send(k, 7 + i, s3.at[k, :, w], r4.at[k, i, :, w], group[i])
-
-    def step4(k):
-        arrive(k, [7, 8, 9])
-        w, o = slice(0, widths[k]), slice(starts[k], starts[k] + widths[k])
-        out_ref[pl.ds(pl.multiple_of(ex * 32, 32), 32), o] = s3[k, :, w].astype(F32)
+            total = total + r3[k][1, i].astype(F32)
+        r4[k][3] = total.astype(BF16)
         for i in range(3):
+            send(k, 6 + i, r4[k].at[3], r4[k].at[i], group[i])
+
+    def step5(k):
+        o = slice(starts[k], starts[k] + widths[k])
+        out_ref[pl.ds(pl.multiple_of(ex * 32, 32), 32), o] = r4[k][3].astype(F32)
+        for i in range(3):
+            started[k, 6 + i].wait()
             rows = pl.ds(pl.multiple_of((ex ^ (i + 1)) * 32, 32), 32)
-            out_ref[rows, o] = r4[k, i, :, w].astype(F32)
-
-    steps = (step0, step1, step2, step3, step4)
-    order = [3, 0, 1, 2]
-    for turn in range(n + len(steps) - 1):
-        for place_in, k in enumerate(order):
-            at = turn - place_in
-            if 0 <= at < len(steps):
-                steps[at](k)
-
-
-def run_finish(ht, dq, dk, dv, d_out, small):
+            out_ref[rows, o] = r4[k][i].astype(F32)
+
+    def dense(step, chunks=CHUNKS):
+        for k in chunks:
+            step(k)
+
+    dense(step0, CHUNKS[:2])
+    for ch in range(3):
+        exp_x(ch)
+    dense(step0, CHUNKS[2:])
+    dense(step1)
+    for ch in range(3):
+        exp_1(ch)
+    exp_x(3)
+    dense(step2)
+    for ch in range(3):
+        exp_2(ch)
+    exp_1(3)
+    exp_x(4)
+    dense(step3)
+    for ch in range(3):
+        exp_3(ch)
+    exp_1(4)
+    exp_2(3)
+    exp_x(5)
+    dense(step4)
+    exp_3(3)
+    exp_1(5)
+    exp_2(4)
+    dense(step5)
+    exp_3(4)
+    exp_2(5)
+    exp_3(5)
+
+
+def run_finish(ht, dq, dk, dv, d_out, small, experts):
     d = ht.shape[0]
-    n, w = 4, d
-    columns = d_out.shape[1] + dq.shape[1] + dk.shape[1] + dv.shape[1] + small.shape[1]
+    widths = [d_out.shape[1], dq.shape[1], dk.shape[1] + dv.shape[1], small.shape[1]]
+    keep_a, _, down_keep_a, _ = experts[0], None, experts[2], None
+    _, kinds, count, per, ff = keep_a.shape
+    down_rows = down_keep_a.shape[3]
+    vmem = pl.BlockSpec(memory_space=pltpu.VMEM)
+    hbm = pl.BlockSpec(memory_space=pl.ANY)
+    shapes = [
+        (2, 2, 2, 4, 32), (2, 2, 4, 32), (2, 2, 4, 32), (2, 4, 32), (2, 4, 32), (2, 4, 32), (4, 32), (4, 32),
+    ]
+    scratch = [pltpu.VMEM(shape + (w,), BF16) for shape in shapes for w in widths]
+    rows = count * per
+    scratch += [
+        pltpu.VMEM((6, 4, rows, ff), BF16),
+        pltpu.VMEM((2, 4, 2, count, per, ff), BF16),
+        pltpu.VMEM((2,) + down_keep_a.shape, BF16),
+        pltpu.VMEM((6, 2, rows, ff), BF16),
+        pltpu.VMEM((6, 2, rows, ff), BF16),
+        pltpu.VMEM((6, rows, ff), BF16),
+        pltpu.SemaphoreType.DMA((len(widths), 9)),
+        pltpu.SemaphoreType.DMA((len(widths), 9)),
+        pltpu.SemaphoreType.DMA((6, 4)),
+        pltpu.SemaphoreType.DMA((6, 4)),
+        pltpu.SemaphoreType.DMA((6 + 96,)),
+    ]
     return pl.pallas_call(
         finish_kernel,
-        in_specs=[pl.BlockSpec(memory_space=pltpu.VMEM)] * 6,
-        out_specs=pl.BlockSpec(memory_space=pltpu.VMEM),
-        out_shape=jax.ShapeDtypeStruct((128, columns), F32),
-        scratch_shapes=[
-            pltpu.VMEM((n, 2, 2, 2, 4, 32, w), BF16),
-            pltpu.VMEM((n, 2, 2, 4, 32, w), BF16),
-            pltpu.VMEM((n, 2, 2, 4, 32, w), BF16),
-            pltpu.VMEM((n, 3, 4, 32, w), BF16),
-            pltpu.VMEM((n, 4, 32, w), BF16),
-            pltpu.VMEM((n, 3, 32, w), BF16),
-            pltpu.VMEM((n, 32, w), BF16),
-            pltpu.VMEM((n, 3, 32, w), BF16),
-            pltpu.SemaphoreType.DMA((n, 10)),
-            pltpu.SemaphoreType.DMA((n, 10)),
-        ],
+        in_specs=[vmem] * 6 + [hbm] * 8,
+        out_specs=[vmem] * 4,
+        out_shape=[
+            jax.ShapeDtypeStruct((128, sum(widths)), F32),
+            jax.ShapeDtypeStruct((2 * count, per, ff), F32),
+            jax.ShapeDtypeStruct((2 * count, per, ff), F32),
+            jax.ShapeDtypeStruct((2 * count, down_rows, d), F32),
+        ],
+        scratch_shapes=scratch,
         compiler_params=pltpu.CompilerParams(
-            vmem_limit_bytes=60 * MIB, collective_id=1, has_side_effects=True
+            vmem_limit_bytes=62 * MIB, collective_id=1, has_side_effects=True
         ),
         cost_estimate=took(60),
         name="finish",
-    )(ht, dq, dk, dv, d_out, small)
+    )(ht, dq, dk, dv, d_out, small, *experts)
+
+
+def gather_kernel(mine_ref, out_ref, sem_s, sem_r, sem_l):
+    dp, ex = lax.axis_index("dp"), lax.axis_index("expert")
+    z = dp // 2
+    core, over_y, over_x = (dp, ex ^ 1), (dp, ex ^ 2), (dp ^ 1, ex)
+    line = [None] + [(dp ^ (2 * k), ex) for k in (1, 2, 3)]
+    barrier = pltpu.get_barrier_semaphore()
+    peers = [core, over_y, over_x] + line[1:]
+    for peer in peers:
+        pl.semaphore_signal(barrier, inc=1, device_id=peer, device_id_type=pl.DeviceIdType.MESH)
+    pl.semaphore_wait(barrier, len(peers))
+    rows = mine_ref.shape[0]
+    width = mine_ref.shape[1]
+    cut = (width // 256 + 1) * 128
+    halves = [pl.ds(0, cut), pl.ds(cut, width - cut)]
+    started = {}
+
+    def block(k, dx, dy):
+        at = (((z ^ k) * 2 + (dp % 2 ^ dx)) * 4 + (ex ^ (2 * dy))) * rows
+        return pl.ds(pl.multiple_of(at, rows), rows)
+
+    def send(key, k, dx, dy, peer, src=None, lanes=None):
+        index = len(started)
+        at = block(k, dx, dy)
+        dst = out_ref.at[at] if lanes is None else out_ref.at[at, lanes]
+        copy = pltpu.make_async_remote_copy(
+            src_ref=dst if src is None else src,
+            dst_ref=dst,
+            send_sem=sem_s.at[index],
+            recv_sem=sem_r.at[index],
+            device_id=peer,
+            device_id_type=pl.DeviceIdType.MESH,
+        )
+        copy.start()
+        started[key] = copy
+
+    for k in (3, 2, 1):
+        send(("z", k), 0, 0, 0, line[k], mine_ref)
+    send(("x", 0), 0, 0, 0, over_x, mine_ref)
+    send(("y", 0), 0, 0, 0, over_y, mine_ref)
+    send(("c", 0), 0, 0, 0, core, mine_ref)
+    own = pltpu.make_async_copy(mine_ref, out_ref.at[block(0, 0, 0)], sem_l)
+    own.start()
+
+    def onward(k):
+        started["x", k].wait_recv()
+        send(("dy", k), k, 1, 0, over_y, None, halves[0])
+        send(("cx", k), k, 1, 0, core)
+        started["y", k].wait_recv()
+        send(("dx", k), k, 0, 1, over_x, None, halves[1])
+        send(("cy", k), k, 0, 1, core)
+
+    def last(k):
+        started["dy", k].wait_recv()
+        started["dx", k].wait_recv()
+        send(("cd", k), k, 1, 1, core)
+
+    onward(0)
+    for k in (1, 2, 3):
+        started["z", k].wait_recv()
+        send(("x", k), k, 0, 0, over_x)
+        send(("y", k), k, 0, 0, over_y)
+        send(("c", k), k, 0, 0, core)
+    last(0)
+    for k in (1, 2, 3):
+        onward(k)
+    for k in (1, 2, 3):
+        last(k)
+    for key, copy in started.items():
+        copy.wait_send()
+        if key[0] in ("c", "cx", "cy", "cd"):
+            copy.wait_recv()
+    own.wait()
+
+
+def run_gather(mine, total):
+    hbm = pl.BlockSpec(memory_space=pl.ANY)
+    return pl.pallas_call(
+        gather_kernel,
+        in_specs=[hbm],
+        out_specs=hbm,
+        out_shape=jax.ShapeDtypeStruct((total, mine.shape[1]), BF16),
+        scratch_shapes=[
+            pltpu.SemaphoreType.DMA((40,)),
+            pltpu.SemaphoreType.DMA((40,)),
+            pltpu.SemaphoreType.DMA,
+        ],
+        compiler_params=pltpu.CompilerParams(collective_id=2, has_side_effects=True),
+        cost_estimate=took(40),
+        name="gather",
+    )(mine)
 
 
 def after(value, *deps):
@@ -807,7 +1093,12 @@
     )
     packed = jnp.concatenate([w_query, keyvalue_weight, w_out, small], axis=1)
     mine = lax.dynamic_slice_in_dim(packed, ex * part, part, axis=0)
-    every = lax.all_gather(mine, ("dp", "expert"), axis=0, tiled=True)
+    local = expert_gate.shape[0]
+    fast = n_dp == 8 and n_ex == 4 and d == 1024 and local == 4 and expert_gate.shape[2] == 512
+    if fast:
+        every = run_gather(mine, d)
+    else:
+        every = lax.all_gather(mine, ("dp", "expert"), axis=0, tiled=True)
     w_all = every
     width = 2 * nq
     full_out = every[:, width : width + d]
@@ -817,7 +1108,7 @@
     gain_one = extra[:, num_experts].reshape(1, d)
     gain_two = extra[:, num_experts + 1].reshape(1, d)
 
-    routes_t = routes.reshape(length, -1).T
+    routes_t = after(routes.reshape(length, -1).T, every)
     cots = {0: cot}
     route_set = {0: routes_t}
     for step in range(1, n_ex):
@@ -859,66 +1150,15 @@
     weights = (expert_gate, expert_up, expert_down)
     half = local // 2
 
-    def scatter(made):
-        if n_dp != 8:
-            done = [
-                lax.psum_scatter(g, "dp", scatter_dimension=0, tiled=True)[0].astype(F32)
-                for g in made
-            ]
-            for _ in range(4):
-                yield made[0]
-            yield done
-            return
-        at = lax.axis_index("dp")
-        z, x = at // 2, at % 2
-
-        def side(which):
-            return jnp.concatenate(
-                [
-                    lax.dynamic_index_in_dim(
-                        g.reshape(4, 2, -1, ff_lanes), which, axis=1, keepdims=False
-                    )
-                    for g in made
-                ],
-                axis=1,
-            )
-
-        sent = side(1 - x)
-        yield sent
-        got = lax.ppermute(sent, "dp", [(i, i ^ 1) for i in range(8)])
-        total = (side(x).astype(F32) + got.astype(F32)).astype(BF16)
-        upper = z // 2
-        far = lax.dynamic_slice_in_dim(total, 2 * (1 - upper), 2, axis=0)
-        near = lax.dynamic_slice_in_dim(total, 2 * upper, 2, axis=0)
-        yield far
-        got = lax.ppermute(far, "dp", [(0, 2), (1, 3), (6, 4), (7, 5)])
-        far = (far.astype(F32) + got.astype(F32)).astype(BF16)
-        yield far
-        got = lax.ppermute(far, "dp", [(2, 4), (3, 5), (4, 2), (5, 3)])
-        near = (near.astype(F32) + got.astype(F32)).astype(BF16)
-        yield near
-        got = lax.ppermute(
-            lax.dynamic_index_in_dim(near, 1 - z % 2, axis=0, keepdims=False),
-            "dp",
-            [(i, i ^ 2) for i in range(8)],
-        )
-        own = lax.dynamic_index_in_dim(near, z % 2, axis=0, keepdims=False)
-        own = own.astype(F32) + got.astype(F32)
-        done, begin = [], 0
-        for g in made:
-            size = g.size // (8 * ff_lanes)
-            done.append(own[begin : begin + size].reshape(g.shape[1:]))
-            begin += size
-        yield done
-
-    ff_lanes = expert_gate.shape[2]
+    dp = lax.axis_index("dp").reshape(1).astype(jnp.int32)
+
     res = {}
     chain = xs[1]
 
     def experts(step, first, count, init=None):
         x = after(xs[step], chain)
         return run_expert(
-            me, x, cots[step], route_set[step], router, *weights, first, count, init
+            me, x, cots[step], route_set[step], router, *weights, first, count, num_experts, init
         )
 
     def grads(first):
@@ -931,7 +1171,7 @@
         made = None
         for at in range(0, n_ex, 4):
             some = [group[at : at + 4] for group in turned + pieces]
-            part = run_weight_grad(*some, half, skips[at : at + 4], n_dp)
+            part = run_weight_grad(dp, *some, half, skips[at : at + 4], n_dp, fast)
             if made is None:
                 made = part
             else:
@@ -953,9 +1193,9 @@
         res[step, 0] = experts(step, 0, half)
         chain = (res[step, 0][0], tops[-1])
         widen_top()
-    made = grads(0)
-    one = scatter(made)
-    chain = (next(one), tops[-1])
+    made_one = grads(0)
+    chain = (made_one[0], tops[-1])
+    got_one = [swap(made_one[k], 1, "dp", n_dp) for k in (1, 3)] if fast else []
     widen_top()
     for step in even:
         init = [
@@ -965,9 +1205,8 @@
         res[step, half] = experts(step, half, half, init + [res[step, 0][2]])
         chain = (res[step, half][0], tops[-1])
         widen_top()
-    made = grads(half)
-    two = scatter(made)
-    chain = (next(two), next(one), tops[-1])
+    made_two = grads(half)
+    chain = (made_two[0], got_one, tops[-1])
     while len(tops) <= len(bits):
         widen_top()
     top = tops[-1]
@@ -999,10 +1238,10 @@
     d_router_w = jnp.einsum("rd,re->de", normed_two, d_logits, preferred_element_type=F32)
 
     dq, dk, dv = run_attn_bwd(
-        prefix, after(q, next(one), top), kd, vd, d_ctx, ctx, lse, cos_l, sin_l, cos_t, sin_t
+        prefix, after(q, top), kd, vd, d_ctx, ctx, lse, cos_l, sin_l, cos_t, sin_t
     )
     grad_tok, d_gain_one = run_back_in(
-        after(dq, next(two), next(one), block_out), dk, dv, w_all, tok, gain_one, d_res
+        after(dq, block_out), dk, dv, w_all, tok, gain_one, d_res
     )
     small_grad = jnp.concatenate(
         [
@@ -1038,16 +1277,30 @@
     core = [("expert", n_ex, 1)]
     y_bits = [("expert", n_ex, 1 << i) for i in range(1, n_ex.bit_length() - 1)][::-1]
     dp_bits = [("dp", n_dp, 1 << i) for i in range(n_dp.bit_length() - 1)]
-    next(two), next(two)
-    ends = [next(one), next(two)]
-    grad_gate, grad_up, grad_down = (
-        jnp.concatenate([ends[0][k], ends[1][k]], axis=0) for k in range(3)
-    )
-    grad_down = jnp.swapaxes(grad_down, 1, 2).reshape(local, -1, d)
-
-    if n_dp == 8 and n_ex == 4 and d == 1024:
-        every_grad = run_finish(normed_one_t, dq, dk, dv, d_out_w, small_grad)
+    if fast:
+        keep_a, _, down_keep_a, _ = made_one
+        keep_b, send_b, down_keep_b, down_send_b = made_two
+        every_grad, grad_gate, grad_up, grad_down = run_finish(
+            normed_one_t,
+            dq,
+            dk,
+            dv,
+            d_out_w,
+            small_grad,
+            [keep_a, got_one[0], down_keep_a, got_one[1], keep_b, send_b, down_keep_b, down_send_b],
+        )
     else:
+        ends = [
+            [
+                lax.psum_scatter(g, "dp", scatter_dimension=0, tiled=True)[0].astype(F32)
+                for g in made
+            ]
+            for made in (made_one, made_two)
+        ]
+        grad_gate, grad_up, grad_down = (
+            jnp.concatenate([ends[0][k], ends[1][k]], axis=0) for k in range(3)
+        )
+        grad_down = jnp.swapaxes(grad_down, 1, 2).reshape(local, -1, d)
 
         def product(right):
             return jnp.dot(normed_one_t, right, preferred_element_type=F32).astype(BF16)

time: 730 us -> 650 us (0.89)
  waiting for transfers between devices: 137 us -> 20.2 us
  Pallas kernels: 449 us -> 555 us
  other arithmetic: 43 us -> 19 us
  starting transfers between devices: 34.8 us -> 17.3 us
  local copies, waits for them, and re-layouts: 36.8 us -> 22 us
  between operations: 15.4 us -> 2.14 us
    pallas_call x9 -> x10, Pallas kernels: 353 us -> 459 us  [the longest x6 200 us: run_expert(): pl.pallas_call(functools.partial(expert_kernel, first, local, num_experts...]
    all_gather x1 -> x0, waiting for transfers between devices: 66.9 us -> none  [on_device(): every = lax.all_gather(mine, ('dp', 'expert'), axis=0, tiled=True)]
    ppermute x8 -> x0, waiting for transfers between devices: 49.3 us -> none  [the longest x2 29.5 us: scatter(): lax.ppermute(lax.dynamic_index_in_dim(near, 1 - z % 2, axis=0, keepdims=F...]
    ppermute x8 -> x0, starting transfers between devices: 18.1 us -> none  [the longest x2 10.2 us: scatter(): got = lax.ppermute(far, 'dp', [(0, 2), (1, 3), (6, 4), (7, 5)])]
    convert_element_type x7 -> x0, other arithmetic: 17.6 us -> none  [the longest x2 6.14 us: scatter(): far = (far.astype(F32) + got.astype(F32)).astype(BF16)]
    squeeze x7 -> x0, local copies, waits for them, and re-layouts: 11.7 us -> none  [the longest x5 10.4 us: side(): lax.dynamic_index_in_dim(g.reshape(4, 2, -1, ff_lanes), which, axis=1, ke...]
    ppermute x23 -> x25, waiting for transfers between devices: 21 us -> 20.2 us  [swap(): return lax.ppermute(value, axis, [(i, i ^ step) for i in range(n)])]
    ppermute x23 -> x25, starting transfers between devices: 16.6 us -> 17.3 us  [swap(): return lax.ppermute(value, axis, [(i, i ^ step) for i in range(n)])]
  transfers between devices with their start and end apart: 32 -> 25, of which waited for: 12 -> 7; matrix products, arithmetic and copies ran while one was open for 10% -> 4% of each run, Pallas kernels for 54% -> 47%
where the time goes in v3:
time: 650 us; the launch traced here: 643 us
  Pallas kernels  555 us (85%)
  local copies, waits for them, and re-layouts  22 us (3%)
  waiting for transfers between devices  20.2 us (3%)
  other arithmetic  19 us (3%)
  starting transfers between devices  17.3 us (3%)
  matrix products  7.66 us (1%)
    pallas_call x6, Pallas kernels, run_expert(): pl.pallas_call(functools.partial(expert_kernel, first, local, num_experts...  200 us
    pallas_call x1, Pallas kernels, run_finish(): pl.pallas_call(finish_kernel, in_specs=[vmem] * 6 + [hbm] * 8, out_specs=...  140 us
    pallas_call x2, Pallas kernels, run_weight_grad(): pl.pallas_call(functools.partial(weight_grad_kernel, n, paired), grid=(co...  75.8 us
    pallas_call x1, Pallas kernels, run_gather(): pl.pallas_call(gather_kernel, in_specs=[hbm], out_specs=hbm, out_shape=ja...  43.5 us
    pallas_call x1, Pallas kernels, run_attn_bwd(): pl.pallas_call(attn_bwd_kernel, grid=(groups,), in_specs=[pl.BlockSpec(me...  32.6 us
    pallas_call x1, Pallas kernels, run_attn_fwd(): pl.pallas_call(attn_fwd_kernel, grid=(groups,), in_specs=[pl.BlockSpec(me...  21.5 us
    ppermute x25, waiting for transfers between devices, swap(): return lax.ppermute(value, axis, [(i, i ^ step) for i in range(n)])  20.2 us
    ppermute x25, starting transfers between devices, swap(): return lax.ppermute(value, axis, [(i, i ^ step) for i in range(n)])  17.3 us
  transfers between devices with their start and end apart: 25, of which 7 were waited for; matrix products, arithmetic and copies ran while one was open for 4% of the time, Pallas kernels for 47%

profile of v3, /device:TPU:0, one launch (start us, length us, event | category | flops | bytes accessed | tf_op | source)
XLA Modules:
  0.0 643.0 jit_solution(16610222376295876644)
XLA Ops:
  5.1 43.5 %gather.1.w_ref = bf16[1024,3200]{1,0:T(8,128)(2,1)} custom-call(bf16[32,3200]{1,0:T(8,128)(2,1)} %constant_dynamic-slice_fusion.mine_ref), custom_call_target="tpu_custom_call" | custom-call | flops 20000000000 | bytes 1000 | tf_op jit(solution)/shard_map/gather/pallas_call | solution.py:1045
  52.0 2.0 collective-permute-done.1.route_ref
  57.3 10.1 %qkv.1 = (bf16[1024,1024]{1,0:T(8,128)(2,1)}, bf16[1024,1024]{1,0:T(8,128)(2,1)}, bf16[1024,1024]{1,0:T(8,128)(2,1)}, bf16[1024,1024]{1,0:T(8,128)(2,1)}) custom-call(bf16[1024,1024]{1,0:T(8,128)(2,1)} %bitcast.33, bf16[1,1024]{1,0:T(2,128)(2,1)} %reshape_squeeze.9.gain_ref, bf16[1024,3200]{1,0:T(8,128)(2,1)} %gather.1.w_ref, ...), custom_call_target="tpu_custom_call" | custom-call | flops 4499999744 | bytes 1000 | tf_op jit(solution)/shard_map/qkv/pallas_call | solution.py:101
  67.4 21.5 %attn_fwd.1 = (bf16[1024,1024]{1,0:T(8,128)(2,1)}, f32[4,8,1024]{2,1,0:T(8,128)}, f32[4,8,128]{2,1,0:T(8,128)}) custom-call(s32[1]{0:T(128)S(6)} %copy.48.prefix_ref, bf16[1024,1024]{1,0:T(8,128)(2,1)} %get-tuple-element.179.q_ref, bf16[1024,1024]{1,0:T(8,128)(2,1)} %get-tuple-element.111.kd_ref, bf16[1024,1024]{1,0:T(8,128)(2,1)} %get-tuple-element.112.vd_ref), custom_call_target="tpu_custom_call" | custom-call | flops 10499999744 | bytes 1000 | tf_op jit(solution)/shard_map/attn_fwd/pallas_call | solution.py:176
  88.8 11.9 %collective-permute-done.4.c_ref = bf16[1024,1024]{1,0:T(8,128)(2,1)} collective-permute-done((bf16[1024,1024]{1,0:T(8,128)(2,1)S(1)}, bf16[1024,1024]{1,0:T(8,128)(2,1)}, u32[]{:S(2)}, u32[]{:S(2)}) %collective-permute-start.4) | collective-permute-done | bytes 2097184 | tf_op jit(solution)/shard_map/ppermute | solution.py:1082
  100.7 3.1 slice.43.w_ref.refs_7_
  105.8 7.2 %mid.1 = (f32[1024,1024]{1,0:T(8,128)}, bf16[1024,1024]{1,0:T(8,128)(2,1)}) custom-call(bf16[1024,1024]{1,0:T(8,128)(2,1)} %bitcast.34, bf16[1024,1024]{1,0:T(8,128)(2,1)} %get-tuple-element.117.ctx_ref, bf16[1024,1024]{1,0:T(8,128)(2,1)} %slice.43.w_ref.refs_7_, bf16[1,1024]{1,0:T(2,128)(2,1)} %reshape_squeeze.10.gain_ref.refs_6_), custom_call_target="tpu_custom_call" | custom-call | flops 2000000000 | bytes 1000 | tf_op jit(solution)/shard_map/mid/pallas_call | solution.py:311
  117.7 46.7 %experts.6 = (bf16[1024,1024]{1,0:T(8,128)(2,1)}, bf16[1024,1024]{1,0:T(8,128)(2,1)}, f32[8,1024]{1,0:T(8,128)}, bf16[1024,2048]{1,0:T(8,128)(2,1)}, bf16[1024,2...) custom-call(s32[1]{0:T(128)} %bitcast.6.me_ref.refs_0_, ...), custom_call_target="tpu_custom_call" | custom-call | flops 24000000000 | bytes 1000 | tf_op jit(solution)/shard_map/experts/pallas_call | solution.py:425
  164.8 46.7 %experts.7 = (bf16[1024,1024]{1,0:T(8,128)(2,1)}, bf16[1024,1024]{1,0:T(8,128)(2,1)}, f32[8,1024]{1,0:T(8,128)}, bf16[1024,2048]{1,0:T(8,128)(2,1)}, bf16[1024,2...) custom-call(s32[1]{0:T(128)} %bitcast.6.me_ref.refs_0_, ...), custom_call_target="tpu_custom_call" | custom-call | flops 24000000000 | bytes 1000 | tf_op jit(solution)/shard_map/experts/pallas_call | solution.py:425
  211.5 27.1 %experts.8 = (bf16[1024,1024]{1,0:T(8,128)(2,1)}, bf16[1024,1024]{1,0:T(8,128)(2,1)}, f32[8,1024]{1,0:T(8,128)}, bf16[1024,1024]{1,0:T(8,128)(2,1)}, bf16[1024,1...) custom-call(s32[1]{0:T(128)} %bitcast.6.me_ref.refs_0_, ...), custom_call_target="tpu_custom_call" | custom-call | flops 12000000000 | bytes 1000 | tf_op jit(solution)/shard_map/experts/pallas_call | solution.py:425
  238.7 25.9 %experts.9 = (bf16[1024,1024]{1,0:T(8,128)(2,1)}, bf16[1024,1024]{1,0:T(8,128)(2,1)}, f32[8,1024]{1,0:T(8,128)}, bf16[1024,1024]{1,0:T(8,128)(2,1)}, bf16[1024,1...) custom-call(s32[1]{0:T(128)} %bitcast.6.me_ref.refs_0_, bf16[1024,1024]{1,0:T(8,128)(2,1)} %collective-permute-done.9.x_ref, ...), custom_call_target="tpu_custom_call" | custom-call | flops 12000000000 | bytes 1000 | tf_op jit(solution)/shard_map/experts/pallas_call | solution.py:425
  265.6 27.3 %experts.10 = (bf16[1024,1024]{1,0:T(8,128)(2,1)}, bf16[1024,1024]{1,0:T(8,128)(2,1)}, f32[8,1024]{1,0:T(8,128)}, bf16[1024,1024]{1,0:T(8,128)(2,1)}, bf16[1024,...) custom-call(s32[1]{0:T(128)} %bitcast.6.me_ref.refs_0_, ...), custom_call_target="tpu_custom_call" | custom-call | flops 12000000000 | bytes 1000 | tf_op jit(solution)/shard_map/experts/pallas_call | solution.py:425
  294.0 37.8 %weight_grad.2 = (bf16[4,2,2,128,512]{4,3,2,1,0:T(8,128)(2,1)}, bf16[4,2,2,128,512]{4,3,2,1,0:T(8,128)(2,1)}, bf16[4,2,2,64,512]{4,3,2,1,0:T(8,128)(2,1)}, bf16[4,2,2,64,512]{4,3,2,1,0:T(8,128)(2,1)}) custom-call(s32[1]{0:T(128)} %bitcast.7.dp_ref, bf16[1024,1024]{1,0:T(8,128)(2,1)} %get-tuple-element.168.refs_0_, ...), custom_call_target="tpu_custom_call" | custom-call | flops 18499999744 | bytes 1000 | tf_op jit(solution)/shard_map/weight_grad/pallas_call | solution.py:518
  337.2 4.1 add_convert_fusion.2.refs_0_
  341.3 3.9 add_convert_fusion.1.refs_1_
  345.2 26.1 %experts.11 = (bf16[1024,1024]{1,0:T(8,128)(2,1)}, bf16[1024,1024]{1,0:T(8,128)(2,1)}, f32[8,1024]{1,0:T(8,128)}, bf16[1024,1024]{1,0:T(8,128)(2,1)}, bf16[1024,...) custom-call(s32[1]{0:T(128)} %bitcast.6.me_ref.refs_0_, bf16[1024,1024]{1,0:T(8,128)(2,1)} %copy-done.13, ...), custom_call_target="tpu_custom_call" | custom-call | flops 12000000000 | bytes 1000 | tf_op jit(solution)/shard_map/experts/pallas_call | solution.py:425
  373.3 38.0 %weight_grad.3 = (bf16[4,2,2,128,512]{4,3,2,1,0:T(8,128)(2,1)}, bf16[4,2,2,128,512]{4,3,2,1,0:T(8,128)(2,1)}, bf16[4,2,2,64,512]{4,3,2,1,0:T(8,128)(2,1)}, bf16[4,2,2,64,512]{4,3,2,1,0:T(8,128)(2,1)}) custom-call(s32[1]{0:T(128)} %bitcast.7.dp_ref, bf16[1024,1024]{1,0:T(8,128)(2,1)} %get-tuple-element.168.refs_0_, ...), custom_call_target="tpu_custom_call" | custom-call | flops 18499999744 | bytes 1000 | tf_op jit(solution)/shard_map/weight_grad/pallas_call | solution.py:518
  420.6 12.6 %back_mid.1 = (f32[1024,1024]{1,0:T(8,128)}, bf16[1024,1024]{1,0:T(8,128)(2,1)}, bf16[1024,1024]{1,0:T(8,128)(2,1)}, bf16[1024,128]{1,0:T(8,128)(2,1)}, f32[1,1024]{1,0:T(1,128)}) custom-call(s32[1]{0:T(128)} %bitcast.6.me_ref.refs_0_, f32[1024,1024]{1,0:T(8,128)} %get-tuple-element.180.refs_1_, bf16[1024,1024]{1,0:T(8,128)(2,1)} %bitcast.30, ...), custom_call_target="tpu_custom_call" | custom-call | flops 5500000256 | bytes 1000 | tf_op jit(solution)/shard_map/back_mid/pallas_call | solution.py:575
  435.2 5.9 convolution_convert_fusion.dout_ref
  441.1 32.6 %attn_bwd.1 = (bf16[1024,1024]{1,0:T(8,128)(2,1)}, bf16[1024,512]{1,0:T(8,128)(2,1)}, bf16[1024,512]{1,0:T(8,128)(2,1)}) custom-call(s32[1]{0:T(128)S(6)} %copy.48.prefix_ref, bf16[1024,1024]{1,0:T(8,128)(2,1)} %get-tuple-element.179.q_ref, bf16[1024,1024]{1,0:T(8,128)(2,1)} %get-tuple-element.111.kd_ref, bf16[1024,1024]{1,0:T(8,128)(2,1)} %get-tuple-element.112.vd_ref, ...), custom_call_target="tpu_custom_call" | custom-call | flops 16499999744 | bytes 1000 | tf_op jit(solution)/shard_map/attn_bwd/pallas_call | solution.py:275
  473.8 6.5 %fusion = bf16[1,1024,1024]{2,1,0:T(8,128)(2,1)} fusion(bf16[1024,1024]{1,0:T(8,128)(2,1)} %collective-permute-done.16, bf16[1024,1024]{1,0:T(8,128)(2,1)} %collective-permute-done.7, f32[1024,1024]{1,0:T(8,128)} %get-tuple-element.180.refs_1_, bf16[1024,1024]{1,0:T(8,128)(2,1)S(1)} %copy-done.2), kind=kLoop, calls=%fused_computation.3 | loop fusion | flops 7340032 | bytes 12582912 | tf_op jit(solution)/shard_map/reshape | solution.py:1235
  480.3 11.5 %back_in.1 = (f32[1024,1024]{1,0:T(8,128)}, f32[1,1024]{1,0:T(1,128)}) custom-call(bf16[1024,1024]{1,0:T(8,128)(2,1)} %get-tuple-element.188.dq_ref, bf16[1024,512]{1,0:T(8,128)(2,1)} %get-tuple-element.189.dk_ref, bf16[1024,512]{1,0:T(8,128)(2,1)} %get-tuple-element.190.dv_ref, bf16[1024,3200]{1,0:T(8,128)(2,1)} %gather.1.w_ref, ...), custom_call_target="tpu_custom_call" | custom-call | flops 5000000000 | bytes 1000 | tf_op jit(solution)/shard_map/back_in/pallas_call | solution.py:634
  493.7 140.1 %finish.1 = (f32[128,3200]{1,0:T(8,128)}, f32[4,128,512]{2,1,0:T(8,128)}, f32[4,128,512]{2,1,0:T(8,128)}, f32[4,64,1024]{2,1,0:T(8,128)}) custom-call(bf16[1024,1024]{1,0:T(8,128)(2,1)} %get-tuple-element.193.ht_ref, bf16[1024,1024]{1,0:T(8,128)(2,1)} %get-tuple-element.188.dq_ref, bf16[1024,512]{1,0:T(8,128)(2,1)} %get-tuple-element.189.dk_ref, ...), custom_call_target="tpu_custom_call" | custom-call | flops 30000001024 | bytes 1000 | tf_op jit(solution)/shard_map/finish/pallas_call | solution.py:950
  636.3 2.6 fusion.3
  (144 shorter events, 46.1 us)
Async XLA Ops:
  48.6 3.4 collective-permute-start.2
  50.1 3.9 collective-permute-start.1
  54.0 46.7 %collective-permute-start.4 = (bf16[1024,1024]{1,0:T(8,128)(2,1)S(1)}, bf16[1024,1024]{1,0:T(8,128)(2,1)}, u32[]{:S(2)}, u32[]{:S(2)}) collective-permute-start(bf16[1024,1024]{1,0:T(8,128)(2,1)S(1)} %bitcast.31), channel_id=1, source_target_pairs={{0,2},{1,3},{2,0},{3,1},{4,6},{5,7},{6,4},{7,5},{8,10},{9,11},{10,... | collective-permute-start | bytes 6291464 | tf_op jit(solution)/shard_map/ppermute | solution.py:1082
  88.8 15.6 %collective-permute-start.3 = (bf16[1024,1024]{1,0:T(8,128)(2,1)S(1)}, bf16[1024,1024]{1,0:T(8,128)(2,1)S(1)}, u32[]{:S(2)}, u32[]{:S(2)}) collective-permute-start(bf16[1024,1024]{1,0:T(8,128)(2,1)S(1)} %bitcast.32), channel_id=1, source_target_pairs={{0,1},{1,0},{2,3},{3,2},{4,5},{5,4},{6,7},{7,6},{8,9},{9,8},{10,11... | collective-permute-start | bytes 6291464 | tf_op jit(solution)/shard_map/ppermute | solution.py:1082
  100.7 5.1 collective-permute-start.5
  113.0 4.6 collective-permute-start.6
  115.2 49.1 %collective-permute-start.8 = (bf16[1024,1024]{1,0:T(8,128)(2,1)}, bf16[1024,1024]{1,0:T(8,128)(2,1)S(1)}, u32[]{:S(2)}, u32[]{:S(2)}) collective-permute-start(bf16[1024,1024]{1,0:T(8,128)(2,1)} %get-tuple-element.120.x_ref.refs_4_), channel_id=1, source_target_pairs={{0,2},{1,3},{2,0},{3,1},{4,6},{5,7},{6,4},{7,5},{8,10},{9,11},{10,... | collective-permute-start | bytes 6291464 | tf_op jit(solution)/shard_map/ppermute | solution.py:1082
  164.3 47.2 %collective-permute-start.9 = (bf16[1024,1024]{1,0:T(8,128)(2,1)S(1)}, bf16[1024,1024]{1,0:T(8,128)(2,1)}, u32[]{:S(2)}, u32[]{:S(2)}) collective-permute-start(bf16[1024,1024]{1,0:T(8,128)(2,1)S(1)} %collective-permute-done.8.x_ref), channel_id=1, source_target_pairs={{0,1},{1,0},{2,3},{3,2},{4,5},{5,4},{6,7},{7,6},{8,9},{9,8},{10,11... | collective-permute-start | bytes 6291464 | tf_op jit(solution)/shard_map/ppermute | solution.py:1082
  264.6 72.6 %collective-permute-start.12 = (bf16[1024,1024]{1,0:T(8,128)(2,1)}, bf16[1024,1024]{1,0:T(8,128)(2,1)S(1)}, u32[]{:S(2)}, u32[]{:S(2)}) collective-permute-start(bf16[1024,1024]{1,0:T(8,128)(2,1)} %get-tuple-element.130), channel_id=1, source_target_pairs={{0,1},{1,0},{2,3},{3,2},{4,5},{5,4},{6,7},{7,6},{8,9},{9,8},{10,11... | collective-permute-start | bytes 6291464 | tf_op jit(solution)/shard_map/ppermute | solution.py:1082
  265.1 27.8 %collective-permute-start.10 = (f32[4,8,4]{2,1,0:T(8,128)S(1)}, f32[4,8,4]{2,1,0:T(8,128)S(1)}, u32[]{:S(2)}, u32[]{:S(2)}) collective-permute-start(f32[4,8,4]{2,1,0:T(8,128)S(1)} %bitcast.24), channel_id=1, source_target_pairs={{0,1},{1,0},{2,3},{3,2},{4,5},{5,4},{6,7},{7,6},{8,9},{9,8},{10,11... | collective-permute-start | bytes 1544 | tf_op jit(solution)/shard_map/ppermute | solution.py:1082
  265.2 76.1 %collective-permute-start.13 = (bf16[1024,1024]{1,0:T(8,128)(2,1)}, bf16[1024,1024]{1,0:T(8,128)(2,1)}, u32[]{:S(2)}, u32[]{:S(2)}) collective-permute-start(bf16[1024,1024]{1,0:T(8,128)(2,1)} %get-tuple-element.159), channel_id=1, source_target_pairs={{0,1},{1,0},{2,3},{3,2},{4,5},{5,4},{6,7},{7,6},{8,9},{9,8},{10,11... | collective-permute-start | bytes 6291464 | tf_op jit(solution)/shard_map/ppermute | solution.py:1082
  292.9 38.9 %collective-permute-start.11 = (f32[4,8,4]{2,1,0:T(8,128)S(1)}, f32[4,8,4]{2,1,0:T(8,128)S(1)}, u32[]{:S(2)}, u32[]{:S(2)}) collective-permute-start(f32[4,8,4]{2,1,0:T(8,128)S(1)} %max.21), channel_id=1, source_target_pairs={{0,2},{1,3},{2,0},{3,1},{4,6},{5,7},{6,4},{7,5},{8,10},{9,11},{10,... | collective-permute-start | bytes 1544 | tf_op jit(solution)/shard_map/ppermute | solution.py:1082
  331.8 3.8 collective-permute-start.17
  333.6 85.2 %collective-permute-start.14 = (bf16[1024,1024]{1,0:T(8,128)(2,1)}, bf16[1024,1024]{1,0:T(8,128)(2,1)}, u32[]{:S(2)}, u32[]{:S(2)}) collective-permute-start(bf16[1024,1024]{1,0:T(8,128)(2,1)} %get-tuple-element.163), channel_id=1, source_target_pairs={{0,1},{1,0},{2,3},{3,2},{4,5},{5,4},{6,7},{7,6},{8,9},{9,8},{10,11... | collective-permute-start | bytes 6291464 | tf_op jit(solution)/shard_map/ppermute | solution.py:1082
  333.6 77.8 %collective-permute-start.20 = (bf16[4,2,2,64,512]{4,3,2,1,0:T(8,128)(2,1)}, bf16[4,2,2,64,512]{4,3,2,1,0:T(8,128)(2,1)S(1)}, u32[]{:S(2)}, u32[]{:S(2)}) collective-permute-start(bf16[4,2,2,64,512]{4,3,2,1,0:T(8,128)(2,1)} %get-tuple-element.177), channel_id=1, source_target_pairs={{0,4},{4,0},{8,12},{12,8},{16,20},{20,16},{24,28},{28,24},{1,5},{5... | collective-permute-start | bytes 3145736 | tf_op jit(solution)/shard_map/ppermute | solution.py:1082
  335.6 75.7 %collective-permute-start.19 = (bf16[4,2,2,128,512]{4,3,2,1,0:T(8,128)(2,1)}, bf16[4,2,2,128,512]{4,3,2,1,0:T(8,128)(2,1)}, u32[]{:S(2)}, u32[]{:S(2)}) collective-permute-start(bf16[4,2,2,128,512]{4,3,2,1,0:T(8,128)(2,1)} %get-tuple-element.176), channel_id=1, source_target_pairs={{0,4},{4,0},{8,12},{12,8},{16,20},{20,16},{24,28},{28,24},{1,5},{5... | collective-permute-start | bytes 6291464 | tf_op jit(solution)/shard_map/ppermute | solution.py:1082
  371.3 40.0 %collective-permute-start.18 = (f32[4,8,4]{2,1,0:T(8,128)S(1)}, f32[4,8,4]{2,1,0:T(8,128)S(1)}, u32[]{:S(2)}, u32[]{:S(2)}) collective-permute-start(f32[4,8,4]{2,1,0:T(8,128)S(1)} %max.23), channel_id=1, source_target_pairs={{0,8},{4,12},{8,0},{12,4},{16,24},{20,28},{24,16},{28,20},{1,9},{5... | collective-permute-start | bytes 1544 | tf_op jit(solution)/shard_map/ppermute | solution.py:1082
  372.3 46.7 %collective-permute-start.15 = (bf16[1024,1024]{1,0:T(8,128)(2,1)}, bf16[1024,1024]{1,0:T(8,128)(2,1)}, u32[]{:S(2)}, u32[]{:S(2)}) collective-permute-start(bf16[1024,1024]{1,0:T(8,128)(2,1)} %get-tuple-element.164), channel_id=1, source_target_pairs={{0,2},{1,3},{2,0},{3,1},{4,6},{5,7},{6,4},{7,5},{8,10},{9,11},{10,... | collective-permute-start | bytes 6291464 | tf_op jit(solution)/shard_map/ppermute | solution.py:1082
  411.4 4.7 collective-permute-start.21
  413.2 6.8 %collective-permute-start.22 = (f32[8,1024]{1,0:T(8,128)S(1)}, f32[8,1024]{1,0:T(8,128)S(1)}, u32[]{:S(2)}, u32[]{:S(2)}) collective-permute-start(f32[8,1024]{1,0:T(8,128)S(1)} %copy-done.17), channel_id=1, source_target_pairs={{0,1},{1,0},{2,3},{3,2},{4,5},{5,4},{6,7},{7,6},{8,9},{9,8},{10,11... | collective-permute-start | bytes 98312 | tf_op jit(solution)/shard_map/ppermute | solution.py:1082
  413.3 6.7 %collective-permute-start.24 = (f32[8,1024]{1,0:T(8,128)S(1)}, f32[8,1024]{1,0:T(8,128)S(1)}, u32[]{:S(2)}, u32[]{:S(2)}) collective-permute-start(f32[8,1024]{1,0:T(8,128)S(1)} %copy-done.18), channel_id=1, source_target_pairs={{0,3},{1,2},{2,1},{3,0},{4,7},{5,6},{6,5},{7,4},{8,11},{9,10},{10,... | collective-permute-start | bytes 98312 | tf_op jit(solution)/shard_map/ppermute | solution.py:1082
  416.1 3.9 collective-permute-start.23
  418.7 55.1 %collective-permute-start.7 = (bf16[1024,1024]{1,0:T(8,128)(2,1)}, bf16[1024,1024]{1,0:T(8,128)(2,1)}, u32[]{:S(2)}, u32[]{:S(2)}) collective-permute-start(bf16[1024,1024]{1,0:T(8,128)(2,1)} %get-tuple-element.123), channel_id=1, source_target_pairs={{0,1},{1,0},{2,3},{3,2},{4,5},{5,4},{6,7},{7,6},{8,9},{9,8},{10,11... | collective-permute-start | bytes 6291464 | tf_op jit(solution)/shard_map/ppermute | solution.py:1082
  419.0 54.8 %collective-permute-start.16 = (bf16[1024,1024]{1,0:T(8,128)(2,1)}, bf16[1024,1024]{1,0:T(8,128)(2,1)}, u32[]{:S(2)}, u32[]{:S(2)}) collective-permute-start(bf16[1024,1024]{1,0:T(8,128)(2,1)} %get-tuple-element.165), channel_id=1, source_target_pairs={{0,2},{1,3},{2,0},{3,1},{4,6},{5,7},{6,4},{7,5},{8,10},{9,11},{10,... | collective-permute-start | bytes 6291464 | tf_op jit(solution)/shard_map/ppermute | solution.py:1082
  (27 other events, 553.5 us)

commit v4 on v3

--- a/solution.py
+++ b/solution.py
@@ -193,7 +193,170 @@
     )(prefix, q, kd, vd)
 
 
-def attn_bwd_kernel(
+def add_rows(dst, srcs, step=64):
+    def body(i, carry):
+        at = pl.ds(pl.multiple_of(i * step, step), step)
+        total = srcs[0][at, :].astype(F32)
+        for src in srcs[1:]:
+            total = total + src[at, :].astype(F32)
+        dst[at, :] = total.astype(dst.dtype)
+        return carry
+
+    lax.fori_loop(0, dst.shape[0] // step, body, 0)
+
+
+def greet(peers):
+    barrier = pltpu.get_barrier_semaphore()
+    for peer in peers:
+        pl.semaphore_signal(barrier, inc=1, device_id=peer, device_id_type=pl.DeviceIdType.MESH)
+    pl.semaphore_wait(barrier, len(peers))
+
+
+class Line:
+    def __init__(self, tot, rz1, rz2, rz3, sem_s, sem_r):
+        self.tot, self.rz1, self.rz2, self.rz3 = tot, rz1, rz2, rz3
+        self.sem_s, self.sem_r = sem_s, sem_r
+        dp, ex = lax.axis_index("dp"), lax.axis_index("expert")
+        self.z = dp // 2
+        self.upper = self.z // 2
+        self.outer = (self.z == 0) | (self.z == 3)
+        self.inner = jnp.logical_not(self.outer)
+        self.near, self.middle = (dp ^ 2, ex), (dp ^ 6, ex)
+
+    def copy(self, ch, stage):
+        if stage == 3:
+            src, dst = self.tot.at[ch, 2 * self.upper + 1 - self.z % 2], self.rz3.at[ch]
+        else:
+            src = self.tot.at[ch, pl.ds(2 * (1 - self.upper), 2)]
+            dst = (self.rz1 if stage == 1 else self.rz2).at[ch]
+        return pltpu.make_async_remote_copy(
+            src_ref=src,
+            dst_ref=dst,
+            send_sem=self.sem_s.at[ch, stage],
+            recv_sem=self.sem_r.at[ch, stage],
+            device_id=self.middle if stage == 2 else self.near,
+            device_id_type=pl.DeviceIdType.MESH,
+        )
+
+    def add(self, ch, first, other):
+        for p in range(2):
+            for e in range(2):
+                dst = self.tot.at[ch, first + p, e]
+                add_rows(dst, [dst, other.at[ch, p, e]])
+
+    def ends(self, ch, inward):
+        @pl.when(self.outer)
+        def _():
+            if inward:
+                self.copy(ch, 1).start()
+            self.copy(ch, 3).start()
+
+    def middle_sends(self, ch, inward):
+        @pl.when(self.inner)
+        def _():
+            if inward:
+                self.copy(ch, 1).wait_recv()
+            self.add(ch, 2 * (1 - self.upper), self.rz1)
+            self.copy(ch, 2).start()
+
+    def middle_adds(self, ch, inward):
+        @pl.when(self.inner)
+        def _():
+            self.copy(ch, 2).wait()
+            self.add(ch, 2 * self.upper, self.rz2)
+            self.copy(ch, 3).start()
+
+        if inward:
+
+            @pl.when(self.outer)
+            def _():
+                self.copy(ch, 1).wait_send()
+
+    def result(self, ch, refs):
+        self.copy(ch, 3).wait()
+        for e in range(2):
+            own, got = self.tot.at[ch, self.z, e], self.rz3.at[ch, e]
+            if ch < 2:
+                add_rows(refs[ch].at[e], [own, got])
+            else:
+                rows, lanes = refs[2].shape[1], own.shape[1]
+                for h in range(2):
+                    at = slice(h * rows, (h + 1) * rows)
+                    dst = refs[2].at[e, :, h * lanes : (h + 1) * lanes]
+                    add_rows(dst, [own.at[at], got.at[at]])
+
+
+def line_scratch(shape):
+    return [
+        pltpu.VMEM((3,) + shape, BF16),
+        pltpu.VMEM((3, 2) + shape[1:], BF16),
+        pltpu.VMEM((3, 2) + shape[1:], BF16),
+        pltpu.VMEM((3,) + shape[1:], BF16),
+        pltpu.SemaphoreType.DMA((3, 4)),
+        pltpu.SemaphoreType.DMA((3, 4)),
+    ]
+
+
+def attn_bwd_kernel(*refs):
+    attn_bwd_body(*refs)
+
+
+def attn_bwd_sum_kernel(*refs):
+    ins, (tot_a, far_a, keep_a, got_a) = refs[:11], refs[11:15]
+    outs, (gate_ref, up_ref, down_ref) = refs[15:18], refs[18:21]
+    scratch, line_refs, (rx, sem_l) = refs[21:24], refs[24:30], refs[30:]
+    step = pl.program_id(0)
+    line = Line(*line_refs)
+    loads = []
+    for k in range(2):
+        loads.append([pltpu.make_async_copy(tot_a.at[:, k], line.tot.at[k], sem_l.at[2 * k])])
+        loads[-1].append(
+            pltpu.make_async_copy(far_a.at[:, k], line.rz1.at[k], sem_l.at[2 * k + 1])
+        )
+    loads.append(
+        [
+            pltpu.make_async_copy(keep_a, line.tot.at[2], sem_l.at[4]),
+            pltpu.make_async_copy(got_a, rx, sem_l.at[5]),
+        ]
+    )
+    @pl.when(step == 0)
+    def _():
+        for group in loads:
+            for copy in group:
+                copy.start()
+        greet([line.near, line.middle])
+        for copy in loads[2]:
+            copy.wait()
+        for zz in range(4):
+            for e in range(2):
+                dst = line.tot.at[2, zz, e]
+                add_rows(dst, [dst, rx.at[zz, e]])
+        line.ends(2, True)
+        for k in range(2):
+            for copy in loads[k]:
+                copy.wait()
+            line.ends(k, False)
+            line.middle_sends(k, False)
+
+    attn_bwd_body(*ins, *outs, *scratch)
+
+    @pl.when(step == 1)
+    def _():
+        line.middle_sends(2, True)
+        line.middle_adds(0, False)
+
+    @pl.when(step == 2)
+    def _():
+        line.middle_adds(1, False)
+
+    @pl.when(step == 3)
+    def _():
+        line.middle_adds(2, True)
+        for ch in range(3):
+            line.result(ch, (gate_ref, up_ref, down_ref))
+
+
+def attn_bwd_body(
     prefix_ref, q_ref, kd_ref, vd_ref, do_ref, ctx_ref, lse_ref, cos_ref, sin_ref, cost_ref, sint_ref,
     dq_ref, dk_ref, dv_ref, dk_acc, dv_acc, kt_ref,
 ):
@@ -267,34 +430,55 @@
     dv_ref[...] = sums[1].astype(BF16)
 
 
-def run_attn_bwd(prefix, q, kd, vd, d_ctx, ctx, lse, cos, sin, cos_t, sin_t):
+def run_attn_bwd(prefix, q, kd, vd, d_ctx, ctx, lse, cos, sin, cos_t, sin_t, sums=None):
     length, nq = q.shape
     groups = nq // 256
     col = lambda g: (0, g)
     wide = spec((length, 256), col)
+    in_specs = [pl.BlockSpec(memory_space=pltpu.SMEM)] + [wide] * 5
+    in_specs += [spec((1, 8, length), lambda g: (g, 0, 0))]
+    in_specs += [whole((length, 128))] * 2 + [whole((cos_t.shape[0], length))] * 2
+    out_specs = [wide, spec((length, 128), col), spec((length, 128), col)]
+    out_shape = [
+        jax.ShapeDtypeStruct((length, nq), BF16),
+        jax.ShapeDtypeStruct((length, nq // 2), BF16),
+        jax.ShapeDtypeStruct((length, nq // 2), BF16),
+    ]
+    scratch = [
+        pltpu.VMEM((2, length, 128), F32),
+        pltpu.VMEM((2, length, 128), F32),
+        pltpu.VMEM((2, 128, length), BF16),
+    ]
+    args = (prefix, q, kd, vd, d_ctx, ctx, lse, cos, sin, cos_t, sin_t)
+    kernel, extra = attn_bwd_kernel, {}
+    if sums is not None:
+        kernel, extra = attn_bwd_sum_kernel, {"collective_id": 3, "has_side_effects": True}
+        hbm = pl.BlockSpec(memory_space=pl.ANY)
+        keep_a = sums[2]
+        _, count, rows, lanes = keep_a.shape
+        made = [(count, rows, lanes)] * 2 + [(count, rows // 2, 2 * lanes)]
+        in_specs += [hbm] * 4
+        out_specs += [whole(shape) for shape in made]
+        out_shape += [jax.ShapeDtypeStruct(shape, F32) for shape in made]
+        scratch += line_scratch(keep_a.shape)
+        scratch += [
+            pltpu.VMEM(keep_a.shape, BF16),
+            pltpu.SemaphoreType.DMA((6,)),
+        ]
+        args += tuple(sums)
     return pl.pallas_call(
-        attn_bwd_kernel,
+        kernel,
         grid=(groups,),
-        in_specs=[pl.BlockSpec(memory_space=pltpu.SMEM)]
-        + [wide] * 5
-        + [spec((1, 8, length), lambda g: (g, 0, 0))]
-        + [whole((length, 128))] * 2
-        + [whole((cos_t.shape[0], length))] * 2,
-        out_specs=[wide, spec((length, 128), col), spec((length, 128), col)],
-        out_shape=[
-            jax.ShapeDtypeStruct((length, nq), BF16),
-            jax.ShapeDtypeStruct((length, nq // 2), BF16),
-            jax.ShapeDtypeStruct((length, nq // 2), BF16),
-        ],
-        scratch_shapes=[
-            pltpu.VMEM((2, length, 128), F32),
-            pltpu.VMEM((2, length, 128), F32),
-            pltpu.VMEM((2, 128, length), BF16),
-        ],
-        compiler_params=params(60),
+        in_specs=in_specs,
+        out_specs=out_specs,
+        out_shape=out_shape,
+        scratch_shapes=scratch,
+        compiler_params=pltpu.CompilerParams(
+            dimension_semantics=("arbitrary",), vmem_limit_bytes=60 * MIB, **extra
+        ),
         cost_estimate=took(33),
         name="attn_bwd",
-    )(prefix, q, kd, vd, d_ctx, ctx, lse, cos, sin, cos_t, sin_t)
+    )(*args)
 
 
 def mid_kernel(tok_ref, ctx_ref, w_ref, gain_ref, res_ref, x_ref):
@@ -304,7 +488,7 @@
     x_ref[...] = (res * r * gain_ref[...].astype(F32)).astype(BF16)
 
 
-def run_mid(tok, ctx, w_out, gain):
+def run_mid(tok, ctx, w_all, gain, at):
     length, d = tok.shape
     b = 256
     row = lambda i: (i, 0)
@@ -314,7 +498,7 @@
         in_specs=[
             spec((b, d), row),
             spec((b, ctx.shape[1]), row),
-            whole(w_out.shape),
+            spec((w_all.shape[0], d), lambda i: (0, at)),
             whole((1, d)),
         ],
         out_specs=[spec((b, d), row)] * 2,
@@ -325,7 +509,7 @@
         compiler_params=params(60),
         cost_estimate=took(4),
         name="mid",
-    )(tok, ctx, w_out, gain)
+    )(tok, ctx, w_all, gain)
 
 
 def gates_of(x, router, routes_t, num_experts):
@@ -374,9 +558,9 @@
         axis=1,
         keepdims=True,
     )
-    gate = dot(x, wg_ref[e])
-    up = dot(x, wu_ref[e])
-    grad = dot_t(c, wd_ref[e])
+    gate = dot(x, wg_ref[0])
+    up = dot(x, wu_ref[0])
+    grad = dot_t(c, wd_ref[0])
     sig = 0.5 * jnp.tanh(0.5 * gate) + 0.5
     act = gate * sig
     hidden = (act * up).astype(BF16).astype(F32)
@@ -388,8 +572,8 @@
     hs_ref[...] = hs
     dup_ref[...] = dup
     dgate_ref[...] = dgate
-    out = dot(hs, wd_ref[e])
-    dx = dot_t(dgate, wg_ref[e]) + dot_t(dup, wu_ref[e])
+    out = dot(hs, wd_ref[0])
+    dx = dot_t(dgate, wg_ref[0]) + dot_t(dup, wu_ref[0])
     dgc_ref[...] += jnp.where(lane == first_expert + e, dg, 0.0)
 
     @pl.when(e < last)
@@ -412,11 +596,7 @@
     top = routes_t.shape[0]
     row = lambda i, e: (i, 0)
     col_t = lambda i, e: (0, i)
-    pick = lambda shape: pl.BlockSpec(
-        (count,) + shape[1:],
-        lambda i, e: (first // count, 0, 0),
-        pipeline_mode=pl.Buffered(1),
-    )
+    pick = lambda shape: pl.BlockSpec((1,) + shape[1:], lambda i, e: (first + e, 0, 0))
     wide = jax.ShapeDtypeStruct((length, count * ff), BF16)
     full = jax.ShapeDtypeStruct((length, d), BF16)
     turned = jax.ShapeDtypeStruct((d, length), BF16)
@@ -430,7 +610,11 @@
             spec((b, d), row),
             spec((b, d), row),
             spec((top, b), col_t),
-            pl.BlockSpec(router.shape, lambda i, e: (0, 0), pipeline_mode=pl.Buffered(1)),
+            pl.BlockSpec(
+                (d, 128),
+                lambda i, e: (0, router.shape[1] // 128 - 1),
+                pipeline_mode=pl.Buffered(1),
+            ),
             pick(wg.shape),
             pick(wu.shape),
             pick(wd.shape),
@@ -470,16 +654,18 @@
     if paired:
         keep_ref, send_ref, down_keep_ref, down_send_ref = refs[5 * n :]
         first = dp_ref[0] % 2 == 0
-        half = gate.shape[0] // 2
-        for k, value in enumerate((gate, up)):
-            keep_ref[0, k, 0] = jnp.where(first, value[:half], value[half:])
-            send_ref[0, k, 0] = jnp.where(first, value[half:], value[:half])
-        rows = down_keep_ref.shape[3]
+
+        def parts(value, z, rows):
+            even = value[2 * z * rows : (2 * z + 1) * rows]
+            odd = value[(2 * z + 1) * rows : (2 * z + 2) * rows]
+            return jnp.where(first, even, odd), jnp.where(first, odd, even)
+
+        for z in range(keep_ref.shape[0]):
+            for k, value in enumerate((gate, up)):
+                keep_ref[z, k, 0], send_ref[z, k, 0] = parts(value, z, keep_ref.shape[3])
         for z in range(down_keep_ref.shape[0]):
-            even = down[2 * z * rows : (2 * z + 1) * rows]
-            odd = down[(2 * z + 1) * rows : (2 * z + 2) * rows]
-            down_keep_ref[z, 0, 0] = jnp.where(first, even, odd)
-            down_send_ref[z, 0, 0] = jnp.where(first, odd, even)
+            rows = down_keep_ref.shape[2]
+            down_keep_ref[z, 0], down_send_ref[z, 0] = parts(down, z, rows)
         return
     gate_ref, up_ref, down_ref = refs[5 * n :]
     for p in range(down_ref.shape[0]):
@@ -495,7 +681,7 @@
     n = len(xt)
     d, length = xt[0].shape
     ff = hs[-1].shape[1] // count
-    m = 256
+    m = 512 if paired else 256
     left = spec((m, length), lambda e, i: (i, 0))
     rights = [
         spec((length, ff), functools.partial(lambda skip, e, i: (0, e + skip), skip))
@@ -504,10 +690,10 @@
     per = d // n_dp
     down_at = lambda e, i: (0, e, i // (ff // m), 0, i % (ff // m))
     if paired:
-        row_spec = spec((1, 2, 1, per, ff), lambda e, i: (i, 0, e, 0, 0))
+        row_spec = spec((m // (2 * per), 2, 1, per, ff), lambda e, i: (i, 0, e, 0, 0))
         rows = jax.ShapeDtypeStruct((n_dp // 2, 2, count, per, ff), BF16)
-        down_spec = spec((n_dp // 2, 1, 1, ff // n_dp, m), down_at)
-        down = jax.ShapeDtypeStruct((n_dp // 2, count, d // ff, ff // n_dp, ff), BF16)
+        down_spec = spec((n_dp // 2, 1, ff // n_dp, m), lambda e, i: (0, e, i, 0))
+        down = jax.ShapeDtypeStruct((n_dp // 2, count, ff // n_dp * (d // ff), ff), BF16)
         out_specs, out_shape = [row_spec] * 2 + [down_spec] * 2, [rows] * 2 + [down] * 2
     else:
         row_spec = spec((m // per, 1, per, ff), lambda e, i: (i, e, 0, 0))
@@ -567,7 +753,7 @@
     dctx_ref[...] = dot_t(d_attn, w_ref[...]).astype(BF16)
 
 
-def run_back_mid(me, res, cot, routes_t, x, router, gain, w_out, dxs, dgs, local):
+def run_back_mid(me, res, cot, routes_t, x, w_all, gain, at, dxs, dgs, local):
     length, d = res.shape
     b = 256
     row = lambda i: (i, 0)
@@ -581,30 +767,30 @@
             spec((b, d), row),
             spec((routes_t.shape[0], b), lambda i: (0, i)),
             spec((b, d), row),
-            whole(router.shape),
+            spec((d, 128), lambda i: (0, w_all.shape[1] // 128 - 1)),
             whole((1, d)),
-            whole(w_out.shape),
+            spec((d, d), lambda i: (0, at)),
         ]
         + [spec((b, d), row)] * n
         + [spec((8, b), lambda i: (0, i))] * n_ex,
         out_specs=[
             spec((b, d), row),
             spec((b, d), row),
-            spec((b, w_out.shape[0]), row),
+            spec((b, d), row),
             spec((b, 128), row),
             whole((1, d)),
         ],
         out_shape=[
             jax.ShapeDtypeStruct((length, d), F32),
             jax.ShapeDtypeStruct((length, d), BF16),
-            jax.ShapeDtypeStruct((length, w_out.shape[0]), BF16),
+            jax.ShapeDtypeStruct((length, d), BF16),
             jax.ShapeDtypeStruct((length, 128), BF16),
             jax.ShapeDtypeStruct((1, d), F32),
         ],
         compiler_params=params(60),
         cost_estimate=took(11),
         name="back_mid",
-    )(me, res, cot, routes_t, x, router, gain, w_out, *dxs, *dgs)
+    )(me, res, cot, routes_t, x, w_all, gain, w_all, *dxs, *dgs)
 
 
 def back_in_kernel(dq_ref, dk_ref, dv_ref, w_ref, tok_ref, gain_ref, dres_ref, gt_ref, ggain_ref):
@@ -654,174 +840,58 @@
 CHUNKS = (3, 0, 1, 2)
 
 
-def add_rows(dst, srcs, step=64):
-    def body(i, carry):
-        at = pl.ds(pl.multiple_of(i * step, step), step)
-        total = srcs[0][at, :].astype(F32)
-        for src in srcs[1:]:
-            total = total + src[at, :].astype(F32)
-        dst[at, :] = total.astype(dst.dtype)
-        return carry
-
-    lax.fori_loop(0, dst.shape[0] // step, body, 0)
-
-
 def finish_kernel(
-    ht_ref, dq_ref, dk_ref, dv_ref, dout_ref, small_ref,
-    keep_a, got_a, down_keep_a, down_got_a, keep_b, send_b, down_keep_b, down_send_b,
+    ht_ref, dq_ref, dk_ref, dv_ref, dout_ref, small_ref, keep_ref, got_ref, down_keep_ref, down_got_ref,
     out_ref, gate_ref, up_ref, down_ref, *scratch,
 ):
     n = len(CHUNKS)
     lists = [scratch[k * n : (k + 1) * n] for k in range(8)]
     b1, r1, s1, r2, s2, r3, s3, r4 = lists
-    tot, rx, rx_down, rz1, rz2, rz3, sem_s, sem_r, sem_es, sem_er, sem_l = scratch[8 * n :]
+    sem_s, sem_r = scratch[8 * n : 8 * n + 2]
+    line = Line(*scratch[8 * n + 2 : 8 * n + 8])
+    rx, sem_l = scratch[8 * n + 8 :]
     dp, ex = lax.axis_index("dp"), lax.axis_index("expert")
     z, x, y, c = dp // 2, dp % 2, ex // 2, ex % 2
     over_core, over_y, over_x = (dp, ex ^ 1), (dp, ex ^ 2), (dp ^ 1, ex)
-    line = [(dp ^ (2 * k), ex) for k in (1, 2, 3)]
+    along = [(dp ^ (2 * k), ex) for k in (1, 2, 3)]
     group = [over_core, over_y, (dp, ex ^ 3)]
-    barrier = pltpu.get_barrier_semaphore()
-    peers = group + [over_x] + line
-    for peer in peers:
-        pl.semaphore_signal(barrier, inc=1, device_id=peer, device_id_type=pl.DeviceIdType.MESH)
-    pl.semaphore_wait(barrier, len(peers))
+    loads = []
+    for k in range(3):
+        keep, got = (down_keep_ref, down_got_ref) if k == 2 else (keep_ref.at[:, k], got_ref.at[:, k])
+        loads.append(
+            [
+                pltpu.make_async_copy(keep, line.tot.at[k], sem_l.at[2 * k]),
+                pltpu.make_async_copy(got, rx.at[k], sem_l.at[2 * k + 1]),
+            ]
+        )
+        for copy in loads[k]:
+            copy.start()
+    greet(group + [over_x] + along)
 
     widths = [dout_ref.shape[1], dq_ref.shape[1], dk_ref.shape[1] + dv_ref.shape[1], 128]
     starts = [sum(widths[:k]) for k in range(n)]
     started = {}
 
-    def remote(key, src, dst, send_sem, recv_sem, peer):
+    def send(k, slot, src, dst, peer):
         copy = pltpu.make_async_remote_copy(
             src_ref=src,
             dst_ref=dst,
-            send_sem=send_sem,
-            recv_sem=recv_sem,
+            send_sem=sem_s.at[k, slot],
+            recv_sem=sem_r.at[k, slot],
             device_id=peer,
             device_id_type=pl.DeviceIdType.MESH,
         )
-        started[key] = copy
-        return copy
-
-    def send(k, slot, src, dst, peer):
-        remote((k, slot), src, dst, sem_s.at[k, slot], sem_r.at[k, slot], peer).start()
-
-    def kind_of(which, keep_like, down_like):
-        return down_like if which == 2 else keep_like.at[:, which]
-
-    def rx_of(ch):
-        return rx_down.at[ch // 3] if ch % 3 == 2 else rx.at[ch // 3, :, ch % 3]
-
-    for ch in range(3, 6):
-        src = kind_of(ch - 3, send_b, down_send_b)
-        remote(("x", ch), src, rx_of(ch), sem_es.at[ch, 0], sem_er.at[ch, 0], over_x).start()
-    loads = {}
-    for ch in range(3):
-        copy = pltpu.make_async_copy(
-            kind_of(ch, got_a, down_got_a), rx_of(ch), sem_l.at[ch]
-        )
         copy.start()
-        loads[ch] = [copy]
-    for ch in range(6):
-        keep, down_keep = (keep_a, down_keep_a) if ch < 3 else (keep_b, down_keep_b)
+        started[k, slot] = copy
+
+    def begin(k):
+        for copy in loads[k]:
+            copy.wait()
         for zz in range(4):
             for e in range(2):
-                if ch % 3 < 2:
-                    copy = pltpu.make_async_copy(
-                        keep.at[zz, ch % 3, e],
-                        tot.at[ch, zz, e * 128 : (e + 1) * 128],
-                        sem_l.at[6 + (ch * 4 + zz) * 4 + e * 2],
-                    )
-                    copy.start()
-                    loads.setdefault(ch, []).append(copy)
-                    continue
-                for h in range(2):
-                    at = e * 128 + h * 64
-                    copy = pltpu.make_async_copy(
-                        down_keep.at[zz, e, h],
-                        tot.at[ch, zz, at : at + 64],
-                        sem_l.at[6 + (ch * 4 + zz) * 4 + e * 2 + h],
-                    )
-                    copy.start()
-                    loads.setdefault(ch, []).append(copy)
-
-    upper = z // 2
-    outer = (z == 0) | (z == 3)
-    inner = jnp.logical_not(outer)
-
-    def z_copy(ch, stage):
-        if stage == 1:
-            src, dst = tot.at[ch, pl.ds(2 * (1 - upper), 2)], rz1.at[ch]
-            peer = (dp ^ 2, ex)
-        elif stage == 2:
-            src, dst = tot.at[ch, pl.ds(2 * (1 - upper), 2)], rz2.at[ch]
-            peer = (dp ^ 6, ex)
-        else:
-            src, dst = tot.at[ch, 2 * upper + 1 - z % 2], rz3.at[ch]
-            peer = (dp ^ 2, ex)
-        key = ("z", ch, stage)
-        if key in started:
-            return started[key]
-        return remote(key, src, dst, sem_es.at[ch, stage], sem_er.at[ch, stage], peer)
-
-    def exp_x(ch):
-        for copy in loads[ch]:
-            copy.wait()
-        if ch >= 3:
-            started["x", ch].wait()
-        for zz in range(4):
-            for e in range(2):
-                if ch % 3 < 2:
-                    dst = tot.at[ch, zz, e * 128 : (e + 1) * 128]
-                    add_rows(dst, [dst, rx.at[ch // 3, zz, ch % 3, e]])
-                else:
-                    for h in range(2):
-                        at = e * 128 + h * 64
-                        dst = tot.at[ch, zz, at : at + 64]
-                        add_rows(dst, [dst, rx_down.at[ch // 3, zz, e, h]])
-        one, three = z_copy(ch, 1), z_copy(ch, 3)
-
-        @pl.when(outer)
-        def _():
-            one.start()
-            three.start()
-
-    def exp_1(ch):
-        two = z_copy(ch, 2)
-
-        @pl.when(inner)
-        def _():
-            z_copy(ch, 1).wait_recv()
-            for p in range(2):
-                dst = tot.at[ch, 2 * (1 - upper) + p]
-                add_rows(dst, [dst, rz1.at[ch, p]])
-            two.start()
-
-    def exp_2(ch):
-        @pl.when(inner)
-        def _():
-            z_copy(ch, 2).wait()
-            for p in range(2):
-                dst = tot.at[ch, 2 * upper + p]
-                add_rows(dst, [dst, rz2.at[ch, p]])
-            z_copy(ch, 3).start()
-
-        @pl.when(outer)
-        def _():
-            z_copy(ch, 1).wait_send()
-
-    def exp_3(ch):
-        z_copy(ch, 3).wait()
-        for e in range(2):
-            at = 2 * (ch // 3) + e
-            if ch % 3 < 2:
-                rows = slice(e * 128, (e + 1) * 128)
-                dst = (gate_ref, up_ref)[ch % 3].at[at]
-                add_rows(dst, [tot.at[ch, z, rows], rz3.at[ch, rows]])
-            else:
-                for h in range(2):
-                    rows = slice(e * 128 + h * 64, e * 128 + (h + 1) * 64)
-                    dst = down_ref.at[at, :, h * 512 : (h + 1) * 512]
-                    add_rows(dst, [tot.at[ch, z, rows], rz3.at[ch, rows]])
+                dst = line.tot.at[k, zz, e]
+                add_rows(dst, [dst, rx.at[k, zz, e]])
+        line.ends(k, True)
 
     def place(k, lanes, value):
         for p in range(8):
@@ -868,7 +938,7 @@
         for zz in range(4):
             s3[k][zz] = (s2[k][x, zz].astype(F32) + r3[k][0, zz].astype(F32)).astype(BF16)
         for i in range(3):
-            send(k, 3 + i, s3[k].at[z ^ (i + 1)], r3[k].at[1, i], line[i])
+            send(k, 3 + i, s3[k].at[z ^ (i + 1)], r3[k].at[1, i], along[i])
 
     def step4(k):
         for i in range(3):
@@ -888,78 +958,71 @@
             rows = pl.ds(pl.multiple_of((ex ^ (i + 1)) * 32, 32), 32)
             out_ref[rows, o] = r4[k][i].astype(F32)
 
-    def dense(step, chunks=CHUNKS):
-        for k in chunks:
-            step(k)
-
-    dense(step0, CHUNKS[:2])
-    for ch in range(3):
-        exp_x(ch)
-    dense(step0, CHUNKS[2:])
-    dense(step1)
-    for ch in range(3):
-        exp_1(ch)
-    exp_x(3)
-    dense(step2)
-    for ch in range(3):
-        exp_2(ch)
-    exp_1(3)
-    exp_x(4)
-    dense(step3)
-    for ch in range(3):
-        exp_3(ch)
-    exp_1(4)
-    exp_2(3)
-    exp_x(5)
-    dense(step4)
-    exp_3(3)
-    exp_1(5)
-    exp_2(4)
-    dense(step5)
-    exp_3(4)
-    exp_2(5)
-    exp_3(5)
+    done = (gate_ref, up_ref, down_ref)
+    step0(3)
+    step0(0)
+    begin(0)
+    step1(3)
+    step1(0)
+    step0(1)
+    begin(1)
+    step1(1)
+    step0(2)
+    begin(2)
+    step1(2)
+    step2(3)
+    step2(0)
+    line.middle_sends(0, True)
+    step2(1)
+    step3(3)
+    step3(0)
+    line.middle_sends(1, True)
+    line.middle_adds(0, True)
+    step2(2)
+    step3(1)
+    line.middle_sends(2, True)
+    line.middle_adds(1, True)
+    step4(3)
+    step4(0)
+    step3(2)
+    line.result(0, done)
+    line.middle_adds(2, True)
+    step4(1)
+    step5(3)
+    step5(0)
+    step4(2)
+    line.result(1, done)
+    line.result(2, done)
+    step5(1)
+    step5(2)
 
 
 def run_finish(ht, dq, dk, dv, d_out, small, experts):
-    d = ht.shape[0]
     widths = [d_out.shape[1], dq.shape[1], dk.shape[1] + dv.shape[1], small.shape[1]]
-    keep_a, _, down_keep_a, _ = experts[0], None, experts[2], None
-    _, kinds, count, per, ff = keep_a.shape
-    down_rows = down_keep_a.shape[3]
+    chunk = experts[2].shape
+    _, count, rows, lanes = chunk
     vmem = pl.BlockSpec(memory_space=pltpu.VMEM)
     hbm = pl.BlockSpec(memory_space=pl.ANY)
     shapes = [
         (2, 2, 2, 4, 32), (2, 2, 4, 32), (2, 2, 4, 32), (2, 4, 32), (2, 4, 32), (2, 4, 32), (4, 32), (4, 32),
     ]
     scratch = [pltpu.VMEM(shape + (w,), BF16) for shape in shapes for w in widths]
-    rows = count * per
-    scratch += [
-        pltpu.VMEM((6, 4, rows, ff), BF16),
-        pltpu.VMEM((2, 4, 2, count, per, ff), BF16),
-        pltpu.VMEM((2,) + down_keep_a.shape, BF16),
-        pltpu.VMEM((6, 2, rows, ff), BF16),
-        pltpu.VMEM((6, 2, rows, ff), BF16),
-        pltpu.VMEM((6, rows, ff), BF16),
-        pltpu.SemaphoreType.DMA((len(widths), 9)),
-        pltpu.SemaphoreType.DMA((len(widths), 9)),
-        pltpu.SemaphoreType.DMA((6, 4)),
-        pltpu.SemaphoreType.DMA((6, 4)),
-        pltpu.SemaphoreType.DMA((6 + 96,)),
-    ]
+    scratch += [pltpu.SemaphoreType.DMA((len(widths), 9))] * 2
+    scratch += line_scratch(chunk)
+    scratch += [pltpu.VMEM((3,) + chunk, BF16), pltpu.SemaphoreType.DMA((6,))]
     return pl.pallas_call(
         finish_kernel,
-        in_specs=[vmem] * 6 + [hbm] * 8,
+        in_specs=[vmem] * 6 + [hbm] * 4,
         out_specs=[vmem] * 4,
         out_shape=[
             jax.ShapeDtypeStruct((128, sum(widths)), F32),
-            jax.ShapeDtypeStruct((2 * count, per, ff), F32),
-            jax.ShapeDtypeStruct((2 * count, per, ff), F32),
-            jax.ShapeDtypeStruct((2 * count, down_rows, d), F32),
+            jax.ShapeDtypeStruct((count, rows, lanes), F32),
+            jax.ShapeDtypeStruct((count, rows, lanes), F32),
+            jax.ShapeDtypeStruct((count, rows // 2, 2 * lanes), F32),
         ],
         scratch_shapes=scratch,
         compiler_params=pltpu.CompilerParams(
-            vmem_limit_bytes=62 * MIB, collective_id=1, has_side_effects=True
+            vmem_limit_bytes=60 * MIB, collective_id=1, has_side_effects=True
         ),
         cost_estimate=took(60),
         name="finish",
@@ -1101,10 +1164,7 @@
         every = lax.all_gather(mine, ("dp", "expert"), axis=0, tiled=True)
     w_all = every
     width = 2 * nq
-    full_out = every[:, width : width + d]
     extra = every[:, width + d :]
-    lanes = lax.broadcasted_iota(jnp.int32, extra.shape, 1)
-    router = jnp.where(lanes < num_experts, extra, jnp.zeros((), BF16))
     gain_one = extra[:, num_experts].reshape(1, d)
     gain_two = extra[:, num_experts + 1].reshape(1, d)
 
@@ -1126,17 +1186,13 @@
 
     normed_one_t, q, kd, vd = run_qkv(tok, gain_one, w_all, cos_l, sin_l, nq)
     ctx, lse, peaks = run_attn_fwd(prefix, q, kd, vd)
-    for step in range(3, n_ex, 2):
-        cots[step] = swap(after(cots[step - 1], ctx), 1)
-    resid, normed_two = run_mid(tok, after(ctx, *cots.values()), full_out, gain_two)
+    resid, normed_two = run_mid(tok, ctx, w_all, gain_two, width // d)
 
     me = ex.reshape(1).astype(jnp.int32)
     xs = {0: normed_two}
     for step in range(1, n_ex):
         if step == 1 or step % 2 == 0:
             xs[step] = swap(normed_two, step)
-        else:
-            xs[step] = swap(xs[step - 1], 1)
     tops = [peaks[:, :, :4]]
     bits = [("expert", n_ex, 1 << i) for i in range(n_ex.bit_length() - 1)]
     bits += [("dp", n_dp, 1 << i) for i in range(n_dp.bit_length() - 1)]
@@ -1153,12 +1209,12 @@
     dp = lax.axis_index("dp").reshape(1).astype(jnp.int32)
 
     res = {}
-    chain = xs[1]
+    chain = (normed_two, [cots[step] for step in range(2, n_ex, 2)])
 
     def experts(step, first, count, init=None):
         x = after(xs[step], chain)
         return run_expert(
-            me, x, cots[step], route_set[step], router, *weights, first, count, num_experts, init
+            me, x, cots[step], route_set[step], w_all, *weights, first, count, num_experts, init
         )
 
     def grads(first):
@@ -1180,16 +1236,14 @@
 
     for step in range(2):
         res[step, 0] = experts(step, 0, local)
-        chain = res[step, 0][0]
+        chain = (res[step, 0][0], tops[-1])
+        widen_top()
+        if step == 0:
+            for other in range(3, n_ex, 2):
+                cots[other] = swap(after(cots[other - 1], chain), 1)
+                xs[other] = swap(after(xs[other - 1], chain), 1)
     odd, even = range(3, n_ex, 2), range(2, n_ex, 2)
-    for step in odd:
-        res[step, 0] = experts(step, 0, half)
-        chain = res[step, 0][0]
-        res[step, half] = experts(step, half, half, res[step, 0][:3])
-        chain = (res[step, half][0], tops[-1])
-        widen_top()
-    partner = {step - 1: [swap(res[step, half][k], 1) for k in (0, 1)] for step in odd}
-    for step in even:
+    for step in [*odd, *even]:
         res[step, 0] = experts(step, 0, half)
         chain = (res[step, 0][0], tops[-1])
         widen_top()
@@ -1197,22 +1251,40 @@
     chain = (made_one[0], tops[-1])
     got_one = [swap(made_one[k], 1, "dp", n_dp) for k in (1, 3)] if fast else []
     widen_top()
-    for step in even:
-        init = [
-            (a.astype(F32) + b.astype(F32)).astype(BF16)
-            for a, b in zip(res[step, 0][:2], partner[step])
-        ]
-        res[step, half] = experts(step, half, half, init + [res[step, 0][2]])
+    for step in odd:
+        res[step, half] = experts(step, half, half, res[step, 0][:3])
         chain = (res[step, half][0], tops[-1])
         widen_top()
+    partner = {step - 1: [swap(res[step, half][k], 1) for k in (0, 1)] for step in odd}
+    for step in even:
+        res[step, half] = experts(step, half, half, res[step, 0][:3])
+        chain = (res[step, half][0], tops[-1])
+        widen_top()
+
+    def with_partner(step, index):
+        own, other = res[step, half][index], partner[step][index]
+        return (own.astype(F32) + other.astype(F32)).astype(BF16)
+
+    to_send = {step: with_partner(step, 1) for step in even}
+    chain = (chain, list(to_send.values()))
+    sums, got_two = None, []
+    if fast:
+        tot_one = (made_one[0].astype(F32) + got_one[0].astype(F32)).astype(BF16)
+        far_one = lax.dynamic_slice_in_dim(tot_one, 2 * (1 - dp[0] // 4), 2, axis=0)
+        chain = (chain, far_one)
+        far_one = lax.ppermute(far_one, "dp", [(0, 2), (1, 3), (6, 4), (7, 5)])
     made_two = grads(half)
     chain = (made_two[0], got_one, tops[-1])
+    if fast:
+        chain = (chain, far_one)
+        sums = [tot_one, far_one, made_one[2], got_one[1]]
+        got_two = [swap(made_two[k], 1, "dp", n_dp) for k in (1, 3)]
     while len(tops) <= len(bits):
         widen_top()
     top = tops[-1]
 
     last = [res[step, 0 if step < 2 else half] for step in range(n_ex)]
-    dxs = [last[0][1], swap(last[1][1], 1)] + [swap(last[step][1], step) for step in even]
+    dxs = [last[0][1], swap(last[1][1], 1)] + [swap(to_send[step], step) for step in even]
     dgs = [last[0][2]] + [swap(last[step][2], step) for step in range(1, n_ex)]
     d_res, d_attn, d_ctx, d_logits, d_gain_two = run_back_mid(
         me,
@@ -1220,15 +1292,15 @@
         cot,
         routes_t,
         normed_two,
-        router,
+        w_all,
         gain_two,
-        full_out,
+        width // d,
         dxs,
         dgs,
         local,
     )
     outs = [last[0][0], swap(last[1][0], 1)]
-    outs += [swap(after(last[step][0], dxs), step) for step in even]
+    outs += [swap(after(with_partner(step, 0), dxs), step) for step in even]
     block = resid
     for piece in outs:
         block = block + piece.astype(F32)
@@ -1237,11 +1309,11 @@
     d_out_w = jnp.einsum("rc,rd->cd", ctx, d_attn, preferred_element_type=F32).astype(BF16)
     d_router_w = jnp.einsum("rd,re->de", normed_two, d_logits, preferred_element_type=F32)
 
-    dq, dk, dv = run_attn_bwd(
-        prefix, after(q, top), kd, vd, d_ctx, ctx, lse, cos_l, sin_l, cos_t, sin_t
+    dq, dk, dv, *halves = run_attn_bwd(
+        prefix, after(q, top), kd, vd, d_ctx, ctx, lse, cos_l, sin_l, cos_t, sin_t, sums
     )
     grad_tok, d_gain_one = run_back_in(
-        after(dq, block_out), dk, dv, w_all, tok, gain_one, d_res
+        after(dq, block_out, got_two), dk, dv, w_all, tok, gain_one, d_res
     )
     small_grad = jnp.concatenate(
         [
@@ -1278,16 +1350,17 @@
     y_bits = [("expert", n_ex, 1 << i) for i in range(1, n_ex.bit_length() - 1)][::-1]
     dp_bits = [("dp", n_dp, 1 << i) for i in range(n_dp.bit_length() - 1)]
     if fast:
-        keep_a, _, down_keep_a, _ = made_one
-        keep_b, send_b, down_keep_b, down_send_b = made_two
-        every_grad, grad_gate, grad_up, grad_down = run_finish(
+        every_grad, *others = run_finish(
             normed_one_t,
             dq,
             dk,
             dv,
             d_out_w,
             small_grad,
-            [keep_a, got_one[0], down_keep_a, got_one[1], keep_b, send_b, down_keep_b, down_send_b],
+            [made_two[0], got_two[0], made_two[2], got_two[1]],
+        )
+        grad_gate, grad_up, grad_down = (
+            jnp.concatenate([halves[k], others[k]], axis=0) for k in range(3)
         )
     else:
         ends = [

time: 650 us -> 589 us (0.906)
  Pallas kernels: 555 us -> 497 us
  local copies, waits for them, and re-layouts: 22 us -> 14.7 us
    pallas_call x2, Pallas kernels: 173 us -> 127 us  [the longest x1 80.8 us: run_finish(): pl.pallas_call(finish_kernel, in_specs=[vmem] * 6 + [hbm] * 4, out_specs=...]
    pallas_call x6, Pallas kernels: 200 us -> 192 us  [run_expert(): pl.pallas_call(functools.partial(expert_kernel, first, local, num_experts...]
    ppermute x25 -> x27, waiting for transfers between devices: 20.2 us -> 14.9 us  [swap(): return lax.ppermute(value, axis, [(i, i ^ step) for i in range(n)])]
    ppermute x25 -> x27, starting transfers between devices: 17.3 us -> 19.5 us  [swap(): return lax.ppermute(value, axis, [(i, i ^ step) for i in range(n)])]
  transfers between devices with their start and end apart: 25 -> 28, of which waited for: 7 -> 5; matrix products, arithmetic and copies ran while one was open for 4% -> 5% of each run, Pallas kernels for 47% -> 62%
where the time goes in v4:
time: 589 us; the launch traced here: 582 us
  Pallas kernels  497 us (84%)
  starting transfers between devices  23.2 us (4%)
  other arithmetic  22.4 us (4%)
  waiting for transfers between devices  14.9 us (3%)
  local copies, waits for them, and re-layouts  14.7 us (2%)
  matrix products  7.23 us (1%)
    pallas_call x6, Pallas kernels, run_expert(): pl.pallas_call(functools.partial(expert_kernel, first, local, num_experts...  192 us
    pallas_call x1, Pallas kernels, run_finish(): pl.pallas_call(finish_kernel, in_specs=[vmem] * 6 + [hbm] * 4, out_specs=...  80.8 us
    pallas_call x2, Pallas kernels, run_weight_grad(): pl.pallas_call(functools.partial(weight_grad_kernel, n, paired), grid=(co...  72.4 us
    pallas_call x1, Pallas kernels, run_attn_bwd(): pl.pallas_call(kernel, grid=(groups,), in_specs=in_specs, out_specs=out_s...  45.9 us
    pallas_call x1, Pallas kernels, run_gather(): pl.pallas_call(gather_kernel, in_specs=[hbm], out_specs=hbm, out_shape=ja...  43.5 us
    pallas_call x1, Pallas kernels, run_attn_fwd(): pl.pallas_call(attn_fwd_kernel, grid=(groups,), in_specs=[pl.BlockSpec(me...  21.5 us
    ppermute x27, starting transfers between devices, swap(): return lax.ppermute(value, axis, [(i, i ^ step) for i in range(n)])  19.5 us
    ppermute x27, waiting for transfers between devices, swap(): return lax.ppermute(value, axis, [(i, i ^ step) for i in range(n)])  14.9 us
  transfers between devices with their start and end apart: 28, of which 5 were waited for; matrix products, arithmetic and copies ran while one was open for 5% of the time, Pallas kernels for 62%

profile of v4, /device:TPU:0, one launch (start us, length us, event | category | flops | bytes accessed | tf_op | source)
XLA Modules:
  0.0 582.0 jit_solution(15707694086472644035)
XLA Ops:
  5.1 43.5 %gather.1.w_ref.router_ref.refs_5_.refs_7_ = bf16[1024,3200]{1,0:T(8,128)(2,1)} custom-call(bf16[32,3200]{1,0:T(8,128)(2,1)} %constant_dynamic-slice_fusion.1.mine_ref), custom_call_target="tpu_custom_call" | custom-call | flops 20000000000 | bytes 1000 | tf_op jit(solution)/shard_map/gather/pallas_call | solution.py:1108
  58.1 10.0 %qkv.1 = (bf16[1024,1024]{1,0:T(8,128)(2,1)}, bf16[1024,1024]{1,0:T(8,128)(2,1)}, bf16[1024,1024]{1,0:T(8,128)(2,1)}, bf16[1024,1024]{1,0:T(8,128)(2,1)}) custom-call(bf16[1024,1024]{1,0:T(8,128)(2,1)} %bitcast.23, bf16[1,1024]{1,0:T(2,128)(2,1)} %reshape_squeeze.9.gain_ref, bf16[1024,3200]{1,0:T(8,128)(2,1)} %gather.1.w_ref.router_ref.refs_5_.refs_7_, ...), custom_call_target="tpu_custom_call" | custom-call | flops 4499999744 | bytes 1000 | tf_op jit(solution)/shard_map/qkv/pallas_call | solution.py:101
  68.1 21.5 %attn_fwd.1 = (bf16[1024,1024]{1,0:T(8,128)(2,1)}, f32[4,8,1024]{2,1,0:T(8,128)}, f32[4,8,128]{2,1,0:T(8,128)}) custom-call(s32[1]{0:T(128)S(6)} %copy.45.prefix_ref.refs_0_, bf16[1024,1024]{1,0:T(8,128)(2,1)} %get-tuple-element.172.q_ref.refs_1_, bf16[1024,1024]{1,0:T(8,128)(2,1)} %get-tuple-element.114.kd_ref.refs_2_, ...), custom_call_target="tpu_custom_call" | custom-call | flops 10499999744 | bytes 1000 | tf_op jit(solution)/shard_map/attn_fwd/pallas_call | solution.py:176
  89.6 7.2 %mid.1 = (f32[1024,1024]{1,0:T(8,128)}, bf16[1024,1024]{1,0:T(8,128)(2,1)}) custom-call(bf16[1024,1024]{1,0:T(8,128)(2,1)} %bitcast.24, bf16[1024,1024]{1,0:T(8,128)(2,1)} %get-tuple-element.116.ctx_ref.refs_5_, bf16[1024,3200]{1,0:T(8,128)(2,1)} %gather.1.w_ref.router_ref.refs_5_.refs_7_, bf16[1,1024]{1,0:T(2,128)(2,1)} %reshape_squeeze.10.gain_ref.refs_6_), custom_call_target="tpu_custom_call" | custom-call | flops 2000000000 | bytes 1000 | tf_op jit(solution)/shard_map/mid/pallas_call | solution.py:495
  98.7 4.0 collective-permute-done.3.c_ref
  102.7 44.4 %experts.6 = (bf16[1024,1024]{1,0:T(8,128)(2,1)}, bf16[1024,1024]{1,0:T(8,128)(2,1)}, f32[8,1024]{1,0:T(8,128)}, bf16[1024,2048]{1,0:T(8,128)(2,1)}, bf16[1024,2...) custom-call(s32[1]{0:T(128)} %bitcast.3.me_ref.refs_0_, ...), custom_call_target="tpu_custom_call" | custom-call | flops 24000000000 | bytes 1000 | tf_op jit(solution)/shard_map/experts/pallas_call | solution.py:605
  147.7 44.1 %experts.7 = (bf16[1024,1024]{1,0:T(8,128)(2,1)}, bf16[1024,1024]{1,0:T(8,128)(2,1)}, f32[8,1024]{1,0:T(8,128)}, bf16[1024,2048]{1,0:T(8,128)(2,1)}, bf16[1024,2...) custom-call(s32[1]{0:T(128)} %bitcast.3.me_ref.refs_0_, ...), custom_call_target="tpu_custom_call" | custom-call | flops 24000000000 | bytes 1000 | tf_op jit(solution)/shard_map/experts/pallas_call | solution.py:605
  195.7 26.4 %experts.8 = (bf16[1024,1024]{1,0:T(8,128)(2,1)}, bf16[1024,1024]{1,0:T(8,128)(2,1)}, f32[8,1024]{1,0:T(8,128)}, bf16[1024,1024]{1,0:T(8,128)(2,1)}, bf16[1024,1...) custom-call(s32[1]{0:T(128)} %bitcast.3.me_ref.refs_0_, ...), custom_call_target="tpu_custom_call" | custom-call | flops 12000000000 | bytes 1000 | tf_op jit(solution)/shard_map/experts/pallas_call | solution.py:605
  223.0 26.2 %experts.9 = (bf16[1024,1024]{1,0:T(8,128)(2,1)}, bf16[1024,1024]{1,0:T(8,128)(2,1)}, f32[8,1024]{1,0:T(8,128)}, bf16[1024,1024]{1,0:T(8,128)(2,1)}, bf16[1024,1...) custom-call(s32[1]{0:T(128)} %bitcast.3.me_ref.refs_0_, ...), custom_call_target="tpu_custom_call" | custom-call | flops 12000000000 | bytes 1000 | tf_op jit(solution)/shard_map/experts/pallas_call | solution.py:605
  250.5 36.3 %weight_grad.2 = (bf16[4,2,2,128,512]{4,3,2,1,0:T(8,128)(2,1)}, bf16[4,2,2,128,512]{4,3,2,1,0:T(8,128)(2,1)}, bf16[4,2,128,512]{3,2,1,0:T(8,128)(2,1)}, bf16[4,2,128,512]{3,2,1,0:T(8,128)(2,1)}) custom-call(s32[1]{0:T(128)} %bitcast.7.dp_ref, bf16[1024,1024]{1,0:T(8,128)(2,1)} %get-tuple-element.174.refs_0_, bf16[1024,1024]{1,0:T(8,128)(2,1)} %get-tuple-element.137.refs_1_, ...), custom_call_target="tpu_custom_call" | custom-call | flops 18499999744 | bytes 1000 | tf_op jit(solution)/shard_map/weight_grad/pallas_call | solution.py:704
  290.4 25.5 %experts.10 = (bf16[1024,1024]{1,0:T(8,128)(2,1)}, bf16[1024,1024]{1,0:T(8,128)(2,1)}, f32[8,1024]{1,0:T(8,128)}, bf16[1024,1024]{1,0:T(8,128)(2,1)}, bf16[1024,...) custom-call(s32[1]{0:T(128)} %bitcast.3.me_ref.refs_0_, bf16[1024,1024]{1,0:T(8,128)(2,1)} %collective-permute-done.8.x_ref, ...), custom_call_target="tpu_custom_call" | custom-call | flops 12000000000 | bytes 1000 | tf_op jit(solution)/shard_map/experts/pallas_call | solution.py:605
  318.2 25.9 %experts.11 = (bf16[1024,1024]{1,0:T(8,128)(2,1)}, bf16[1024,1024]{1,0:T(8,128)(2,1)}, f32[8,1024]{1,0:T(8,128)}, bf16[1024,1024]{1,0:T(8,128)(2,1)}, bf16[1024,...) custom-call(s32[1]{0:T(128)} %bitcast.3.me_ref.refs_0_, bf16[1024,1024]{1,0:T(8,128)(2,1)} %collective-permute-done.7.x_ref, ...), custom_call_target="tpu_custom_call" | custom-call | flops 12000000000 | bytes 1000 | tf_op jit(solution)/shard_map/experts/pallas_call | solution.py:605
  344.0 2.9 add_convert_fusion.refs_11_
  347.1 3.7 collective-permute-start.22
  350.8 4.1 add_convert_fusion.2
  356.2 36.1 %weight_grad.3 = (bf16[4,2,2,128,512]{4,3,2,1,0:T(8,128)(2,1)}, bf16[4,2,2,128,512]{4,3,2,1,0:T(8,128)(2,1)}, bf16[4,2,128,512]{3,2,1,0:T(8,128)(2,1)}, bf16[4,2,128,512]{3,2,1,0:T(8,128)(2,1)}) custom-call(s32[1]{0:T(128)} %bitcast.7.dp_ref, bf16[1024,1024]{1,0:T(8,128)(2,1)} %get-tuple-element.174.refs_0_, bf16[1024,1024]{1,0:T(8,128)(2,1)} %get-tuple-element.137.refs_1_, ...), custom_call_target="tpu_custom_call" | custom-call | flops 18499999744 | bytes 1000 | tf_op jit(solution)/shard_map/weight_grad/pallas_call | solution.py:704
  394.6 3.9 add_convert_fusion.3
  398.5 4.7 collective-permute-done.18.refs_10_
  407.3 12.4 %back_mid.1 = (f32[1024,1024]{1,0:T(8,128)}, bf16[1024,1024]{1,0:T(8,128)(2,1)}, bf16[1024,1024]{1,0:T(8,128)(2,1)}, bf16[1024,128]{1,0:T(8,128)(2,1)}, f32[1,1024]{1,0:T(1,128)}) custom-call(s32[1]{0:T(128)} %bitcast.3.me_ref.refs_0_, f32[1024,1024]{1,0:T(8,128)} %get-tuple-element.183.refs_1_, bf16[1024,1024]{1,0:T(8,128)(2,1)} %bitcast.27, ...), custom_call_target="tpu_custom_call" | custom-call | flops 5500000256 | bytes 1000 | tf_op jit(solution)/shard_map/back_mid/pallas_call | solution.py:761
  422.3 45.9 %attn_bwd.1 = (bf16[1024,1024]{1,0:T(8,128)(2,1)}, bf16[1024,512]{1,0:T(8,128)(2,1)}, bf16[1024,512]{1,0:T(8,128)(2,1)}, f32[2,128,512]{2,1,0:T(8,128)}, f32[2,128,512]{2,1,0:T(8,128)}, /*index=5*/f32[2,64,1024]{2,1,0:T(8,128)}) custom-call(s32[1]{0:T(128)S(6)} %copy.45.prefix_ref.refs_0_, bf16[1024,1024]{1,0:T(8,128)(2,1)} %get-tuple-element.172.q_ref.refs_1_, ...), custom_call_target="tpu_custom_call" | custom-call | flops 16499999744 | bytes 1000 | tf_op jit(solution)/shard_map/attn_bwd/pallas_call | solution.py:469
  468.2 5.5 convolution_convert_fusion.dout_ref
  473.8 5.2 fusion
  479.0 11.3 %back_in.1 = (f32[1024,1024]{1,0:T(8,128)}, f32[1,1024]{1,0:T(1,128)}) custom-call(bf16[1024,1024]{1,0:T(8,128)(2,1)} %get-tuple-element.194.dq_ref, bf16[1024,512]{1,0:T(8,128)(2,1)} %get-tuple-element.195.dk_ref, bf16[1024,512]{1,0:T(8,128)(2,1)} %get-tuple-element.196.dv_ref, bf16[1024,3200]{1,0:T(8,128)(2,1)} %gather.1.w_ref.router_ref.refs_5_.refs_7_, ...), custom_call_target="tpu_custom_call" | custom-call | flops 5000000000 | bytes 1000 | tf_op jit(solution)/shard_map/back_in/pallas_call | solution.py:820
  492.2 80.8 %finish.1 = (f32[128,3200]{1,0:T(8,128)}, f32[2,128,512]{2,1,0:T(8,128)}, f32[2,128,512]{2,1,0:T(8,128)}, f32[2,64,1024]{2,1,0:T(8,128)}) custom-call(bf16[1024,1024]{1,0:T(8,128)(2,1)} %get-tuple-element.199.ht_ref, bf16[1024,1024]{1,0:T(8,128)(2,1)} %get-tuple-element.194.dq_ref, bf16[1024,512]{1,0:T(8,128)(2,1)} %get-tuple-element.195.dk_ref, ...), custom_call_target="tpu_custom_call" | custom-call | flops 30000001024 | bytes 1000 | tf_op jit(solution)/shard_map/finish/pallas_call | solution.py:1013
  (152 shorter events, 48.5 us)
Async XLA Ops:
  54.1 48.6 %collective-permute-start.3 = (bf16[1024,1024]{1,0:T(8,128)(2,1)S(1)}, bf16[1024,1024]{1,0:T(8,128)(2,1)}, u32[]{:S(2)}, u32[]{:S(2)}) collective-permute-start(bf16[1024,1024]{1,0:T(8,128)(2,1)S(1)} %bitcast.28), channel_id=1, source_target_pairs={{0,2},{1,3},{2,0},{3,1},{4,6},{5,7},{6,4},{7,5},{8,10},{9,11},{10,... | collective-permute-start | bytes 6291464 | tf_op jit(solution)/shard_map/ppermute | solution.py:1145
  96.8 50.3 %collective-permute-start.7 = (bf16[1024,1024]{1,0:T(8,128)(2,1)}, bf16[1024,1024]{1,0:T(8,128)(2,1)}, u32[]{:S(2)}, u32[]{:S(2)}) collective-permute-start(bf16[1024,1024]{1,0:T(8,128)(2,1)} %get-tuple-element.121.x_ref.refs_4_), channel_id=1, source_target_pairs={{0,2},{1,3},{2,0},{3,1},{4,6},{5,7},{6,4},{7,5},{8,10},{9,11},{10,... | collective-permute-start | bytes 6291464 | tf_op jit(solution)/shard_map/ppermute | solution.py:1145
  98.1 49.0 %collective-permute-start.4 = (bf16[1024,1024]{1,0:T(8,128)(2,1)}, bf16[1024,1024]{1,0:T(8,128)(2,1)}, u32[]{:S(2)}, u32[]{:S(2)}) collective-permute-start(bf16[1024,1024]{1,0:T(8,128)(2,1)} %get-tuple-element.121.x_ref.refs_4_), channel_id=1, source_target_pairs={{0,1},{1,0},{2,3},{3,2},{4,5},{5,4},{6,7},{7,6},{8,9},{9,8},{10,11... | collective-permute-start | bytes 6291464 | tf_op jit(solution)/shard_map/ppermute | solution.py:1145
  98.1 49.6 %collective-permute-start.5 = (bf16[1024,1024]{1,0:T(8,128)(2,1)S(1)}, bf16[1024,1024]{1,0:T(8,128)(2,1)}, u32[]{:S(2)}, u32[]{:S(2)}) collective-permute-start(bf16[1024,1024]{1,0:T(8,128)(2,1)S(1)} %bitcast.29), channel_id=1, source_target_pairs={{0,1},{1,0},{2,3},{3,2},{4,5},{5,4},{6,7},{7,6},{8,9},{9,8},{10,11... | collective-permute-start | bytes 6291464 | tf_op jit(solution)/shard_map/ppermute | solution.py:1145
  147.1 48.6 %collective-permute-start.8 = (bf16[1024,1024]{1,0:T(8,128)(2,1)}, bf16[1024,1024]{1,0:T(8,128)(2,1)}, u32[]{:S(2)}, u32[]{:S(2)}) collective-permute-start(bf16[1024,1024]{1,0:T(8,128)(2,1)} %collective-permute-done.7.x_ref), channel_id=1, source_target_pairs={{0,1},{1,0},{2,3},{3,2},{4,5},{5,4},{6,7},{7,6},{8,9},{9,8},{10,11... | collective-permute-start | bytes 6291464 | tf_op jit(solution)/shard_map/ppermute | solution.py:1145
  147.2 44.7 %collective-permute-start.9 = (f32[4,8,4]{2,1,0:T(8,128)S(1)}, f32[4,8,4]{2,1,0:T(8,128)S(1)}, u32[]{:S(2)}, u32[]{:S(2)}) collective-permute-start(f32[4,8,4]{2,1,0:T(8,128)S(1)} %bitcast.36), channel_id=1, source_target_pairs={{0,1},{1,0},{2,3},{3,2},{4,5},{5,4},{6,7},{7,6},{8,9},{9,8},{10,11... | collective-permute-start | bytes 1544 | tf_op jit(solution)/shard_map/ppermute | solution.py:1145
  147.7 48.0 %collective-permute-start.10 = (bf16[1024,1024]{1,0:T(8,128)(2,1)}, bf16[1024,1024]{1,0:T(8,128)(2,1)}, u32[]{:S(2)}, u32[]{:S(2)}) collective-permute-start(bf16[1024,1024]{1,0:T(8,128)(2,1)} %collective-permute-done.3.c_ref), channel_id=1, source_target_pairs={{0,1},{1,0},{2,3},{3,2},{4,5},{5,4},{6,7},{7,6},{8,9},{9,8},{10,11... | collective-permute-start | bytes 6291464 | tf_op jit(solution)/shard_map/ppermute | solution.py:1145
  192.9 205.6 %collective-permute-start.16 = (bf16[1024,1024]{1,0:T(8,128)(2,1)}, bf16[1024,1024]{1,0:T(8,128)(2,1)}, u32[]{:S(2)}, u32[]{:S(2)}) collective-permute-start(bf16[1024,1024]{1,0:T(8,128)(2,1)} %get-tuple-element.168), channel_id=1, source_target_pairs={{0,1},{1,0},{2,3},{3,2},{4,5},{5,4},{6,7},{7,6},{8,9},{9,8},{10,11... | collective-permute-start | bytes 6291464 | tf_op jit(solution)/shard_map/ppermute | solution.py:1145
  222.0 27.1 %collective-permute-start.12 = (f32[4,8,4]{2,1,0:T(8,128)S(1)}, f32[4,8,4]{2,1,0:T(8,128)S(1)}, u32[]{:S(2)}, u32[]{:S(2)}) collective-permute-start(f32[4,8,4]{2,1,0:T(8,128)S(1)} %max.22), channel_id=1, source_target_pairs={{0,4},{4,0},{8,12},{12,8},{16,20},{20,16},{24,28},{28,24},{1,5},{5... | collective-permute-start | bytes 1544 | tf_op jit(solution)/shard_map/ppermute | solution.py:1145
  249.2 39.6 %collective-permute-start.13 = (f32[4,8,4]{2,1,0:T(8,128)S(1)}, f32[4,8,4]{2,1,0:T(8,128)S(1)}, u32[]{:S(2)}, u32[]{:S(2)}) collective-permute-start(f32[4,8,4]{2,1,0:T(8,128)S(1)} %max.23), channel_id=1, source_target_pairs={{0,8},{4,12},{8,0},{12,4},{16,24},{20,28},{24,16},{28,20},{1,9},{5... | collective-permute-start | bytes 1544 | tf_op jit(solution)/shard_map/ppermute | solution.py:1145
  286.7 57.3 %collective-permute-start.20 = (bf16[4,2,2,128,512]{4,3,2,1,0:T(8,128)(2,1)}, bf16[4,2,2,128,512]{4,3,2,1,0:T(8,128)(2,1)}, u32[]{:S(2)}, u32[]{:S(2)}) collective-permute-start(bf16[4,2,2,128,512]{4,3,2,1,0:T(8,128)(2,1)} %get-tuple-element.173), channel_id=1, source_target_pairs={{0,4},{4,0},{8,12},{12,8},{16,20},{20,16},{24,28},{28,24},{1,5},{5... | collective-permute-start | bytes 6291464 | tf_op jit(solution)/shard_map/ppermute | solution.py:1145
  287.6 104.7 %collective-permute-start.21 = (bf16[4,2,128,512]{3,2,1,0:T(8,128)(2,1)}, bf16[4,2,128,512]{3,2,1,0:T(8,128)(2,1)}, u32[]{:S(2)}, u32[]{:S(2)}) collective-permute-start(bf16[4,2,128,512]{3,2,1,0:T(8,128)(2,1)} %get-tuple-element.182), channel_id=1, source_target_pairs={{0,4},{4,0},{8,12},{12,8},{16,20},{20,16},{24,28},{28,24},{1,5},{5... | collective-permute-start | bytes 3145736 | tf_op jit(solution)/shard_map/ppermute | solution.py:1145
  288.8 27.2 %collective-permute-start.14 = (f32[4,8,4]{2,1,0:T(8,128)S(1)}, f32[4,8,4]{2,1,0:T(8,128)S(1)}, u32[]{:S(2)}, u32[]{:S(2)}) collective-permute-start(f32[4,8,4]{2,1,0:T(8,128)S(1)} %max.24), channel_id=1, source_target_pairs={{0,16},{4,20},{8,24},{12,28},{16,0},{20,4},{24,8},{28,12},{1,17},{... | collective-permute-start | bytes 1544 | tf_op jit(solution)/shard_map/ppermute | solution.py:1145
  315.9 76.5 %collective-permute-start.15 = (bf16[1024,1024]{1,0:T(8,128)(2,1)}, bf16[1024,1024]{1,0:T(8,128)(2,1)S(1)}, u32[]{:S(2)}, u32[]{:S(2)}) collective-permute-start(bf16[1024,1024]{1,0:T(8,128)(2,1)} %get-tuple-element.161), channel_id=1, source_target_pairs={{0,1},{1,0},{2,3},{3,2},{4,5},{5,4},{6,7},{7,6},{8,9},{9,8},{10,11... | collective-permute-start | bytes 6291464 | tf_op jit(solution)/shard_map/ppermute | solution.py:1145
  316.0 34.7 %collective-permute-start.17 = (bf16[1024,1024]{1,0:T(8,128)(2,1)}, bf16[1024,1024]{1,0:T(8,128)(2,1)}, u32[]{:S(2)}, u32[]{:S(2)}) collective-permute-start(bf16[1024,1024]{1,0:T(8,128)(2,1)} %get-tuple-element.170), channel_id=1, source_target_pairs={{0,1},{1,0},{2,3},{3,2},{4,5},{5,4},{6,7},{7,6},{8,9},{9,8},{10,11... | collective-permute-start | bytes 6291464 | tf_op jit(solution)/shard_map/ppermute | solution.py:1145
  347.1 46.1 %collective-permute-start.22 = (bf16[2,2,2,128,512]{4,3,2,1,0:T(8,128)(2,1)S(1)}, bf16[2,2,2,128,512]{4,3,2,1,0:T(8,128)(2,1)}, u32[]{:S(2)}, u32[]{:S(2)}) collective-permute-start(bf16[2,2,2,128,512]{4,3,2,1,0:T(8,128)(2,1)S(1)} %constant_dynamic-slice_fusion), channel_id=1, source_target_pairs={{0,8},{4,12},{24,16},{28,20},{1,9},{5,13},{25,17},{29,21},{2,10},{... | collective-permute-start | bytes 3145736 | tf_op jit(solution)/shard_map/ppermute | solution.py:1275
  354.9 48.4 %collective-permute-start.18 = (bf16[1024,1024]{1,0:T(8,128)(2,1)}, bf16[1024,1024]{1,0:T(8,128)(2,1)}, u32[]{:S(2)}, u32[]{:S(2)}) collective-permute-start(bf16[1024,1024]{1,0:T(8,128)(2,1)} %add_convert_fusion.2), channel_id=1, source_target_pairs={{0,2},{1,3},{2,0},{3,1},{4,6},{5,7},{6,4},{7,5},{8,10},{9,11},{10,... | collective-permute-start | bytes 6291464 | tf_op jit(solution)/shard_map/ppermute | solution.py:1145
  392.4 11.7 %collective-permute-start.23 = (f32[8,1024]{1,0:T(8,128)S(1)}, f32[8,1024]{1,0:T(8,128)S(1)}, u32[]{:S(2)}, u32[]{:S(2)}) collective-permute-start(f32[8,1024]{1,0:T(8,128)S(1)} %copy-done.23), channel_id=1, source_target_pairs={{0,1},{1,0},{2,3},{3,2},{4,5},{5,4},{6,7},{7,6},{8,9},{9,8},{10,11... | collective-permute-start | bytes 98312 | tf_op jit(solution)/shard_map/ppermute | solution.py:1145
  392.5 12.8 %collective-permute-start.25 = (f32[8,1024]{1,0:T(8,128)S(1)}, f32[8,1024]{1,0:T(8,128)S(1)}, u32[]{:S(2)}, u32[]{:S(2)}) collective-permute-start(f32[8,1024]{1,0:T(8,128)S(1)} %copy-done.25), channel_id=1, source_target_pairs={{0,3},{1,2},{2,1},{3,0},{4,7},{5,6},{6,5},{7,4},{8,11},{9,10},{10,... | collective-permute-start | bytes 98312 | tf_op jit(solution)/shard_map/ppermute | solution.py:1145
  393.2 13.4 %collective-permute-start.24 = (f32[8,1024]{1,0:T(8,128)S(1)}, f32[8,1024]{1,0:T(8,128)S(1)}, u32[]{:S(2)}, u32[]{:S(2)}) collective-permute-start(f32[8,1024]{1,0:T(8,128)S(1)} %copy-done.27), channel_id=1, source_target_pairs={{0,2},{1,3},{2,0},{3,1},{4,6},{5,7},{6,4},{7,5},{8,10},{9,11},{10,... | collective-permute-start | bytes 98312 | tf_op jit(solution)/shard_map/ppermute | solution.py:1145
  398.5 75.2 %collective-permute-start.6 = (bf16[1024,1024]{1,0:T(8,128)(2,1)}, bf16[1024,1024]{1,0:T(8,128)(2,1)}, u32[]{:S(2)}, u32[]{:S(2)}) collective-permute-start(bf16[1024,1024]{1,0:T(8,128)(2,1)} %get-tuple-element.125), channel_id=1, source_target_pairs={{0,1},{1,0},{2,3},{3,2},{4,5},{5,4},{6,7},{7,6},{8,9},{9,8},{10,11... | collective-permute-start | bytes 6291464 | tf_op jit(solution)/shard_map/ppermute | solution.py:1145
  403.2 75.7 %collective-permute-start.26 = (bf16[4,2,2,128,512]{4,3,2,1,0:T(8,128)(2,1)}, bf16[4,2,2,128,512]{4,3,2,1,0:T(8,128)(2,1)}, u32[]{:S(2)}, u32[]{:S(2)}) collective-permute-start(bf16[4,2,2,128,512]{4,3,2,1,0:T(8,128)(2,1)} %get-tuple-element.192), channel_id=1, source_target_pairs={{0,4},{4,0},{8,12},{12,8},{16,20},{20,16},{24,28},{28,24},{1,5},{5... | collective-permute-start | bytes 6291464 | tf_op jit(solution)/shard_map/ppermute | solution.py:1145
  404.1 74.9 %collective-permute-start.27 = (bf16[4,2,128,512]{3,2,1,0:T(8,128)(2,1)}, bf16[4,2,128,512]{3,2,1,0:T(8,128)(2,1)}, u32[]{:S(2)}, u32[]{:S(2)}) collective-permute-start(bf16[4,2,128,512]{3,2,1,0:T(8,128)(2,1)} %get-tuple-element.193), channel_id=1, source_target_pairs={{0,4},{4,0},{8,12},{12,8},{16,20},{20,16},{24,28},{28,24},{1,5},{5... | collective-permute-start | bytes 3145736 | tf_op jit(solution)/shard_map/ppermute | solution.py:1145
  405.3 68.5 %collective-permute-start.19 = (bf16[1024,1024]{1,0:T(8,128)(2,1)}, bf16[1024,1024]{1,0:T(8,128)(2,1)}, u32[]{:S(2)}, u32[]{:S(2)}) collective-permute-start(bf16[1024,1024]{1,0:T(8,128)(2,1)} %add_convert_fusion.3), channel_id=1, source_target_pairs={{0,2},{1,3},{2,0},{3,1},{4,6},{5,7},{6,4},{7,5},{8,10},{9,11},{10,... | collective-permute-start | bytes 6291464 | tf_op jit(solution)/shard_map/ppermute | solution.py:1145
  (32 other events, 558.5 us)

commit v5 on v4

--- a/solution.py
+++ b/solution.py
@@ -14,7 +14,7 @@
 BF16 = jnp.bfloat16
 NEG = -1e30
 MIB = 1 << 20
-SCALE = 0.5
+SCALE = 0.35
 
 
 def dot(a, b):
@@ -524,35 +524,68 @@
     return e / jnp.sum(e, axis=0, keepdims=True)
 
 
-def expert_kernel(
-    first_expert, local, num_experts, with_init, me_ref, x_ref, c_ref, route_ref, router_ref, wg_ref, wu_ref, wd_ref, *refs
-):
+def expert_kernel(first_expert, local, num_experts, with_init, with_carry, n_row, *refs):
+    me_ref, router_ref, wg_ref, wu_ref, wd_ref = refs[:5]
+    x_refs, c_refs, route_refs = refs[5:7], refs[7:9], refs[9:11]
+    refs = refs[11:]
     if with_init:
-        out_in, dx_in, dg_in, refs = refs[0], refs[1], refs[2], refs[3:]
-        out_ref, dx_ref, dg_ref, hs_ref, dgate_ref, dup_ref, out_acc, dx_acc, gp_ref, dgc_ref = refs
-    else:
-        out_ref, dx_ref, dg_ref, hs_ref, dgate_ref, dup_ref, xt_ref, ct_ref, out_acc, dx_acc, gp_ref, dgc_ref = refs
-    e = pl.program_id(1)
+        out_ins, dx_ins, dg_ins, refs = refs[:2], refs[2:4], refs[4:6], refs[6:]
+    if with_carry:
+        sent_ref, refs = refs[0], refs[1:]
+    out_refs, dx_refs, dg_refs = refs[:2], refs[2:4], refs[4:6]
+    hs_ref, dgate_ref, dup_ref = refs[6:9]
+    refs = refs[9:]
+    if not with_init:
+        xt_ref, ct_ref, refs = refs[0], refs[1], refs[2:]
+    if with_carry:
+        got_ref, refs = refs[0], refs[1:]
+    x_now, c_now, out_acc, dx_acc, gp_ref, dgc_ref = refs[:6]
+    i, e = pl.program_id(0), pl.program_id(1)
     last = pl.num_programs(1) - 1
-    x, c = x_ref[...], c_ref[...]
-    b = x.shape[0]
+    if with_carry:
+        over_x = (lax.axis_index("dp") ^ 1, lax.axis_index("expert"))
+
+        def carry():
+            return pltpu.make_async_remote_copy(
+                src_ref=sent_ref,
+                dst_ref=got_ref,
+                send_sem=refs[6].at[0],
+                recv_sem=refs[6].at[1],
+                device_id=over_x,
+                device_id_type=pl.DeviceIdType.MESH,
+            )
+
+        @pl.when((i == 0) & (e == 0))
+        def _():
+            greet([over_x])
+            carry().start()
+
+    b = x_now.shape[0]
     lane = lax.broadcasted_iota(jnp.int32, (b, 128), 1)
 
-    @pl.when(e == 0)
-    def _():
-        gates = gates_of(x, router_ref[...], route_ref[...], num_experts)
-        fill = jnp.zeros((128 - gates.shape[0], b), F32)
-        gp_ref[...] = jnp.concatenate([gates, fill], axis=0).T
-        dgc_ref[...] = jnp.zeros_like(dgc_ref)
-        if with_init:
-            out_acc[...] = out_in[...].astype(F32)
-            dx_acc[...] = dx_in[...].astype(F32)
-        else:
-            out_acc[...] = jnp.zeros_like(out_acc)
-            dx_acc[...] = jnp.zeros_like(dx_acc)
-            xt_ref[...] = x.T
-            ct_ref[...] = c.T
-
+    for source in range(2):
+
+        @pl.when((e == 0) & ((i < n_row) if source == 0 else (i >= n_row)))
+        def _():
+            x, c = x_refs[source][...], c_refs[source][...]
+            x_now[...] = x
+            c_now[...] = c
+            gates = gates_of(x, router_ref[...], route_refs[source][...], num_experts)
+            fill = jnp.zeros((128 - gates.shape[0], b), F32)
+            gp_ref[...] = jnp.concatenate([gates, fill], axis=0).T
+            if with_init:
+                out_acc[...] = out_ins[source][...].astype(F32)
+                dx_acc[...] = dx_ins[source][...].astype(F32)
+                fill = jnp.zeros((120, b), F32)
+                dgc_ref[...] = jnp.concatenate([dg_ins[source][...], fill], axis=0).T
+            else:
+                out_acc[...] = jnp.zeros_like(out_acc)
+                dx_acc[...] = jnp.zeros_like(dx_acc)
+                dgc_ref[...] = jnp.zeros_like(dgc_ref)
+                xt_ref[...] = x.T
+                ct_ref[...] = c.T
+
+    x, c = x_now[...], c_now[...]
     gp = jnp.sum(
         jnp.where(lane == me_ref[0] * local + first_expert + e, gp_ref[...], 0.0),
         axis=1,
@@ -575,41 +608,63 @@
     out = dot(hs, wd_ref[0])
     dx = dot_t(dgate, wg_ref[0]) + dot_t(dup, wu_ref[0])
     dgc_ref[...] += jnp.where(lane == first_expert + e, dg, 0.0)
-
-    @pl.when(e < last)
-    def _():
-        out_acc[...] += out
-        dx_acc[...] += dx
-
-    @pl.when(e == last)
-    def _():
-        out_ref[...] = (out_acc[...] + out).astype(BF16)
-        dx_ref[...] = (dx_acc[...] + dx).astype(BF16)
-        dg_t = dgc_ref[...].T[:8]
-        dg_ref[...] = dg_t + dg_in[...] if with_init else dg_t
-
-
-def run_expert(me, x, c, routes_t, router, wg, wu, wd, first, count, num_experts, init=None):
-    length, d = x.shape
+    out_acc[...] += out
+    dx_acc[...] += dx
+    for source in range(2):
+
+        @pl.when((e == last) & ((i < n_row) if source == 0 else (i >= n_row)))
+        def _():
+            out_refs[source][...] = out_acc[...].astype(BF16)
+            dx_refs[source][...] = dx_acc[...].astype(BF16)
+            dg_refs[source][...] = dgc_ref[...].T[:8]
+
+    if with_carry:
+
+        @pl.when((i == 2 * n_row - 1) & (e == last))
+        def _():
+            carry().wait()
+
+
+def run_expert(me, xs, cs, routes, router, wg, wu, wd, first, count, num_experts, init=None, sent=None):
+    length, d = xs[0].shape
     local, _, ff = wg.shape
     b = 512
-    top = routes_t.shape[0]
-    row = lambda i, e: (i, 0)
-    col_t = lambda i, e: (0, i)
+    n_row = length // b
+    top = routes[0].shape[0]
+
+    def clamp(i, source):
+        return jnp.minimum(i, n_row - 1) if source == 0 else jnp.maximum(i - n_row, 0)
+
+    rows = [
+        spec((b, d), functools.partial(lambda src, i, e: (clamp(i, src), 0), src))
+        for src in range(2)
+    ]
+
+    def lanes(height):
+        return [
+            spec((height, b), functools.partial(lambda src, i, e: (0, clamp(i, src)), src))
+            for src in range(2)
+        ]
+
     pick = lambda shape: pl.BlockSpec((1,) + shape[1:], lambda i, e: (first + e, 0, 0))
-    wide = jax.ShapeDtypeStruct((length, count * ff), BF16)
+    wide = jax.ShapeDtypeStruct((2 * length, count * ff), BF16)
     full = jax.ShapeDtypeStruct((length, d), BF16)
-    turned = jax.ShapeDtypeStruct((d, length), BF16)
+    small = jax.ShapeDtypeStruct((8, length), F32)
+    turned = jax.ShapeDtypeStruct((d, 2 * length), BF16)
     wide_spec = spec((b, ff), lambda i, e: (i, e))
+    turned_spec = spec((d, b), lambda i, e: (0, i))
     with_init = init is not None
-    return pl.pallas_call(
-        functools.partial(expert_kernel, first, local, num_experts, with_init),
-        grid=(length // b, count),
+    carried, extra = [], {}
+    if sent is not None:
+        carried = [pl.BlockSpec(memory_space=pl.ANY)]
+        extra = {"collective_id": 4, "has_side_effects": True}
+    made = pl.pallas_call(
+        functools.partial(
+            expert_kernel, first, local, num_experts, with_init, sent is not None, n_row
+        ),
+        grid=(2 * n_row, count),
         in_specs=[
             pl.BlockSpec(memory_space=pltpu.SMEM),
-            spec((b, d), row),
-            spec((b, d), row),
-            spec((top, b), col_t),
             pl.BlockSpec(
                 (d, 128),
                 lambda i, e: (0, router.shape[1] // 128 - 1),
@@ -619,23 +674,36 @@
             pick(wu.shape),
             pick(wd.shape),
         ]
-        + ([spec((b, d), row)] * 2 + [spec((8, b), col_t)] if with_init else []),
-        out_specs=[spec((b, d), row)] * 2
-        + [spec((8, b), col_t)]
+        + rows * 2
+        + lanes(top)
+        + (rows * 2 + lanes(8) if with_init else [])
+        + carried,
+        out_specs=rows * 2
+        + lanes(8)
         + [wide_spec] * 3
-        + ([] if with_init else [spec((d, b), col_t)] * 2),
-        out_shape=[full, full, jax.ShapeDtypeStruct((8, length), F32), wide, wide, wide]
-        + ([] if with_init else [turned, turned]),
+        + ([] if with_init else [turned_spec] * 2)
+        + carried,
+        out_shape=[full] * 4
+        + [small] * 2
+        + [wide] * 3
+        + ([] if with_init else [turned] * 2)
+        + ([] if sent is None else [jax.ShapeDtypeStruct(sent.shape, sent.dtype)]),
         scratch_shapes=[
+            pltpu.VMEM((b, d), BF16),
+            pltpu.VMEM((b, d), BF16),
             pltpu.VMEM((b, d), F32),
             pltpu.VMEM((b, d), F32),
             pltpu.VMEM((b, 128), F32),
             pltpu.VMEM((b, 128), F32),
-        ],
-        compiler_params=params(60, 2),
-        cost_estimate=took(12 * count),
+        ]
+        + ([] if sent is None else [pltpu.SemaphoreType.DMA((2,))]),
+        compiler_params=pltpu.CompilerParams(
+            dimension_semantics=("arbitrary",) * 2, vmem_limit_bytes=62 * MIB, **extra
+        ),
+        cost_estimate=took(24 * count),
         name="experts",
-    )(me, x, c, routes_t, router, wg, wu, wd, *(init if with_init else ()))
+    )(me, router, wg, wu, wd, *xs, *cs, *routes, *(init or ()), *([] if sent is None else [sent]))
+    return {"out": made[:2], "dx": made[2:4], "dg": made[4:6], "wide": made[6:9], "turned": made[9:11], "got": made[9:]}
 
 
 def weight_grad_kernel(n, paired, dp_ref, *refs):
@@ -677,10 +745,9 @@
         up_ref[p, 0] = up[p * rows : (p + 1) * rows]
 
 
-def run_weight_grad(dp, xt, ct, dgate, dup, hs, count, skips, n_dp, paired):
+def run_weight_grad(dp, xt, ct, dgate, dup, hs, count, skips, n_dp, paired, ff):
     n = len(xt)
     d, length = xt[0].shape
-    ff = hs[-1].shape[1] // count
     m = 512 if paired else 256
     left = spec((m, length), lambda e, i: (i, 0))
     rights = [
@@ -842,7 +909,7 @@
 
 def finish_kernel(
     ht_ref, dq_ref, dk_ref, dv_ref, dout_ref, small_ref, keep_ref, got_ref, down_keep_ref, down_got_ref,
-    out_ref, gate_ref, up_ref, down_ref, *scratch,
+    gate_a, up_a, down_a, out_o, out_q, out_kv, out_small, gate_ref, up_ref, down_ref, *scratch,
 ):
     n = len(CHUNKS)
     lists = [scratch[k * n : (k + 1) * n] for k in range(8)]
@@ -850,6 +917,11 @@
     sem_s, sem_r = scratch[8 * n : 8 * n + 2]
     line = Line(*scratch[8 * n + 2 : 8 * n + 8])
     rx, sem_l = scratch[8 * n + 8 :]
+    count = gate_a.shape[0]
+    halves = []
+    for k, (src, dst) in enumerate(((gate_a, gate_ref), (up_a, up_ref), (down_a, down_ref))):
+        halves.append(pltpu.make_async_copy(src, dst.at[:count], sem_l.at[6 + k]))
+        halves[k].start()
     dp, ex = lax.axis_index("dp"), lax.axis_index("expert")
     z, x, y, c = dp // 2, dp % 2, ex // 2, ex % 2
     over_core, over_y, over_x = (dp, ex ^ 1), (dp, ex ^ 2), (dp ^ 1, ex)
@@ -869,7 +941,7 @@
     greet(group + [over_x] + along)
 
     widths = [dout_ref.shape[1], dq_ref.shape[1], dk_ref.shape[1] + dv_ref.shape[1], 128]
-    starts = [sum(widths[:k]) for k in range(n)]
+    outs = (out_o, out_q, out_kv, out_small)
     started = {}
 
     def send(k, slot, src, dst, peer):
@@ -951,14 +1023,13 @@
             send(k, 6 + i, r4[k].at[3], r4[k].at[i], group[i])
 
     def step5(k):
-        o = slice(starts[k], starts[k] + widths[k])
-        out_ref[pl.ds(pl.multiple_of(ex * 32, 32), 32), o] = r4[k][3].astype(F32)
+        outs[k][pl.ds(pl.multiple_of(ex * 32, 32), 32), :] = r4[k][3].astype(F32)
         for i in range(3):
             started[k, 6 + i].wait()
             rows = pl.ds(pl.multiple_of((ex ^ (i + 1)) * 32, 32), 32)
-            out_ref[rows, o] = r4[k][i].astype(F32)
-
-    done = (gate_ref, up_ref, down_ref)
+            outs[k][rows, :] = r4[k][i].astype(F32)
+
+    done = tuple(ref.at[count:] for ref in (gate_ref, up_ref, down_ref))
     step0(3)
     step0(0)
     begin(0)
@@ -995,6 +1066,8 @@
     line.result(2, done)
     step5(1)
     step5(2)
+    for copy in halves:
+        copy.wait()
 
 
 def run_finish(ht, dq, dk, dv, d_out, small, experts):
@@ -1009,16 +1082,16 @@
     scratch = [pltpu.VMEM(shape + (w,), BF16) for shape in shapes for w in widths]
     scratch += [pltpu.SemaphoreType.DMA((len(widths), 9))] * 2
     scratch += line_scratch(chunk)
-    scratch += [pltpu.VMEM((3,) + chunk, BF16), pltpu.SemaphoreType.DMA((6,))]
+    scratch += [pltpu.VMEM((3,) + chunk, BF16), pltpu.SemaphoreType.DMA((9,))]
     return pl.pallas_call(
         finish_kernel,
-        in_specs=[vmem] * 6 + [hbm] * 4,
-        out_specs=[vmem] * 4,
+        in_specs=[vmem] * 6 + [hbm] * 7,
+        out_specs=[vmem] * 7,
         out_shape=[
-            jax.ShapeDtypeStruct((128, sum(widths)), F32),
-            jax.ShapeDtypeStruct((count, rows, lanes), F32),
-            jax.ShapeDtypeStruct((count, rows, lanes), F32),
-            jax.ShapeDtypeStruct((count, rows // 2, 2 * lanes), F32),
+            *(jax.ShapeDtypeStruct((128, w), F32) for w in widths),
+            jax.ShapeDtypeStruct((2 * count, rows, lanes), F32),
+            jax.ShapeDtypeStruct((2 * count, rows, lanes), F32),
+            jax.ShapeDtypeStruct((2 * count, rows // 2, 2 * lanes), F32),
         ],
         scratch_shapes=scratch,
         compiler_params=pltpu.CompilerParams(
@@ -1168,12 +1241,10 @@
     gain_one = extra[:, num_experts].reshape(1, d)
     gain_two = extra[:, num_experts + 1].reshape(1, d)
 
-    routes_t = after(routes.reshape(length, -1).T, every)
+    routes_t = routes.reshape(length, -1).T
     cots = {0: cot}
     route_set = {0: routes_t}
-    for step in range(1, n_ex):
-        route_set[step] = swap(routes_t, step)
-    cot_late = after(cot, every, *route_set.values())
+    cot_late = after(cot, every)
     for step in range(1, n_ex):
         if step == 1 or step % 2 == 0:
             cots[step] = swap(cot_late, step)
@@ -1185,6 +1256,8 @@
     sin_t = jnp.asarray(np.ascontiguousarray(sin_np.T))
 
     normed_one_t, q, kd, vd = run_qkv(tok, gain_one, w_all, cos_l, sin_l, nq)
+    for step in range(1, n_ex):
+        route_set[step] = swap(after(routes_t, q), step)
     ctx, lse, peaks = run_attn_fwd(prefix, q, kd, vd)
     resid, normed_two = run_mid(tok, ctx, w_all, gain_two, width // d)
 
@@ -1211,81 +1284,83 @@
     res = {}
     chain = (normed_two, [cots[step] for step in range(2, n_ex, 2)])
 
-    def experts(step, first, count, init=None):
-        x = after(xs[step], chain)
+    def experts(steps, first, count, init=None, sent=None):
+        x = [after(xs[steps[0]], chain), xs[steps[1]]]
+        cot_pair, route_pair = [cots[k] for k in steps], [route_set[k] for k in steps]
         return run_expert(
-            me, x, cots[step], route_set[step], w_all, *weights, first, count, num_experts, init
+            me, x, cot_pair, route_pair, w_all, *weights, first, count, num_experts, init, sent
         )
 
     def grads(first):
-        skips = [first if step < 2 else 0 for step in range(n_ex)]
-        pieces = [
-            [res[step, 0 if step < 2 else first][k] for step in range(n_ex)] for k in (4, 5, 3)
-        ]
-        turned = [[res[step, 0][k] for step in range(n_ex)] for k in (6, 7)]
-        turned[0][0] = after(turned[0][0], chain)
+        pairs = [res[k, 0] for k in range(0, n_ex, 2)]
+        wides = [res[0, 0]] + [res[k, first] for k in range(2, n_ex, 2)]
+        groups = [[pair["turned"][k] for pair in pairs] for k in (0, 1)]
+        groups += [[pair["wide"][k] for pair in wides] for k in (1, 2, 0)]
+        groups[0][0] = after(groups[0][0], chain)
+        skips = [first if k == 0 else 0 for k in range(len(pairs))]
         made = None
-        for at in range(0, n_ex, 4):
-            some = [group[at : at + 4] for group in turned + pieces]
-            part = run_weight_grad(dp, *some, half, skips[at : at + 4], n_dp, fast)
+        for at in range(0, len(pairs), 2):
+            some = [group[at : at + 2] for group in groups]
+            part = run_weight_grad(
+                dp, *some, half, skips[at : at + 2], n_dp, fast, expert_gate.shape[2]
+            )
             if made is None:
                 made = part
             else:
                 made = [(a.astype(F32) + b.astype(F32)).astype(BF16) for a, b in zip(made, part)]
         return made
 
-    for step in range(2):
-        res[step, 0] = experts(step, 0, local)
-        chain = (res[step, 0][0], tops[-1])
-        widen_top()
-        if step == 0:
-            for other in range(3, n_ex, 2):
-                cots[other] = swap(after(cots[other - 1], chain), 1)
-                xs[other] = swap(after(xs[other - 1], chain), 1)
-    odd, even = range(3, n_ex, 2), range(2, n_ex, 2)
-    for step in [*odd, *even]:
-        res[step, 0] = experts(step, 0, half)
-        chain = (res[step, 0][0], tops[-1])
+    res[0, 0] = experts((0, 1), 0, local)
+    chain = (res[0, 0]["dg"][0], tops[-1])
+    widen_top()
+    widen_top()
+    for other in range(3, n_ex, 2):
+        cots[other] = swap(after(cots[other - 1], chain), 1)
+        xs[other] = swap(after(xs[other - 1], chain), 1)
+    even = range(2, n_ex, 2)
+    for step in even:
+        res[step, 0] = experts((step, step + 1), 0, half)
+        chain = (res[step, 0]["dg"][0], tops[-1])
         widen_top()
     made_one = grads(0)
     chain = (made_one[0], tops[-1])
-    got_one = [swap(made_one[k], 1, "dp", n_dp) for k in (1, 3)] if fast else []
     widen_top()
-    for step in odd:
-        res[step, half] = experts(step, half, half, res[step, 0][:3])
-        chain = (res[step, half][0], tops[-1])
+    for step in even:
+        init = [*res[step, 0]["out"], *res[step, 0]["dx"], *res[step, 0]["dg"]]
+        sent = made_one[1] if fast else None
+        res[step, half] = experts((step, step + 1), half, half, init, sent)
+        chain = (res[step, half]["dg"][0], tops[-1])
         widen_top()
-    partner = {step - 1: [swap(res[step, half][k], 1) for k in (0, 1)] for step in odd}
-    for step in even:
-        res[step, half] = experts(step, half, half, res[step, 0][:3])
-        chain = (res[step, half][0], tops[-1])
-        widen_top()
-
-    def with_partner(step, index):
-        own, other = res[step, half][index], partner[step][index]
-        return (own.astype(F32) + other.astype(F32)).astype(BF16)
-
-    to_send = {step: with_partner(step, 1) for step in even}
+
+    def with_partner(step, what):
+        own, other = res[step, half][what]
+        return (own.astype(F32) + swap(other, 1).astype(F32)).astype(BF16)
+
+    to_send = {step: with_partner(step, "dx") for step in even}
     chain = (chain, list(to_send.values()))
     sums, got_two = None, []
     if fast:
+        down_sent = after(made_one[3], chain)
+        got_one = [res[2, half]["got"][0], swap(down_sent, 1, "dp", n_dp)]
         tot_one = (made_one[0].astype(F32) + got_one[0].astype(F32)).astype(BF16)
         far_one = lax.dynamic_slice_in_dim(tot_one, 2 * (1 - dp[0] // 4), 2, axis=0)
         chain = (chain, far_one)
         far_one = lax.ppermute(far_one, "dp", [(0, 2), (1, 3), (6, 4), (7, 5)])
     made_two = grads(half)
-    chain = (made_two[0], got_one, tops[-1])
+    chain = (made_two[0], tops[-1])
     if fast:
-        chain = (chain, far_one)
+        chain = (chain, far_one, got_one)
         sums = [tot_one, far_one, made_one[2], got_one[1]]
         got_two = [swap(made_two[k], 1, "dp", n_dp) for k in (1, 3)]
     while len(tops) <= len(bits):
         widen_top()
     top = tops[-1]
 
-    last = [res[step, 0 if step < 2 else half] for step in range(n_ex)]
-    dxs = [last[0][1], swap(last[1][1], 1)] + [swap(to_send[step], step) for step in even]
-    dgs = [last[0][2]] + [swap(last[step][2], step) for step in range(1, n_ex)]
+    final = [res[0, 0]] + [res[step, half] for step in even]
+    dxs = [final[0]["dx"][0], swap(final[0]["dx"][1], 1)]
+    dxs += [swap(to_send[step], step) for step in even]
+    dgs = [part for pair in final for part in pair["dg"]]
+    dgs = [swap(dgs[step], step) if step else dgs[0] for step in range(n_ex)]
     d_res, d_attn, d_ctx, d_logits, d_gain_two = run_back_mid(
         me,
         after(resid, chain),
@@ -1299,8 +1374,8 @@
         dgs,
         local,
     )
-    outs = [last[0][0], swap(last[1][0], 1)]
-    outs += [swap(after(with_partner(step, 0), dxs), step) for step in even]
+    outs = [final[0]["out"][0], swap(final[0]["out"][1], 1)]
+    outs += [swap(after(with_partner(step, "out"), dxs), step) for step in even]
     block = resid
     for piece in outs:
         block = block + piece.astype(F32)
@@ -1350,17 +1425,14 @@
     y_bits = [("expert", n_ex, 1 << i) for i in range(1, n_ex.bit_length() - 1)][::-1]
     dp_bits = [("dp", n_dp, 1 << i) for i in range(n_dp.bit_length() - 1)]
     if fast:
-        every_grad, *others = run_finish(
+        grad_out, grad_query, grad_keyval, rest, grad_gate, grad_up, grad_down = run_finish(
             normed_one_t,
             dq,
             dk,
             dv,
             d_out_w,
             small_grad,
-            [made_two[0], got_two[0], made_two[2], got_two[1]],
-        )
-        grad_gate, grad_up, grad_down = (
-            jnp.concatenate([halves[k], others[k]], axis=0) for k in range(3)
+            [made_two[0], got_two[0], made_two[2], got_two[1], *halves],
         )
     else:
         ends = [
@@ -1382,12 +1454,13 @@
             [d_out_w, product(dq), product(dk), product(dv), small_grad], axis=1
         )
         every_grad = share(reduce_all(every_grad, core + y_bits + dp_bits[::-1]))
-    grad_out = every_grad[:, :d]
-    grad_query = every_grad[:, d : d + nq]
-    grad_keyval = every_grad[:, d + nq : d + 2 * nq]
-    grad_router = every_grad[:, d + 2 * nq : d + 2 * nq + num_experts]
-    grad_gain_one = every_grad[:, d + 2 * nq + num_experts]
-    grad_gain_two = every_grad[:, d + 2 * nq + num_experts + 1]
+        grad_out = every_grad[:, :d]
+        grad_query = every_grad[:, d : d + nq]
+        grad_keyval = every_grad[:, d + nq : d + 2 * nq]
+        rest = every_grad[:, d + 2 * nq :]
+    grad_router = rest[:, :num_experts]
+    grad_gain_one = rest[:, num_experts]
+    grad_gain_two = rest[:, num_experts + 1]
 
     head_logit_peak = top[:, 0, :].reshape(heads)
     per_group = heads // kv_heads

time: 589 us -> 575 us (0.976)
  Pallas kernels: 497 us -> 481 us
  local copies, waits for them, and re-layouts: 14.7 us -> 22.9 us
    pallas_call x6 -> x3, Pallas kernels: 192 us -> 175 us  [run_expert(): pl.pallas_call(functools.partial(expert_kernel, first, local, num_experts...]
    unnamed x58 -> x66, local copies, waits for them, and re-layouts: 2.2 us -> 13.8 us
    ppermute x27 -> x26, waiting for transfers between devices: 14.9 us -> 12.6 us  [swap(): return lax.ppermute(value, axis, [(i, i ^ step) for i in range(n)])]
    ppermute x27 -> x26, starting transfers between devices: 19.5 us -> 18 us  [swap(): return lax.ppermute(value, axis, [(i, i ^ step) for i in range(n)])]
  transfers between devices with their start and end apart: 28 -> 27, of which waited for: 5 -> 5; matrix products, arithmetic and copies ran while one was open for 5% -> 5% of each run, Pallas kernels for 62% -> 43%
where the time goes in v5:
time: 575 us; the launch traced here: 568 us
  Pallas kernels  481 us (84%)
  local copies, waits for them, and re-layouts  22.9 us (4%)
  starting transfers between devices  21.6 us (4%)
  other arithmetic  20.4 us (4%)
  waiting for transfers between devices  12.6 us (2%)
  matrix products  7.2 us (1%)
    pallas_call x3, Pallas kernels, run_expert(): pl.pallas_call(functools.partial(expert_kernel, first, local, num_experts...  175 us
    pallas_call x1, Pallas kernels, run_finish(): pl.pallas_call(finish_kernel, in_specs=[vmem] * 6 + [hbm] * 7, out_specs=...  82.4 us
    pallas_call x2, Pallas kernels, run_weight_grad(): pl.pallas_call(functools.partial(weight_grad_kernel, n, paired), grid=(co...  72.3 us
    pallas_call x1, Pallas kernels, run_attn_bwd(): pl.pallas_call(kernel, grid=(groups,), in_specs=in_specs, out_specs=out_s...  45.9 us
    pallas_call x1, Pallas kernels, run_gather(): pl.pallas_call(gather_kernel, in_specs=[hbm], out_specs=hbm, out_shape=ja...  43.5 us
    pallas_call x1, Pallas kernels, run_attn_fwd(): pl.pallas_call(attn_fwd_kernel, grid=(groups,), in_specs=[pl.BlockSpec(me...  21.4 us
    ppermute x26, starting transfers between devices, swap(): return lax.ppermute(value, axis, [(i, i ^ step) for i in range(n)])  18 us
    unnamed x66, local copies, waits for them, and re-layouts  13.8 us
  transfers between devices with their start and end apart: 27, of which 5 were waited for; matrix products, arithmetic and copies ran while one was open for 5% of the time, Pallas kernels for 43%

profile of v5, /device:TPU:0, one launch (start us, length us, event | category | flops | bytes accessed | tf_op | source)
XLA Modules:
  0.0 567.8 jit_solution(1200985804635679419)
XLA Ops:
  5.1 43.5 %gather.1.w_ref.refs_1_.refs_5_.refs_7_ = bf16[1024,3200]{1,0:T(8,128)(2,1)} custom-call(bf16[32,3200]{1,0:T(8,128)(2,1)} %constant_dynamic-slice_fusion.1.mine_ref), custom_call_target="tpu_custom_call" | custom-call | flops 14000000000 | bytes 1000 | tf_op jit(solution)/shard_map/gather/pallas_call | solution.py:1181
  53.4 10.0 %qkv.1 = (bf16[1024,1024]{1,0:T(8,128)(2,1)}, bf16[1024,1024]{1,0:T(8,128)(2,1)}, bf16[1024,1024]{1,0:T(8,128)(2,1)}, bf16[1024,1024]{1,0:T(8,128)(2,1)}) custom-call(bf16[1024,1024]{1,0:T(8,128)(2,1)} %bitcast.24, bf16[1,1024]{1,0:T(2,128)(2,1)} %reshape_squeeze.9.gain_ref, bf16[1024,3200]{1,0:T(8,128)(2,1)} %gather.1.w_ref.refs_1_.refs_5_.refs_7_, ...), custom_call_target="tpu_custom_call" | custom-call | flops 3150000128 | bytes 1000 | tf_op jit(solution)/shard_map/qkv/pallas_call | solution.py:101
  63.4 21.4 %attn_fwd.1 = (bf16[1024,1024]{1,0:T(8,128)(2,1)}, f32[4,8,1024]{2,1,0:T(8,128)}, f32[4,8,128]{2,1,0:T(8,128)}) custom-call(s32[1]{0:T(128)S(6)} %copy.51.prefix_ref.refs_0_, bf16[1024,1024]{1,0:T(8,128)(2,1)} %get-tuple-element.149.q_ref.refs_1_, bf16[1024,1024]{1,0:T(8,128)(2,1)} %get-tuple-element.102.kd_ref.refs_2_, ...), custom_call_target="tpu_custom_call" | custom-call | flops 7350000128 | bytes 1000 | tf_op jit(solution)/shard_map/attn_fwd/pallas_call | solution.py:176
  84.8 7.3 %mid.1 = (f32[1024,1024]{1,0:T(8,128)}, bf16[1024,1024]{1,0:T(8,128)(2,1)}) custom-call(bf16[1024,1024]{1,0:T(8,128)(2,1)} %bitcast.25, bf16[1024,1024]{1,0:T(8,128)(2,1)} %get-tuple-element.104.ctx_ref.refs_5_, bf16[1024,3200]{1,0:T(8,128)(2,1)} %gather.1.w_ref.refs_1_.refs_5_.refs_7_, bf16[1,1024]{1,0:T(2,128)(2,1)} %reshape_squeeze.10.gain_ref.refs_6_), custom_call_target="tpu_custom_call" | custom-call | flops 1400000000 | bytes 1000 | tf_op jit(solution)/shard_map/mid/pallas_call | solution.py:495
  93.3 3.8 collective-permute-done.refs_7_
  97.1 2.2 collective-permute-done.3.refs_10_
  102.0 75.9 %experts.3 = (bf16[1024,1024]{1,0:T(8,128)(2,1)}, bf16[1024,1024]{1,0:T(8,128)(2,1)}, bf16[1024,1024]{1,0:T(8,128)(2,1)}, bf16[1024,1024]{1,0:T(8,128)(2,1)}, f3...) custom-call(s32[1]{0:T(128)} %bitcast.3.refs_0_, ...), custom_call_target="tpu_custom_call" | custom-call | flops 33600000000 | bytes 1000 | tf_op jit(solution)/shard_map/experts/pallas_call | solution.py:661
  182.8 3.2 collective-permute-done.11
  186.6 44.2 %experts.4 = (bf16[1024,1024]{1,0:T(8,128)(2,1)}, bf16[1024,1024]{1,0:T(8,128)(2,1)}, bf16[1024,1024]{1,0:T(8,128)(2,1)}, bf16[1024,1024]{1,0:T(8,128)(2,1)}, f3...) custom-call(s32[1]{0:T(128)} %bitcast.3.refs_0_, ...), custom_call_target="tpu_custom_call" | custom-call | flops 16800000000 | bytes 1000 | tf_op jit(solution)/shard_map/experts/pallas_call | solution.py:661
  231.5 36.0 %weight_grad.2 = (bf16[4,2,2,128,512]{4,3,2,1,0:T(8,128)(2,1)}, bf16[4,2,2,128,512]{4,3,2,1,0:T(8,128)(2,1)}, bf16[4,2,128,512]{3,2,1,0:T(8,128)(2,1)}, bf16[4,2,128,512]{3,2,1,0:T(8,128)(2,1)}) custom-call(s32[1]{0:T(128)} %bitcast.8.dp_ref, bf16[1024,2048]{1,0:T(8,128)(2,1)} %get-tuple-element.151.refs_0_, bf16[1024,2048]{1,0:T(8,128)(2,1)} %get-tuple-element.121.refs_1_, ...), custom_call_target="tpu_custom_call" | custom-call | flops 12949999616 | bytes 1000 | tf_op jit(solution)/shard_map/weight_grad/pallas_call | solution.py:771
  267.5 54.4 %experts.5 = (bf16[1024,1024]{1,0:T(8,128)(2,1)}, bf16[1024,1024]{1,0:T(8,128)(2,1)}, bf16[1024,1024]{1,0:T(8,128)(2,1)}, bf16[1024,1024]{1,0:T(8,128)(2,1)}, f3...) custom-call(s32[1]{0:T(128)} %bitcast.3.refs_0_, ...), custom_call_target="tpu_custom_call" | custom-call | flops 16800000000 | bytes 1000 | tf_op jit(solution)/shard_map/experts/pallas_call | solution.py:661
  324.0 2.9 add_convert_fusion.refs_11_
  328.6 3.6 collective-permute-start.20
  332.4 3.9 add_convert_fusion.2
  340.7 36.3 %weight_grad.3 = (bf16[4,2,2,128,512]{4,3,2,1,0:T(8,128)(2,1)}, bf16[4,2,2,128,512]{4,3,2,1,0:T(8,128)(2,1)}, bf16[4,2,128,512]{3,2,1,0:T(8,128)(2,1)}, bf16[4,2,128,512]{3,2,1,0:T(8,128)(2,1)}) custom-call(s32[1]{0:T(128)} %bitcast.8.dp_ref, bf16[1024,2048]{1,0:T(8,128)(2,1)} %get-tuple-element.151.refs_0_, bf16[1024,2048]{1,0:T(8,128)(2,1)} %get-tuple-element.121.refs_1_, ...), custom_call_target="tpu_custom_call" | custom-call | flops 12949999616 | bytes 1000 | tf_op jit(solution)/shard_map/weight_grad/pallas_call | solution.py:771
  379.0 3.9 add_convert_fusion.3
  389.4 12.2 %back_mid.1 = (f32[1024,1024]{1,0:T(8,128)}, bf16[1024,1024]{1,0:T(8,128)(2,1)}, bf16[1024,1024]{1,0:T(8,128)(2,1)}, bf16[1024,128]{1,0:T(8,128)(2,1)}, f32[1,1024]{1,0:T(1,128)}) custom-call(s32[1]{0:T(128)} %bitcast.3.refs_0_, f32[1024,1024]{1,0:T(8,128)} %get-tuple-element.158.refs_1_, bf16[1024,1024]{1,0:T(8,128)(2,1)} %bitcast.28, s32[8,1024]{1,0:T(8,128)} %bitcast.34, ...), custom_call_target="tpu_custom_call" | custom-call | flops 3849999872 | bytes 1000 | tf_op jit(solution)/shard_map/back_mid/pallas_call | solution.py:828
  404.3 45.9 %attn_bwd.1 = (bf16[1024,1024]{1,0:T(8,128)(2,1)}, bf16[1024,512]{1,0:T(8,128)(2,1)}, bf16[1024,512]{1,0:T(8,128)(2,1)}, f32[2,128,512]{2,1,0:T(8,128)}, f32[2,128,512]{2,1,0:T(8,128)}, /*index=5*/f32[2,64,1024]{2,1,0:T(8,128)}) custom-call(s32[1]{0:T(128)S(6)} %copy.51.prefix_ref.refs_0_, bf16[1024,1024]{1,0:T(8,128)(2,1)} %get-tuple-element.149.q_ref.refs_1_, ...), custom_call_target="tpu_custom_call" | custom-call | flops 11550000128 | bytes 1000 | tf_op jit(solution)/shard_map/attn_bwd/pallas_call | solution.py:469
  450.3 5.5 convolution_convert_fusion.dout_ref
  455.8 5.2 fusion
  461.0 11.3 %back_in.1 = (f32[1024,1024]{1,0:T(8,128)}, f32[1,1024]{1,0:T(1,128)}) custom-call(bf16[1024,1024]{1,0:T(8,128)(2,1)} %get-tuple-element.167.dq_ref, bf16[1024,512]{1,0:T(8,128)(2,1)} %get-tuple-element.168.dk_ref, bf16[1024,512]{1,0:T(8,128)(2,1)} %get-tuple-element.169.dv_ref, bf16[1024,3200]{1,0:T(8,128)(2,1)} %gather.1.w_ref.refs_1_.refs_5_.refs_7_, ...), custom_call_target="tpu_custom_call" | custom-call | flops 3500000000 | bytes 1000 | tf_op jit(solution)/shard_map/back_in/pallas_call | solution.py:887
  474.1 82.4 %finish.1 = (f32[128,1024]{1,0:T(8,128)}, f32[128,1024]{1,0:T(8,128)}, f32[128,1024]{1,0:T(8,128)}, f32[128,128]{1,0:T(8,128)}, f32[4,128,512]{2,1,0:T(8,128)}, ...) custom-call(bf16[1024,1024]{1,0:T(8,128)(2,1)} %get-tuple-element.172.ht_ref, ...), custom_call_target="tpu_custom_call" | custom-call | flops 20999999488 | bytes 1000 | tf_op jit(solution)/shard_map/finish/pallas_call | solution.py:1086
  559.8 1.9 copy.52
  561.6 2.0 copy.53
  (151 shorter events, 46.6 us)
Async XLA Ops:
  48.6 48.6 %collective-permute-start = (bf16[1024,1024]{1,0:T(8,128)(2,1)S(1)}, bf16[1024,1024]{1,0:T(8,128)(2,1)}, u32[]{:S(2)}, u32[]{:S(2)}) collective-permute-start(bf16[1024,1024]{1,0:T(8,128)(2,1)S(1)} %bitcast.29), channel_id=1, source_target_pairs={{0,2},{1,3},{2,0},{3,1},{4,6},{5,7},{6,4},{7,5},{8,10},{9,11},{10,... | collective-permute-start | bytes 6291464 | tf_op jit(solution)/shard_map/ppermute | solution.py:1218
  92.1 7.2 %collective-permute-start.1 = (bf16[1024,1024]{1,0:T(8,128)(2,1)}, bf16[1024,1024]{1,0:T(8,128)(2,1)S(1)}, u32[]{:S(2)}, u32[]{:S(2)}) collective-permute-start(bf16[1024,1024]{1,0:T(8,128)(2,1)} %get-tuple-element.108.refs_5_.refs_4_), channel_id=1, source_target_pairs={{0,1},{1,0},{2,3},{3,2},{4,5},{5,4},{6,7},{7,6},{8,9},{9,8},{10,11... | collective-permute-start | bytes 6291464 | tf_op jit(solution)/shard_map/ppermute | solution.py:1218
  92.2 7.1 %collective-permute-start.2 = (bf16[1024,1024]{1,0:T(8,128)(2,1)S(1)}, bf16[1024,1024]{1,0:T(8,128)(2,1)S(1)}, u32[]{:S(2)}, u32[]{:S(2)}) collective-permute-start(bf16[1024,1024]{1,0:T(8,128)(2,1)S(1)} %bitcast.30), channel_id=1, source_target_pairs={{0,1},{1,0},{2,3},{3,2},{4,5},{5,4},{6,7},{7,6},{8,9},{9,8},{10,11... | collective-permute-start | bytes 6291464 | tf_op jit(solution)/shard_map/ppermute | solution.py:1218
  92.6 6.7 %collective-permute-start.3 = (s32[8,1024]{1,0:T(8,128)S(1)}, s32[8,1024]{1,0:T(8,128)S(1)}, u32[]{:S(2)}, u32[]{:S(2)}) collective-permute-start(s32[8,1024]{1,0:T(8,128)S(1)} %bitcast.35), channel_id=1, source_target_pairs={{0,1},{1,0},{2,3},{3,2},{4,5},{5,4},{6,7},{7,6},{8,9},{9,8},{10,11... | collective-permute-start | bytes 98312 | tf_op jit(solution)/shard_map/ppermute | solution.py:1218
  92.7 85.4 %collective-permute-start.5 = (bf16[1024,1024]{1,0:T(8,128)(2,1)}, bf16[1024,1024]{1,0:T(8,128)(2,1)}, u32[]{:S(2)}, u32[]{:S(2)}) collective-permute-start(bf16[1024,1024]{1,0:T(8,128)(2,1)} %get-tuple-element.108.refs_5_.refs_4_), channel_id=1, source_target_pairs={{0,2},{1,3},{2,0},{3,1},{4,6},{5,7},{6,4},{7,5},{8,10},{9,11},{10,... | collective-permute-start | bytes 6291464 | tf_op jit(solution)/shard_map/ppermute | solution.py:1218
  178.0 8.1 %collective-permute-start.7 = (bf16[1024,1024]{1,0:T(8,128)(2,1)}, bf16[1024,1024]{1,0:T(8,128)(2,1)}, u32[]{:S(2)}, u32[]{:S(2)}) collective-permute-start(bf16[1024,1024]{1,0:T(8,128)(2,1)} %collective-permute-done.refs_7_), channel_id=1, source_target_pairs={{0,1},{1,0},{2,3},{3,2},{4,5},{5,4},{6,7},{7,6},{8,9},{9,8},{10,11... | collective-permute-start | bytes 6291464 | tf_op jit(solution)/shard_map/ppermute | solution.py:1218
  178.2 7.9 %collective-permute-start.6 = (bf16[1024,1024]{1,0:T(8,128)(2,1)}, bf16[1024,1024]{1,0:T(8,128)(2,1)}, u32[]{:S(2)}, u32[]{:S(2)}) collective-permute-start(bf16[1024,1024]{1,0:T(8,128)(2,1)} %collective-permute-done.5.refs_5_), channel_id=1, source_target_pairs={{0,1},{1,0},{2,3},{3,2},{4,5},{5,4},{6,7},{7,6},{8,9},{9,8},{10,11... | collective-permute-start | bytes 6291464 | tf_op jit(solution)/shard_map/ppermute | solution.py:1218
  178.6 7.4 %collective-permute-start.8 = (s32[8,1024]{1,0:T(8,128)S(1)}, s32[8,1024]{1,0:T(8,128)S(1)}, u32[]{:S(2)}, u32[]{:S(2)}) collective-permute-start(s32[8,1024]{1,0:T(8,128)S(1)} %bitcast.36), channel_id=1, source_target_pairs={{0,2},{1,3},{2,0},{3,1},{4,6},{5,7},{6,4},{7,5},{8,10},{9,11},{10,... | collective-permute-start | bytes 98312 | tf_op jit(solution)/shard_map/ppermute | solution.py:1218
  179.1 6.9 %collective-permute-start.9 = (s32[8,1024]{1,0:T(8,128)S(1)}, s32[8,1024]{1,0:T(8,128)S(1)}, u32[]{:S(2)}, u32[]{:S(2)}) collective-permute-start(s32[8,1024]{1,0:T(8,128)S(1)} %bitcast.37), channel_id=1, source_target_pairs={{0,3},{1,2},{2,1},{3,0},{4,7},{5,6},{6,5},{7,4},{8,11},{9,10},{10,... | collective-permute-start | bytes 98312 | tf_op jit(solution)/shard_map/ppermute | solution.py:1218
  230.9 36.6 %collective-permute-start.12 = (f32[4,8,4]{2,1,0:T(8,128)S(1)}, f32[4,8,4]{2,1,0:T(8,128)S(1)}, u32[]{:S(2)}, u32[]{:S(2)}) collective-permute-start(f32[4,8,4]{2,1,0:T(8,128)S(1)} %max.22), channel_id=1, source_target_pairs={{0,4},{4,0},{8,12},{12,8},{16,20},{20,16},{24,28},{28,24},{1,5},{5... | collective-permute-start | bytes 1544 | tf_op jit(solution)/shard_map/ppermute | solution.py:1218
  321.9 10.5 %collective-permute-start.15 = (bf16[1024,1024]{1,0:T(8,128)(2,1)}, bf16[1024,1024]{1,0:T(8,128)(2,1)}, u32[]{:S(2)}, u32[]{:S(2)}) collective-permute-start(bf16[1024,1024]{1,0:T(8,128)(2,1)} %get-tuple-element.144), channel_id=1, source_target_pairs={{0,1},{1,0},{2,3},{3,2},{4,5},{5,4},{6,7},{7,6},{8,9},{9,8},{10,11... | collective-permute-start | bytes 6291464 | tf_op jit(solution)/shard_map/ppermute | solution.py:1218
  322.3 60.6 %collective-permute-start.14 = (bf16[1024,1024]{1,0:T(8,128)(2,1)}, bf16[1024,1024]{1,0:T(8,128)(2,1)}, u32[]{:S(2)}, u32[]{:S(2)}) collective-permute-start(bf16[1024,1024]{1,0:T(8,128)(2,1)} %get-tuple-element.142), channel_id=1, source_target_pairs={{0,1},{1,0},{2,3},{3,2},{4,5},{5,4},{6,7},{7,6},{8,9},{9,8},{10,11... | collective-permute-start | bytes 6291464 | tf_op jit(solution)/shard_map/ppermute | solution.py:1218
  326.9 5.2 collective-permute-start.19
  328.6 48.4 %collective-permute-start.20 = (bf16[2,2,2,128,512]{4,3,2,1,0:T(8,128)(2,1)S(1)}, bf16[2,2,2,128,512]{4,3,2,1,0:T(8,128)(2,1)}, u32[]{:S(2)}, u32[]{:S(2)}) collective-permute-start(bf16[2,2,2,128,512]{4,3,2,1,0:T(8,128)(2,1)S(1)} %constant_dynamic-slice_fusion), channel_id=1, source_target_pairs={{0,8},{4,12},{24,16},{28,20},{1,9},{5,13},{25,17},{29,21},{2,10},{... | collective-permute-start | bytes 3145736 | tf_op jit(solution)/shard_map/ppermute | solution.py:1348
  332.2 44.9 %collective-permute-start.13 = (bf16[1024,1024]{1,0:T(8,128)(2,1)}, bf16[1024,1024]{1,0:T(8,128)(2,1)}, u32[]{:S(2)}, u32[]{:S(2)}) collective-permute-start(bf16[1024,1024]{1,0:T(8,128)(2,1)} %get-tuple-element.140), channel_id=1, source_target_pairs={{0,1},{1,0},{2,3},{3,2},{4,5},{5,4},{6,7},{7,6},{8,9},{9,8},{10,11... | collective-permute-start | bytes 6291464 | tf_op jit(solution)/shard_map/ppermute | solution.py:1218
  336.3 48.7 %collective-permute-start.16 = (bf16[1024,1024]{1,0:T(8,128)(2,1)}, bf16[1024,1024]{1,0:T(8,128)(2,1)}, u32[]{:S(2)}, u32[]{:S(2)}) collective-permute-start(bf16[1024,1024]{1,0:T(8,128)(2,1)} %add_convert_fusion.2), channel_id=1, source_target_pairs={{0,2},{1,3},{2,0},{3,1},{4,6},{5,7},{6,4},{7,5},{8,10},{9,11},{10,... | collective-permute-start | bytes 6291464 | tf_op jit(solution)/shard_map/ppermute | solution.py:1218
  340.3 38.0 %collective-permute-start.21 = (bf16[4,2,128,512]{3,2,1,0:T(8,128)(2,1)}, bf16[4,2,128,512]{3,2,1,0:T(8,128)(2,1)}, u32[]{:S(2)}, u32[]{:S(2)}) collective-permute-start(bf16[4,2,128,512]{3,2,1,0:T(8,128)(2,1)} %get-tuple-element.157), channel_id=1, source_target_pairs={{0,4},{4,0},{8,12},{12,8},{16,20},{20,16},{24,28},{28,24},{1,5},{5... | collective-permute-start | bytes 3145736 | tf_op jit(solution)/shard_map/ppermute | solution.py:1218
  377.0 9.2 %collective-permute-start.22 = (f32[8,1024]{1,0:T(8,128)S(1)}, f32[8,1024]{1,0:T(8,128)S(1)}, u32[]{:S(2)}, u32[]{:S(2)}) collective-permute-start(f32[8,1024]{1,0:T(8,128)S(1)} %copy-done.23), channel_id=1, source_target_pairs={{0,1},{1,0},{2,3},{3,2},{4,5},{5,4},{6,7},{7,6},{8,9},{9,8},{10,11... | collective-permute-start | bytes 98312 | tf_op jit(solution)/shard_map/ppermute | solution.py:1218
  377.1 10.0 %collective-permute-start.23 = (f32[8,1024]{1,0:T(8,128)S(1)}, f32[8,1024]{1,0:T(8,128)S(1)}, u32[]{:S(2)}, u32[]{:S(2)}) collective-permute-start(f32[8,1024]{1,0:T(8,128)S(1)} %copy-done.25), channel_id=1, source_target_pairs={{0,2},{1,3},{2,0},{3,1},{4,6},{5,7},{6,4},{7,5},{8,10},{9,11},{10,... | collective-permute-start | bytes 98312 | tf_op jit(solution)/shard_map/ppermute | solution.py:1218
  378.3 10.5 %collective-permute-start.24 = (f32[8,1024]{1,0:T(8,128)S(1)}, f32[8,1024]{1,0:T(8,128)S(1)}, u32[]{:S(2)}, u32[]{:S(2)}) collective-permute-start(f32[8,1024]{1,0:T(8,128)S(1)} %copy-done.24), channel_id=1, source_target_pairs={{0,3},{1,2},{2,1},{3,0},{4,7},{5,6},{6,5},{7,4},{8,11},{9,10},{10,... | collective-permute-start | bytes 98312 | tf_op jit(solution)/shard_map/ppermute | solution.py:1218
  382.9 72.9 %collective-permute-start.4 = (bf16[1024,1024]{1,0:T(8,128)(2,1)}, bf16[1024,1024]{1,0:T(8,128)(2,1)}, u32[]{:S(2)}, u32[]{:S(2)}) collective-permute-start(bf16[1024,1024]{1,0:T(8,128)(2,1)} %get-tuple-element.111), channel_id=1, source_target_pairs={{0,1},{1,0},{2,3},{3,2},{4,5},{5,4},{6,7},{7,6},{8,9},{9,8},{10,11... | collective-permute-start | bytes 6291464 | tf_op jit(solution)/shard_map/ppermute | solution.py:1218
  385.1 75.9 %collective-permute-start.25 = (bf16[4,2,2,128,512]{4,3,2,1,0:T(8,128)(2,1)}, bf16[4,2,2,128,512]{4,3,2,1,0:T(8,128)(2,1)}, u32[]{:S(2)}, u32[]{:S(2)}) collective-permute-start(bf16[4,2,2,128,512]{4,3,2,1,0:T(8,128)(2,1)} %get-tuple-element.165), channel_id=1, source_target_pairs={{0,4},{4,0},{8,12},{12,8},{16,20},{20,16},{24,28},{28,24},{1,5},{5... | collective-permute-start | bytes 6291464 | tf_op jit(solution)/shard_map/ppermute | solution.py:1218
  386.2 74.8 %collective-permute-start.26 = (bf16[4,2,128,512]{3,2,1,0:T(8,128)(2,1)}, bf16[4,2,128,512]{3,2,1,0:T(8,128)(2,1)}, u32[]{:S(2)}, u32[]{:S(2)}) collective-permute-start(bf16[4,2,128,512]{3,2,1,0:T(8,128)(2,1)} %get-tuple-element.166), channel_id=1, source_target_pairs={{0,4},{4,0},{8,12},{12,8},{16,20},{20,16},{24,28},{28,24},{1,5},{5... | collective-permute-start | bytes 3145736 | tf_op jit(solution)/shard_map/ppermute | solution.py:1218
  387.1 68.6 %collective-permute-start.17 = (bf16[1024,1024]{1,0:T(8,128)(2,1)}, bf16[1024,1024]{1,0:T(8,128)(2,1)}, u32[]{:S(2)}, u32[]{:S(2)}) collective-permute-start(bf16[1024,1024]{1,0:T(8,128)(2,1)} %add_convert_fusion.3), channel_id=1, source_target_pairs={{0,2},{1,3},{2,0},{3,1},{4,6},{5,7},{6,4},{7,5},{8,10},{9,11},{10,... | collective-permute-start | bytes 6291464 | tf_op jit(solution)/shard_map/ppermute | solution.py:1218
  (32 other events, 576.3 us)

commit v6 on v5

--- a/solution.py
+++ b/solution.py
@@ -196,10 +196,10 @@
 def add_rows(dst, srcs, step=64):
     def body(i, carry):
         at = pl.ds(pl.multiple_of(i * step, step), step)
-        total = srcs[0][at, :].astype(F32)
-        for src in srcs[1:]:
-            total = total + src[at, :].astype(F32)
-        dst[at, :] = total.astype(dst.dtype)
+        one, two = srcs[0][at, :], srcs[1][at, :]
+        if dst.dtype != one.dtype:
+            one, two = one.astype(dst.dtype), two.astype(dst.dtype)
+        dst[at, :] = one + two
         return carry
 
     lax.fori_loop(0, dst.shape[0] // step, body, 0)
@@ -249,7 +249,8 @@
         def _():
             if inward:
                 self.copy(ch, 1).start()
-            self.copy(ch, 3).start()
+            else:
+                self.copy(ch, 3).start()
 
     def middle_sends(self, ch, inward):
         @pl.when(self.inner)
@@ -259,18 +260,19 @@
             self.add(ch, 2 * (1 - self.upper), self.rz1)
             self.copy(ch, 2).start()
 
-    def middle_adds(self, ch, inward):
+        if inward:
+
+            @pl.when(self.outer)
+            def _():
+                self.copy(ch, 1).wait_send()
+                self.copy(ch, 3).start()
+
+    def middle_adds(self, ch):
         @pl.when(self.inner)
         def _():
             self.copy(ch, 2).wait()
             self.add(ch, 2 * self.upper, self.rz2)
             self.copy(ch, 3).start()
-
-        if inward:
-
-            @pl.when(self.outer)
-            def _():
-                self.copy(ch, 1).wait_send()
 
     def result(self, ch, refs):
         self.copy(ch, 3).wait()
@@ -302,11 +304,36 @@
 
 
 def attn_bwd_sum_kernel(*refs):
-    ins, (tot_a, far_a, keep_a, got_a) = refs[:11], refs[11:15]
-    outs, (gate_ref, up_ref, down_ref) = refs[15:18], refs[18:21]
-    scratch, line_refs, (rx, sem_l) = refs[21:24], refs[24:30], refs[30:]
+    ins, (tot_a, far_a, keep_a, got_a, peak_ref) = refs[:11], refs[11:16]
+    outs, (gate_ref, up_ref, down_ref, top_ref) = refs[16:19], refs[19:23]
+    scratch, line_refs, (rx, sem_l, top_s, top_r, sem_ts, sem_tr) = refs[23:26], refs[26:32], refs[32:]
     step = pl.program_id(0)
     line = Line(*line_refs)
+    dp, ex = lax.axis_index("dp"), lax.axis_index("expert")
+    bits = [(dp, ex ^ 1), (dp, ex ^ 2), (dp ^ 1, ex), (dp ^ 2, ex), (dp ^ 4, ex)]
+
+    def top_copy(k):
+        return pltpu.make_async_remote_copy(
+            src_ref=top_s.at[k],
+            dst_ref=top_r.at[k],
+            send_sem=sem_ts.at[k],
+            recv_sem=sem_tr.at[k],
+            device_id=bits[k],
+            device_id_type=pl.DeviceIdType.MESH,
+        )
+
+    def top_round(k):
+        if k == 0:
+            top_s[0] = peak_ref[...]
+        else:
+            top_copy(k - 1).wait()
+            both = jnp.maximum(top_s[k - 1], top_r[k - 1])
+            if k == len(bits):
+                top_ref[...] = both
+                return
+            top_s[k] = both
+        top_copy(k).start()
+
     loads = []
     for k in range(2):
         loads.append([pltpu.make_async_copy(tot_a.at[:, k], line.tot.at[k], sem_l.at[2 * k])])
@@ -324,7 +351,8 @@
         for group in loads:
             for copy in group:
                 copy.start()
-        greet([line.near, line.middle])
+        greet(bits + [line.middle])
+        top_round(0)
         for copy in loads[2]:
             copy.wait()
         for zz in range(4):
@@ -338,22 +366,33 @@
             line.ends(k, False)
             line.middle_sends(k, False)
 
+    @pl.when(step == 3)
+    def _():
+        top_round(4)
+
     attn_bwd_body(*ins, *outs, *scratch)
+
+    @pl.when(step == 0)
+    def _():
+        top_round(1)
 
     @pl.when(step == 1)
     def _():
+        top_round(2)
         line.middle_sends(2, True)
-        line.middle_adds(0, False)
+        line.middle_adds(0)
 
     @pl.when(step == 2)
     def _():
-        line.middle_adds(1, False)
+        top_round(3)
+        line.middle_adds(1)
 
     @pl.when(step == 3)
     def _():
-        line.middle_adds(2, True)
+        line.middle_adds(2)
         for ch in range(3):
             line.result(ch, (gate_ref, up_ref, down_ref))
+        top_round(5)
 
 
 def attn_bwd_body(
@@ -457,13 +496,19 @@
         keep_a = sums[2]
         _, count, rows, lanes = keep_a.shape
         made = [(count, rows, lanes)] * 2 + [(count, rows // 2, 2 * lanes)]
-        in_specs += [hbm] * 4
+        peaks = sums[4]
+        made.append(peaks.shape)
+        in_specs += [hbm] * 4 + [whole(peaks.shape)]
         out_specs += [whole(shape) for shape in made]
         out_shape += [jax.ShapeDtypeStruct(shape, F32) for shape in made]
         scratch += line_scratch(keep_a.shape)
         scratch += [
             pltpu.VMEM(keep_a.shape, BF16),
             pltpu.SemaphoreType.DMA((6,)),
+            pltpu.VMEM((5,) + peaks.shape, F32),
+            pltpu.VMEM((5,) + peaks.shape, F32),
+            pltpu.SemaphoreType.DMA((5,)),
+            pltpu.SemaphoreType.DMA((5,)),
         ]
         args += tuple(sums)
     return pl.pallas_call(
@@ -908,15 +953,16 @@
 
 
 def finish_kernel(
-    ht_ref, dq_ref, dk_ref, dv_ref, dout_ref, small_ref, keep_ref, got_ref, down_keep_ref, down_got_ref,
-    gate_a, up_a, down_a, out_o, out_q, out_kv, out_small, gate_ref, up_ref, down_ref, *scratch,
+    gain_lane, ht_ref, dq_ref, dk_ref, dv_ref, dout_ref, small_ref, keep_ref, got_ref, down_keep_ref, down_got_ref,
+    gate_a, up_a, down_a, w_ref, tok_ref, gain_ref, dres_ref,
+    out_o, out_q, out_kv, out_small, gate_ref, up_ref, down_ref, gt_ref, *scratch,
 ):
     n = len(CHUNKS)
-    lists = [scratch[k * n : (k + 1) * n] for k in range(8)]
-    b1, r1, s1, r2, s2, r3, s3, r4 = lists
-    sem_s, sem_r = scratch[8 * n : 8 * n + 2]
-    line = Line(*scratch[8 * n + 2 : 8 * n + 8])
-    rx, sem_l = scratch[8 * n + 8 :]
+    lists = [scratch[k * n : (k + 1) * n] for k in range(7)]
+    b1, r1, r2, s2, r3, s3, r4 = lists
+    sem_s, sem_r = scratch[7 * n : 7 * n + 2]
+    line = Line(*scratch[7 * n + 2 : 7 * n + 8])
+    rx, sem_l, w_now, gt_now, gain_sum = scratch[7 * n + 8 :]
     count = gate_a.shape[0]
     halves = []
     for k, (src, dst) in enumerate(((gate_a, gate_ref), (up_a, up_ref), (down_a, down_ref))):
@@ -925,6 +971,9 @@
     dp, ex = lax.axis_index("dp"), lax.axis_index("expert")
     z, x, y, c = dp // 2, dp % 2, ex // 2, ex % 2
     over_core, over_y, over_x = (dp, ex ^ 1), (dp, ex ^ 2), (dp ^ 1, ex)
+    s1 = [ref.at[c] for ref in b1]
+    load_w = pltpu.make_async_copy(w_ref.at[:, : w_now.shape[1]], w_now, sem_l.at[9])
+    load_w.start()
     along = [(dp ^ (2 * k), ex) for k in (1, 2, 3)]
     group = [over_core, over_y, (dp, ex ^ 3)]
     loads = []
@@ -983,7 +1032,9 @@
             place(k, slice(0, half), dot(ht_ref[...], dk_ref[...]).astype(BF16))
             place(k, slice(half, 2 * half), dot(ht_ref[...], dv_ref[...]).astype(BF16))
         else:
-            place(k, slice(0, 128), small_ref[...])
+            turned = jnp.broadcast_to(gain_sum[...], (128, gain_sum.shape[1])).T.astype(BF16)
+            lane = lax.broadcasted_iota(jnp.int32, turned.shape, 1)
+            place(k, slice(0, 128), jnp.where(lane == gain_lane, turned, small_ref[...]))
         send(k, 0, b1[k].at[1 - c], r1[k], over_core)
 
     def step1(k):
@@ -991,24 +1042,20 @@
         for yy in range(2):
             for xx in range(2):
                 for zz in range(4):
-                    s1[k][yy, xx, zz] = (
-                        b1[k][c, yy, xx, zz].astype(F32) + r1[k][yy, xx, zz].astype(F32)
-                    ).astype(BF16)
+                    s1[k][yy, xx, zz] = s1[k][yy, xx, zz] + r1[k][yy, xx, zz]
         send(k, 1, s1[k].at[1 - y], r2[k], over_y)
 
     def step2(k):
         started[k, 1].wait()
         for xx in range(2):
             for zz in range(4):
-                s2[k][xx, zz] = (
-                    s1[k][y, xx, zz].astype(F32) + r2[k][xx, zz].astype(F32)
-                ).astype(BF16)
+                s2[k][xx, zz] = s1[k][y, xx, zz] + r2[k][xx, zz]
         send(k, 2, s2[k].at[1 - x], r3[k].at[0], over_x)
 
     def step3(k):
         started[k, 2].wait()
         for zz in range(4):
-            s3[k][zz] = (s2[k][x, zz].astype(F32) + r3[k][0, zz].astype(F32)).astype(BF16)
+            s3[k][zz] = s2[k][x, zz] + r3[k][0, zz]
         for i in range(3):
             send(k, 3 + i, s3[k].at[z ^ (i + 1)], r3[k].at[1, i], along[i])
 
@@ -1029,11 +1076,35 @@
             rows = pl.ds(pl.multiple_of((ex ^ (i + 1)) * 32, 32), 32)
             outs[k][rows, :] = r4[k][i].astype(F32)
 
+    size = gt_now.shape[1]
+
+    def stored(r):
+        rows = slice(r * size, (r + 1) * size)
+        return pltpu.make_async_copy(gt_now.at[r % 2], gt_ref.at[rows], sem_l.at[10 + r])
+
+    def back(r):
+        if r == 0:
+            load_w.wait()
+        if r >= 2:
+            stored(r - 2).wait()
+        rows = slice(r * size, (r + 1) * size)
+        nq, nk = dq_ref.shape[1], dk_ref.shape[1]
+        d_norm = dot_t(dq_ref[rows], w_now[:, :nq])
+        d_norm = d_norm + dot_t(dk_ref[rows], w_now[:, nq : nq + nk])
+        d_norm = d_norm + dot_t(dv_ref[rows], w_now[:, nq + nk : nq + 2 * nk])
+        value = tok_ref[rows].astype(F32)
+        inv = lax.rsqrt(jnp.mean(value * value, axis=1, keepdims=True) + EPS)
+        scaled = value * inv
+        part = jnp.sum(d_norm * scaled, axis=0, keepdims=True)
+        gain_sum[...] = part if r == 0 else gain_sum[...] + part
+        u = d_norm * gain_ref[...].astype(F32)
+        mean = jnp.mean(u * value, axis=1, keepdims=True)
+        gt_now[r % 2] = dres_ref[rows] + inv * u - scaled * (inv * inv) * mean
+        stored(r).start()
+
     done = tuple(ref.at[count:] for ref in (gate_ref, up_ref, down_ref))
-    step0(3)
     step0(0)
     begin(0)
-    step1(3)
     step1(0)
     step0(1)
     begin(1)
@@ -1041,65 +1112,81 @@
     step0(2)
     begin(2)
     step1(2)
-    step2(3)
+    back(0)
     step2(0)
     line.middle_sends(0, True)
+    back(1)
     step2(1)
-    step3(3)
+    back(2)
     step3(0)
     line.middle_sends(1, True)
-    line.middle_adds(0, True)
+    line.middle_adds(0)
+    back(3)
+    step0(3)
     step2(2)
+    step1(3)
     step3(1)
     line.middle_sends(2, True)
-    line.middle_adds(1, True)
-    step4(3)
+    line.middle_adds(1)
+    step2(3)
     step4(0)
     step3(2)
+    step3(3)
     line.result(0, done)
-    line.middle_adds(2, True)
+    line.middle_adds(2)
     step4(1)
-    step5(3)
     step5(0)
     step4(2)
+    step4(3)
     line.result(1, done)
     line.result(2, done)
     step5(1)
     step5(2)
+    step5(3)
     for copy in halves:
         copy.wait()
-
-
-def run_finish(ht, dq, dk, dv, d_out, small, experts):
+    for r in range(2, 4):
+        stored(r).wait()
+
+
+def run_finish(ht, dq, dk, dv, d_out, small, experts, w_all, tok, gain, d_res, gain_lane):
     widths = [d_out.shape[1], dq.shape[1], dk.shape[1] + dv.shape[1], small.shape[1]]
     chunk = experts[2].shape
     _, count, rows, lanes = chunk
     vmem = pl.BlockSpec(memory_space=pltpu.VMEM)
     hbm = pl.BlockSpec(memory_space=pl.ANY)
     shapes = [
-        (2, 2, 2, 4, 32), (2, 2, 4, 32), (2, 2, 4, 32), (2, 4, 32), (2, 4, 32), (2, 4, 32), (4, 32), (4, 32),
+        (2, 2, 2, 4, 32), (2, 2, 4, 32), (2, 4, 32), (2, 4, 32), (2, 4, 32), (4, 32), (4, 32),
     ]
+    length, d = tok.shape
     scratch = [pltpu.VMEM(shape + (w,), BF16) for shape in shapes for w in widths]
     scratch += [pltpu.SemaphoreType.DMA((len(widths), 9))] * 2
     scratch += line_scratch(chunk)
-    scratch += [pltpu.VMEM((3,) + chunk, BF16), pltpu.SemaphoreType.DMA((9,))]
+    scratch += [
+        pltpu.VMEM((3,) + chunk, BF16),
+        pltpu.SemaphoreType.DMA((14,)),
+        pltpu.VMEM((d, sum(widths[1:3])), BF16),
+        pltpu.VMEM((2, length // 4, d), F32),
+        pltpu.VMEM((1, d), F32),
+    ]
     return pl.pallas_call(
-        finish_kernel,
-        in_specs=[vmem] * 6 + [hbm] * 7,
-        out_specs=[vmem] * 7,
+        functools.partial(finish_kernel, gain_lane),
+        in_specs=[vmem] * 6 + [hbm] * 8 + [vmem] * 3,
+        out_specs=[vmem] * 7 + [hbm],
         out_shape=[
             *(jax.ShapeDtypeStruct((128, w), F32) for w in widths),
             jax.ShapeDtypeStruct((2 * count, rows, lanes), F32),
             jax.ShapeDtypeStruct((2 * count, rows, lanes), F32),
             jax.ShapeDtypeStruct((2 * count, rows // 2, 2 * lanes), F32),
+            jax.ShapeDtypeStruct((length, d), F32),
         ],
         scratch_shapes=scratch,
         compiler_params=pltpu.CompilerParams(
-            vmem_limit_bytes=60 * MIB, collective_id=1, has_side_effects=True
+            vmem_limit_bytes=63 * MIB, collective_id=1, has_side_effects=True
         ),
         cost_estimate=took(60),
         name="finish",
-    )(ht, dq, dk, dv, d_out, small, *experts)
+    )(ht, dq, dk, dv, d_out, small, *experts, w_all, tok, gain, d_res)
 
 
 def gather_kernel(mine_ref, out_ref, sem_s, sem_r, sem_l):
@@ -1271,7 +1358,7 @@
     bits += [("dp", n_dp, 1 << i) for i in range(n_dp.bit_length() - 1)]
 
     def widen_top():
-        if len(tops) <= len(bits):
+        if len(tops) <= len(bits) and not fast:
             axis, n, step = bits[len(tops) - 1]
             top = after(tops[-1], chain)
             tops.append(jnp.maximum(top, swap(top, step, axis, n)))
@@ -1350,9 +1437,9 @@
     chain = (made_two[0], tops[-1])
     if fast:
         chain = (chain, far_one, got_one)
-        sums = [tot_one, far_one, made_one[2], got_one[1]]
+        sums = [tot_one, far_one, made_one[2], got_one[1], peaks]
         got_two = [swap(made_two[k], 1, "dp", n_dp) for k in (1, 3)]
-    while len(tops) <= len(bits):
+    while len(tops) <= len(bits) and not fast:
         widen_top()
     top = tops[-1]
 
@@ -1385,11 +1472,12 @@
     d_router_w = jnp.einsum("rd,re->de", normed_two, d_logits, preferred_element_type=F32)
 
     dq, dk, dv, *halves = run_attn_bwd(
-        prefix, after(q, top), kd, vd, d_ctx, ctx, lse, cos_l, sin_l, cos_t, sin_t, sums
+        prefix, q, kd, vd, d_ctx, ctx, lse, cos_l, sin_l, cos_t, sin_t, sums
     )
-    grad_tok, d_gain_one = run_back_in(
-        after(dq, block_out, got_two), dk, dv, w_all, tok, gain_one, d_res
-    )
+    if not fast:
+        grad_tok, d_gain_one = run_back_in(dq, dk, dv, w_all, tok, gain_one, d_res)
+    else:
+        d_gain_one = jnp.zeros((1, d), F32)
     small_grad = jnp.concatenate(
         [
             d_router_w[:, :num_experts].astype(BF16),
@@ -1425,14 +1513,19 @@
     y_bits = [("expert", n_ex, 1 << i) for i in range(1, n_ex.bit_length() - 1)][::-1]
     dp_bits = [("dp", n_dp, 1 << i) for i in range(n_dp.bit_length() - 1)]
     if fast:
-        grad_out, grad_query, grad_keyval, rest, grad_gate, grad_up, grad_down = run_finish(
+        grad_out, grad_query, grad_keyval, rest, grad_gate, grad_up, grad_down, grad_tok = run_finish(
             normed_one_t,
-            dq,
+            after(dq, block_out),
             dk,
             dv,
             d_out_w,
             small_grad,
-            [made_two[0], got_two[0], made_two[2], got_two[1], *halves],
+            [made_two[0], got_two[0], made_two[2], got_two[1], *halves[:3]],
+            w_all,
+            tok,
+            gain_one,
+            d_res,
+            num_experts,
         )
     else:
         ends = [
@@ -1462,6 +1555,8 @@
     grad_gain_one = rest[:, num_experts]
     grad_gain_two = rest[:, num_experts + 1]
 
+    if fast:
+        top = halves[3][:, :, :4]
     head_logit_peak = top[:, 0, :].reshape(heads)
     per_group = heads // kv_heads
     query_factor = jnp.sqrt(query_logit_cap / jnp.maximum(head_logit_peak, query_logit_cap))

time: 575 us -> 589 us (1.024)
  Pallas kernels: 481 us -> 500 us
    pallas_call x1, Pallas kernels: 45.9 us -> 73.5 us  [run_attn_bwd(): pl.pallas_call(kernel, grid=(groups,), in_specs=in_specs, out_specs=out_s...]
    pallas_call x2 -> x1, Pallas kernels: 93.7 us -> 84.3 us  [run_finish(): pl.pallas_call(functools.partial(finish_kernel, gain_lane), in_specs=[vme...]
    ppermute x26 -> x21, starting transfers between devices: 18 us -> 12.6 us  [swap(): return lax.ppermute(value, axis, [(i, i ^ step) for i in range(n)])]
    unnamed x66 -> x79, local copies, waits for them, and re-layouts: 13.8 us -> 17.4 us
    ppermute x26 -> x21, waiting for transfers between devices: 12.6 us -> 14.9 us  [swap(): return lax.ppermute(value, axis, [(i, i ^ step) for i in range(n)])]
  transfers between devices with their start and end apart: 27 -> 22, of which waited for: 5 -> 5; matrix products, arithmetic and copies ran while one was open for 5% -> 4% of each run, Pallas kernels for 43% -> 41%
where the time goes in v6:
time: 589 us; the launch traced here: 581 us
  Pallas kernels  500 us (85%)
  local copies, waits for them, and re-layouts  26.9 us (5%)
  starting transfers between devices  16.6 us (3%)
  other arithmetic  16.1 us (3%)
  waiting for transfers between devices  14.9 us (3%)
    pallas_call x3, Pallas kernels, run_expert(): pl.pallas_call(functools.partial(expert_kernel, first, local, num_experts...  176 us
    pallas_call x1, Pallas kernels, run_finish(): pl.pallas_call(functools.partial(finish_kernel, gain_lane), in_specs=[vme...  84.3 us
    pallas_call x1, Pallas kernels, run_attn_bwd(): pl.pallas_call(kernel, grid=(groups,), in_specs=in_specs, out_specs=out_s...  73.5 us
    pallas_call x2, Pallas kernels, run_weight_grad(): pl.pallas_call(functools.partial(weight_grad_kernel, n, paired), grid=(co...  72.3 us
    pallas_call x1, Pallas kernels, run_gather(): pl.pallas_call(gather_kernel, in_specs=[hbm], out_specs=hbm, out_shape=ja...  43.5 us
    pallas_call x1, Pallas kernels, run_attn_fwd(): pl.pallas_call(attn_fwd_kernel, grid=(groups,), in_specs=[pl.BlockSpec(me...  21.4 us
    unnamed x79, local copies, waits for them, and re-layouts  17.4 us
    ppermute x21, waiting for transfers between devices, swap(): return lax.ppermute(value, axis, [(i, i ^ step) for i in range(n)])  14.9 us
  transfers between devices with their start and end apart: 22, of which 5 were waited for; matrix products, arithmetic and copies ran while one was open for 4% of the time, Pallas kernels for 41%

profile of v6, /device:TPU:0, one launch (start us, length us, event | category | flops | bytes accessed | tf_op | source)
XLA Modules:
  0.0 581.5 jit_solution(14032559991586106562)
XLA Ops:
  5.1 43.5 %gather.1.w_ref.refs_1_.refs_5_.refs_7_ = bf16[1024,3200]{1,0:T(8,128)(2,1)} custom-call(bf16[32,3200]{1,0:T(8,128)(2,1)} %constant_dynamic-slice_fusion.1.mine_ref), custom_call_target="tpu_custom_call" | custom-call | flops 14000000000 | bytes 1000 | tf_op jit(solution)/shard_map/gather/pallas_call | solution.py:1268
  53.4 10.0 %qkv.1 = (bf16[1024,1024]{1,0:T(8,128)(2,1)}, bf16[1024,1024]{1,0:T(8,128)(2,1)}, bf16[1024,1024]{1,0:T(8,128)(2,1)}, bf16[1024,1024]{1,0:T(8,128)(2,1)}) custom-call(bf16[1024,1024]{1,0:T(8,128)(2,1)} %bitcast.23, bf16[1,1024]{1,0:T(2,128)(2,1)} %reshape_squeeze.9.gain_ref, bf16[1024,3200]{1,0:T(8,128)(2,1)} %gather.1.w_ref.refs_1_.refs_5_.refs_7_, ...), custom_call_target="tpu_custom_call" | custom-call | flops 3150000128 | bytes 1000 | tf_op jit(solution)/shard_map/qkv/pallas_call | solution.py:101
  63.4 21.4 %attn_fwd.1 = (bf16[1024,1024]{1,0:T(8,128)(2,1)}, f32[4,8,1024]{2,1,0:T(8,128)}, f32[4,8,128]{2,1,0:T(8,128)}) custom-call(s32[1]{0:T(128)S(6)} %copy.51.prefix_ref.refs_0_, bf16[1024,1024]{1,0:T(8,128)(2,1)} %get-tuple-element.95.q_ref.refs_1_, bf16[1024,1024]{1,0:T(8,128)(2,1)} %get-tuple-element.96.kd_ref.refs_2_, ...), custom_call_target="tpu_custom_call" | custom-call | flops 7350000128 | bytes 1000 | tf_op jit(solution)/shard_map/attn_fwd/pallas_call | solution.py:176
  84.8 7.3 %mid.1 = (f32[1024,1024]{1,0:T(8,128)}, bf16[1024,1024]{1,0:T(8,128)(2,1)}) custom-call(bf16[1024,1024]{1,0:T(8,128)(2,1)} %bitcast.24, bf16[1024,1024]{1,0:T(8,128)(2,1)} %get-tuple-element.98.ctx_ref.refs_5_, bf16[1024,3200]{1,0:T(8,128)(2,1)} %gather.1.w_ref.refs_1_.refs_5_.refs_7_, bf16[1,1024]{1,0:T(2,128)(2,1)} %reshape_squeeze.10.gain_ref.refs_6_), custom_call_target="tpu_custom_call" | custom-call | flops 1400000000 | bytes 1000 | tf_op jit(solution)/shard_map/mid/pallas_call | solution.py:540
  93.2 3.9 collective-permute-done.refs_7_
  97.2 2.1 collective-permute-done.3.refs_10_
  102.0 76.0 %experts.3 = (bf16[1024,1024]{1,0:T(8,128)(2,1)}, bf16[1024,1024]{1,0:T(8,128)(2,1)}, bf16[1024,1024]{1,0:T(8,128)(2,1)}, bf16[1024,1024]{1,0:T(8,128)(2,1)}, f3...) custom-call(s32[1]{0:T(128)} %bitcast.3.refs_0_, ...), custom_call_target="tpu_custom_call" | custom-call | flops 33600000000 | bytes 1000 | tf_op jit(solution)/shard_map/experts/pallas_call | solution.py:706
  180.0 2.8 collective-permute-done.8.refs_9_
  182.8 2.7 collective-permute-done.6.refs_6_
  185.5 44.2 %experts.4 = (bf16[1024,1024]{1,0:T(8,128)(2,1)}, bf16[1024,1024]{1,0:T(8,128)(2,1)}, bf16[1024,1024]{1,0:T(8,128)(2,1)}, bf16[1024,1024]{1,0:T(8,128)(2,1)}, f3...) custom-call(s32[1]{0:T(128)} %bitcast.3.refs_0_, ...), custom_call_target="tpu_custom_call" | custom-call | flops 16800000000 | bytes 1000 | tf_op jit(solution)/shard_map/experts/pallas_call | solution.py:706
  229.8 36.0 %weight_grad.2 = (bf16[4,2,2,128,512]{4,3,2,1,0:T(8,128)(2,1)}, bf16[4,2,2,128,512]{4,3,2,1,0:T(8,128)(2,1)}, bf16[4,2,128,512]{3,2,1,0:T(8,128)(2,1)}, bf16[4,2,128,512]{3,2,1,0:T(8,128)(2,1)}) custom-call(s32[1]{0:T(128)} %bitcast.8.dp_ref, bf16[1024,2048]{1,0:T(8,128)(2,1)} %get-tuple-element.140.refs_0_, bf16[1024,2048]{1,0:T(8,128)(2,1)} %get-tuple-element.113.refs_1_, ...), custom_call_target="tpu_custom_call" | custom-call | flops 12949999616 | bytes 1000 | tf_op jit(solution)/shard_map/weight_grad/pallas_call | solution.py:816
  265.8 55.5 %experts.5 = (bf16[1024,1024]{1,0:T(8,128)(2,1)}, bf16[1024,1024]{1,0:T(8,128)(2,1)}, bf16[1024,1024]{1,0:T(8,128)(2,1)}, bf16[1024,1024]{1,0:T(8,128)(2,1)}, f3...) custom-call(s32[1]{0:T(128)} %bitcast.3.refs_0_, ...), custom_call_target="tpu_custom_call" | custom-call | flops 16800000000 | bytes 1000 | tf_op jit(solution)/shard_map/experts/pallas_call | solution.py:706
  322.3 3.4 collective-permute-done.12
  325.7 4.2 add_convert_fusion.2
  332.9 4.0 collective-permute-start.15
  338.5 36.3 %weight_grad.3 = (bf16[4,2,2,128,512]{4,3,2,1,0:T(8,128)(2,1)}, bf16[4,2,2,128,512]{4,3,2,1,0:T(8,128)(2,1)}, bf16[4,2,128,512]{3,2,1,0:T(8,128)(2,1)}, bf16[4,2,128,512]{3,2,1,0:T(8,128)(2,1)}) custom-call(s32[1]{0:T(128)} %bitcast.8.dp_ref, bf16[1024,2048]{1,0:T(8,128)(2,1)} %get-tuple-element.140.refs_0_, bf16[1024,2048]{1,0:T(8,128)(2,1)} %get-tuple-element.113.refs_1_, ...), custom_call_target="tpu_custom_call" | custom-call | flops 12949999616 | bytes 1000 | tf_op jit(solution)/shard_map/weight_grad/pallas_call | solution.py:816
  376.7 3.9 add_convert_fusion.3
  384.3 12.2 %back_mid.1 = (f32[1024,1024]{1,0:T(8,128)}, bf16[1024,1024]{1,0:T(8,128)(2,1)}, bf16[1024,1024]{1,0:T(8,128)(2,1)}, bf16[1024,128]{1,0:T(8,128)(2,1)}, f32[1,1024]{1,0:T(1,128)}) custom-call(s32[1]{0:T(128)} %bitcast.3.refs_0_, f32[1024,1024]{1,0:T(8,128)} %get-tuple-element.147.refs_1_, bf16[1024,1024]{1,0:T(8,128)(2,1)} %bitcast.27, s32[8,1024]{1,0:T(8,128)} %bitcast.33, ...), custom_call_target="tpu_custom_call" | custom-call | flops 3849999872 | bytes 1000 | tf_op jit(solution)/shard_map/back_mid/pallas_call | solution.py:873
  396.6 73.5 %attn_bwd.1 = (bf16[1024,1024]{1,0:T(8,128)(2,1)}, bf16[1024,512]{1,0:T(8,128)(2,1)}, bf16[1024,512]{1,0:T(8,128)(2,1)}, f32[2,128,512]{2,1,0:T(8,128)}, f32[2,1...) custom-call(s32[1]{0:T(128)S(6)} %copy.51.prefix_ref.refs_0_, ...), custom_call_target="tpu_custom_call" | custom-call | flops 11550000128 | bytes 1000 | tf_op jit(solution)/shard_map/attn_bwd/pallas_call | solution.py:514
  474.3 3.8 convolution_convert_fusion.dout_ref
  478.1 5.2 fusion
  483.3 84.3 %finish.1 = (f32[128,1024]{1,0:T(8,128)}, f32[128,1024]{1,0:T(8,128)}, f32[128,1024]{1,0:T(8,128)}, f32[128,128]{1,0:T(8,128)}, f32[4,128,512]{2,1,0:T(8,128)}, ...) custom-call(bf16[1024,1024]{1,0:T(8,128)(2,1)} %get-tuple-element.137.ht_ref, ...), custom_call_target="tpu_custom_call" | custom-call | flops 20999999488 | bytes 1000 | tf_op jit(solution)/shard_map/finish/pallas_call | solution.py:1172
  567.7 1.6 slice_reduce_fusion.2
  570.8 4.9 copy.52
  (147 shorter events, 36.6 us)
Async XLA Ops:
  48.6 48.6 %collective-permute-start = (bf16[1024,1024]{1,0:T(8,128)(2,1)S(1)}, bf16[1024,1024]{1,0:T(8,128)(2,1)}, u32[]{:S(2)}, u32[]{:S(2)}) collective-permute-start(bf16[1024,1024]{1,0:T(8,128)(2,1)S(1)} %bitcast.28), channel_id=1, source_target_pairs={{0,2},{1,3},{2,0},{3,1},{4,6},{5,7},{6,4},{7,5},{8,10},{9,11},{10,... | collective-permute-start | bytes 6291464 | tf_op jit(solution)/shard_map/ppermute | solution.py:1305
  92.1 7.2 %collective-permute-start.1 = (bf16[1024,1024]{1,0:T(8,128)(2,1)}, bf16[1024,1024]{1,0:T(8,128)(2,1)S(1)}, u32[]{:S(2)}, u32[]{:S(2)}) collective-permute-start(bf16[1024,1024]{1,0:T(8,128)(2,1)} %get-tuple-element.102.refs_5_.refs_4_), channel_id=1, source_target_pairs={{0,1},{1,0},{2,3},{3,2},{4,5},{5,4},{6,7},{7,6},{8,9},{9,8},{10,11... | collective-permute-start | bytes 6291464 | tf_op jit(solution)/shard_map/ppermute | solution.py:1305
  92.2 7.1 %collective-permute-start.2 = (bf16[1024,1024]{1,0:T(8,128)(2,1)S(1)}, bf16[1024,1024]{1,0:T(8,128)(2,1)S(1)}, u32[]{:S(2)}, u32[]{:S(2)}) collective-permute-start(bf16[1024,1024]{1,0:T(8,128)(2,1)S(1)} %bitcast.29), channel_id=1, source_target_pairs={{0,1},{1,0},{2,3},{3,2},{4,5},{5,4},{6,7},{7,6},{8,9},{9,8},{10,11... | collective-permute-start | bytes 6291464 | tf_op jit(solution)/shard_map/ppermute | solution.py:1305
  92.6 6.7 %collective-permute-start.3 = (s32[8,1024]{1,0:T(8,128)S(1)}, s32[8,1024]{1,0:T(8,128)S(1)}, u32[]{:S(2)}, u32[]{:S(2)}) collective-permute-start(s32[8,1024]{1,0:T(8,128)S(1)} %bitcast.34), channel_id=1, source_target_pairs={{0,1},{1,0},{2,3},{3,2},{4,5},{5,4},{6,7},{7,6},{8,9},{9,8},{10,11... | collective-permute-start | bytes 98312 | tf_op jit(solution)/shard_map/ppermute | solution.py:1305
  92.7 85.5 %collective-permute-start.5 = (bf16[1024,1024]{1,0:T(8,128)(2,1)}, bf16[1024,1024]{1,0:T(8,128)(2,1)}, u32[]{:S(2)}, u32[]{:S(2)}) collective-permute-start(bf16[1024,1024]{1,0:T(8,128)(2,1)} %get-tuple-element.102.refs_5_.refs_4_), channel_id=1, source_target_pairs={{0,2},{1,3},{2,0},{3,1},{4,6},{5,7},{6,4},{7,5},{8,10},{9,11},{10,... | collective-permute-start | bytes 6291464 | tf_op jit(solution)/shard_map/ppermute | solution.py:1305
  102.0 76.6 %copy-start.19 = (s32[1,1024,8]{1,2,0:T(8,128)S(1)}, s32[1,1024,8]{1,2,0:T(8,128)}, u32[]{:S(2)}) copy-start(s32[1,1024,8]{1,2,0:T(8,128)} %param.20) | copy-start | bytes 98308
  178.0 4.8 collective-permute-start.7
  178.2 7.4 %collective-permute-start.6 = (bf16[1024,1024]{1,0:T(8,128)(2,1)}, bf16[1024,1024]{1,0:T(8,128)(2,1)}, u32[]{:S(2)}, u32[]{:S(2)}) collective-permute-start(bf16[1024,1024]{1,0:T(8,128)(2,1)} %collective-permute-done.5.refs_5_), channel_id=1, source_target_pairs={{0,1},{1,0},{2,3},{3,2},{4,5},{5,4},{6,7},{7,6},{8,9},{9,8},{10,11... | collective-permute-start | bytes 6291464 | tf_op jit(solution)/shard_map/ppermute | solution.py:1305
  178.6 4.2 collective-permute-start.8
  179.1 3.7 collective-permute-start.9
  321.3 4.4 collective-permute-start.12
  321.7 58.9 %collective-permute-start.11 = (bf16[1024,1024]{1,0:T(8,128)(2,1)}, bf16[1024,1024]{1,0:T(8,128)(2,1)}, u32[]{:S(2)}, u32[]{:S(2)}) collective-permute-start(bf16[1024,1024]{1,0:T(8,128)(2,1)} %get-tuple-element.133), channel_id=1, source_target_pairs={{0,1},{1,0},{2,3},{3,2},{4,5},{5,4},{6,7},{7,6},{8,9},{9,8},{10,11... | collective-permute-start | bytes 6291464 | tf_op jit(solution)/shard_map/ppermute | solution.py:1305
  322.3 52.6 %collective-permute-start.10 = (bf16[1024,1024]{1,0:T(8,128)(2,1)}, bf16[1024,1024]{1,0:T(8,128)(2,1)}, u32[]{:S(2)}, u32[]{:S(2)}) collective-permute-start(bf16[1024,1024]{1,0:T(8,128)(2,1)} %get-tuple-element.131), channel_id=1, source_target_pairs={{0,1},{1,0},{2,3},{3,2},{4,5},{5,4},{6,7},{7,6},{8,9},{9,8},{10,11... | collective-permute-start | bytes 6291464 | tf_op jit(solution)/shard_map/ppermute | solution.py:1305
  329.9 51.1 %collective-permute-start.13 = (bf16[1024,1024]{1,0:T(8,128)(2,1)}, bf16[1024,1024]{1,0:T(8,128)(2,1)}, u32[]{:S(2)}, u32[]{:S(2)}) collective-permute-start(bf16[1024,1024]{1,0:T(8,128)(2,1)} %add_convert_fusion.2), channel_id=1, source_target_pairs={{0,2},{1,3},{2,0},{3,1},{4,6},{5,7},{6,4},{7,5},{8,10},{9,11},{10,... | collective-permute-start | bytes 6291464 | tf_op jit(solution)/shard_map/ppermute | solution.py:1305
  332.9 41.8 %collective-permute-start.15 = (bf16[2,2,2,128,512]{4,3,2,1,0:T(8,128)(2,1)S(1)}, bf16[2,2,2,128,512]{4,3,2,1,0:T(8,128)(2,1)}, u32[]{:S(2)}, u32[]{:S(2)}) collective-permute-start(bf16[2,2,2,128,512]{4,3,2,1,0:T(8,128)(2,1)S(1)} %constant_dynamic-slice_fusion), channel_id=1, source_target_pairs={{0,8},{4,12},{24,16},{28,20},{1,9},{5,13},{25,17},{29,21},{2,10},{... | collective-permute-start | bytes 3145736 | tf_op jit(solution)/shard_map/ppermute | solution.py:1435
  337.0 38.5 %collective-permute-start.16 = (bf16[4,2,128,512]{3,2,1,0:T(8,128)(2,1)}, bf16[4,2,128,512]{3,2,1,0:T(8,128)(2,1)}, u32[]{:S(2)}, u32[]{:S(2)}) collective-permute-start(bf16[4,2,128,512]{3,2,1,0:T(8,128)(2,1)} %get-tuple-element.146), channel_id=1, source_target_pairs={{0,4},{4,0},{8,12},{12,8},{16,20},{20,16},{24,28},{28,24},{1,5},{5... | collective-permute-start | bytes 3145736 | tf_op jit(solution)/shard_map/ppermute | solution.py:1305
  374.8 6.8 %collective-permute-start.17 = (f32[8,1024]{1,0:T(8,128)S(1)}, f32[8,1024]{1,0:T(8,128)S(1)}, u32[]{:S(2)}, u32[]{:S(2)}) collective-permute-start(f32[8,1024]{1,0:T(8,128)S(1)} %copy-done.29), channel_id=1, source_target_pairs={{0,1},{1,0},{2,3},{3,2},{4,5},{5,4},{6,7},{7,6},{8,9},{9,8},{10,11... | collective-permute-start | bytes 98312 | tf_op jit(solution)/shard_map/ppermute | solution.py:1305
  374.9 8.2 %collective-permute-start.18 = (f32[8,1024]{1,0:T(8,128)S(1)}, f32[8,1024]{1,0:T(8,128)S(1)}, u32[]{:S(2)}, u32[]{:S(2)}) collective-permute-start(f32[8,1024]{1,0:T(8,128)S(1)} %copy-done.31), channel_id=1, source_target_pairs={{0,2},{1,3},{2,0},{3,1},{4,6},{5,7},{6,4},{7,5},{8,10},{9,11},{10,... | collective-permute-start | bytes 98312 | tf_op jit(solution)/shard_map/ppermute | solution.py:1305
  375.5 8.1 %collective-permute-start.19 = (f32[8,1024]{1,0:T(8,128)S(1)}, f32[8,1024]{1,0:T(8,128)S(1)}, u32[]{:S(2)}, u32[]{:S(2)}) collective-permute-start(f32[8,1024]{1,0:T(8,128)S(1)} %copy-done.30), channel_id=1, source_target_pairs={{0,3},{1,2},{2,1},{3,0},{4,7},{5,6},{6,5},{7,4},{8,11},{9,10},{10,... | collective-permute-start | bytes 98312 | tf_op jit(solution)/shard_map/ppermute | solution.py:1305
  380.7 97.5 %collective-permute-start.4 = (bf16[1024,1024]{1,0:T(8,128)(2,1)}, bf16[1024,1024]{1,0:T(8,128)(2,1)}, u32[]{:S(2)}, u32[]{:S(2)}) collective-permute-start(bf16[1024,1024]{1,0:T(8,128)(2,1)} %get-tuple-element.105), channel_id=1, source_target_pairs={{0,1},{1,0},{2,3},{3,2},{4,5},{5,4},{6,7},{7,6},{8,9},{9,8},{10,11... | collective-permute-start | bytes 6291464 | tf_op jit(solution)/shard_map/ppermute | solution.py:1305
  381.0 102.3 %collective-permute-start.20 = (bf16[4,2,2,128,512]{4,3,2,1,0:T(8,128)(2,1)}, bf16[4,2,2,128,512]{4,3,2,1,0:T(8,128)(2,1)}, u32[]{:S(2)}, u32[]{:S(2)}) collective-permute-start(bf16[4,2,2,128,512]{4,3,2,1,0:T(8,128)(2,1)} %get-tuple-element.160), channel_id=1, source_target_pairs={{0,4},{4,0},{8,12},{12,8},{16,20},{20,16},{24,28},{28,24},{1,5},{5... | collective-permute-start | bytes 6291464 | tf_op jit(solution)/shard_map/ppermute | solution.py:1305
  381.6 101.8 %collective-permute-start.21 = (bf16[4,2,128,512]{3,2,1,0:T(8,128)(2,1)}, bf16[4,2,128,512]{3,2,1,0:T(8,128)(2,1)}, u32[]{:S(2)}, u32[]{:S(2)}) collective-permute-start(bf16[4,2,128,512]{3,2,1,0:T(8,128)(2,1)} %get-tuple-element.162), channel_id=1, source_target_pairs={{0,4},{4,0},{8,12},{12,8},{16,20},{20,16},{24,28},{28,24},{1,5},{5... | collective-permute-start | bytes 3145736 | tf_op jit(solution)/shard_map/ppermute | solution.py:1305
  383.1 95.1 %collective-permute-start.14 = (bf16[1024,1024]{1,0:T(8,128)(2,1)}, bf16[1024,1024]{1,0:T(8,128)(2,1)}, u32[]{:S(2)}, u32[]{:S(2)}) collective-permute-start(bf16[1024,1024]{1,0:T(8,128)(2,1)} %add_convert_fusion.3), channel_id=1, source_target_pairs={{0,2},{1,3},{2,0},{3,1},{4,6},{5,7},{6,4},{7,5},{8,10},{9,11},{10,... | collective-permute-start | bytes 6291464 | tf_op jit(solution)/shard_map/ppermute | solution.py:1305
  396.5 75.1 %copy-start.1 = (bf16[1024,1024]{1,0:T(8,128)(2,1)S(1)}, bf16[1024,1024]{1,0:T(8,128)(2,1)}, u32[]{:S(2)}) copy-start(bf16[1024,1024]{1,0:T(8,128)(2,1)} %get-tuple-element.102.refs_5_.refs_4_) | copy-start | bytes 6291460
  (33 other events, 467.0 us)

commit v7 on v6

--- a/solution.py
+++ b/solution.py
@@ -304,36 +304,11 @@
 
 
 def attn_bwd_sum_kernel(*refs):
-    ins, (tot_a, far_a, keep_a, got_a, peak_ref) = refs[:11], refs[11:16]
-    outs, (gate_ref, up_ref, down_ref, top_ref) = refs[16:19], refs[19:23]
-    scratch, line_refs, (rx, sem_l, top_s, top_r, sem_ts, sem_tr) = refs[23:26], refs[26:32], refs[32:]
+    ins, (tot_a, far_a, keep_a, got_a) = refs[:11], refs[11:15]
+    outs, (gate_ref, up_ref, down_ref) = refs[15:18], refs[18:21]
+    scratch, line_refs, (rx, sem_l) = refs[21:24], refs[24:30], refs[30:]
     step = pl.program_id(0)
     line = Line(*line_refs)
-    dp, ex = lax.axis_index("dp"), lax.axis_index("expert")
-    bits = [(dp, ex ^ 1), (dp, ex ^ 2), (dp ^ 1, ex), (dp ^ 2, ex), (dp ^ 4, ex)]
-
-    def top_copy(k):
-        return pltpu.make_async_remote_copy(
-            src_ref=top_s.at[k],
-            dst_ref=top_r.at[k],
-            send_sem=sem_ts.at[k],
-            recv_sem=sem_tr.at[k],
-            device_id=bits[k],
-            device_id_type=pl.DeviceIdType.MESH,
-        )
-
-    def top_round(k):
-        if k == 0:
-            top_s[0] = peak_ref[...]
-        else:
-            top_copy(k - 1).wait()
-            both = jnp.maximum(top_s[k - 1], top_r[k - 1])
-            if k == len(bits):
-                top_ref[...] = both
-                return
-            top_s[k] = both
-        top_copy(k).start()
-
     loads = []
     for k in range(2):
         loads.append([pltpu.make_async_copy(tot_a.at[:, k], line.tot.at[k], sem_l.at[2 * k])])
@@ -351,8 +326,7 @@
         for group in loads:
             for copy in group:
                 copy.start()
-        greet(bits + [line.middle])
-        top_round(0)
+        greet([line.near, line.middle])
         for copy in loads[2]:
             copy.wait()
         for zz in range(4):
@@ -366,25 +340,15 @@
             line.ends(k, False)
             line.middle_sends(k, False)
 
-    @pl.when(step == 3)
-    def _():
-        top_round(4)
-
     attn_bwd_body(*ins, *outs, *scratch)
-
-    @pl.when(step == 0)
-    def _():
-        top_round(1)
 
     @pl.when(step == 1)
     def _():
-        top_round(2)
         line.middle_sends(2, True)
         line.middle_adds(0)
 
     @pl.when(step == 2)
     def _():
-        top_round(3)
         line.middle_adds(1)
 
     @pl.when(step == 3)
@@ -392,7 +356,6 @@
         line.middle_adds(2)
         for ch in range(3):
             line.result(ch, (gate_ref, up_ref, down_ref))
-        top_round(5)
 
 
 def attn_bwd_body(
@@ -496,19 +459,13 @@
         keep_a = sums[2]
         _, count, rows, lanes = keep_a.shape
         made = [(count, rows, lanes)] * 2 + [(count, rows // 2, 2 * lanes)]
-        peaks = sums[4]
-        made.append(peaks.shape)
-        in_specs += [hbm] * 4 + [whole(peaks.shape)]
+        in_specs += [hbm] * 4
         out_specs += [whole(shape) for shape in made]
         out_shape += [jax.ShapeDtypeStruct(shape, F32) for shape in made]
         scratch += line_scratch(keep_a.shape)
         scratch += [
             pltpu.VMEM(keep_a.shape, BF16),
             pltpu.SemaphoreType.DMA((6,)),
-            pltpu.VMEM((5,) + peaks.shape, F32),
-            pltpu.VMEM((5,) + peaks.shape, F32),
-            pltpu.SemaphoreType.DMA((5,)),
-            pltpu.SemaphoreType.DMA((5,)),
         ]
         args += tuple(sums)
     return pl.pallas_call(
@@ -569,20 +526,51 @@
     return e / jnp.sum(e, axis=0, keepdims=True)
 
 
-def expert_kernel(first_expert, local, num_experts, with_init, with_carry, n_row, *refs):
+class Tops:
+    def __init__(self, peak_ref, top_ref, sent, got, sem_s, sem_r):
+        self.peak_ref, self.top_ref, self.sent, self.got = peak_ref, top_ref, sent, got
+        self.sem_s, self.sem_r = sem_s, sem_r
+        dp, ex = lax.axis_index("dp"), lax.axis_index("expert")
+        self.peers = [(dp, ex ^ 1), (dp, ex ^ 2), (dp ^ 1, ex), (dp ^ 2, ex), (dp ^ 4, ex)]
+
+    def copy(self, k):
+        return pltpu.make_async_remote_copy(
+            src_ref=self.sent.at[k],
+            dst_ref=self.got.at[k],
+            send_sem=self.sem_s.at[k],
+            recv_sem=self.sem_r.at[k],
+            device_id=self.peers[k],
+            device_id_type=pl.DeviceIdType.MESH,
+        )
+
+    def turn(self, k):
+        if k == 0:
+            greet(self.peers)
+            self.sent[0] = self.peak_ref[...]
+        else:
+            self.copy(k - 1).wait()
+            both = jnp.maximum(self.sent[k - 1], self.got[k - 1])
+            if k == len(self.peers):
+                self.top_ref[...] = both
+                return
+            self.sent[k] = both
+        self.copy(k).start()
+
+
+def expert_kernel(first_expert, local, num_experts, with_init, with_carry, with_top, n_row, *refs):
     me_ref, router_ref, wg_ref, wu_ref, wd_ref = refs[:5]
     x_refs, c_refs, route_refs = refs[5:7], refs[7:9], refs[9:11]
     refs = refs[11:]
     if with_init:
         out_ins, dx_ins, dg_ins, refs = refs[:2], refs[2:4], refs[4:6], refs[6:]
-    if with_carry:
+    if with_carry or with_top:
         sent_ref, refs = refs[0], refs[1:]
     out_refs, dx_refs, dg_refs = refs[:2], refs[2:4], refs[4:6]
     hs_ref, dgate_ref, dup_ref = refs[6:9]
     refs = refs[9:]
     if not with_init:
         xt_ref, ct_ref, refs = refs[0], refs[1], refs[2:]
-    if with_carry:
+    if with_carry or with_top:
         got_ref, refs = refs[0], refs[1:]
     x_now, c_now, out_acc, dx_acc, gp_ref, dgc_ref = refs[:6]
     i, e = pl.program_id(0), pl.program_id(1)
@@ -607,6 +595,14 @@
 
     b = x_now.shape[0]
     lane = lax.broadcasted_iota(jnp.int32, (b, 128), 1)
+
+    if with_top:
+        tops = Tops(sent_ref, got_ref, *refs[6:])
+        for k in range(6):
+
+            @pl.when(i * pl.num_programs(1) + e == k)
+            def _():
+                tops.turn(k)
 
     for source in range(2):
 
@@ -670,7 +666,7 @@
             carry().wait()
 
 
-def run_expert(me, xs, cs, routes, router, wg, wu, wd, first, count, num_experts, init=None, sent=None):
+def run_expert(me, xs, cs, routes, router, wg, wu, wd, first, count, num_experts, init=None, sent=None, peaks=None):
     length, d = xs[0].shape
     local, _, ff = wg.shape
     b = 512
@@ -699,13 +695,27 @@
     wide_spec = spec((b, ff), lambda i, e: (i, e))
     turned_spec = spec((d, b), lambda i, e: (0, i))
     with_init = init is not None
-    carried, extra = [], {}
+    carried, extra, more = [], {}, []
+    with_sent = sent is not None
     if sent is not None:
         carried = [pl.BlockSpec(memory_space=pl.ANY)]
         extra = {"collective_id": 4, "has_side_effects": True}
+        more = [pltpu.SemaphoreType.DMA((2,))]
+    if peaks is not None:
+        sent = peaks
+        carried = [whole(peaks.shape)]
+        extra = {"collective_id": 5, "has_side_effects": True}
+        more = [pltpu.VMEM((5,) + peaks.shape, F32)] * 2 + [pltpu.SemaphoreType.DMA((5,))] * 2
     made = pl.pallas_call(
         functools.partial(
-            expert_kernel, first, local, num_experts, with_init, sent is not None, n_row
+            expert_kernel,
+            first,
+            local,
+            num_experts,
+            with_init,
+            with_sent,
+            peaks is not None,
+            n_row,
         ),
         grid=(2 * n_row, count),
         in_specs=[
@@ -741,14 +751,14 @@
             pltpu.VMEM((b, 128), F32),
             pltpu.VMEM((b, 128), F32),
         ]
-        + ([] if sent is None else [pltpu.SemaphoreType.DMA((2,))]),
+        + more,
         compiler_params=pltpu.CompilerParams(
             dimension_semantics=("arbitrary",) * 2, vmem_limit_bytes=62 * MIB, **extra
         ),
         cost_estimate=took(24 * count),
         name="experts",
     )(me, router, wg, wu, wd, *xs, *cs, *routes, *(init or ()), *([] if sent is None else [sent]))
-    return {"out": made[:2], "dx": made[2:4], "dg": made[4:6], "wide": made[6:9], "turned": made[9:11], "got": made[9:]}
+    return {"out": made[:2], "dx": made[2:4], "dg": made[4:6], "wide": made[6:9], "turned": made[9:11], "got": made[-1:]}
 
 
 def weight_grad_kernel(n, paired, dp_ref, *refs):
@@ -1371,11 +1381,22 @@
     res = {}
     chain = (normed_two, [cots[step] for step in range(2, n_ex, 2)])
 
-    def experts(steps, first, count, init=None, sent=None):
+    def experts(steps, first, count, init=None, sent=None, peaks=None):
         x = [after(xs[steps[0]], chain), xs[steps[1]]]
         cot_pair, route_pair = [cots[k] for k in steps], [route_set[k] for k in steps]
         return run_expert(
-            me, x, cot_pair, route_pair, w_all, *weights, first, count, num_experts, init, sent
+            me,
+            x,
+            cot_pair,
+            route_pair,
+            w_all,
+            *weights,
+            first,
+            count,
+            num_experts,
+            init,
+            sent,
+            peaks,
         )
 
     def grads(first):
@@ -1406,7 +1427,7 @@
         xs[other] = swap(after(xs[other - 1], chain), 1)
     even = range(2, n_ex, 2)
     for step in even:
-        res[step, 0] = experts((step, step + 1), 0, half)
+        res[step, 0] = experts((step, step + 1), 0, half, peaks=peaks if fast else None)
         chain = (res[step, 0]["dg"][0], tops[-1])
         widen_top()
     made_one = grads(0)
@@ -1437,7 +1458,7 @@
     chain = (made_two[0], tops[-1])
     if fast:
         chain = (chain, far_one, got_one)
-        sums = [tot_one, far_one, made_one[2], got_one[1], peaks]
+        sums = [tot_one, far_one, made_one[2], got_one[1]]
         got_two = [swap(made_two[k], 1, "dp", n_dp) for k in (1, 3)]
     while len(tops) <= len(bits) and not fast:
         widen_top()
@@ -1556,7 +1577,7 @@
     grad_gain_two = rest[:, num_experts + 1]
 
     if fast:
-        top = halves[3][:, :, :4]
+        top = res[2, 0]["got"][0][:, :, :4]
     head_logit_peak = top[:, 0, :].reshape(heads)
     per_group = heads // kv_heads
     query_factor = jnp.sqrt(query_logit_cap / jnp.maximum(head_logit_peak, query_logit_cap))

time: 589 us -> 567 us (0.963)
  Pallas kernels: 500 us -> 473 us
    pallas_call x1, Pallas kernels: 73.5 us -> 44.8 us  [run_attn_bwd(): pl.pallas_call(kernel, grid=(groups,), in_specs=in_specs, out_specs=out_s...]
    unnamed x79 -> x69, local copies, waits for them, and re-layouts: 17.4 us -> 17.2 us
  transfers between devices with their start and end apart: 22 -> 22, of which waited for: 5 -> 5; matrix products, arithmetic and copies ran while one was open for 4% -> 6% of each run, Pallas kernels for 41% -> 37%
where the time goes in v7:
time: 567 us; the launch traced here: 560 us
  Pallas kernels  473 us (83%)
  local copies, waits for them, and re-layouts  26.8 us (5%)
  other arithmetic  19.7 us (3%)
  starting transfers between devices  18 us (3%)
  waiting for transfers between devices  12.8 us (2%)
  matrix products  7.14 us (1%)
    pallas_call x3, Pallas kernels, run_expert(): pl.pallas_call(functools.partial(expert_kernel, first, local, num_experts...  177 us
    pallas_call x1, Pallas kernels, run_finish(): pl.pallas_call(functools.partial(finish_kernel, gain_lane), in_specs=[vme...  85 us
    pallas_call x2, Pallas kernels, run_weight_grad(): pl.pallas_call(functools.partial(weight_grad_kernel, n, paired), grid=(co...  72.3 us
    pallas_call x1, Pallas kernels, run_attn_bwd(): pl.pallas_call(kernel, grid=(groups,), in_specs=in_specs, out_specs=out_s...  44.8 us
    pallas_call x1, Pallas kernels, run_gather(): pl.pallas_call(gather_kernel, in_specs=[hbm], out_specs=hbm, out_shape=ja...  43.5 us
    pallas_call x1, Pallas kernels, run_attn_fwd(): pl.pallas_call(attn_fwd_kernel, grid=(groups,), in_specs=[pl.BlockSpec(me...  21.4 us
    unnamed x69, local copies, waits for them, and re-layouts  17.2 us
    ppermute x21, starting transfers between devices, swap(): return lax.ppermute(value, axis, [(i, i ^ step) for i in range(n)])  13.4 us
  transfers between devices with their start and end apart: 22, of which 5 were waited for; matrix products, arithmetic and copies ran while one was open for 6% of the time, Pallas kernels for 37%

profile of v7, /device:TPU:0, one launch (start us, length us, event | category | flops | bytes accessed | tf_op | source)
XLA Modules:
  0.0 559.8 jit_solution(8219884511204608331)
XLA Ops:
  5.1 43.5 %gather.1.w_ref.refs_1_.refs_5_.refs_7_ = bf16[1024,3200]{1,0:T(8,128)(2,1)} custom-call(bf16[32,3200]{1,0:T(8,128)(2,1)} %constant_dynamic-slice_fusion.1.mine_ref), custom_call_target="tpu_custom_call" | custom-call | flops 14000000000 | bytes 1000 | tf_op jit(solution)/shard_map/gather/pallas_call | solution.py:1278
  53.4 10.1 %qkv.1 = (bf16[1024,1024]{1,0:T(8,128)(2,1)}, bf16[1024,1024]{1,0:T(8,128)(2,1)}, bf16[1024,1024]{1,0:T(8,128)(2,1)}, bf16[1024,1024]{1,0:T(8,128)(2,1)}) custom-call(bf16[1024,1024]{1,0:T(8,128)(2,1)} %bitcast.23, bf16[1,1024]{1,0:T(2,128)(2,1)} %reshape_squeeze.9.gain_ref, bf16[1024,3200]{1,0:T(8,128)(2,1)} %gather.1.w_ref.refs_1_.refs_5_.refs_7_, ...), custom_call_target="tpu_custom_call" | custom-call | flops 3150000128 | bytes 1000 | tf_op jit(solution)/shard_map/qkv/pallas_call | solution.py:101
  63.4 21.4 %attn_fwd.1 = (bf16[1024,1024]{1,0:T(8,128)(2,1)}, f32[4,8,1024]{2,1,0:T(8,128)}, f32[4,8,128]{2,1,0:T(8,128)}) custom-call(s32[1]{0:T(128)S(6)} %copy.51.prefix_ref.refs_0_, bf16[1024,1024]{1,0:T(8,128)(2,1)} %get-tuple-element.95.q_ref.refs_1_, bf16[1024,1024]{1,0:T(8,128)(2,1)} %get-tuple-element.96.kd_ref.refs_2_, ...), custom_call_target="tpu_custom_call" | custom-call | flops 7350000128 | bytes 1000 | tf_op jit(solution)/shard_map/attn_fwd/pallas_call | solution.py:176
  84.9 7.3 %mid.1 = (f32[1024,1024]{1,0:T(8,128)}, bf16[1024,1024]{1,0:T(8,128)(2,1)}) custom-call(bf16[1024,1024]{1,0:T(8,128)(2,1)} %bitcast.24, bf16[1024,1024]{1,0:T(8,128)(2,1)} %get-tuple-element.98.ctx_ref.refs_5_, bf16[1024,3200]{1,0:T(8,128)(2,1)} %gather.1.w_ref.refs_1_.refs_5_.refs_7_, bf16[1,1024]{1,0:T(2,128)(2,1)} %reshape_squeeze.10.gain_ref.refs_6_), custom_call_target="tpu_custom_call" | custom-call | flops 1400000000 | bytes 1000 | tf_op jit(solution)/shard_map/mid/pallas_call | solution.py:497
  93.3 3.8 collective-permute-done.refs_7_
  97.1 2.3 collective-permute-done.3.refs_10_
  102.1 75.9 %experts.3 = (bf16[1024,1024]{1,0:T(8,128)(2,1)}, bf16[1024,1024]{1,0:T(8,128)(2,1)}, bf16[1024,1024]{1,0:T(8,128)(2,1)}, bf16[1024,1024]{1,0:T(8,128)(2,1)}, f3...) custom-call(s32[1]{0:T(128)} %bitcast.3.refs_0_, ...), custom_call_target="tpu_custom_call" | custom-call | flops 33600000000 | bytes 1000 | tf_op jit(solution)/shard_map/experts/pallas_call | solution.py:709
  180.1 2.8 collective-permute-done.8.refs_9_
  182.9 2.7 collective-permute-done.7.refs_8_
  185.6 45.6 %experts.4 = (bf16[1024,1024]{1,0:T(8,128)(2,1)}, bf16[1024,1024]{1,0:T(8,128)(2,1)}, bf16[1024,1024]{1,0:T(8,128)(2,1)}, bf16[1024,1024]{1,0:T(8,128)(2,1)}, f3...) custom-call(s32[1]{0:T(128)} %bitcast.3.refs_0_, ...), custom_call_target="tpu_custom_call" | custom-call | flops 16800000000 | bytes 1000 | tf_op jit(solution)/shard_map/experts/pallas_call | solution.py:709
  231.2 36.0 %weight_grad.2 = (bf16[4,2,2,128,512]{4,3,2,1,0:T(8,128)(2,1)}, bf16[4,2,2,128,512]{4,3,2,1,0:T(8,128)(2,1)}, bf16[4,2,128,512]{3,2,1,0:T(8,128)(2,1)}, bf16[4,2,128,512]{3,2,1,0:T(8,128)(2,1)}) custom-call(s32[1]{0:T(128)} %bitcast.8.dp_ref, bf16[1024,2048]{1,0:T(8,128)(2,1)} %get-tuple-element.140.refs_0_, bf16[1024,2048]{1,0:T(8,128)(2,1)} %get-tuple-element.113.refs_1_, ...), custom_call_target="tpu_custom_call" | custom-call | flops 12949999616 | bytes 1000 | tf_op jit(solution)/shard_map/weight_grad/pallas_call | solution.py:826
  267.2 55.2 %experts.5 = (bf16[1024,1024]{1,0:T(8,128)(2,1)}, bf16[1024,1024]{1,0:T(8,128)(2,1)}, bf16[1024,1024]{1,0:T(8,128)(2,1)}, bf16[1024,1024]{1,0:T(8,128)(2,1)}, f3...) custom-call(s32[1]{0:T(128)} %bitcast.3.refs_0_, ...), custom_call_target="tpu_custom_call" | custom-call | flops 16800000000 | bytes 1000 | tf_op jit(solution)/shard_map/experts/pallas_call | solution.py:709
  323.5 2.9 add_convert_fusion.refs_11_
  327.8 4.5 collective-permute-start.15
  333.3 3.9 add_convert_fusion.2
  338.8 1.9 multiply_convert_fusion
  342.2 36.3 %weight_grad.3 = (bf16[4,2,2,128,512]{4,3,2,1,0:T(8,128)(2,1)}, bf16[4,2,2,128,512]{4,3,2,1,0:T(8,128)(2,1)}, bf16[4,2,128,512]{3,2,1,0:T(8,128)(2,1)}, bf16[4,2,128,512]{3,2,1,0:T(8,128)(2,1)}) custom-call(s32[1]{0:T(128)} %bitcast.8.dp_ref, bf16[1024,2048]{1,0:T(8,128)(2,1)} %get-tuple-element.140.refs_0_, bf16[1024,2048]{1,0:T(8,128)(2,1)} %get-tuple-element.113.refs_1_, ...), custom_call_target="tpu_custom_call" | custom-call | flops 12949999616 | bytes 1000 | tf_op jit(solution)/shard_map/weight_grad/pallas_call | solution.py:826
  380.5 3.9 add_convert_fusion.3
  389.8 12.2 %back_mid.1 = (f32[1024,1024]{1,0:T(8,128)}, bf16[1024,1024]{1,0:T(8,128)(2,1)}, bf16[1024,1024]{1,0:T(8,128)(2,1)}, bf16[1024,128]{1,0:T(8,128)(2,1)}, f32[1,1024]{1,0:T(1,128)}) custom-call(s32[1]{0:T(128)} %bitcast.3.refs_0_, f32[1024,1024]{1,0:T(8,128)} %get-tuple-element.147.refs_1_, bf16[1024,1024]{1,0:T(8,128)(2,1)} %bitcast.27, s32[8,1024]{1,0:T(8,128)} %bitcast.33, ...), custom_call_target="tpu_custom_call" | custom-call | flops 3849999872 | bytes 1000 | tf_op jit(solution)/shard_map/back_mid/pallas_call | solution.py:883
  405.5 44.8 %attn_bwd.1 = (bf16[1024,1024]{1,0:T(8,128)(2,1)}, bf16[1024,512]{1,0:T(8,128)(2,1)}, bf16[1024,512]{1,0:T(8,128)(2,1)}, f32[2,128,512]{2,1,0:T(8,128)}, f32[2,128,512]{2,1,0:T(8,128)}, /*index=5*/f32[2,64,1024]{2,1,0:T(8,128)}) custom-call(s32[1]{0:T(128)S(6)} %copy.51.prefix_ref.refs_0_, bf16[1024,1024]{1,0:T(8,128)(2,1)} %get-tuple-element.95.q_ref.refs_1_, ...), custom_call_target="tpu_custom_call" | custom-call | flops 11550000128 | bytes 1000 | tf_op jit(solution)/shard_map/attn_bwd/pallas_call | solution.py:471
  450.4 5.4 convolution_convert_fusion.dout_ref
  455.8 5.2 fusion
  461.0 85.0 %finish.1 = (f32[128,1024]{1,0:T(8,128)}, f32[128,1024]{1,0:T(8,128)}, f32[128,1024]{1,0:T(8,128)}, f32[128,128]{1,0:T(8,128)}, f32[4,128,512]{2,1,0:T(8,128)}, ...) custom-call(bf16[1024,1024]{1,0:T(8,128)(2,1)} %get-tuple-element.137.ht_ref, ...), custom_call_target="tpu_custom_call" | custom-call | flops 20999999488 | bytes 1000 | tf_op jit(solution)/shard_map/finish/pallas_call | solution.py:1182
  549.1 4.9 copy.52
  (137 shorter events, 40.2 us)
Async XLA Ops:
  48.6 48.5 %collective-permute-start = (bf16[1024,1024]{1,0:T(8,128)(2,1)S(1)}, bf16[1024,1024]{1,0:T(8,128)(2,1)}, u32[]{:S(2)}, u32[]{:S(2)}) collective-permute-start(bf16[1024,1024]{1,0:T(8,128)(2,1)S(1)} %bitcast.28), channel_id=1, source_target_pairs={{0,2},{1,3},{2,0},{3,1},{4,6},{5,7},{6,4},{7,5},{8,10},{9,11},{10,... | collective-permute-start | bytes 6291464 | tf_op jit(solution)/shard_map/ppermute | solution.py:1315
  92.2 7.2 %collective-permute-start.1 = (bf16[1024,1024]{1,0:T(8,128)(2,1)}, bf16[1024,1024]{1,0:T(8,128)(2,1)S(1)}, u32[]{:S(2)}, u32[]{:S(2)}) collective-permute-start(bf16[1024,1024]{1,0:T(8,128)(2,1)} %get-tuple-element.102.refs_5_.refs_4_), channel_id=1, source_target_pairs={{0,1},{1,0},{2,3},{3,2},{4,5},{5,4},{6,7},{7,6},{8,9},{9,8},{10,11... | collective-permute-start | bytes 6291464 | tf_op jit(solution)/shard_map/ppermute | solution.py:1315
  92.2 7.1 %collective-permute-start.2 = (bf16[1024,1024]{1,0:T(8,128)(2,1)S(1)}, bf16[1024,1024]{1,0:T(8,128)(2,1)S(1)}, u32[]{:S(2)}, u32[]{:S(2)}) collective-permute-start(bf16[1024,1024]{1,0:T(8,128)(2,1)S(1)} %bitcast.29), channel_id=1, source_target_pairs={{0,1},{1,0},{2,3},{3,2},{4,5},{5,4},{6,7},{7,6},{8,9},{9,8},{10,11... | collective-permute-start | bytes 6291464 | tf_op jit(solution)/shard_map/ppermute | solution.py:1315
  92.7 6.7 %collective-permute-start.3 = (s32[8,1024]{1,0:T(8,128)S(1)}, s32[8,1024]{1,0:T(8,128)S(1)}, u32[]{:S(2)}, u32[]{:S(2)}) collective-permute-start(s32[8,1024]{1,0:T(8,128)S(1)} %bitcast.34), channel_id=1, source_target_pairs={{0,1},{1,0},{2,3},{3,2},{4,5},{5,4},{6,7},{7,6},{8,9},{9,8},{10,11... | collective-permute-start | bytes 98312 | tf_op jit(solution)/shard_map/ppermute | solution.py:1315
  92.8 85.2 %collective-permute-start.5 = (bf16[1024,1024]{1,0:T(8,128)(2,1)}, bf16[1024,1024]{1,0:T(8,128)(2,1)}, u32[]{:S(2)}, u32[]{:S(2)}) collective-permute-start(bf16[1024,1024]{1,0:T(8,128)(2,1)} %get-tuple-element.102.refs_5_.refs_4_), channel_id=1, source_target_pairs={{0,2},{1,3},{2,0},{3,1},{4,6},{5,7},{6,4},{7,5},{8,10},{9,11},{10,... | collective-permute-start | bytes 6291464 | tf_op jit(solution)/shard_map/ppermute | solution.py:1315
  102.1 76.5 %copy-start.16 = (s32[1,1024,8]{1,2,0:T(8,128)S(1)}, s32[1,1024,8]{1,2,0:T(8,128)}, u32[]{:S(2)}) copy-start(s32[1,1024,8]{1,2,0:T(8,128)} %param.20) | copy-start | bytes 98308
  178.0 4.8 collective-permute-start.6
  178.2 7.4 %collective-permute-start.7 = (bf16[1024,1024]{1,0:T(8,128)(2,1)}, bf16[1024,1024]{1,0:T(8,128)(2,1)}, u32[]{:S(2)}, u32[]{:S(2)}) collective-permute-start(bf16[1024,1024]{1,0:T(8,128)(2,1)} %collective-permute-done.refs_7_), channel_id=1, source_target_pairs={{0,1},{1,0},{2,3},{3,2},{4,5},{5,4},{6,7},{7,6},{8,9},{9,8},{10,11... | collective-permute-start | bytes 6291464 | tf_op jit(solution)/shard_map/ppermute | solution.py:1315
  178.6 4.3 collective-permute-start.8
  179.2 3.7 collective-permute-start.9
  267.2 55.5 %copy-start.20 = (f32[16]{0:T(128)S(1)}, f32[16]{0:T(128)}, u32[]{:S(2)}) copy-start(f32[16]{0:T(128)} %param.31) | copy-start | bytes 196
  322.4 10.9 %collective-permute-start.12 = (bf16[1024,1024]{1,0:T(8,128)(2,1)}, bf16[1024,1024]{1,0:T(8,128)(2,1)}, u32[]{:S(2)}, u32[]{:S(2)}) collective-permute-start(bf16[1024,1024]{1,0:T(8,128)(2,1)} %get-tuple-element.135), channel_id=1, source_target_pairs={{0,1},{1,0},{2,3},{3,2},{4,5},{5,4},{6,7},{7,6},{8,9},{9,8},{10,11... | collective-permute-start | bytes 6291464 | tf_op jit(solution)/shard_map/ppermute | solution.py:1315
  322.9 61.5 %collective-permute-start.11 = (bf16[1024,1024]{1,0:T(8,128)(2,1)}, bf16[1024,1024]{1,0:T(8,128)(2,1)}, u32[]{:S(2)}, u32[]{:S(2)}) collective-permute-start(bf16[1024,1024]{1,0:T(8,128)(2,1)} %get-tuple-element.133), channel_id=1, source_target_pairs={{0,1},{1,0},{2,3},{3,2},{4,5},{5,4},{6,7},{7,6},{8,9},{9,8},{10,11... | collective-permute-start | bytes 6291464 | tf_op jit(solution)/shard_map/ppermute | solution.py:1315
  323.4 55.2 %collective-permute-start.10 = (bf16[1024,1024]{1,0:T(8,128)(2,1)}, bf16[1024,1024]{1,0:T(8,128)(2,1)}, u32[]{:S(2)}, u32[]{:S(2)}) collective-permute-start(bf16[1024,1024]{1,0:T(8,128)(2,1)} %get-tuple-element.131), channel_id=1, source_target_pairs={{0,1},{1,0},{2,3},{3,2},{4,5},{5,4},{6,7},{7,6},{8,9},{9,8},{10,11... | collective-permute-start | bytes 6291464 | tf_op jit(solution)/shard_map/ppermute | solution.py:1315
  327.8 50.6 %collective-permute-start.15 = (bf16[2,2,2,128,512]{4,3,2,1,0:T(8,128)(2,1)S(1)}, bf16[2,2,2,128,512]{4,3,2,1,0:T(8,128)(2,1)}, u32[]{:S(2)}, u32[]{:S(2)}) collective-permute-start(bf16[2,2,2,128,512]{4,3,2,1,0:T(8,128)(2,1)S(1)} %constant_dynamic-slice_fusion), channel_id=1, source_target_pairs={{0,8},{4,12},{24,16},{28,20},{1,9},{5,13},{25,17},{29,21},{2,10},{... | collective-permute-start | bytes 3145736 | tf_op jit(solution)/shard_map/ppermute | solution.py:1456
  337.3 48.7 %collective-permute-start.13 = (bf16[1024,1024]{1,0:T(8,128)(2,1)}, bf16[1024,1024]{1,0:T(8,128)(2,1)}, u32[]{:S(2)}, u32[]{:S(2)}) collective-permute-start(bf16[1024,1024]{1,0:T(8,128)(2,1)} %add_convert_fusion.2), channel_id=1, source_target_pairs={{0,2},{1,3},{2,0},{3,1},{4,6},{5,7},{6,4},{7,5},{8,10},{9,11},{10,... | collective-permute-start | bytes 6291464 | tf_op jit(solution)/shard_map/ppermute | solution.py:1315
  340.7 38.5 %collective-permute-start.16 = (bf16[4,2,128,512]{3,2,1,0:T(8,128)(2,1)}, bf16[4,2,128,512]{3,2,1,0:T(8,128)(2,1)}, u32[]{:S(2)}, u32[]{:S(2)}) collective-permute-start(bf16[4,2,128,512]{3,2,1,0:T(8,128)(2,1)} %get-tuple-element.146), channel_id=1, source_target_pairs={{0,4},{4,0},{8,12},{12,8},{16,20},{20,16},{24,28},{28,24},{1,5},{5... | collective-permute-start | bytes 3145736 | tf_op jit(solution)/shard_map/ppermute | solution.py:1315
  378.5 8.6 %collective-permute-start.17 = (f32[8,1024]{1,0:T(8,128)S(1)}, f32[8,1024]{1,0:T(8,128)S(1)}, u32[]{:S(2)}, u32[]{:S(2)}) collective-permute-start(f32[8,1024]{1,0:T(8,128)S(1)} %copy-done.24), channel_id=1, source_target_pairs={{0,1},{1,0},{2,3},{3,2},{4,5},{5,4},{6,7},{7,6},{8,9},{9,8},{10,11... | collective-permute-start | bytes 98312 | tf_op jit(solution)/shard_map/ppermute | solution.py:1315
  378.6 9.4 %collective-permute-start.18 = (f32[8,1024]{1,0:T(8,128)S(1)}, f32[8,1024]{1,0:T(8,128)S(1)}, u32[]{:S(2)}, u32[]{:S(2)}) collective-permute-start(f32[8,1024]{1,0:T(8,128)S(1)} %copy-done.26), channel_id=1, source_target_pairs={{0,2},{1,3},{2,0},{3,1},{4,6},{5,7},{6,4},{7,5},{8,10},{9,11},{10,... | collective-permute-start | bytes 98312 | tf_op jit(solution)/shard_map/ppermute | solution.py:1315
  379.2 9.9 %collective-permute-start.19 = (f32[8,1024]{1,0:T(8,128)S(1)}, f32[8,1024]{1,0:T(8,128)S(1)}, u32[]{:S(2)}, u32[]{:S(2)}) collective-permute-start(f32[8,1024]{1,0:T(8,128)S(1)} %copy-done.25), channel_id=1, source_target_pairs={{0,3},{1,2},{2,1},{3,0},{4,7},{5,6},{6,5},{7,4},{8,11},{9,10},{10,... | collective-permute-start | bytes 98312 | tf_op jit(solution)/shard_map/ppermute | solution.py:1315
  384.4 71.4 %collective-permute-start.4 = (bf16[1024,1024]{1,0:T(8,128)(2,1)}, bf16[1024,1024]{1,0:T(8,128)(2,1)}, u32[]{:S(2)}, u32[]{:S(2)}) collective-permute-start(bf16[1024,1024]{1,0:T(8,128)(2,1)} %get-tuple-element.105), channel_id=1, source_target_pairs={{0,1},{1,0},{2,3},{3,2},{4,5},{5,4},{6,7},{7,6},{8,9},{9,8},{10,11... | collective-permute-start | bytes 6291464 | tf_op jit(solution)/shard_map/ppermute | solution.py:1315
  386.0 75.1 %collective-permute-start.20 = (bf16[4,2,2,128,512]{4,3,2,1,0:T(8,128)(2,1)}, bf16[4,2,2,128,512]{4,3,2,1,0:T(8,128)(2,1)}, u32[]{:S(2)}, u32[]{:S(2)}) collective-permute-start(bf16[4,2,2,128,512]{4,3,2,1,0:T(8,128)(2,1)} %get-tuple-element.160), channel_id=1, source_target_pairs={{0,4},{4,0},{8,12},{12,8},{16,20},{20,16},{24,28},{28,24},{1,5},{5... | collective-permute-start | bytes 6291464 | tf_op jit(solution)/shard_map/ppermute | solution.py:1315
  387.1 74.0 %collective-permute-start.21 = (bf16[4,2,128,512]{3,2,1,0:T(8,128)(2,1)}, bf16[4,2,128,512]{3,2,1,0:T(8,128)(2,1)}, u32[]{:S(2)}, u32[]{:S(2)}) collective-permute-start(bf16[4,2,128,512]{3,2,1,0:T(8,128)(2,1)} %get-tuple-element.162), channel_id=1, source_target_pairs={{0,4},{4,0},{8,12},{12,8},{16,20},{20,16},{24,28},{28,24},{1,5},{5... | collective-permute-start | bytes 3145736 | tf_op jit(solution)/shard_map/ppermute | solution.py:1315
  388.0 67.8 %collective-permute-start.14 = (bf16[1024,1024]{1,0:T(8,128)(2,1)}, bf16[1024,1024]{1,0:T(8,128)(2,1)}, u32[]{:S(2)}, u32[]{:S(2)}) collective-permute-start(bf16[1024,1024]{1,0:T(8,128)(2,1)} %add_convert_fusion.3), channel_id=1, source_target_pairs={{0,2},{1,3},{2,0},{3,1},{4,6},{5,7},{6,4},{7,5},{8,10},{9,11},{10,... | collective-permute-start | bytes 6291464 | tf_op jit(solution)/shard_map/ppermute | solution.py:1315
  (28 other events, 357.0 us)

commit v8 on v7

--- a/solution.py
+++ b/solution.py
@@ -963,7 +963,7 @@
 
 
 def finish_kernel(
-    gain_lane, ht_ref, dq_ref, dk_ref, dv_ref, dout_ref, small_ref, keep_ref, got_ref, down_keep_ref, down_got_ref,
+    gain_lane, ht_ref, dq_ref, dk_ref, dv_ref, ctx_ref, dattn_ref, small_ref, keep_ref, got_ref, down_keep_ref, down_got_ref,
     gate_a, up_a, down_a, w_ref, tok_ref, gain_ref, dres_ref,
     out_o, out_q, out_kv, out_small, gate_ref, up_ref, down_ref, gt_ref, *scratch,
 ):
@@ -999,7 +999,7 @@
             copy.start()
     greet(group + [over_x] + along)
 
-    widths = [dout_ref.shape[1], dq_ref.shape[1], dk_ref.shape[1] + dv_ref.shape[1], 128]
+    widths = [dattn_ref.shape[1], dq_ref.shape[1], dk_ref.shape[1] + dv_ref.shape[1], 128]
     outs = (out_o, out_q, out_kv, out_small)
     started = {}
 
@@ -1032,7 +1032,14 @@
 
     def step0(k):
         if k == 0:
-            place(k, slice(0, widths[k]), dout_ref[...])
+            for col in range(0, widths[0], 512):
+                part = lax.dot_general(
+                    ctx_ref[...],
+                    dattn_ref[:, col : col + 512],
+                    (((0,), (0,)), ((), ())),
+                    preferred_element_type=F32,
+                )
+                place(k, slice(col, col + 512), part.astype(BF16))
         elif k == 1:
             for col in range(0, widths[1], 512):
                 part = dot(ht_ref[...], dq_ref[:, col : col + 512])
@@ -1113,45 +1120,45 @@
         stored(r).start()
 
     done = tuple(ref.at[count:] for ref in (gate_ref, up_ref, down_ref))
-    step0(0)
     begin(0)
-    step1(0)
     step0(1)
     begin(1)
     step1(1)
     step0(2)
     begin(2)
     step1(2)
+    step0(0)
+    step1(0)
     back(0)
-    step2(0)
+    step2(1)
     line.middle_sends(0, True)
     back(1)
-    step2(1)
+    step2(2)
     back(2)
-    step3(0)
+    step3(1)
     line.middle_sends(1, True)
     line.middle_adds(0)
     back(3)
     step0(3)
-    step2(2)
+    step2(0)
     step1(3)
-    step3(1)
+    step3(2)
     line.middle_sends(2, True)
     line.middle_adds(1)
     step2(3)
-    step4(0)
-    step3(2)
+    step4(1)
+    step3(0)
     step3(3)
     line.result(0, done)
     line.middle_adds(2)
-    step4(1)
-    step5(0)
     step4(2)
+    step5(1)
+    step4(0)
     step4(3)
     line.result(1, done)
     line.result(2, done)
-    step5(1)
     step5(2)
+    step5(0)
     step5(3)
     for copy in halves:
         copy.wait()
@@ -1159,8 +1166,8 @@
         stored(r).wait()
 
 
-def run_finish(ht, dq, dk, dv, d_out, small, experts, w_all, tok, gain, d_res, gain_lane):
-    widths = [d_out.shape[1], dq.shape[1], dk.shape[1] + dv.shape[1], small.shape[1]]
+def run_finish(ht, dq, dk, dv, ctx, d_attn, small, experts, w_all, tok, gain, d_res, gain_lane):
+    widths = [d_attn.shape[1], dq.shape[1], dk.shape[1] + dv.shape[1], small.shape[1]]
     chunk = experts[2].shape
     _, count, rows, lanes = chunk
     vmem = pl.BlockSpec(memory_space=pltpu.VMEM)
@@ -1181,7 +1188,7 @@
     ]
     return pl.pallas_call(
         functools.partial(finish_kernel, gain_lane),
-        in_specs=[vmem] * 6 + [hbm] * 8 + [vmem] * 3,
+        in_specs=[vmem] * 7 + [hbm] * 8 + [vmem] * 3,
         out_specs=[vmem] * 7 + [hbm],
         out_shape=[
             *(jax.ShapeDtypeStruct((128, w), F32) for w in widths),
@@ -1196,7 +1203,7 @@
         ),
         cost_estimate=took(60),
         name="finish",
-    )(ht, dq, dk, dv, d_out, small, *experts, w_all, tok, gain, d_res)
+    )(ht, dq, dk, dv, ctx, d_attn, small, *experts, w_all, tok, gain, d_res)
 
 
 def gather_kernel(mine_ref, out_ref, sem_s, sem_r, sem_l):
@@ -1539,7 +1546,8 @@
             after(dq, block_out),
             dk,
             dv,
-            d_out_w,
+            ctx,
+            d_attn,
             small_grad,
             [made_two[0], got_two[0], made_two[2], got_two[1], *halves[:3]],
             w_all,

time: 567 us -> 565 us (level)
  matrix products: 7.14 us -> 0.76 us
    unnamed x69 -> x67, local copies, waits for them, and re-layouts: 17.2 us -> 17.8 us
  transfers between devices with their start and end apart: 22 -> 22, of which waited for: 5 -> 5; matrix products, arithmetic and copies ran while one was open for 6% -> 5% of each run, Pallas kernels for 37% -> 37%
where the time goes in v8:
time: 565 us; the launch traced here: 558 us
  Pallas kernels  476 us (84%)
  local copies, waits for them, and re-layouts  27.4 us (5%)
  other arithmetic  20.3 us (4%)
  starting transfers between devices  18 us (3%)
  waiting for transfers between devices  12.8 us (2%)
    pallas_call x3, Pallas kernels, run_expert(): pl.pallas_call(functools.partial(expert_kernel, first, local, num_experts...  177 us
    pallas_call x1, Pallas kernels, run_finish(): pl.pallas_call(functools.partial(finish_kernel, gain_lane), in_specs=[vme...  88.4 us
    pallas_call x2, Pallas kernels, run_weight_grad(): pl.pallas_call(functools.partial(weight_grad_kernel, n, paired), grid=(co...  72.3 us
    pallas_call x1, Pallas kernels, run_attn_bwd(): pl.pallas_call(kernel, grid=(groups,), in_specs=in_specs, out_specs=out_s...  44.6 us
    pallas_call x1, Pallas kernels, run_gather(): pl.pallas_call(gather_kernel, in_specs=[hbm], out_specs=hbm, out_shape=ja...  43.5 us
    pallas_call x1, Pallas kernels, run_attn_fwd(): pl.pallas_call(attn_fwd_kernel, grid=(groups,), in_specs=[pl.BlockSpec(me...  21.4 us
    unnamed x67, local copies, waits for them, and re-layouts  17.8 us
    ppermute x21, starting transfers between devices, swap(): return lax.ppermute(value, axis, [(i, i ^ step) for i in range(n)])  13.4 us
  transfers between devices with their start and end apart: 22, of which 5 were waited for; matrix products, arithmetic and copies ran while one was open for 5% of the time, Pallas kernels for 37%

profile of v8, /device:TPU:0, one launch (start us, length us, event | category | flops | bytes accessed | tf_op | source)
XLA Modules:
  0.0 557.7 jit_solution(8634243386722275417)
XLA Ops:
  5.1 43.5 %gather.1.w_ref.refs_1_.refs_5_.refs_7_ = bf16[1024,3200]{1,0:T(8,128)(2,1)} custom-call(bf16[32,3200]{1,0:T(8,128)(2,1)} %constant_dynamic-slice_fusion.1.mine_ref), custom_call_target="tpu_custom_call" | custom-call | flops 14000000000 | bytes 1000 | tf_op jit(solution)/shard_map/gather/pallas_call | solution.py:1285
  53.4 10.0 %qkv.1 = (bf16[1024,1024]{1,0:T(8,128)(2,1)}, bf16[1024,1024]{1,0:T(8,128)(2,1)}, bf16[1024,1024]{1,0:T(8,128)(2,1)}, bf16[1024,1024]{1,0:T(8,128)(2,1)}) custom-call(bf16[1024,1024]{1,0:T(8,128)(2,1)} %bitcast.21, bf16[1,1024]{1,0:T(2,128)(2,1)} %reshape_squeeze.9.gain_ref, bf16[1024,3200]{1,0:T(8,128)(2,1)} %gather.1.w_ref.refs_1_.refs_5_.refs_7_, ...), custom_call_target="tpu_custom_call" | custom-call | flops 3150000128 | bytes 1000 | tf_op jit(solution)/shard_map/qkv/pallas_call | solution.py:101
  63.4 21.4 %attn_fwd.1 = (bf16[1024,1024]{1,0:T(8,128)(2,1)}, f32[4,8,1024]{2,1,0:T(8,128)}, f32[4,8,128]{2,1,0:T(8,128)}) custom-call(s32[1]{0:T(128)S(6)} %copy.51.prefix_ref.refs_0_, bf16[1024,1024]{1,0:T(8,128)(2,1)} %get-tuple-element.95.q_ref.refs_1_, bf16[1024,1024]{1,0:T(8,128)(2,1)} %get-tuple-element.96.kd_ref.refs_2_, ...), custom_call_target="tpu_custom_call" | custom-call | flops 7350000128 | bytes 1000 | tf_op jit(solution)/shard_map/attn_fwd/pallas_call | solution.py:176
  84.8 7.2 %mid.1 = (f32[1024,1024]{1,0:T(8,128)}, bf16[1024,1024]{1,0:T(8,128)(2,1)}) custom-call(bf16[1024,1024]{1,0:T(8,128)(2,1)} %bitcast.22, bf16[1024,1024]{1,0:T(8,128)(2,1)} %get-tuple-element.98.ctx_ref.refs_5_, bf16[1024,3200]{1,0:T(8,128)(2,1)} %gather.1.w_ref.refs_1_.refs_5_.refs_7_, bf16[1,1024]{1,0:T(2,128)(2,1)} %reshape_squeeze.10.gain_ref.refs_6_), custom_call_target="tpu_custom_call" | custom-call | flops 1400000000 | bytes 1000 | tf_op jit(solution)/shard_map/mid/pallas_call | solution.py:497
  93.3 3.9 collective-permute-done.refs_7_
  97.2 2.1 collective-permute-done.3.refs_10_
  102.0 75.9 %experts.3 = (bf16[1024,1024]{1,0:T(8,128)(2,1)}, bf16[1024,1024]{1,0:T(8,128)(2,1)}, bf16[1024,1024]{1,0:T(8,128)(2,1)}, bf16[1024,1024]{1,0:T(8,128)(2,1)}, f3...) custom-call(s32[1]{0:T(128)} %bitcast.3.refs_0_, ...), custom_call_target="tpu_custom_call" | custom-call | flops 33600000000 | bytes 1000 | tf_op jit(solution)/shard_map/experts/pallas_call | solution.py:709
  180.0 2.8 collective-permute-done.8.refs_9_
  182.8 2.7 collective-permute-done.7.refs_8_
  185.5 45.6 %experts.4 = (bf16[1024,1024]{1,0:T(8,128)(2,1)}, bf16[1024,1024]{1,0:T(8,128)(2,1)}, bf16[1024,1024]{1,0:T(8,128)(2,1)}, bf16[1024,1024]{1,0:T(8,128)(2,1)}, f3...) custom-call(s32[1]{0:T(128)} %bitcast.3.refs_0_, ...), custom_call_target="tpu_custom_call" | custom-call | flops 16800000000 | bytes 1000 | tf_op jit(solution)/shard_map/experts/pallas_call | solution.py:709
  231.1 36.0 %weight_grad.2 = (bf16[4,2,2,128,512]{4,3,2,1,0:T(8,128)(2,1)}, bf16[4,2,2,128,512]{4,3,2,1,0:T(8,128)(2,1)}, bf16[4,2,128,512]{3,2,1,0:T(8,128)(2,1)}, bf16[4,2,128,512]{3,2,1,0:T(8,128)(2,1)}) custom-call(s32[1]{0:T(128)} %bitcast.8.dp_ref, bf16[1024,2048]{1,0:T(8,128)(2,1)} %get-tuple-element.140.refs_0_, bf16[1024,2048]{1,0:T(8,128)(2,1)} %get-tuple-element.113.refs_1_, ...), custom_call_target="tpu_custom_call" | custom-call | flops 12949999616 | bytes 1000 | tf_op jit(solution)/shard_map/weight_grad/pallas_call | solution.py:826
  267.1 55.2 %experts.5 = (bf16[1024,1024]{1,0:T(8,128)(2,1)}, bf16[1024,1024]{1,0:T(8,128)(2,1)}, bf16[1024,1024]{1,0:T(8,128)(2,1)}, bf16[1024,1024]{1,0:T(8,128)(2,1)}, f3...) custom-call(s32[1]{0:T(128)} %bitcast.3.refs_0_, ...), custom_call_target="tpu_custom_call" | custom-call | flops 16800000000 | bytes 1000 | tf_op jit(solution)/shard_map/experts/pallas_call | solution.py:709
  323.4 2.9 add_convert_fusion.refs_11_
  327.7 4.5 collective-permute-start.15
  333.2 3.9 add_convert_fusion.2
  338.7 1.9 multiply_convert_fusion
  342.0 36.3 %weight_grad.3 = (bf16[4,2,2,128,512]{4,3,2,1,0:T(8,128)(2,1)}, bf16[4,2,2,128,512]{4,3,2,1,0:T(8,128)(2,1)}, bf16[4,2,128,512]{3,2,1,0:T(8,128)(2,1)}, bf16[4,2,128,512]{3,2,1,0:T(8,128)(2,1)}) custom-call(s32[1]{0:T(128)} %bitcast.8.dp_ref, bf16[1024,2048]{1,0:T(8,128)(2,1)} %get-tuple-element.140.refs_0_, bf16[1024,2048]{1,0:T(8,128)(2,1)} %get-tuple-element.113.refs_1_, ...), custom_call_target="tpu_custom_call" | custom-call | flops 12949999616 | bytes 1000 | tf_op jit(solution)/shard_map/weight_grad/pallas_call | solution.py:826
  380.3 3.9 add_convert_fusion.3
  389.6 12.3 %back_mid.1 = (f32[1024,1024]{1,0:T(8,128)}, bf16[1024,1024]{1,0:T(8,128)(2,1)}, bf16[1024,1024]{1,0:T(8,128)(2,1)}, bf16[1024,128]{1,0:T(8,128)(2,1)}, f32[1,1024]{1,0:T(1,128)}) custom-call(s32[1]{0:T(128)} %bitcast.3.refs_0_, f32[1024,1024]{1,0:T(8,128)} %get-tuple-element.147.refs_1_, bf16[1024,1024]{1,0:T(8,128)(2,1)} %bitcast.25, s32[8,1024]{1,0:T(8,128)} %bitcast.31, ...), custom_call_target="tpu_custom_call" | custom-call | flops 3849999872 | bytes 1000 | tf_op jit(solution)/shard_map/back_mid/pallas_call | solution.py:883
  402.8 44.6 %attn_bwd.1 = (bf16[1024,1024]{1,0:T(8,128)(2,1)}, bf16[1024,512]{1,0:T(8,128)(2,1)}, bf16[1024,512]{1,0:T(8,128)(2,1)}, f32[2,128,512]{2,1,0:T(8,128)}, f32[2,128,512]{2,1,0:T(8,128)}, /*index=5*/f32[2,64,1024]{2,1,0:T(8,128)}) custom-call(s32[1]{0:T(128)S(6)} %copy.51.prefix_ref.refs_0_, bf16[1024,1024]{1,0:T(8,128)(2,1)} %get-tuple-element.95.q_ref.refs_1_, ...), custom_call_target="tpu_custom_call" | custom-call | flops 11550000128 | bytes 1000 | tf_op jit(solution)/shard_map/attn_bwd/pallas_call | solution.py:471
  449.7 5.8 %fusion = bf16[1,1024,1024]{2,1,0:T(8,128)(2,1)} fusion(bf16[1024,1024]{1,0:T(8,128)(2,1)} %collective-permute-done.14, bf16[1024,1024]{1,0:T(8,128)(2,1)} %collective-permute-done.4, f32[1024,1024]{1,0:T(8,128)S(1)} %copy-done, bf16[1024,1024]{1,0:T(8,128)(2,1)} %get-tuple-element.104), kind=kLoop, calls=%fused_computation.4 | loop fusion | flops 7340032 | bytes 12582912 | tf_op jit(solution)/shard_map/reshape | solution.py:1497
  455.6 88.4 %finish.1 = (f32[128,1024]{1,0:T(8,128)}, f32[128,1024]{1,0:T(8,128)}, f32[128,1024]{1,0:T(8,128)}, f32[128,128]{1,0:T(8,128)}, f32[4,128,512]{2,1,0:T(8,128)}, ...) custom-call(bf16[1024,1024]{1,0:T(8,128)(2,1)} %get-tuple-element.137.ht_ref, ...), custom_call_target="tpu_custom_call" | custom-call | flops 20999999488 | bytes 1000 | tf_op jit(solution)/shard_map/finish/pallas_call | solution.py:1189
  543.9 1.6 slice_reduce_fusion.2
  547.1 4.9 copy.52
  (134 shorter events, 38.2 us)
Async XLA Ops:
  48.6 48.6 %collective-permute-start = (bf16[1024,1024]{1,0:T(8,128)(2,1)S(1)}, bf16[1024,1024]{1,0:T(8,128)(2,1)}, u32[]{:S(2)}, u32[]{:S(2)}) collective-permute-start(bf16[1024,1024]{1,0:T(8,128)(2,1)S(1)} %bitcast.26), channel_id=1, source_target_pairs={{0,2},{1,3},{2,0},{3,1},{4,6},{5,7},{6,4},{7,5},{8,10},{9,11},{10,... | collective-permute-start | bytes 6291464 | tf_op jit(solution)/shard_map/ppermute | solution.py:1322
  92.1 7.2 %collective-permute-start.1 = (bf16[1024,1024]{1,0:T(8,128)(2,1)}, bf16[1024,1024]{1,0:T(8,128)(2,1)S(1)}, u32[]{:S(2)}, u32[]{:S(2)}) collective-permute-start(bf16[1024,1024]{1,0:T(8,128)(2,1)} %get-tuple-element.102.refs_5_.refs_4_), channel_id=1, source_target_pairs={{0,1},{1,0},{2,3},{3,2},{4,5},{5,4},{6,7},{7,6},{8,9},{9,8},{10,11... | collective-permute-start | bytes 6291464 | tf_op jit(solution)/shard_map/ppermute | solution.py:1322
  92.2 7.1 %collective-permute-start.2 = (bf16[1024,1024]{1,0:T(8,128)(2,1)S(1)}, bf16[1024,1024]{1,0:T(8,128)(2,1)S(1)}, u32[]{:S(2)}, u32[]{:S(2)}) collective-permute-start(bf16[1024,1024]{1,0:T(8,128)(2,1)S(1)} %bitcast.27), channel_id=1, source_target_pairs={{0,1},{1,0},{2,3},{3,2},{4,5},{5,4},{6,7},{7,6},{8,9},{9,8},{10,11... | collective-permute-start | bytes 6291464 | tf_op jit(solution)/shard_map/ppermute | solution.py:1322
  92.6 6.7 %collective-permute-start.3 = (s32[8,1024]{1,0:T(8,128)S(1)}, s32[8,1024]{1,0:T(8,128)S(1)}, u32[]{:S(2)}, u32[]{:S(2)}) collective-permute-start(s32[8,1024]{1,0:T(8,128)S(1)} %bitcast.32), channel_id=1, source_target_pairs={{0,1},{1,0},{2,3},{3,2},{4,5},{5,4},{6,7},{7,6},{8,9},{9,8},{10,11... | collective-permute-start | bytes 98312 | tf_op jit(solution)/shard_map/ppermute | solution.py:1322
  92.7 85.2 %collective-permute-start.5 = (bf16[1024,1024]{1,0:T(8,128)(2,1)}, bf16[1024,1024]{1,0:T(8,128)(2,1)}, u32[]{:S(2)}, u32[]{:S(2)}) collective-permute-start(bf16[1024,1024]{1,0:T(8,128)(2,1)} %get-tuple-element.102.refs_5_.refs_4_), channel_id=1, source_target_pairs={{0,2},{1,3},{2,0},{3,1},{4,6},{5,7},{6,4},{7,5},{8,10},{9,11},{10,... | collective-permute-start | bytes 6291464 | tf_op jit(solution)/shard_map/ppermute | solution.py:1322
  102.0 76.5 %copy-start.15 = (s32[1,1024,8]{1,2,0:T(8,128)S(1)}, s32[1,1024,8]{1,2,0:T(8,128)}, u32[]{:S(2)}) copy-start(s32[1,1024,8]{1,2,0:T(8,128)} %param.20) | copy-start | bytes 98308
  177.9 4.8 collective-permute-start.6
  178.1 7.4 %collective-permute-start.7 = (bf16[1024,1024]{1,0:T(8,128)(2,1)}, bf16[1024,1024]{1,0:T(8,128)(2,1)}, u32[]{:S(2)}, u32[]{:S(2)}) collective-permute-start(bf16[1024,1024]{1,0:T(8,128)(2,1)} %collective-permute-done.refs_7_), channel_id=1, source_target_pairs={{0,1},{1,0},{2,3},{3,2},{4,5},{5,4},{6,7},{7,6},{8,9},{9,8},{10,11... | collective-permute-start | bytes 6291464 | tf_op jit(solution)/shard_map/ppermute | solution.py:1322
  178.5 4.3 collective-permute-start.8
  179.1 3.7 collective-permute-start.9
  267.1 55.5 %copy-start.19 = (f32[16]{0:T(128)S(1)}, f32[16]{0:T(128)}, u32[]{:S(2)}) copy-start(f32[16]{0:T(128)} %param.31) | copy-start | bytes 196
  322.3 10.9 %collective-permute-start.12 = (bf16[1024,1024]{1,0:T(8,128)(2,1)}, bf16[1024,1024]{1,0:T(8,128)(2,1)}, u32[]{:S(2)}, u32[]{:S(2)}) collective-permute-start(bf16[1024,1024]{1,0:T(8,128)(2,1)} %get-tuple-element.135), channel_id=1, source_target_pairs={{0,1},{1,0},{2,3},{3,2},{4,5},{5,4},{6,7},{7,6},{8,9},{9,8},{10,11... | collective-permute-start | bytes 6291464 | tf_op jit(solution)/shard_map/ppermute | solution.py:1322
  322.8 61.5 %collective-permute-start.11 = (bf16[1024,1024]{1,0:T(8,128)(2,1)}, bf16[1024,1024]{1,0:T(8,128)(2,1)}, u32[]{:S(2)}, u32[]{:S(2)}) collective-permute-start(bf16[1024,1024]{1,0:T(8,128)(2,1)} %get-tuple-element.133), channel_id=1, source_target_pairs={{0,1},{1,0},{2,3},{3,2},{4,5},{5,4},{6,7},{7,6},{8,9},{9,8},{10,11... | collective-permute-start | bytes 6291464 | tf_op jit(solution)/shard_map/ppermute | solution.py:1322
  323.3 55.1 %collective-permute-start.10 = (bf16[1024,1024]{1,0:T(8,128)(2,1)}, bf16[1024,1024]{1,0:T(8,128)(2,1)}, u32[]{:S(2)}, u32[]{:S(2)}) collective-permute-start(bf16[1024,1024]{1,0:T(8,128)(2,1)} %get-tuple-element.131), channel_id=1, source_target_pairs={{0,1},{1,0},{2,3},{3,2},{4,5},{5,4},{6,7},{7,6},{8,9},{9,8},{10,11... | collective-permute-start | bytes 6291464 | tf_op jit(solution)/shard_map/ppermute | solution.py:1322
  327.7 50.6 %collective-permute-start.15 = (bf16[2,2,2,128,512]{4,3,2,1,0:T(8,128)(2,1)S(1)}, bf16[2,2,2,128,512]{4,3,2,1,0:T(8,128)(2,1)}, u32[]{:S(2)}, u32[]{:S(2)}) collective-permute-start(bf16[2,2,2,128,512]{4,3,2,1,0:T(8,128)(2,1)S(1)} %constant_dynamic-slice_fusion), channel_id=1, source_target_pairs={{0,8},{4,12},{24,16},{28,20},{1,9},{5,13},{25,17},{29,21},{2,10},{... | collective-permute-start | bytes 3145736 | tf_op jit(solution)/shard_map/ppermute | solution.py:1463
  337.1 48.7 %collective-permute-start.13 = (bf16[1024,1024]{1,0:T(8,128)(2,1)}, bf16[1024,1024]{1,0:T(8,128)(2,1)}, u32[]{:S(2)}, u32[]{:S(2)}) collective-permute-start(bf16[1024,1024]{1,0:T(8,128)(2,1)} %add_convert_fusion.2), channel_id=1, source_target_pairs={{0,2},{1,3},{2,0},{3,1},{4,6},{5,7},{6,4},{7,5},{8,10},{9,11},{10,... | collective-permute-start | bytes 6291464 | tf_op jit(solution)/shard_map/ppermute | solution.py:1322
  340.5 38.5 %collective-permute-start.16 = (bf16[4,2,128,512]{3,2,1,0:T(8,128)(2,1)}, bf16[4,2,128,512]{3,2,1,0:T(8,128)(2,1)}, u32[]{:S(2)}, u32[]{:S(2)}) collective-permute-start(bf16[4,2,128,512]{3,2,1,0:T(8,128)(2,1)} %get-tuple-element.146), channel_id=1, source_target_pairs={{0,4},{4,0},{8,12},{12,8},{16,20},{20,16},{24,28},{28,24},{1,5},{5... | collective-permute-start | bytes 3145736 | tf_op jit(solution)/shard_map/ppermute | solution.py:1322
  378.4 8.6 %collective-permute-start.17 = (f32[8,1024]{1,0:T(8,128)S(1)}, f32[8,1024]{1,0:T(8,128)S(1)}, u32[]{:S(2)}, u32[]{:S(2)}) collective-permute-start(f32[8,1024]{1,0:T(8,128)S(1)} %copy-done.23), channel_id=1, source_target_pairs={{0,1},{1,0},{2,3},{3,2},{4,5},{5,4},{6,7},{7,6},{8,9},{9,8},{10,11... | collective-permute-start | bytes 98312 | tf_op jit(solution)/shard_map/ppermute | solution.py:1322
  378.5 9.4 %collective-permute-start.18 = (f32[8,1024]{1,0:T(8,128)S(1)}, f32[8,1024]{1,0:T(8,128)S(1)}, u32[]{:S(2)}, u32[]{:S(2)}) collective-permute-start(f32[8,1024]{1,0:T(8,128)S(1)} %copy-done.25), channel_id=1, source_target_pairs={{0,2},{1,3},{2,0},{3,1},{4,6},{5,7},{6,4},{7,5},{8,10},{9,11},{10,... | collective-permute-start | bytes 98312 | tf_op jit(solution)/shard_map/ppermute | solution.py:1322
  379.0 10.0 %collective-permute-start.19 = (f32[8,1024]{1,0:T(8,128)S(1)}, f32[8,1024]{1,0:T(8,128)S(1)}, u32[]{:S(2)}, u32[]{:S(2)}) collective-permute-start(f32[8,1024]{1,0:T(8,128)S(1)} %copy-done.24), channel_id=1, source_target_pairs={{0,3},{1,2},{2,1},{3,0},{4,7},{5,6},{6,5},{7,4},{8,11},{9,10},{10,... | collective-permute-start | bytes 98312 | tf_op jit(solution)/shard_map/ppermute | solution.py:1322
  384.2 64.9 %collective-permute-start.4 = (bf16[1024,1024]{1,0:T(8,128)(2,1)}, bf16[1024,1024]{1,0:T(8,128)(2,1)}, u32[]{:S(2)}, u32[]{:S(2)}) collective-permute-start(bf16[1024,1024]{1,0:T(8,128)(2,1)} %get-tuple-element.105), channel_id=1, source_target_pairs={{0,1},{1,0},{2,3},{3,2},{4,5},{5,4},{6,7},{7,6},{8,9},{9,8},{10,11... | collective-permute-start | bytes 6291464 | tf_op jit(solution)/shard_map/ppermute | solution.py:1322
  385.9 69.7 %collective-permute-start.20 = (bf16[4,2,2,128,512]{4,3,2,1,0:T(8,128)(2,1)}, bf16[4,2,2,128,512]{4,3,2,1,0:T(8,128)(2,1)}, u32[]{:S(2)}, u32[]{:S(2)}) collective-permute-start(bf16[4,2,2,128,512]{4,3,2,1,0:T(8,128)(2,1)} %get-tuple-element.160), channel_id=1, source_target_pairs={{0,4},{4,0},{8,12},{12,8},{16,20},{20,16},{24,28},{28,24},{1,5},{5... | collective-permute-start | bytes 6291464 | tf_op jit(solution)/shard_map/ppermute | solution.py:1322
  386.9 68.6 %collective-permute-start.21 = (bf16[4,2,128,512]{3,2,1,0:T(8,128)(2,1)}, bf16[4,2,128,512]{3,2,1,0:T(8,128)(2,1)}, u32[]{:S(2)}, u32[]{:S(2)}) collective-permute-start(bf16[4,2,128,512]{3,2,1,0:T(8,128)(2,1)} %get-tuple-element.162), channel_id=1, source_target_pairs={{0,4},{4,0},{8,12},{12,8},{16,20},{20,16},{24,28},{28,24},{1,5},{5... | collective-permute-start | bytes 3145736 | tf_op jit(solution)/shard_map/ppermute | solution.py:1322
  387.9 61.2 %collective-permute-start.14 = (bf16[1024,1024]{1,0:T(8,128)(2,1)}, bf16[1024,1024]{1,0:T(8,128)(2,1)}, u32[]{:S(2)}, u32[]{:S(2)}) collective-permute-start(bf16[1024,1024]{1,0:T(8,128)(2,1)} %add_convert_fusion.3), channel_id=1, source_target_pairs={{0,2},{1,3},{2,0},{3,1},{4,6},{5,7},{6,4},{7,5},{8,10},{9,11},{10,... | collective-permute-start | bytes 6291464 | tf_op jit(solution)/shard_map/ppermute | solution.py:1322
  (27 other events, 376.8 us)
